TPU v7x, 32 devices: a whole 2x2x4 slice. The times are simulated.
32 devices in a mesh: seq: 4 (over z), exp: 8 (over y, x, core).
Axes of the slice: x: 2, y: 2, z: 4, core: 2. Of those that a mesh axis runs over, the one named last changes fastest.
Arguments:
- tokens: bfloat16 [8192, 4096], P(('seq', 'exp')), may hold values from -3 to 3
- cotangent: bfloat16 [8192, 4096], P(('seq', 'exp')), may hold values from -2 to 2
- router: bfloat16 [4096, 8], replicated, may hold values from -0.09375 to 0.09375
- threshold: float32 [8], replicated, may hold values from -1 to 1
- w_gate: bfloat16 [8, 4096, 1536], P('exp', None, 'seq'), may hold values from -0.09375 to 0.09375
- w_up: bfloat16 [8, 4096, 1536], P('exp', None, 'seq'), may hold values from -0.09375 to 0.09375
- w_down: bfloat16 [8, 1536, 4096], P('exp', 'seq'), may hold values from -0.15625 to 0.15625
- hid_scale: float32 [8, 1536], P('exp', 'seq'), may hold values from 0.5 to 2
- picks: int32 [32, 8, 4], P(('seq', 'exp')), may hold values from 0 to 255, as said below
- counts: int32 [32, 8], P(('seq', 'exp')), may hold values from 1 to 4, as said below
Outputs:
- mixture: bfloat16 [8192, 4096], P(('seq', 'exp'))
- token_grad: bfloat16 [8192, 4096], P(('seq', 'exp'))
- router_grad: float32 [4096, 8], P(('seq', 'exp'))
- threshold_grad: float32 [8], replicated
- gate_grad: float32 [8, 4096, 1536], P('exp', None, 'seq')
- up_grad: float32 [8, 4096, 1536], P('exp', None, 'seq')
- down_grad: float32 [8, 1536, 4096], P('exp', 'seq')
Inputs may be any that keep to these rules, and one draw needn't show every extreme that they name: Each list picks[p, e] holds 4 distinct local rows of owner p. `counts`: for every expert some owner fills all 4 slots.
All inputs are finite; a program needn't handle non-finite values.
Results may differ from a plain program's by a relative error of at most 0.018.
Values may be sent and summed in bfloat16 or wider, within the bound.
No kernel may reach another device: no remote copies, remote signals or barrier semaphores. Data moves between devices by JAX's collectives and lax.ppermute only.
A program may use at most 128 MiB of HBM per device.

v0:
```python
import jax
import jax.numpy as jnp
from jax import lax
from jax.sharding import PartitionSpec as P


def on_device(tokens, cotangent, router, threshold, w_gate, w_up, w_down, hid_scale, picks, counts):
    experts = router.shape[1]
    slot_count = picks.shape[2]
    features = tokens.shape[1]
    row_count = tokens.shape[0]
    seq_count = lax.axis_size("seq")
    chosen = picks[0]
    active = (jnp.arange(slot_count, dtype=jnp.int32)[None, :] < counts[0][:, None]).astype(
        jnp.float32
    )
    scores = jnp.dot(tokens, router, preferred_element_type=jnp.float32)
    gates_all = jax.nn.sigmoid(scores - threshold[None, :])
    column = jnp.broadcast_to(jnp.arange(experts, dtype=jnp.int32)[:, None], (experts, slot_count))
    raw_gate = gates_all[chosen, column]
    gate_value = raw_gate * active
    picked_rows = tokens[chosen]
    picked_cot = cotangent[chosen].astype(jnp.float32)
    scaled_cot = (picked_cot * gate_value[:, :, None]).astype(jnp.bfloat16)
    stacked = jnp.stack([picked_rows, scaled_cot], axis=1)
    copies = jnp.tile(stacked, (seq_count, 1, 1, 1))
    arrived = lax.all_to_all(copies, ("seq", "exp"), split_axis=0, concat_axis=2, tiled=True)
    expert_rows = arrived[0, 0]
    expert_cot = arrived[0, 1]
    gate_mat = w_gate[0]
    up_mat = w_up[0]
    down_mat = w_down[0]
    scale_row = hid_scale[0][None, :]
    pre_gate = jnp.dot(expert_rows, gate_mat, preferred_element_type=jnp.float32)
    pre_up = jnp.dot(expert_rows, up_mat, preferred_element_type=jnp.float32)
    sigmoid_val = jax.nn.sigmoid(pre_gate)
    activated = pre_gate * sigmoid_val
    hidden = (activated * pre_up * scale_row).astype(jnp.bfloat16)
    scaled_grad = jnp.dot(expert_cot, down_mat.T, preferred_element_type=jnp.float32) * scale_row
    gate_delta = (
        scaled_grad * pre_up * sigmoid_val * (1.0 + pre_gate * (1.0 - sigmoid_val))
    ).astype(jnp.bfloat16)
    up_delta = (scaled_grad * activated).astype(jnp.bfloat16)
    contract_rows = (((0,), (0,)), ((), ()))
    down_grad = lax.dot_general(
        hidden, expert_cot, contract_rows, preferred_element_type=jnp.float32
    )
    gate_grad = lax.dot_general(
        expert_rows, gate_delta, contract_rows, preferred_element_type=jnp.float32
    )
    up_grad = lax.dot_general(
        expert_rows, up_delta, contract_rows, preferred_element_type=jnp.float32
    )
    out_mine = lax.psum_scatter(
        jnp.dot(hidden, down_mat, preferred_element_type=jnp.float32).astype(jnp.bfloat16),
        "seq",
        scatter_dimension=0,
        tiled=True,
    )
    contract_hidden = (((1,), (1,)), ((), ()))
    first_term = lax.dot_general(
        gate_delta, gate_mat, contract_hidden, preferred_element_type=jnp.float32
    )
    grad_mine = lax.psum_scatter(
        (
            first_term
            + lax.dot_general(up_delta, up_mat, contract_hidden, preferred_element_type=jnp.float32)
        ).astype(jnp.bfloat16),
        "seq",
        scatter_dimension=0,
        tiled=True,
    )
    packed = jnp.stack([out_mine, grad_mine]).reshape(2, experts, slot_count, features)
    returned = lax.all_to_all(packed, "exp", split_axis=1, concat_axis=1, tiled=True)
    out_wide = returned[0].astype(jnp.float32)
    flat_index = chosen.reshape(-1)
    mixture = (
        jnp.zeros((row_count, features), jnp.float32)
        .at[flat_index]
        .add((gate_value[:, :, None] * out_wide).reshape(-1, features))
    )
    gate_pull = active * jnp.sum(picked_cot * out_wide, axis=-1)
    score_pick = gate_pull * raw_gate * (1.0 - raw_gate)
    score_grad = jnp.zeros((row_count, experts), jnp.float32).at[chosen, column].add(score_pick)
    token_grad = (
        jnp.zeros((row_count, features), jnp.float32)
        .at[flat_index]
        .add(returned[1].astype(jnp.float32).reshape(-1, features))
    )
    token_grad = token_grad + jnp.dot(
        score_grad, router.astype(jnp.float32).T, precision=lax.Precision.HIGHEST
    )
    router_term = jnp.dot(tokens.astype(jnp.float32).T, score_grad, precision=lax.Precision.HIGHEST)
    router_grad = lax.psum_scatter(router_term, ("seq", "exp"), scatter_dimension=0, tiled=True)
    threshold_grad = -lax.psum(jnp.sum(score_grad, axis=0), ("seq", "exp"))
    return (
        mixture.astype(jnp.bfloat16),
        token_grad.astype(jnp.bfloat16),
        router_grad,
        threshold_grad,
        gate_grad[None],
        up_grad[None],
        down_grad[None],
    )


def solution(mesh):
    placed = (
        P(("seq", "exp"), None),
        P(("seq", "exp"), None),
        P(),
        P(),
        P("exp", None, "seq"),
        P("exp", None, "seq"),
        P("exp", "seq", None),
        P("exp", "seq"),
        P(("seq", "exp"), None, None),
        P(("seq", "exp"), None),
    )
    return jax.shard_map(
        on_device,
        mesh=mesh,
        in_specs=placed,
        out_specs=(
            P(("seq", "exp"), None),
            P(("seq", "exp"), None),
            P(("seq", "exp"), None),
            P(),
            P("exp", None, "seq"),
            P("exp", None, "seq"),
            P("exp", "seq", None),
        ),
        check_vma=False,
    )
```

profile of v0, /device:TPU:0, one launch (start us, length us, event | category | flops | bytes accessed | tf_op | source)
XLA Modules:
  0.0 362.1 jit_solution(6575650195036713064)
XLA Ops:
  7.2 0.8 fusion.36
  8.4 2.3 fusion.19
  10.7 0.7 gather_fusion
  11.5 3.5 gather_fusion.1
  15.0 2.8 gather_fusion.2
  17.8 1.8 stack.16
  19.6 1.0 reshape.152
  20.6 1.2 multiply_convert_fusion
  21.8 1.3 pad_maximum_fusion
  23.1 0.5 copy.35
  23.7 3.4 tile.4
  27.1 7.4 %all-to-all-start = ((bf16[32,2,4,4096]{3,1,2,0:T(2,128)(2,1)}), bf16[32,2,4,4096]{3,1,2,0:T(2,128)(2,1)}, u32[]{:S(2)}, u32[]{:S(2)}) async-start(bf16[32,2,4,4096]{3,1,2,0:T(2,128)(2,1)} %bitcast.86), calls=%async_computation | async-start | bytes 4194304 | tf_op jit(solution)/shard_map/all_to_all | solution.py:27
  34.6 48.8 %all-to-all-done = bf16[32,2,4,4096]{3,1,2,0:T(2,128)(2,1)} async-done(((bf16[32,2,4,4096]{3,1,2,0:T(2,128)(2,1)}), bf16[32,2,4,4096]{3,1,2,0:T(2,128)(2,1)}, u32[]{:S(2)}, u32[]{:S(2)}) %all-to-all-start) | async-done | bytes 2097184 | tf_op jit(solution)/shard_map/all_to_all | solution.py:27
  83.4 6.1 %fusion.38 = (bf16[1,1,128,4096]{3,1,2,0:T(2,128)(2,1)S(1)}, bf16[1,1,128,4096]{3,1,2,0:T(2,128)(2,1)S(1)}) fusion(bf16[1,2,128,4096]{3,1,2,0:T(2,128)(2,1)} %bitcast.6), kind=kLoop, calls=%fused_computation.68 | loop fusion | bytes 4194304 | tf_op jit(solution)/shard_map/slice | solution.py:29
  89.6 1.2 copy.39
  90.8 1.4 copy-done.4
  92.2 0.8 fusion.9
  93.0 0.2 copy-done.3
  93.2 1.7 fusion.13
  94.9 1.5 multiply_convert_fusion.3
  96.3 1.7 convolution_convert_fusion
  98.0 0.2 reduce-scatter.6.cloned.1.call-start
  98.3 3.1 fusion.7
  101.4 2.1 fusion
  103.7 1.0 reshape.203
  104.9 19.8 %reduce-scatter.4.cloned.1.call-done = bf16[32,4096]{1,0:T(8,128)(2,1)} async-done(((bf16[128,4096]{1,0:T(8,128)(2,1)}), bf16[32,4096]{1,0:T(8,128)(2,1)}) %reduce-scatter.4.cloned.1.call-update) | async-done | bytes 262160 | tf_op jit(solution)/shard_map/reduce_scatter | solution.py:54
  124.8 1.1 stack.18
  125.8 27.7 %reduce-scatter.6.cloned.1.call-done = bf16[32,4096]{1,0:T(8,128)(2,1)} async-done(((bf16[128,4096]{1,0:T(8,128)(2,1)}), bf16[32,4096]{1,0:T(8,128)(2,1)}) %reduce-scatter.6.cloned.1.call-update) | async-done | bytes 262160 | tf_op jit(solution)/shard_map/reduce_scatter | solution.py:64
  153.6 1.8 stack.19
  155.3 2.1 pad_maximum_fusion.1
  157.4 4.2 %all-to-all-start.1 = ((bf16[2,8,4,4096]{3,2,0,1:T(4,128)(2,1)}), bf16[2,8,4,4096]{3,2,0,1:T(4,128)(2,1)}, u32[]{:S(2)}, u32[]{:S(2)}) async-start(bf16[2,8,4,4096]{3,2,0,1:T(4,128)(2,1)} %pad_maximum_fusion.1), calls=%async_computation.3 | async-start | bytes 1048576 | tf_op jit(solution)/shard_map/all_to_all | solution.py:74
  161.6 6.1 %convolution_bitcast_fusion = f32[1,384,4096]{2,1,0:T(8,128)} fusion(bf16[128,384]{1,0:T(8,128)(2,1)S(1)} %get-tuple-element.11, bf16[1,1,128,4096]{3,1,2,0:T(2,128)(2,1)} %copy-done.5), kind=kOutput, calls=%fused_computation.6 | convolution fusion | flops 402653184 | bytes 7438336 | tf_op jit(solution)/shard_map/dot_general | solution.py:45
  167.7 3.7 %convolution_bitcast_fusion.1 = f32[1,4096,384]{2,1,0:T(8,128)} fusion(bf16[128,384]{1,0:T(8,128)(2,1)S(1)} %copy-done.7, bf16[1,1,128,4096]{3,2,1,0:T(8,128)(2,1)S(1)} %copy-done.2), kind=kOutput, calls=%fused_computation.7 | convolution fusion | flops 402653184 | bytes 7438336 | tf_op jit(solution)/shard_map/dot_general | solution.py:51
  171.5 3.7 %convolution_bitcast_fusion.2 = f32[1,4096,384]{2,1,0:T(8,128)} fusion(bf16[128,384]{1,0:T(8,128)(2,1)S(1)} %copy-done.8, bf16[1,1,128,4096]{3,2,1,0:T(8,128)(2,1)S(1)} %copy-done.2), kind=kOutput, calls=%fused_computation.8 | convolution fusion | flops 402653184 | bytes 7438336 | tf_op jit(solution)/shard_map/dot_general | solution.py:48
  175.2 1.3 fusion.26
  176.7 2.1 scatter_fusion
  178.9 3.2 convolution_bitcast_fusion.3
  182.1 39.2 %psum.7 = f32[8]{0:T(128)S(1)} all-reduce(f32[8]{0:T(128)S(1)} %reduce_sum.19), channel_id=1, replica_groups=mesh['seq'=4,'exp'=8] {'seq','exp'}, use_global_device_ids=true, to_apply=%region_8.0 | all-reduce | flops 8 | bytes 64 | tf_op jit(solution)/shard_map/psum | solution.py:95
  221.3 0.5 neg.11
  221.9 2.1 slice_convert_fusion
  224.0 2.0 reshape.196
  226.0 2.0 reshape.153
  228.0 4.0 %scatter_custom_fusion = f32[256,4096]{1,0:T(8,128)} fusion(s32[32]{0:T(128)S(1)} %fusion.37, f32[]{:T(128)} %constant.4.clone.1, f32[32,4096]{1,0:T(8,128)} %reshape.153, f32[32]{0:T(128)S(1)} %mul.79), kind=kCustom, calls=%fused_computation.23 | custom fusion | flops 262144 | bytes 4719108 | tf_op jit(solution)/shard_map/scatter-add | solution.py:80
  232.0 3.8 %convert_element_type.78 = bf16[256,4096]{1,0:T(8,128)(2,1)} convert(f32[256,4096]{1,0:T(8,128)} %scatter_custom_fusion) | non-fusion elementwise | flops 1048576 | bytes 6291456 | tf_op jit(solution)/shard_map/convert_element_type | solution.py:97
  235.8 3.8 %fusion.39 = f32[256,4096]{1,0:T(8,128)} fusion(f32[256,8]{0,1:T(8,128)S(1)} %scatter_fusion, bf16[4096,8]{0,1:T(8,128)(2,1)S(1)} %copy-done.9), kind=kOutput, calls=%fused_computation.69 | convolution fusion | flops 100663296 | bytes 4268032 | tf_op jit(solution)/shard_map/dot_general | solution.py:90
  239.6 5.8 %scatter_fusion.1 = f32[256,4096]{1,0:T(8,128)} fusion(f32[256,4096]{1,0:T(8,128)} %fusion.39, s32[32]{0:T(128)S(1)} %fusion.37, f32[32,4096]{1,0:T(8,128)} %reshape.196), kind=kCustom, calls=%fused_computation.5 | custom fusion | flops 131072 | bytes 1572992 | tf_op jit(solution)/shard_map/scatter-add | solution.py:88
  245.5 3.8 %convert_element_type.84 = bf16[256,4096]{1,0:T(8,128)(2,1)} convert(f32[256,4096]{1,0:T(8,128)} %scatter_fusion.1) | non-fusion elementwise | flops 1048576 | bytes 6291456 | tf_op jit(solution)/shard_map/convert_element_type | solution.py:98
  249.2 106.3 %reduce-scatter.8.cloned.1.call-done = f32[128,8]{0,1:T(8,128)} async-done(((f32[4096,8]{0,1:T(8,128)}), f32[128,8]{0,1:T(8,128)}) %reduce-scatter.8.cloned.1.call-update) | async-done | bytes 4112 | tf_op jit(solution)/shard_map/reduce_scatter | solution.py:94
  (48 shorter events, 1.4 us)
Async XLA Ops:
  7.2 87.7 %copy-start = (bf16[1,4096,384]{2,1,0:T(8,128)(2,1)S(1)}, bf16[1,4096,384]{2,1,0:T(8,128)(2,1)}, u32[]{:S(2)}) copy-start(bf16[1,4096,384]{2,1,0:T(8,128)(2,1)} %param.15) | copy-start | bytes 9437188
  11.4 9.1 %copy-start.11 = (s32[1,8]{1,0:T(1,128)S(1)}, s32[1,8]{1,0:T(1,128)}, u32[]{:S(2)}) copy-start(s32[1,8]{1,0:T(1,128)} %param.19) | copy-start | bytes 100
  23.7 10.9 %copy-start.12 = (f32[1,384]{1,0:T(1,128)S(1)}, f32[1,384]{1,0:T(1,128)}, u32[]{:S(2)}) copy-start(f32[1,384]{1,0:T(1,128)} %param.17) | copy-start | bytes 4612
  27.1 56.3 %all-to-all-start = ((bf16[32,2,4,4096]{3,1,2,0:T(2,128)(2,1)}), bf16[32,2,4,4096]{3,1,2,0:T(2,128)(2,1)}, u32[]{:S(2)}, u32[]{:S(2)}) async-start(bf16[32,2,4,4096]{3,1,2,0:T(2,128)(2,1)} %bitcast.86), calls=%async_computation | async-start | bytes 4194304 | tf_op jit(solution)/shard_map/all_to_all | solution.py:27
  34.6 90.2 %reduce-scatter.4.cloned.1.call-start = ((), (), s32[]{:S(2)}) async-start(), calls=%async_computation.5 | async-start | bytes 1310720 | tf_op jit(solution)/shard_map/reduce_scatter | solution.py:54
  89.6 3.4 copy-start.5
  89.6 2.6 copy-start.4
  89.6 3.6 copy-start.3
  92.2 2.6 copy-start.1
  98.0 55.5 %reduce-scatter.6.cloned.1.call-start = ((), (), s32[]{:S(2)}) async-start(), calls=%async_computation.6 | async-start | bytes 1310720 | tf_op jit(solution)/shard_map/reduce_scatter | solution.py:64
  98.3 3.1 copy-start.6
  101.4 2.2 copy-start.10
  157.4 17.8 %all-to-all-start.1 = ((bf16[2,8,4,4096]{3,2,0,1:T(4,128)(2,1)}), bf16[2,8,4,4096]{3,2,0,1:T(4,128)(2,1)}, u32[]{:S(2)}, u32[]{:S(2)}) async-start(bf16[2,8,4,4096]{3,2,0,1:T(4,128)(2,1)} %pad_maximum_fusion.1), calls=%async_computation.3 | async-start | bytes 1048576 | tf_op jit(solution)/shard_map/all_to_all | solution.py:74
  161.6 6.2 %copy-start.7 = (bf16[128,384]{1,0:T(8,128)(2,1)S(1)}, bf16[128,384]{1,0:T(8,128)(2,1)}, u32[]{:S(2)}) copy-start(bf16[128,384]{1,0:T(8,128)(2,1)} %get-tuple-element.13) | copy-start | bytes 294916
  161.6 194.0 %reduce-scatter.8.cloned.1.call-start = ((), (), s32[]{:S(2)}) async-start(), calls=%async_computation.7 | async-start | bytes 135168 | tf_op jit(solution)/shard_map/reduce_scatter | solution.py:94
  161.6 6.1 %copy-start.2 = (bf16[1,1,128,4096]{3,2,1,0:T(8,128)(2,1)S(1)}, bf16[1,1,128,4096]{3,2,1,0:T(8,128)(2,1)}, u32[]{:S(2)}) copy-start(bf16[1,1,128,4096]{3,2,1,0:T(8,128)(2,1)} %copy-done.1) | copy-start | bytes 3145732
  167.7 3.7 %copy-start.8 = (bf16[128,384]{1,0:T(8,128)(2,1)S(1)}, bf16[128,384]{1,0:T(8,128)(2,1)}, u32[]{:S(2)}) copy-start(bf16[128,384]{1,0:T(8,128)(2,1)} %get-tuple-element.12) | copy-start | bytes 294916
  232.0 3.8 %copy-start.9 = (bf16[4096,8]{0,1:T(8,128)(2,1)S(1)}, bf16[4096,8]{0,1:T(8,128)(2,1)}, u32[]{:S(2)}) copy-start(bf16[4096,8]{0,1:T(8,128)(2,1)} %param.12) | copy-start | bytes 196612
Sparse Core Ops, SparseCore 0:
  98.2 26.5 reduce-scatter.3
  127.7 25.7 reduce-scatter.5
  222.0 133.5 reduce-scatter.7
where the time goes:
time: 363 us; the launch traced here: 362 us
  waiting for transfers between devices  203 us (56%)
  blocking collectives  39.2 us (11%)
  matrix products  33.6 us (9%)
  local copies, waits for them, and re-layouts  31.4 us (9%)
  other arithmetic  29.3 us (8%)
  between operations  14 us (4%)
  starting transfers between devices  11.9 us (3%)
    reduce_scatter x1, waiting for transfers between devices, on_device(): lax.psum_scatter(router_term, ('seq', 'exp'), scatter_dimension=0, tiled=...  106 us
    all_to_all x1, waiting for transfers between devices, on_device(): lax.all_to_all(copies, ('seq', 'exp'), split_axis=0, concat_axis=2, tiled...  48.8 us
    psum x1, blocking collectives, on_device(): threshold_grad = -lax.psum(jnp.sum(score_grad, axis=0), ('seq', 'exp'))  39.2 us
    reduce_scatter x1, waiting for transfers between devices, on_device(): lax.psum_scatter((first_term + lax.dot_general(up_delta, up_mat, contract...  27.7 us
    reduce_scatter x1, waiting for transfers between devices, on_device(): lax.psum_scatter(jnp.dot(hidden, down_mat, preferred_element_type=jnp.flo...  19.8 us
    all_to_all x1, starting transfers between devices, on_device(): lax.all_to_all(copies, ('seq', 'exp'), split_axis=0, concat_axis=2, tiled...  7.43 us
  transfers between devices with their start and end apart: 5, of which 4 were waited for; matrix products, arithmetic and copies ran while one was open for 13% of the time, Pallas kernels for 0%

commit v1 on v0

v1 whole, which is shorter than its diff:
```python
import jax
import jax.numpy as jnp
from jax import lax
from jax.sharding import PartitionSpec as P

BOTH = ("seq", "exp")
F32 = jnp.float32
BF16 = jnp.bfloat16


def mm(a, b, dims=((1,), (0,))):
    return lax.dot_general(a, b, (dims, ((), ())), preferred_element_type=F32)


def split3(v):
    hi = lax.reduce_precision(v, 8, 7)
    rest = v - hi
    mid = lax.reduce_precision(rest, 8, 7)
    low = rest - mid
    return [part.astype(BF16) for part in (hi, mid, low)]


def on_device(tokens, cotangent, router, threshold, w_gate, w_up, w_down, hid_scale, picks, counts):
    experts, slots = picks.shape[1:]
    own, features = tokens.shape
    seq_n = lax.axis_size("seq")
    everyone = seq_n * lax.axis_size("exp")
    expert = lax.axis_index("exp")

    live = jnp.arange(slots, dtype=jnp.int32)[None, :] < counts[0][:, None]
    flat = picks[0].reshape(-1)
    hit = flat[:, None] == jnp.arange(own, dtype=jnp.int32)[None, :]
    hit_live = (hit & live.reshape(-1)[:, None]).astype(BF16)
    hit = hit.astype(BF16)

    def dispatch(chooser, rows):
        many = jnp.tile(chooser, (seq_n, 1))
        sent = mm(many, rows).astype(BF16).reshape(everyone, slots, features)
        return lax.all_to_all(sent, BOTH, split_axis=0, concat_axis=0, tiled=True).reshape(-1, features)

    def bring_back(rows):
        sent = rows.reshape(everyone, slots, features)
        back = lax.all_to_all(sent, BOTH, split_axis=0, concat_axis=0, tiled=True).reshape(-1, features)
        return mm(jnp.tile(hit_live, (seq_n, 1)), back, ((0,), (0,))).astype(BF16)

    rows = dispatch(hit, tokens)
    cots = dispatch(hit_live, cotangent)

    gate_mat, up_mat, down_mat = w_gate[0], w_up[0], w_down[0]
    scale = hid_scale[0][None, :]
    column = lax.dynamic_slice_in_dim(router, expert, 1, axis=1)
    gates = jax.nn.sigmoid(mm(rows, column) - lax.dynamic_slice_in_dim(threshold, expert, 1)[None, :])
    pre_gate = mm(rows, gate_mat)
    pre_up = mm(rows, up_mat)
    sig = jax.nn.sigmoid(pre_gate)
    act = pre_gate * sig
    hidden = (act * pre_up * scale).astype(BF16)
    out = mm(hidden, down_mat)
    mixture = bring_back((out * gates).astype(BF16))

    cots_wide = cots.astype(F32)
    scaled = (cots_wide * gates).astype(BF16)
    grad = mm(scaled, down_mat, ((1,), (1,))) * scale
    gate_delta = (grad * pre_up * sig * (1.0 + pre_gate * (1.0 - sig))).astype(BF16)
    up_delta = (grad * act).astype(BF16)
    score = jnp.sum(cots_wide * out, axis=1, keepdims=True) * gates * (1.0 - gates)
    back = mm(gate_delta, gate_mat, ((1,), (1,))) + mm(up_delta, up_mat, ((1,), (1,)))
    back = back + score * column.astype(F32).reshape(1, -1)
    token_grad = bring_back(back.astype(BF16))

    parts = jnp.concatenate(split3(score), axis=1)
    router_part = jnp.sum(mm(parts, rows, ((0,), (0,))), axis=0)
    message = jnp.concatenate(
        [router_part.reshape(everyone, -1), jnp.broadcast_to(-jnp.sum(score), (everyone, 1))], axis=1
    )
    told = lax.all_to_all(message, BOTH, split_axis=0, concat_axis=0, tiled=True)
    told = jnp.sum(told.reshape(seq_n, experts, -1), axis=0)
    router_grad = told[:, :-1].T
    threshold_grad = told[:, -1]

    gate_grad = mm(rows, gate_delta, ((0,), (0,)))
    up_grad = mm(rows, up_delta, ((0,), (0,)))
    down_grad = mm(hidden, scaled, ((0,), (0,)))
    return (
        mixture,
        token_grad,
        router_grad,
        threshold_grad,
        gate_grad[None],
        up_grad[None],
        down_grad[None],
    )


def solution(mesh):
    by_owner = P(BOTH, None)
    columns = P("exp", None, "seq")
    down = P("exp", "seq", None)
    return jax.shard_map(
        on_device,
        mesh=mesh,
        in_specs=(
            by_owner,
            by_owner,
            P(),
            P(),
            columns,
            columns,
            down,
            P("exp", "seq"),
            P(BOTH, None, None),
            by_owner,
        ),
        out_specs=(by_owner, by_owner, by_owner, P(), columns, columns, down),
        check_vma=False,
    )
```

time: 363 us -> 165 us (0.45)
  waiting for transfers between devices: 203 us -> 66.5 us
  blocking collectives: 39.2 us -> 0 us
  other arithmetic: 29.3 us -> 4.52 us
  between operations: 14 us -> 1.48 us
  matrix products: 33.6 us -> 44.9 us
  starting transfers between devices: 11.9 us -> 22 us
  local copies, waits for them, and re-layouts: 31.4 us -> 24.5 us
    reduce_scatter x3 -> x0, waiting for transfers between devices: 154 us -> none  [the longest x1 106 us: on_device(): lax.psum_scatter(router_term, ('seq', 'exp'), scatter_dimension=0, tiled=...]
    psum x1 -> x0, blocking collectives: 39.2 us -> none  [on_device(): threshold_grad = -lax.psum(jnp.sum(score_grad, axis=0), ('seq', 'exp'))]
    all_to_all x2 -> x5, waiting for transfers between devices: 48.8 us -> 66.5 us  [the longest x2 36.8 us: dispatch(): lax.all_to_all(sent, BOTH, split_axis=0, concat_axis=0, tiled=True)]
    reshape x0 -> x7, local copies, waits for them, and re-layouts: none -> 15.4 us  [the longest x2 4.5 us: dispatch(): sent = mm(many, rows).astype(BF16).reshape(everyone, slots, features)]
    scatter-add x3 -> x0, other arithmetic: 12 us -> none  [the longest x1 5.83 us: on_device(): token_grad = jnp.zeros((row_count, features), jnp.float32).at[flat_index]...]
    dot_general x12 -> x15, matrix products: 33.6 us -> 44.9 us  [mm(): return lax.dot_general(a, b, (dims, ((), ())), preferred_element_type=F32)]
    all_to_all x2 -> x5, starting transfers between devices: 11.6 us -> 22 us  [the longest x2 11.2 us: dispatch(): lax.all_to_all(sent, BOTH, split_axis=0, concat_axis=0, tiled=True)]
    another operation x6 -> x2, local copies, waits for them, and re-layouts: 8.6 us -> 0.01 us  [the longest x1 0.01 us: dispatch(): many = jnp.tile(chooser, (seq_n, 1))]
  transfers between devices with their start and end apart: 5 -> 5, of which waited for: 4 -> 5; matrix products, arithmetic and copies ran while one was open for 13% -> 28% of each run, Pallas kernels for 0% -> 0%
where the time goes in v1:
time: 165 us; the launch traced here: 164 us
  waiting for transfers between devices  66.5 us (40%)
  matrix products  44.9 us (27%)
  local copies, waits for them, and re-layouts  24.5 us (15%)
  starting transfers between devices  22 us (13%)
  other arithmetic  4.52 us (3%)
    dot_general x15, matrix products, mm(): return lax.dot_general(a, b, (dims, ((), ())), preferred_element_type=F32)  44.9 us
    all_to_all x2, waiting for transfers between devices, dispatch(): lax.all_to_all(sent, BOTH, split_axis=0, concat_axis=0, tiled=True)  36.8 us
    all_to_all x2, waiting for transfers between devices, bring_back(): lax.all_to_all(sent, BOTH, split_axis=0, concat_axis=0, tiled=True)  24.7 us
    all_to_all x2, starting transfers between devices, dispatch(): lax.all_to_all(sent, BOTH, split_axis=0, concat_axis=0, tiled=True)  11.2 us
    all_to_all x2, starting transfers between devices, bring_back(): lax.all_to_all(sent, BOTH, split_axis=0, concat_axis=0, tiled=True)  7.25 us
    all_to_all x1, waiting for transfers between devices, on_device(): lax.all_to_all(message, BOTH, split_axis=0, concat_axis=0, tiled=True)  5.01 us
    reshape x2, local copies, waits for them, and re-layouts, dispatch(): sent = mm(many, rows).astype(BF16).reshape(everyone, slots, features)  4.5 us
    reshape x2, local copies, waits for them, and re-layouts, bring_back(): sent = rows.reshape(everyone, slots, features)  4.49 us
  transfers between devices with their start and end apart: 5, of which 5 were waited for; matrix products, arithmetic and copies ran while one was open for 28% of the time, Pallas kernels for 0%

profile of v1, /device:TPU:0, one launch (start us, length us, event | category | flops | bytes accessed | tf_op | source)
XLA Modules:
  0.0 163.9 jit_solution(12529217602350089511)
XLA Ops:
  0.6 0.0 copy-start
  0.6 0.9 iota_compare_fusion.1
  1.5 0.1 lt.30
  1.6 0.8 copy.19
  2.4 0.1 eq.22
  2.5 0.1 fusion.23
  2.6 3.0 %convolution_convert_fusion.3 = bf16[128,4096]{1,0:T(8,128)(2,1)} fusion(bf16[128,256]{1,0:T(8,128)(2,1)S(1)} %bitcast.78, bf16[256,4096]{1,0:T(8,128)(2,1)} %param.10), kind=kOutput, calls=%fused_computation.9 | convolution fusion | flops 268959744 | bytes 3211264 | tf_op jit(solution)/shard_map/dot_general | solution.py:12
  5.6 2.2 %reshape.152 = bf16[32,4,4096]{2,1,0:T(4,128)(2,1)} reshape(bf16[128,4096]{1,0:T(8,128)(2,1)} %convolution_convert_fusion.3) | data formatting | bytes 2097152 | tf_op jit(solution)/shard_map/reshape | solution.py:38
  7.8 7.4 %all-to-all-start = ((bf16[32,4,4096]{2,1,0:T(4,128)(2,1)}), bf16[32,4,4096]{2,1,0:T(4,128)(2,1)}, u32[]{:S(2)}, u32[]{:S(2)}) async-start(bf16[32,4,4096]{2,1,0:T(4,128)(2,1)} %reshape.152), calls=%async_computation | async-start | bytes 2097152 | tf_op jit(solution)/shard_map/all_to_all | solution.py:39
  15.3 3.0 %convolution_convert_fusion.2 = bf16[128,4096]{1,0:T(8,128)(2,1)} fusion(bf16[128,256]{1,0:T(8,128)(2,1)S(1)} %bitcast.75, bf16[256,4096]{1,0:T(8,128)(2,1)} %param.11), kind=kOutput, calls=%fused_computation.8 | convolution fusion | flops 268959744 | bytes 3211264 | tf_op jit(solution)/shard_map/dot_general | solution.py:12
  18.3 2.3 %reshape.157 = bf16[32,4,4096]{2,1,0:T(4,128)(2,1)} reshape(bf16[128,4096]{1,0:T(8,128)(2,1)} %convolution_convert_fusion.2) | data formatting | bytes 2097152 | tf_op jit(solution)/shard_map/reshape | solution.py:38
  20.5 20.9 %all-to-all-done = bf16[32,4,4096]{2,1,0:T(4,128)(2,1)} async-done(((bf16[32,4,4096]{2,1,0:T(4,128)(2,1)}), bf16[32,4,4096]{2,1,0:T(4,128)(2,1)}, u32[]{:S(2)}, u32[]{:S(2)}) %all-to-all-start) | async-done | bytes 1048608 | tf_op jit(solution)/shard_map/all_to_all | solution.py:39
  41.5 3.7 %all-to-all-start.2 = ((bf16[32,4,4096]{2,1,0:T(4,128)(2,1)}), bf16[32,4,4096]{2,1,0:T(4,128)(2,1)}, u32[]{:S(2)}, u32[]{:S(2)}) async-start(bf16[32,4,4096]{2,1,0:T(4,128)(2,1)} %reshape.157), calls=%async_computation.2 | async-start | bytes 2097152 | tf_op jit(solution)/shard_map/all_to_all | solution.py:39
  45.2 0.6 dynamic_slice.7
  45.8 2.1 %reshape.153 = bf16[128,4096]{1,0:T(8,128)(2,1)} reshape(bf16[32,4,4096]{2,1,0:T(4,128)(2,1)} %all-to-all-done) | data formatting | bytes 2097152 | tf_op jit(solution)/shard_map/reshape | solution.py:39
  48.0 2.2 %fusion.20 = f32[128]{0:T(128)S(1)} fusion(bf16[128,4096]{1,0:T(8,128)(2,1)} %reshape.153, bf16[4096,8]{0,1:T(8,128)(2,1)} %param.12, s32[]{:T(128)S(6)} %select_n.4, f32[]{:T(128)} %bitcast.7), kind=kOutput, calls=%fused_computation.32 | convolution fusion | flops 1049088 | bytes 1065988 | tf_op jit(solution)/shard_map/dot_general | solution.py:12
  50.2 0.1 mul.92
  50.4 3.7 %fusion.7 = f32[128,384]{1,0:T(8,128)} fusion(bf16[128,4096]{1,0:T(8,128)(2,1)} %reshape.153, bf16[1,4096,384]{2,1,0:T(8,128)(2,1)} %param.15), kind=kOutput, calls=%fused_computation.15 | convolution fusion | flops 402653184 | bytes 4390912 | tf_op jit(solution)/shard_map/dot_general | solution.py:12
  54.1 1.4 fusion.11
  55.5 15.9 %all-to-all-done.2 = bf16[32,4,4096]{2,1,0:T(4,128)(2,1)} async-done(((bf16[32,4,4096]{2,1,0:T(4,128)(2,1)}), bf16[32,4,4096]{2,1,0:T(4,128)(2,1)}, u32[]{:S(2)}, u32[]{:S(2)}) %all-to-all-start.2) | async-done | bytes 1048608 | tf_op jit(solution)/shard_map/all_to_all | solution.py:39
  71.4 2.9 %multiply_convert_fusion.1 = bf16[32,4,4096]{2,1,0:T(4,128)(2,1)} fusion(f32[32,4]{1,0:T(8,128)S(1)} %mul.92, bf16[32,4,4096]{2,1,0:T(4,128)(2,1)} %all-to-all-done.2), kind=kLoop, calls=%fused_computation.23 | loop fusion | flops 1572864 | bytes 2097664 | tf_op jit(solution)/shard_map/convert_element_type | solution.py:62
  74.3 2.1 %convert_element_type.86 = bf16[128,4096]{1,0:T(8,128)(2,1)} reshape(bf16[32,4,4096]{2,1,0:T(4,128)(2,1)} %multiply_convert_fusion.1) | data formatting | bytes 2097152 | tf_op jit(solution)/shard_map/convert_element_type | solution.py:62
  76.5 2.4 %multiply_convert_fusion.4 = (bf16[128,384]{1,0:T(8,128)(2,1)S(1)}, bf16[128,384]{1,0:T(8,128)(2,1)S(1)}, bf16[128,384]{1,0:T(8,128)(2,1)S(1)}) fusion(f32[128,384]{1,0:T(8,128)} %fusion.11, f32[128,384]{1,0:T(8,128)} %fusion.7, f32[384]{0:T(512)S(1)} %reduce.1, bf16[128,4096]{1,0:T(8,128)(2,1)} %convert_element_type.86, bf16[1,384,4096]{2,1,0:T(8,128)(2,1)S(1)} %copy-done), kind=kOutput, calls=%fused_computation.34 | convolution fusion | flops 403488768 | bytes 4883968 | tf_op jit(solution)/shard_map/dot_general | solution.py:12
  78.9 2.4 %reshape.162 = f32[128,4096]{1,0:T(8,128)} reshape(bf16[32,4,4096]{2,1,0:T(4,128)(2,1)} %all-to-all-done.2) | data formatting | bytes 3145728 | tf_op jit(solution)/shard_map/convert_element_type | solution.py:61
  81.3 3.3 %multiply_reduce_fusion = (f32[128]{0:T(128)S(1)}, bf16[128,4096]{1,0:T(8,128)(2,1)}) fusion(f32[128,4096]{1,0:T(8,128)} %reshape.162, f32[128]{0:T(128)S(1)} %fusion.20, bf16[128,384]{1,0:T(8,128)(2,1)S(1)} %get-tuple-element.13, bf16[1,384,4096]{2,1,0:T(8,128)(2,1)S(1)} %copy-done), kind=kOutput, calls=%fused_computation.22 | convolution fusion | flops 404750208 | bytes 6390784 | tf_op jit(solution)/shard_map/dot_general | solution.py:12
  84.7 0.6 fusion.38
  85.9 1.5 convolution_reduce_fusion
  87.4 0.6 all_to_all.22
  88.1 3.6 %all-to-all-start.4 = ((f32[32,1,129]{2,1,0:T(1,128)}), f32[32,1,129]{2,1,0:T(1,128)S(1)}, u32[]{:S(2)}, u32[]{:S(2)}) async-start(f32[32,1,129]{2,1,0:T(1,128)} %all_to_all.22), calls=%async_computation.4 | async-start | bytes 65536 | tf_op jit(solution)/shard_map/all_to_all | solution.py:76
  91.7 2.2 %reshape.155 = bf16[32,4,4096]{2,1,0:T(4,128)(2,1)} reshape(bf16[128,4096]{1,0:T(8,128)(2,1)} %get-tuple-element.10) | data formatting | bytes 2097152 | tf_op jit(solution)/shard_map/reshape | solution.py:42
  93.9 5.0 %all-to-all-done.4 = f32[32,1,129]{2,1,0:T(1,128)S(1)} async-done(((f32[32,1,129]{2,1,0:T(1,128)}), f32[32,1,129]{2,1,0:T(1,128)S(1)}, u32[]{:S(2)}, u32[]{:S(2)}) %all-to-all-start.4) | async-done | bytes 16544 | tf_op jit(solution)/shard_map/all_to_all | solution.py:76
  98.9 3.4 %all-to-all-start.1 = ((bf16[32,4,4096]{2,1,0:T(4,128)(2,1)}), bf16[32,4,4096]{2,1,0:T(4,128)(2,1)}, u32[]{:S(2)}, u32[]{:S(2)}) async-start(bf16[32,4,4096]{2,1,0:T(4,128)(2,1)} %reshape.155), calls=%async_computation.1 | async-start | bytes 2097152 | tf_op jit(solution)/shard_map/all_to_all | solution.py:43
  102.3 0.9 dynamic-slice_reduce_fusion
  103.3 3.1 %fusion.9 = f32[128,4096]{1,0:T(8,128)S(1)} fusion(bf16[128,384]{1,0:T(8,128)(2,1)S(1)} %get-tuple-element.12, bf16[1,4096,384]{2,1,0:T(8,128)(2,1)} %param.14), kind=kOutput, calls=%fused_computation.17 | convolution fusion | flops 402653184 | bytes 5341184 | tf_op jit(solution)/shard_map/dot_general | solution.py:12
  106.4 2.1 %fusion.1 = bf16[128,4096]{1,0:T(8,128)(2,1)} fusion(f32[128,4096]{1,0:T(8,128)S(1)} %fusion.9, bf16[128,384]{1,0:T(8,128)(2,1)S(1)} %get-tuple-element.11, bf16[1,4096,384]{2,1,0:T(8,128)(2,1)S(1)} %copy-done.4, f32[4096]{0:T(1024)S(1)} %mul.105, f32[128]{0:T(128)S(1)} %get-tuple-element.8), kind=kOutput, calls=%fused_computation.7 | convolution fusion | flops 404750336 | bytes 6406656 | tf_op jit(solution)/shard_map/dot_general | solution.py:12
  108.5 2.2 %reshape.158 = bf16[32,4,4096]{2,1,0:T(4,128)(2,1)} reshape(bf16[128,4096]{1,0:T(8,128)(2,1)} %fusion.1) | data formatting | bytes 2097152 | tf_op jit(solution)/shard_map/reshape | solution.py:42
  110.8 17.8 %all-to-all-done.1 = bf16[32,4,4096]{2,1,0:T(4,128)(2,1)} async-done(((bf16[32,4,4096]{2,1,0:T(4,128)(2,1)}), bf16[32,4,4096]{2,1,0:T(4,128)(2,1)}, u32[]{:S(2)}, u32[]{:S(2)}) %all-to-all-start.1) | async-done | bytes 1048608 | tf_op jit(solution)/shard_map/all_to_all | solution.py:43
  128.5 3.9 %all-to-all-start.3 = ((bf16[32,4,4096]{2,1,0:T(4,128)(2,1)}), bf16[32,4,4096]{2,1,0:T(4,128)(2,1)}, u32[]{:S(2)}, u32[]{:S(2)}) async-start(bf16[32,4,4096]{2,1,0:T(4,128)(2,1)} %reshape.158), calls=%async_computation.3 | async-start | bytes 2097152 | tf_op jit(solution)/shard_map/all_to_all | solution.py:43
  132.4 5.0 %convolution_bitcast_fusion.1 = f32[1,4096,384]{2,1,0:T(8,128)} fusion(bf16[128,4096]{1,0:T(8,128)(2,1)} %reshape.153, bf16[128,384]{1,0:T(8,128)(2,1)S(1)} %get-tuple-element.11), kind=kOutput, calls=%fused_computation.1 | convolution fusion | flops 402653184 | bytes 7438336 | tf_op jit(solution)/shard_map/dot_general | solution.py:12
  137.4 3.7 %convolution_bitcast_fusion.2 = f32[1,4096,384]{2,1,0:T(8,128)} fusion(bf16[128,4096]{1,0:T(8,128)(2,1)S(1)} %copy-done.2, bf16[128,384]{1,0:T(8,128)(2,1)S(1)} %get-tuple-element.12), kind=kOutput, calls=%fused_computation.2 | convolution fusion | flops 402653184 | bytes 7438336 | tf_op jit(solution)/shard_map/dot_general | solution.py:12
  141.2 3.7 %convolution_bitcast_fusion = f32[1,384,4096]{2,1,0:T(8,128)} fusion(bf16[128,384]{1,0:T(8,128)(2,1)S(1)} %get-tuple-element.13, f32[128,4096]{1,0:T(8,128)S(1)} %copy-done.3, f32[128]{0:T(128)S(1)} %fusion.20), kind=kOutput, calls=%fused_computation | convolution fusion | flops 403701760 | bytes 8487424 | tf_op jit(solution)/shard_map/dot_general | solution.py:12
  144.9 0.6 slice_reduce_fusion
  145.5 0.6 slice_bitcast_fusion
  146.1 2.1 %reshape.156 = bf16[128,4096]{1,0:T(8,128)(2,1)} reshape(bf16[32,4,4096]{2,1,0:T(4,128)(2,1)} %all-to-all-done.1) | data formatting | bytes 2097152 | tf_op jit(solution)/shard_map/reshape | solution.py:43
  148.3 3.3 %convolution_convert_fusion.1 = bf16[256,4096]{1,0:T(8,128)(2,1)} fusion(bf16[128,256]{1,0:T(8,128)(2,1)S(1)} %bitcast.76, bf16[128,4096]{1,0:T(8,128)(2,1)} %reshape.156), kind=kOutput, calls=%fused_computation.4 | convolution fusion | flops 269484032 | bytes 3211264 | tf_op jit(solution)/shard_map/dot_general | solution.py:12
  151.5 6.9 %all-to-all-done.3 = bf16[32,4,4096]{2,1,0:T(4,128)(2,1)} async-done(((bf16[32,4,4096]{2,1,0:T(4,128)(2,1)}), bf16[32,4,4096]{2,1,0:T(4,128)(2,1)}, u32[]{:S(2)}, u32[]{:S(2)}) %all-to-all-start.3) | async-done | bytes 1048608 | tf_op jit(solution)/shard_map/all_to_all | solution.py:43
  158.4 2.2 %reshape.159 = bf16[128,4096]{1,0:T(8,128)(2,1)} reshape(bf16[32,4,4096]{2,1,0:T(4,128)(2,1)} %all-to-all-done.3) | data formatting | bytes 2097152 | tf_op jit(solution)/shard_map/reshape | solution.py:43
  160.6 3.3 %convolution_convert_fusion = bf16[256,4096]{1,0:T(8,128)(2,1)} fusion(bf16[128,256]{1,0:T(8,128)(2,1)S(1)} %bitcast.77, bf16[128,4096]{1,0:T(8,128)(2,1)} %reshape.159), kind=kOutput, calls=%fused_computation.3 | convolution fusion | flops 269484032 | bytes 3211264 | tf_op jit(solution)/shard_map/dot_general | solution.py:12
  (22 shorter events, 0.1 us)
Async XLA Ops:
  0.6 75.8 %copy-start = (bf16[1,384,4096]{2,1,0:T(8,128)(2,1)S(1)}, bf16[1,384,4096]{2,1,0:T(8,128)(2,1)}, u32[]{:S(2)}) copy-start(bf16[1,384,4096]{2,1,0:T(8,128)(2,1)} %param.16) | copy-start | bytes 9437188
  7.8 33.6 %all-to-all-start = ((bf16[32,4,4096]{2,1,0:T(4,128)(2,1)}), bf16[32,4,4096]{2,1,0:T(4,128)(2,1)}, u32[]{:S(2)}, u32[]{:S(2)}) async-start(bf16[32,4,4096]{2,1,0:T(4,128)(2,1)} %reshape.152), calls=%async_computation | async-start | bytes 2097152 | tf_op jit(solution)/shard_map/all_to_all | solution.py:39
  18.3 27.0 %copy-start.7 = (f32[8]{0:T(128)S(1)}, f32[8]{0:T(128)}, u32[]{:S(2)}) copy-start(f32[8]{0:T(128)} %param.13) | copy-start | bytes 100
  18.3 27.5 %copy-start.6 = (f32[1,384]{1,0:T(1,128)S(1)}, f32[1,384]{1,0:T(1,128)}, u32[]{:S(2)}) copy-start(f32[1,384]{1,0:T(1,128)} %param.17) | copy-start | bytes 4612
  41.5 30.0 %all-to-all-start.2 = ((bf16[32,4,4096]{2,1,0:T(4,128)(2,1)}), bf16[32,4,4096]{2,1,0:T(4,128)(2,1)}, u32[]{:S(2)}, u32[]{:S(2)}) async-start(bf16[32,4,4096]{2,1,0:T(4,128)(2,1)} %reshape.157), calls=%async_computation.2 | async-start | bytes 2097152 | tf_op jit(solution)/shard_map/all_to_all | solution.py:39
  50.3 3.8 %copy-start.1 = (bf16[128,4096]{1,0:T(8,128)(2,1)S(1)}, bf16[128,4096]{1,0:T(8,128)(2,1)}, u32[]{:S(2)}) copy-start(bf16[128,4096]{1,0:T(8,128)(2,1)} %reshape.153) | copy-start | bytes 3145732
  50.4 3.8 %copy-start.5 = (bf16[1,4096,384]{2,1,0:T(8,128)(2,1)S(1)}, bf16[1,4096,384]{2,1,0:T(8,128)(2,1)}, u32[]{:S(2)}) copy-start(bf16[1,4096,384]{2,1,0:T(8,128)(2,1)} %param.14) | copy-start | bytes 9437188
  88.1 10.9 %all-to-all-start.4 = ((f32[32,1,129]{2,1,0:T(1,128)}), f32[32,1,129]{2,1,0:T(1,128)S(1)}, u32[]{:S(2)}, u32[]{:S(2)}) async-start(f32[32,1,129]{2,1,0:T(1,128)} %all_to_all.22), calls=%async_computation.4 | async-start | bytes 65536 | tf_op jit(solution)/shard_map/all_to_all | solution.py:76
  98.9 29.6 %all-to-all-start.1 = ((bf16[32,4,4096]{2,1,0:T(4,128)(2,1)}), bf16[32,4,4096]{2,1,0:T(4,128)(2,1)}, u32[]{:S(2)}, u32[]{:S(2)}) async-start(bf16[32,4,4096]{2,1,0:T(4,128)(2,1)} %reshape.155), calls=%async_computation.1 | async-start | bytes 2097152 | tf_op jit(solution)/shard_map/all_to_all | solution.py:43
  103.3 3.2 %copy-start.4 = (bf16[1,4096,384]{2,1,0:T(8,128)(2,1)S(1)}, bf16[1,4096,384]{2,1,0:T(8,128)(2,1)}, u32[]{:S(2)}) copy-start(bf16[1,4096,384]{2,1,0:T(8,128)(2,1)} %param.15) | copy-start | bytes 9437188
  128.5 29.9 %all-to-all-start.3 = ((bf16[32,4,4096]{2,1,0:T(4,128)(2,1)}), bf16[32,4,4096]{2,1,0:T(4,128)(2,1)}, u32[]{:S(2)}, u32[]{:S(2)}) async-start(bf16[32,4,4096]{2,1,0:T(4,128)(2,1)} %reshape.158), calls=%async_computation.3 | async-start | bytes 2097152 | tf_op jit(solution)/shard_map/all_to_all | solution.py:43
  132.4 5.0 %copy-start.2 = (bf16[128,4096]{1,0:T(8,128)(2,1)S(1)}, bf16[128,4096]{1,0:T(8,128)(2,1)}, u32[]{:S(2)}) copy-start(bf16[128,4096]{1,0:T(8,128)(2,1)} %reshape.153) | copy-start | bytes 3145732
  137.4 3.7 %copy-start.3 = (f32[128,4096]{1,0:T(8,128)S(1)}, f32[128,4096]{1,0:T(8,128)}, u32[]{:S(2)}) copy-start(f32[128,4096]{1,0:T(8,128)} %reshape.162) | copy-start | bytes 6291460

commit v2 on v1

v2 whole, which is shorter than its diff:
```python
import functools

import jax
import jax.numpy as jnp
from jax import lax
from jax.experimental import pallas as pl
from jax.experimental.pallas import tpu as pltpu
from jax.sharding import PartitionSpec as P

BOTH = ("seq", "exp")
F32 = jnp.float32
BF16 = jnp.bfloat16
ROWS = ((0,), (0,))
LAST = ((1,), (1,))
STEPS = 4
PARAMS = pltpu.CompilerParams(vmem_limit_bytes=40 * 2**20)


def mm(a, b, dims=((1,), (0,))):
    return lax.dot_general(a, b, (dims, ((), ())), preferred_element_type=F32)


def spec(block, index):
    return pl.BlockSpec(block, index)


def whole(shape):
    return pl.BlockSpec(shape, lambda *_: (0,) * len(shape))


def in_smem():
    return pl.BlockSpec(memory_space=pltpu.SMEM)


def choosers(picks_ref, counts_ref, own, pack, only_live):
    slots, experts = picks_ref.shape
    shape = (experts * pack * slots, own)
    row = lax.broadcasted_iota(jnp.int32, shape, 0)
    token = lax.broadcasted_iota(jnp.int32, shape, 1)
    expert = row // (pack * slots)
    slot = row % slots
    part = (row // slots) % pack
    want = jnp.full(shape, -1, jnp.int32)
    for e in range(experts):
        for k in range(slots):
            pick = picks_ref[k, e]
            if only_live:
                pick = jnp.where(k < counts_ref[0, e], pick, -1)
            want = jnp.where((expert == e) & (slot == k), pick, want)
    return [jnp.where((want == token) & (part == h), 1.0, 0.0).astype(BF16) for h in range(pack)]


def choose_rows(rows, picks, counts, pack, only_live):
    own, features = rows.shape
    slots, experts = picks.shape
    count = experts * pack * slots
    width = features // pack // STEPS

    def body(picks_ref, counts_ref, *refs):
        parts, out_ref, one_hot = refs[:pack], refs[pack], refs[pack + 1]

        @pl.when(pl.program_id(0) == 0)
        def _():
            for h, chooser in enumerate(choosers(picks_ref, counts_ref, own, pack, only_live)):
                one_hot[h] = chooser

        out_ref[...] = sum(mm(one_hot[h], parts[h][...]) for h in range(pack)).astype(BF16)

    return pl.pallas_call(
        body,
        grid=(STEPS,),
        in_specs=[in_smem(), in_smem()]
        + [spec((own, width), lambda i, h=h: (0, h * STEPS + i)) for h in range(pack)],
        out_specs=spec((count, width), lambda i: (0, i)),
        out_shape=jax.ShapeDtypeStruct((count, features // pack), BF16),
        scratch_shapes=[pltpu.VMEM((pack, count, own), BF16)],
        compiler_params=PARAMS,
        cost_estimate=pl.CostEstimate(
            flops=2 * count * own * features, bytes_accessed=2 * features * own, transcendentals=0
        ),
    )(picks, counts, *([rows] * pack))


def scatter_rows(back, picks, counts, own, pack):
    count, part_width = back.shape
    width = part_width // STEPS

    def body(picks_ref, counts_ref, back_ref, out_ref, one_hot):
        @pl.when((pl.program_id(0) == 0) & (pl.program_id(1) == 0))
        def _():
            for h, chooser in enumerate(choosers(picks_ref, counts_ref, own, pack, True)):
                one_hot[h] = chooser

        out_ref[...] = mm(one_hot[pl.program_id(0)], back_ref[...], ROWS).astype(BF16)

    return pl.pallas_call(
        body,
        grid=(pack, STEPS),
        in_specs=[in_smem(), in_smem(), spec((count, width), lambda h, i: (0, i))],
        out_specs=spec((own, width), lambda h, i: (0, h * STEPS + i)),
        out_shape=jax.ShapeDtypeStruct((own, part_width * pack), BF16),
        scratch_shapes=[pltpu.VMEM((pack, count, own), BF16)],
        compiler_params=PARAMS,
        cost_estimate=pl.CostEstimate(
            flops=2 * count * own * part_width * pack,
            bytes_accessed=2 * part_width * pack * own,
            transcendentals=0,
        ),
    )(picks, counts, back)


def first_part(rows, pack, slots):
    row = lax.broadcasted_iota(jnp.int32, (rows, 1), 0)
    return (row // slots) % pack == 0


def fold(parts, slots):
    rows = parts[0].shape[0]
    total = parts[0]
    for h in range(1, len(parts)):
        total = total + pltpu.roll(parts[h], rows - h * slots, 0)
    return total


def spread(value, pack, slots):
    return [value if h == 0 else pltpu.roll(value, h * slots, 0) for h in range(pack)]


def arrange(refs):
    near = len(refs) // 2
    blocks = [refs[0][...]]
    for k in range(1, near + 1):
        blocks.append(refs[k][...] + refs[2 * near + 1 - k][...])
    return jnp.concatenate(blocks, axis=0)


def expert_forward(blocks, seq_n, slots, pack, router, threshold, w_gate, w_up, w_down, hid_scale):
    block_rows, part_width = blocks[0].shape
    rows = block_rows * seq_n
    hidden_n = w_gate.shape[2]
    experts = router.shape[1]
    width = part_width // STEPS
    ready = STEPS - 1

    def first(i):
        return jnp.minimum(i, ready)

    def second(i):
        return jnp.maximum(i - STEPS, 0)

    n_blocks = len(blocks)

    def body(*refs):
        refs = list(refs)
        block_refs = [refs.pop(0) for _ in range(n_blocks)]
        router_refs = [refs.pop(0) for _ in range(pack)]
        gate_refs = [refs.pop(0) for _ in range(pack)]
        up_refs = [refs.pop(0) for _ in range(pack)]
        down_refs = [refs.pop(0) for _ in range(pack)]
        threshold_ref, scale_ref = refs.pop(0), refs.pop(0)
        x_ref, gate_ref, up_ref, g_ref, hidden_ref = [refs.pop(0) for _ in range(5)]
        out_refs = [refs.pop(0) for _ in range(seq_n)]
        acc_gate, acc_up, acc_score = refs
        i = pl.program_id(0)

        @pl.when(i == 0)
        def _():
            acc_gate[...] = jnp.zeros_like(acc_gate)
            acc_up[...] = jnp.zeros_like(acc_up)
            acc_score[...] = jnp.zeros_like(acc_score)

        @pl.when(i < STEPS)
        def _():
            x = arrange(block_refs)
            x_ref[...] = x
            for h in range(pack):
                acc_score[h] += mm(x, router_refs[h][...])
                acc_gate[h] += mm(x, gate_refs[h][...])
                acc_up[h] += mm(x, up_refs[h][...])

        @pl.when(i == ready)
        def _():
            mine = lax.broadcasted_iota(jnp.int32, (rows, experts), 1) == lax.axis_index("exp")
            score = fold([acc_score[h] for h in range(pack)], slots) - threshold_ref[...]
            g = jax.nn.sigmoid(jnp.sum(jnp.where(mine, score, 0.0), axis=1, keepdims=True))
            g_ref[...] = jnp.broadcast_to(g, g_ref.shape)
            gate = fold([acc_gate[h] for h in range(pack)], slots)
            up = fold([acc_up[h] for h in range(pack)], slots)
            gate_ref[...] = gate
            up_ref[...] = up
            hidden = gate * jax.nn.sigmoid(gate) * up * scale_ref[...] * g
            hidden = jnp.where(first_part(rows, pack, slots), hidden, 0.0)
            for h, value in enumerate(spread(hidden, pack, slots)):
                hidden_ref[h] = value.astype(BF16)

        @pl.when(i >= STEPS)
        def _():
            out = sum(mm(hidden_ref[h], down_refs[h][...]) for h in range(pack)).astype(BF16)
            for k in range(seq_n):
                out_refs[k][...] = out[k * block_rows : (k + 1) * block_rows]

    in_specs = (
        [spec((block_rows, width), lambda i: (0, first(i))) for _ in blocks]
        + [spec((width, experts), lambda i, h=h: (h * STEPS + first(i), 0)) for h in range(pack)]
        + [spec((None, width, hidden_n), lambda i, h=h: (0, h * STEPS + first(i), 0)) for h in range(pack)] * 2
        + [spec((None, hidden_n, width), lambda i, h=h: (0, 0, h * STEPS + second(i))) for h in range(pack)]
        + [whole((1, experts)), whole((1, hidden_n))]
    )
    out_specs = [
        spec((rows, width), lambda i: (0, first(i))),
        whole((rows, hidden_n)),
        whole((rows, hidden_n)),
        whole((rows, 128)),
        whole((pack, rows, hidden_n)),
    ] + [spec((block_rows, width), lambda i: (0, second(i)))] * seq_n
    out_shape = [
        jax.ShapeDtypeStruct((rows, part_width), BF16),
        jax.ShapeDtypeStruct((rows, hidden_n), F32),
        jax.ShapeDtypeStruct((rows, hidden_n), F32),
        jax.ShapeDtypeStruct((rows, 128), F32),
        jax.ShapeDtypeStruct((pack, rows, hidden_n), BF16),
    ] + [jax.ShapeDtypeStruct((block_rows, part_width), BF16)] * seq_n
    return pl.pallas_call(
        body,
        grid=(2 * STEPS,),
        in_specs=in_specs,
        out_specs=out_specs,
        out_shape=out_shape,
        scratch_shapes=[
            pltpu.VMEM((pack, rows, hidden_n), F32),
            pltpu.VMEM((pack, rows, hidden_n), F32),
            pltpu.VMEM((pack, rows, experts), F32),
        ],
        compiler_params=PARAMS,
        cost_estimate=pl.CostEstimate(
            flops=6 * rows * part_width * pack * hidden_n,
            bytes_accessed=6 * part_width * pack * hidden_n,
            transcendentals=0,
        ),
    )(
        *blocks,
        *([router] * pack),
        *([w_gate] * pack),
        *([w_up] * pack),
        *([w_down] * pack),
        threshold.reshape(1, -1),
        hid_scale,
    )


def split3(v):
    hi = v.astype(BF16)
    rest = v - hi.astype(F32)
    mid = rest.astype(BF16)
    return hi, mid, (rest - mid.astype(F32)).astype(BF16)


def expert_backward(blocks, seq_n, slots, pack, x, pre_gate, pre_up, gates, router, w_gate, w_up, w_down, hid_scale):
    block_rows, part_width = blocks[0].shape
    rows = block_rows * seq_n
    hidden_n = w_gate.shape[2]
    experts = router.shape[1]
    width = part_width // STEPS
    ready = STEPS - 1

    def first(i):
        return jnp.minimum(i, ready)

    def second(i):
        return jnp.maximum(i - STEPS, 0)

    n_blocks = len(blocks)

    def body(*refs):
        refs = list(refs)
        block_refs = [refs.pop(0) for _ in range(n_blocks)]
        router_refs = [refs.pop(0) for _ in range(pack)]
        gate_refs = [refs.pop(0) for _ in range(pack)]
        up_refs = [refs.pop(0) for _ in range(pack)]
        down_refs = [refs.pop(0) for _ in range(pack)]
        scale_ref, x_ref, pre_gate_ref, pre_up_ref, g_ref = [refs.pop(0) for _ in range(5)]
        c_ref, gate_delta, up_delta, router_ref, total_ref = [refs.pop(0) for _ in range(5)]
        out_refs = [refs.pop(0) for _ in range(seq_n)]
        acc, columns = refs
        i = pl.program_id(0)

        @pl.when(i == 0)
        def _():
            acc[...] = jnp.zeros_like(acc)

        @pl.when(i < STEPS)
        def _():
            c = arrange(block_refs)
            c_ref[...] = c
            for h in range(pack):
                acc[h] += mm(c, down_refs[h][...], LAST)

        @pl.when(i == ready)
        def _():
            keep = first_part(rows, pack, slots)
            raw = fold([acc[h] for h in range(pack)], slots) * scale_ref[...]
            raw = jnp.where(keep, raw, 0.0)
            g = g_ref[:, :1]
            gate = pre_gate_ref[...]
            up = pre_up_ref[...]
            sig = jax.nn.sigmoid(gate)
            act = gate * sig
            score = jnp.sum(act * up * raw, axis=1, keepdims=True) * g * (1.0 - g)
            grad = raw * g
            to_gate = grad * up * sig * (1.0 + gate * (1.0 - sig))
            to_up = grad * act
            mine = lax.broadcasted_iota(jnp.int32, (rows, experts), 1) == lax.axis_index("exp")
            for h, value in enumerate(spread(to_gate, pack, slots)):
                gate_delta[h] = value.astype(BF16)
            for h, value in enumerate(spread(to_up, pack, slots)):
                up_delta[h] = value.astype(BF16)
            column = jnp.where(mine, score, 0.0)
            for h, value in enumerate(spread(column, pack, slots)):
                for n, piece in enumerate(split3(value)):
                    columns[h, n] = piece
            total_ref[...] = jnp.broadcast_to(-jnp.sum(score, axis=0, keepdims=True), total_ref.shape)

        @pl.when(i >= STEPS)
        def _():
            out = jnp.zeros((rows, width), F32)
            x_now = x_ref[...]
            for h in range(pack):
                out = out + mm(gate_delta[h], gate_refs[h][...], LAST)
                out = out + mm(up_delta[h], up_refs[h][...], LAST)
                out = out + mm(columns[h, 0], router_refs[h][...], LAST)
                out = out + mm(columns[h, 1], router_refs[h][...], LAST)
                part = sum(mm(columns[h, n], x_now, ROWS) for n in range(3))
                router_ref[h : h + 1, :] = jnp.sum(part, axis=0, keepdims=True)
            out = out.astype(BF16)
            for k in range(seq_n):
                out_refs[k][...] = out[k * block_rows : (k + 1) * block_rows]

    in_specs = (
        [spec((block_rows, width), lambda i: (0, first(i))) for _ in blocks]
        + [spec((width, experts), lambda i, h=h: (h * STEPS + second(i), 0)) for h in range(pack)]
        + [spec((None, width, hidden_n), lambda i, h=h: (0, h * STEPS + second(i), 0)) for h in range(pack)] * 2
        + [spec((None, hidden_n, width), lambda i, h=h: (0, 0, h * STEPS + first(i))) for h in range(pack)]
        + [
            whole((1, hidden_n)),
            spec((rows, width), lambda i: (0, second(i))),
            whole((rows, hidden_n)),
            whole((rows, hidden_n)),
            whole((rows, 128)),
        ]
    )
    out_specs = [
        spec((rows, width), lambda i: (0, first(i))),
        whole((pack, rows, hidden_n)),
        whole((pack, rows, hidden_n)),
        spec((pack, width), lambda i: (0, second(i))),
        whole((1, 128)),
    ] + [spec((block_rows, width), lambda i: (0, second(i)))] * seq_n
    out_shape = [
        jax.ShapeDtypeStruct((rows, part_width), BF16),
        jax.ShapeDtypeStruct((pack, rows, hidden_n), BF16),
        jax.ShapeDtypeStruct((pack, rows, hidden_n), BF16),
        jax.ShapeDtypeStruct((pack, part_width), F32),
        jax.ShapeDtypeStruct((1, 128), F32),
    ] + [jax.ShapeDtypeStruct((block_rows, part_width), BF16)] * seq_n
    return pl.pallas_call(
        body,
        grid=(2 * STEPS,),
        in_specs=in_specs,
        out_specs=out_specs,
        out_shape=out_shape,
        scratch_shapes=[
            pltpu.VMEM((pack, rows, hidden_n), F32),
            pltpu.VMEM((pack, 3, rows, experts), BF16),
        ],
        compiler_params=PARAMS,
        cost_estimate=pl.CostEstimate(
            flops=6 * rows * part_width * pack * hidden_n,
            bytes_accessed=6 * part_width * pack * hidden_n,
            transcendentals=0,
        ),
    )(
        *blocks,
        *([router] * pack),
        *([w_gate] * pack),
        *([w_up] * pack),
        *([w_down] * pack),
        hid_scale,
        x,
        pre_gate,
        pre_up,
        gates,
    )


def weight_grads(x, c, hidden, gate_delta, up_delta):
    rows, part_width = x.shape
    pack, _, hidden_n = hidden.shape
    width = part_width // STEPS

    def body(x_ref, c_ref, hidden_ref, gate_ref, up_ref, gate_out, up_out, down_out):
        x_now = x_ref[...]
        gate_out[...] = mm(x_now, gate_ref[...], ROWS)
        up_out[...] = mm(x_now, up_ref[...], ROWS)
        down_out[...] = mm(hidden_ref[...], c_ref[...], ROWS)

    part = spec((None, rows, hidden_n), lambda h, i: (h, 0, 0))
    tall = spec((None, width, hidden_n), lambda h, i: (0, h * STEPS + i, 0))
    return pl.pallas_call(
        body,
        grid=(pack, STEPS),
        in_specs=[spec((rows, width), lambda h, i: (0, i))] * 2 + [part] * 3,
        out_specs=[tall, tall, spec((None, hidden_n, width), lambda h, i: (0, 0, h * STEPS + i))],
        out_shape=[
            jax.ShapeDtypeStruct((1, part_width * pack, hidden_n), F32),
            jax.ShapeDtypeStruct((1, part_width * pack, hidden_n), F32),
            jax.ShapeDtypeStruct((1, hidden_n, part_width * pack), F32),
        ],
        compiler_params=PARAMS,
        cost_estimate=pl.CostEstimate(
            flops=6 * rows * part_width * pack * hidden_n,
            bytes_accessed=12 * part_width * pack * hidden_n,
            transcendentals=0,
        ),
    )(x, c, hidden, gate_delta, up_delta)


def line_gather(block, n):
    rights, lefts = [], []
    right = left = block
    for j in range(1, n):
        right = lax.ppermute(right, "seq", [(s, s + 1) for s in range(j - 1, n - 1)])
        left = lax.ppermute(left, "seq", [(s, s - 1) for s in range(1, n - j + 1)])
        rights.append(right)
        lefts.append(left)
    return [block] + rights + lefts


def add(*parts):
    return sum(part.astype(F32) for part in parts).astype(BF16)


def line_sum(parts, n):
    right, left = parts[1], parts[n - 1]
    for j in range(1, n):
        if j > 1:
            right, left = add(parts[j], right), add(parts[n - j], left)
        right = lax.ppermute(right, "seq", [(s, s + 1) for s in range(j)])
        left = lax.ppermute(left, "seq", [(s, s - 1) for s in range(n - j, n)])
    return add(parts[0], right, left)


def on_device(tokens, cotangent, router, threshold, w_gate, w_up, w_down, hid_scale, picks, counts):
    experts, slots = picks.shape[1:]
    own, features = tokens.shape
    seq_n = lax.axis_size("seq")
    everyone = seq_n * lax.axis_size("exp")
    pack = max(1, 8 // slots)
    chosen = picks[0].T

    def to_experts(block):
        block = block.reshape(experts, -1, block.shape[1])
        return lax.all_to_all(block, "exp", split_axis=0, concat_axis=0, tiled=True).reshape(-1, block.shape[2])

    x_blocks = line_gather(to_experts(choose_rows(tokens, chosen, counts, pack, False)), seq_n)
    c_blocks = line_gather(to_experts(choose_rows(cotangent, chosen, counts, pack, True)), seq_n)

    x, pre_gate, pre_up, gates, hidden, *out = expert_forward(
        x_blocks, seq_n, slots, pack, router, threshold, w_gate, w_up, w_down, hid_scale
    )
    mixture = scatter_rows(to_experts(line_sum(out, seq_n)), chosen, counts, own, pack)

    c, gate_delta, up_delta, router_part, total, *back = expert_backward(
        c_blocks, seq_n, slots, pack, x, pre_gate, pre_up, gates, router, w_gate, w_up, w_down, hid_scale
    )
    token_grad = scatter_rows(to_experts(line_sum(back, seq_n)), chosen, counts, own, pack)

    message = jnp.concatenate(
        [router_part.reshape(everyone, -1), jnp.broadcast_to(total[:, :1], (everyone, 1))], axis=1
    )
    told = lax.all_to_all(message, BOTH, split_axis=0, concat_axis=0, tiled=True)
    told = jnp.sum(told.reshape(seq_n, experts, -1), axis=0)

    gate_grad, up_grad, down_grad = weight_grads(x, c, hidden, gate_delta, up_delta)
    return mixture, token_grad, told[:, :-1].T, told[:, -1], gate_grad, up_grad, down_grad


def solution(mesh):
    by_owner = P(BOTH, None)
    columns = P("exp", None, "seq")
    down = P("exp", "seq", None)
    return jax.shard_map(
        on_device,
        mesh=mesh,
        in_specs=(
            by_owner,
            by_owner,
            P(),
            P(),
            columns,
            columns,
            down,
            P("exp", "seq"),
            P(BOTH, None, None),
            by_owner,
        ),
        out_specs=(by_owner, by_owner, by_owner, P(), columns, columns, down),
        check_vma=False,
    )
```

time: 165 us -> 171 us (1.036)
  matrix products: 44.9 us -> 0 us
  starting transfers between devices: 22 us -> 64.5 us
  Pallas kernels: 0 us -> 41.9 us
  waiting for transfers between devices: 66.5 us -> 30.4 us
  local copies, waits for them, and re-layouts: 24.5 us -> 29 us
  other arithmetic: 4.52 us -> 2.1 us
    all_to_all x4, waiting for transfers between devices: 61.5 us -> 10.8 us  [to_experts(): lax.all_to_all(block, 'exp', split_axis=0, concat_axis=0, tiled=True)]
    ppermute x0 -> x24, starting transfers between devices: none -> 45.8 us  [the longest x6 19.6 us: line_sum(): right = lax.ppermute(right, 'seq', [(s, s + 1) for s in range(j)])]
    dot_general x15 -> x0, matrix products: 44.9 us -> none  [mm(): return lax.dot_general(a, b, (dims, ((), ())), preferred_element_type=F32)]
    pallas_call x0 -> x7, Pallas kernels: none -> 41.9 us  [the longest x1 10.7 us: expert_backward(): pl.pallas_call(body, grid=(2 * STEPS,), in_specs=in_specs, out_specs=out_...]
    unnamed x17 -> x91, local copies, waits for them, and re-layouts: 0.81 us -> 27.1 us
    ppermute x0 -> x24, waiting for transfers between devices: none -> 19.6 us  [the longest x6 15.5 us: line_gather(): left = lax.ppermute(left, 'seq', [(s, s - 1) for s in range(1, n - j + 1)])]
    reshape x7 -> x1, local copies, waits for them, and re-layouts: 15.4 us -> 0.02 us  [on_device(): router_part.reshape(everyone, -1)]
    all_to_all x1, waiting for transfers between devices: 5.01 us -> 0.01 us  [on_device(): lax.all_to_all(message, BOTH, split_axis=0, concat_axis=0, tiled=True)]
  transfers between devices with their start and end apart: 5 -> 29, of which waited for: 5 -> 12; matrix products, arithmetic and copies ran while one was open for 28% -> 3% of each run, Pallas kernels for 0% -> 14%
where the time goes in v2:
time: 171 us; the launch traced here: 169 us
  starting transfers between devices  64.5 us (38%)
  Pallas kernels  41.9 us (25%)
  waiting for transfers between devices  30.4 us (18%)
  local copies, waits for them, and re-layouts  29 us (17%)
  other arithmetic  2.1 us (1%)
    unnamed x91, local copies, waits for them, and re-layouts  27.1 us
    ppermute x6, starting transfers between devices, line_sum(): right = lax.ppermute(right, 'seq', [(s, s + 1) for s in range(j)])  19.6 us
    all_to_all x4, starting transfers between devices, to_experts(): lax.all_to_all(block, 'exp', split_axis=0, concat_axis=0, tiled=True)  15.8 us
    ppermute x6, waiting for transfers between devices, line_gather(): left = lax.ppermute(left, 'seq', [(s, s - 1) for s in range(1, n - j + 1)])  15.5 us
    ppermute x6, starting transfers between devices, line_gather(): lax.ppermute(right, 'seq', [(s, s + 1) for s in range(j - 1, n - 1)])  13.2 us
    all_to_all x4, waiting for transfers between devices, to_experts(): lax.all_to_all(block, 'exp', split_axis=0, concat_axis=0, tiled=True)  10.8 us
    pallas_call x1, Pallas kernels, expert_backward(): pl.pallas_call(body, grid=(2 * STEPS,), in_specs=in_specs, out_specs=out_...  10.7 us
    pallas_call x2, Pallas kernels, scatter_rows(): pl.pallas_call(body, grid=(pack, STEPS), in_specs=[in_smem(), in_smem(),...  9.56 us
  transfers between devices with their start and end apart: 29, of which 12 were waited for; matrix products, arithmetic and copies ran while one was open for 3% of the time, Pallas kernels for 14%

profile of v2, /device:TPU:0, one launch (start us, length us, event | category | flops | bytes accessed | tf_op | source)
XLA Modules:
  0.0 169.1 jit_solution(9056753984704570161)
XLA Ops:
  0.7 1.6 copy-done.3
  3.6 2.7 %shard_map.153 = bf16[64,2048]{1,0:T(8,128)(2,1)} custom-call(s32[4,8]{1,0:T(4,128)S(1)} %bitcast.29, s32[1,8]{1,0:T(1,128)S(1)} %copy-done.32, bf16[256,4096]{1,0:T(8,128)(2,1)S(1)} %copy-done.3, bf16[256,4096]{1,0:T(8,128)(2,1)S(1)} %copy-done.3), custom_call_target="tpu_custom_call" | custom-call | flops 134217728 | bytes 2097152 | tf_op jit(solution)/shard_map/pallas_call | solution.py:69
  6.2 5.3 %all-to-all-start = ((bf16[8,8,2048]{2,1,0:T(8,128)(2,1)}), bf16[8,8,2048]{2,1,0:T(8,128)(2,1)S(1)}, u32[]{:S(2)}, u32[]{:S(2)}) async-start(bf16[8,8,2048]{2,1,0:T(8,128)(2,1)} %bitcast.3), calls=%async_computation | async-start | bytes 524288 | tf_op jit(solution)/shard_map/all_to_all | solution.py:462
  11.6 1.6 copy-done.4
  13.2 1.7 %shard_map.156 = bf16[64,2048]{1,0:T(8,128)(2,1)S(1)} custom-call(s32[4,8]{1,0:T(4,128)S(1)} %bitcast.30, s32[1,8]{1,0:T(1,128)S(1)} %copy-done.33, bf16[256,4096]{1,0:T(8,128)(2,1)S(1)} %copy-done.4, bf16[256,4096]{1,0:T(8,128)(2,1)S(1)} %copy-done.4), custom_call_target="tpu_custom_call" | custom-call | flops 134217728 | bytes 2097152 | tf_op jit(solution)/shard_map/pallas_call | solution.py:69
  15.6 2.9 %all-to-all-done = bf16[8,8,2048]{2,1,0:T(8,128)(2,1)S(1)} async-done(((bf16[8,8,2048]{2,1,0:T(8,128)(2,1)}), bf16[8,8,2048]{2,1,0:T(8,128)(2,1)S(1)}, u32[]{:S(2)}, u32[]{:S(2)}) %all-to-all-start) | async-done | bytes 262176 | tf_op jit(solution)/shard_map/all_to_all | solution.py:462
  19.2 3.4 %all-to-all-start.2 = ((bf16[8,8,2048]{2,1,0:T(8,128)(2,1)}), bf16[8,8,2048]{2,1,0:T(8,128)(2,1)S(1)}, u32[]{:S(2)}, u32[]{:S(2)}) async-start(bf16[8,8,2048]{2,1,0:T(8,128)(2,1)} %bitcast.27), calls=%async_computation.2 | async-start | bytes 524288 | tf_op jit(solution)/shard_map/all_to_all | solution.py:462
  22.6 4.2 %collective-permute-start = (bf16[64,2048]{1,0:T(8,128)(2,1)}, bf16[64,2048]{1,0:T(8,128)(2,1)}, u32[]{:S(2)}, u32[]{:S(2)}) collective-permute-start(bf16[64,2048]{1,0:T(8,128)(2,1)} %bitcast.23), channel_id=1, source_target_pairs={{0,8},{8,16},{16,24},{1,9},{9,17},{17,25},{2,10},{10,18},{18,26},{... | collective-permute-start | bytes 786440 | tf_op jit(solution)/shard_map/ppermute | solution.py:431
  26.8 1.3 collective-permute-start.3
  28.1 1.3 all-to-all-done.2
  29.5 3.5 %collective-permute-start.12 = (bf16[64,2048]{1,0:T(8,128)(2,1)S(1)}, bf16[64,2048]{1,0:T(8,128)(2,1)S(1)}, u32[]{:S(2)}, u32[]{:S(2)}) collective-permute-start(bf16[64,2048]{1,0:T(8,128)(2,1)S(1)} %bitcast.20), channel_id=1, source_target_pairs={{0,8},{8,16},{16,24},{1,9},{9,17},{17,25},{2,10},{10,18},{18,26},{... | collective-permute-start | bytes 786440 | tf_op jit(solution)/shard_map/ppermute | solution.py:431
  33.0 1.3 collective-permute-start.15
  34.3 1.4 collective-permute-start.1
  35.7 2.1 %collective-permute-done.3.refs_4_ = bf16[64,2048]{1,0:T(8,128)(2,1)} collective-permute-done((bf16[64,2048]{1,0:T(8,128)(2,1)}, bf16[64,2048]{1,0:T(8,128)(2,1)}, u32[]{:S(2)}, u32[]{:S(2)}) %collective-permute-start.3) | collective-permute-done | bytes 262176 | tf_op jit(solution)/shard_map/ppermute | solution.py:432
  37.8 1.3 collective-permute-start.4
  39.1 1.4 collective-permute-start.13
  41.2 1.9 %collective-permute-done.15.refs_4_ = bf16[64,2048]{1,0:T(8,128)(2,1)S(1)} collective-permute-done((bf16[64,2048]{1,0:T(8,128)(2,1)S(1)}, bf16[64,2048]{1,0:T(8,128)(2,1)S(1)}, u32[]{:S(2)}, u32[]{:S(2)}) %collective-permute-start.15) | collective-permute-done | bytes 262176 | tf_op jit(solution)/shard_map/ppermute | solution.py:432
  43.0 1.3 collective-permute-start.16
  45.0 1.4 collective-permute-start.2
  46.4 2.2 %collective-permute-done.4.refs_5_ = bf16[64,2048]{1,0:T(8,128)(2,1)} collective-permute-done((bf16[64,2048]{1,0:T(8,128)(2,1)}, bf16[64,2048]{1,0:T(8,128)(2,1)}, u32[]{:S(2)}, u32[]{:S(2)}) %collective-permute-start.4) | collective-permute-done | bytes 262176 | tf_op jit(solution)/shard_map/ppermute | solution.py:432
  48.6 1.3 collective-permute-start.5
  49.9 1.4 collective-permute-start.14
  51.2 6.4 %collective-permute-done.16.refs_5_ = bf16[64,2048]{1,0:T(8,128)(2,1)} collective-permute-done((bf16[64,2048]{1,0:T(8,128)(2,1)S(1)}, bf16[64,2048]{1,0:T(8,128)(2,1)}, u32[]{:S(2)}, u32[]{:S(2)}) %collective-permute-start.16) | collective-permute-done | bytes 262176 | tf_op jit(solution)/shard_map/ppermute | solution.py:432
  57.6 1.3 collective-permute-start.17
  58.9 1.3 copy.25.refs_7_.refs_8_
  60.2 3.0 %collective-permute-done.5.refs_6_ = bf16[64,2048]{1,0:T(8,128)(2,1)} collective-permute-done((bf16[64,2048]{1,0:T(8,128)(2,1)}, bf16[64,2048]{1,0:T(8,128)(2,1)}, u32[]{:S(2)}, u32[]{:S(2)}) %collective-permute-start.5) | collective-permute-done | bytes 262176 | tf_op jit(solution)/shard_map/ppermute | solution.py:432
  63.2 1.9 %copy-done.1 = bf16[1,4096,384]{2,1,0:T(8,128)(2,1)S(1)} copy-done((bf16[1,4096,384]{2,1,0:T(8,128)(2,1)S(1)}, bf16[1,4096,384]{2,1,0:T(8,128)(2,1)}, u32[]{:S(2)}) %copy-start.1) | copy-done | bytes 3145752
  65.1 1.2 copy-done.2
  67.3 9.0 %shard_map.154 = (bf16[256,2048]{1,0:T(8,128)(2,1)S(1)}, f32[256,384]{1,0:T(8,128)S(1)}, f32[256,384]{1,0:T(8,128)S(1)}, f32[256,128]{1,0:T(8,128)S(1)}, bf16[2,...) custom-call(bf16[64,2048]{1,0:T(8,128)(2,1)S(1)} %bitcast.25, ...), custom_call_target="tpu_custom_call" | custom-call | flops 2415919104 | bytes 9437184 | tf_op jit(solution)/shard_map/pallas_call | solution.py:223
  80.0 10.7 %shard_map.157 = (bf16[256,2048]{1,0:T(8,128)(2,1)S(1)}, bf16[2,256,384]{2,1,0:T(8,128)(2,1)S(1)}, bf16[2,256,384]{2,1,0:T(8,128)(2,1)S(1)}, f32[2,2048]{1,0:T(2...) custom-call(bf16[64,2048]{1,0:T(8,128)(2,1)S(1)} %bitcast.22, ...), custom_call_target="tpu_custom_call" | custom-call | flops 2415919104 | bytes 9437184 | tf_op jit(solution)/shard_map/pallas_call | solution.py:365
  96.7 2.9 %all-to-all-start.4 = ((f32[32,1,129]{2,1,0:T(1,128)}), f32[32,1,129]{2,1,0:T(1,128)S(1)}, u32[]{:S(2)}, u32[]{:S(2)}) async-start(f32[32,1,129]{2,1,0:T(1,128)} %all_to_all.22), calls=%async_computation.4 | async-start | bytes 65536 | tf_op jit(solution)/shard_map/all_to_all | solution.py:480
  99.6 3.7 %collective-permute-start.18 = (bf16[64,2048]{1,0:T(8,128)(2,1)}, bf16[64,2048]{1,0:T(8,128)(2,1)S(1)}, u32[]{:S(2)}, u32[]{:S(2)}) collective-permute-start(bf16[64,2048]{1,0:T(8,128)(2,1)} %copy-done.18), channel_id=1, source_target_pairs={{0,8},{1,9},{2,10},{3,11},{4,12},{5,13},{6,14},{7,15}} | collective-permute-start | bytes 786440 | tf_op jit(solution)/shard_map/ppermute | solution.py:447
  104.0 1.3 collective-permute-start.6
  107.2 1.2 copy-done.37
  111.4 8.3 %shard_map.159 = (f32[1,4096,384]{2,1,0:T(8,128)}, f32[1,4096,384]{2,1,0:T(8,128)}, f32[1,384,4096]{2,1,0:T(8,128)}) custom-call(bf16[256,2048]{1,0:T(8,128)(2,1)S(1)} %copy-done.8, bf16[256,2048]{1,0:T(8,128)(2,1)S(1)} %copy-done.37, bf16[2,256,384]{2,1,0:T(8,128)(2,1)S(1)} %copy-done.39, bf16[2,256,384]{2,1,0:T(8,128)(2,1)S(1)} %copy-done.41, ...), custom_call_target="tpu_custom_call" | custom-call | flops 2415919104 | bytes 18874368 | tf_op jit(solution)/shard_map/pallas_call | solution.py:408
  120.5 1.4 collective-permute-start.19
  122.8 4.0 %collective-permute-start.7 = (bf16[64,2048]{1,0:T(8,128)(2,1)S(1)}, bf16[64,2048]{1,0:T(8,128)(2,1)S(1)}, u32[]{:S(2)}, u32[]{:S(2)}) collective-permute-start(bf16[64,2048]{1,0:T(8,128)(2,1)S(1)} %get-tuple-element.51), channel_id=1, source_target_pairs={{0,8},{8,16},{1,9},{9,17},{2,10},{10,18},{3,11},{11,19},{4,12},{12... | collective-permute-start | bytes 786440 | tf_op jit(solution)/shard_map/ppermute | solution.py:447
  128.7 4.4 %collective-permute-start.20 = (bf16[64,2048]{1,0:T(8,128)(2,1)S(1)}, bf16[64,2048]{1,0:T(8,128)(2,1)S(1)}, u32[]{:S(2)}, u32[]{:S(2)}) collective-permute-start(bf16[64,2048]{1,0:T(8,128)(2,1)S(1)} %add_convert_fusion.2), channel_id=1, source_target_pairs={{0,8},{8,16},{16,24},{1,9},{9,17},{17,25},{2,10},{10,18},{18,26},{... | collective-permute-start | bytes 786440 | tf_op jit(solution)/shard_map/ppermute | solution.py:447
  133.2 1.3 collective-permute-start.23
  134.6 4.8 %collective-permute-start.8 = (bf16[64,2048]{1,0:T(8,128)(2,1)S(1)}, bf16[64,2048]{1,0:T(8,128)(2,1)S(1)}, u32[]{:S(2)}, u32[]{:S(2)}) collective-permute-start(bf16[64,2048]{1,0:T(8,128)(2,1)S(1)} %add_convert_fusion.5), channel_id=1, source_target_pairs={{0,8},{8,16},{16,24},{1,9},{9,17},{17,25},{2,10},{10,18},{18,26},{... | collective-permute-start | bytes 786440 | tf_op jit(solution)/shard_map/ppermute | solution.py:447
  139.5 1.3 collective-permute-start.11
  140.8 1.8 %collective-permute-done.23 = bf16[64,2048]{1,0:T(8,128)(2,1)S(1)} collective-permute-done((bf16[64,2048]{1,0:T(8,128)(2,1)S(1)}, bf16[64,2048]{1,0:T(8,128)(2,1)S(1)}, u32[]{:S(2)}, u32[]{:S(2)}) %collective-permute-start.23) | collective-permute-done | bytes 262176 | tf_op jit(solution)/shard_map/ppermute | solution.py:448
  143.4 3.7 %all-to-all-start.3 = ((bf16[8,8,2048]{2,1,0:T(8,128)(2,1)}), bf16[8,8,2048]{2,1,0:T(8,128)(2,1)S(1)}, u32[]{:S(2)}, u32[]{:S(2)}) async-start(bf16[8,8,2048]{2,1,0:T(8,128)(2,1)} %fusion.5), calls=%async_computation.3 | async-start | bytes 524288 | tf_op jit(solution)/shard_map/all_to_all | solution.py:462
  149.0 5.0 %all-to-all-done.3 = bf16[8,8,2048]{2,1,0:T(8,128)(2,1)S(1)} async-done(((bf16[8,8,2048]{2,1,0:T(8,128)(2,1)}), bf16[8,8,2048]{2,1,0:T(8,128)(2,1)S(1)}, u32[]{:S(2)}, u32[]{:S(2)}) %all-to-all-start.3) | async-done | bytes 262176 | tf_op jit(solution)/shard_map/all_to_all | solution.py:462
  154.0 3.4 %all-to-all-start.1 = ((bf16[8,8,2048]{2,1,0:T(8,128)(2,1)}), bf16[8,8,2048]{2,1,0:T(8,128)(2,1)S(1)}, u32[]{:S(2)}, u32[]{:S(2)}) async-start(bf16[8,8,2048]{2,1,0:T(8,128)(2,1)} %fusion.4), calls=%async_computation.1 | async-start | bytes 524288 | tf_op jit(solution)/shard_map/all_to_all | solution.py:462
  158.0 4.8 %shard_map.158 = bf16[256,4096]{1,0:T(8,128)(2,1)} custom-call(s32[4,8]{1,0:T(4,128)S(1)} %bitcast.31, s32[1,8]{1,0:T(1,128)S(1)} %copy-done.33, bf16[64,2048]{1,0:T(8,128)(2,1)S(1)} %bitcast.26), custom_call_target="tpu_custom_call" | custom-call | flops 134217728 | bytes 2097152 | tf_op jit(solution)/shard_map/pallas_call | solution.py:96
  162.8 1.5 all-to-all-done.1
  164.3 4.8 %shard_map.155 = bf16[256,4096]{1,0:T(8,128)(2,1)} custom-call(s32[4,8]{1,0:T(4,128)S(1)} %bitcast.32, s32[1,8]{1,0:T(1,128)S(1)} %copy-done.33, bf16[64,2048]{1,0:T(8,128)(2,1)S(1)} %bitcast.28), custom_call_target="tpu_custom_call" | custom-call | flops 134217728 | bytes 2097152 | tf_op jit(solution)/shard_map/pallas_call | solution.py:96
  (122 shorter events, 27.2 us)
Async XLA Ops:
  0.6 10.9 %copy-start.33 = (s32[1,8]{1,0:T(1,128)S(1)}, s32[1,8]{1,0:T(1,128)}, u32[]{:S(2)}) copy-start(s32[1,8]{1,0:T(1,128)} %counts_ref.7) | copy-start | bytes 100
  0.6 1.6 copy-start.3
  3.6 8.0 %copy-start.31 = (s32[1,8,4]{1,2,0:T(4,128)S(1)}, s32[1,8,4]{1,2,0:T(4,128)}, u32[]{:S(2)}) copy-start(s32[1,8,4]{1,2,0:T(4,128)} %param.18) | copy-start | bytes 388
  6.2 52.7 %copy-start.44 = (bf16[4096,8]{0,1:T(8,128)(2,1)S(1)}, bf16[4096,8]{0,1:T(8,128)(2,1)}, u32[]{:S(2)}) copy-start(bf16[4096,8]{0,1:T(8,128)(2,1)} %param.12) | copy-start | bytes 196612
  6.2 12.2 %all-to-all-start = ((bf16[8,8,2048]{2,1,0:T(8,128)(2,1)}), bf16[8,8,2048]{2,1,0:T(8,128)(2,1)S(1)}, u32[]{:S(2)}, u32[]{:S(2)}) async-start(bf16[8,8,2048]{2,1,0:T(8,128)(2,1)} %bitcast.3), calls=%async_computation | async-start | bytes 524288 | tf_op jit(solution)/shard_map/all_to_all | solution.py:462
  13.2 50.1 %copy-start = (bf16[1,4096,384]{2,1,0:T(8,128)(2,1)S(1)}, bf16[1,4096,384]{2,1,0:T(8,128)(2,1)}, u32[]{:S(2)}) copy-start(bf16[1,4096,384]{2,1,0:T(8,128)(2,1)} %refs_10_.3) | copy-start | bytes 9437188
  13.2 50.1 %copy-start.34 = (f32[1,384]{1,0:T(1,128)S(1)}, f32[1,384]{1,0:T(1,128)}, u32[]{:S(2)}) copy-start(f32[1,384]{1,0:T(1,128)} %refs_15_.1) | copy-start | bytes 4612
  13.2 50.1 %copy-start.35 = (f32[8]{0:T(128)S(1)}, f32[8]{0:T(128)}, u32[]{:S(2)}) copy-start(f32[8]{0:T(128)} %param.13) | copy-start | bytes 100
  19.2 10.3 %all-to-all-start.2 = ((bf16[8,8,2048]{2,1,0:T(8,128)(2,1)}), bf16[8,8,2048]{2,1,0:T(8,128)(2,1)S(1)}, u32[]{:S(2)}, u32[]{:S(2)}) async-start(bf16[8,8,2048]{2,1,0:T(8,128)(2,1)} %bitcast.27), calls=%async_computation.2 | async-start | bytes 524288 | tf_op jit(solution)/shard_map/all_to_all | solution.py:462
  22.6 11.7 %collective-permute-start = (bf16[64,2048]{1,0:T(8,128)(2,1)}, bf16[64,2048]{1,0:T(8,128)(2,1)}, u32[]{:S(2)}, u32[]{:S(2)}) collective-permute-start(bf16[64,2048]{1,0:T(8,128)(2,1)} %bitcast.23), channel_id=1, source_target_pairs={{0,8},{8,16},{16,24},{1,9},{9,17},{17,25},{2,10},{10,18},{18,26},{... | collective-permute-start | bytes 786440 | tf_op jit(solution)/shard_map/ppermute | solution.py:431
  26.8 10.9 %collective-permute-start.3 = (bf16[64,2048]{1,0:T(8,128)(2,1)}, bf16[64,2048]{1,0:T(8,128)(2,1)}, u32[]{:S(2)}, u32[]{:S(2)}) collective-permute-start(bf16[64,2048]{1,0:T(8,128)(2,1)} %bitcast.24), channel_id=1, source_target_pairs={{8,0},{16,8},{24,16},{9,1},{17,9},{25,17},{10,2},{18,10},{26,18},{... | collective-permute-start | bytes 786440 | tf_op jit(solution)/shard_map/ppermute | solution.py:432
  29.5 9.6 %collective-permute-start.12 = (bf16[64,2048]{1,0:T(8,128)(2,1)S(1)}, bf16[64,2048]{1,0:T(8,128)(2,1)S(1)}, u32[]{:S(2)}, u32[]{:S(2)}) collective-permute-start(bf16[64,2048]{1,0:T(8,128)(2,1)S(1)} %bitcast.20), channel_id=1, source_target_pairs={{0,8},{8,16},{16,24},{1,9},{9,17},{17,25},{2,10},{10,18},{18,26},{... | collective-permute-start | bytes 786440 | tf_op jit(solution)/shard_map/ppermute | solution.py:431
  33.0 10.1 %collective-permute-start.15 = (bf16[64,2048]{1,0:T(8,128)(2,1)S(1)}, bf16[64,2048]{1,0:T(8,128)(2,1)S(1)}, u32[]{:S(2)}, u32[]{:S(2)}) collective-permute-start(bf16[64,2048]{1,0:T(8,128)(2,1)S(1)} %bitcast.21), channel_id=1, source_target_pairs={{8,0},{16,8},{24,16},{9,1},{17,9},{25,17},{10,2},{18,10},{26,18},{... | collective-permute-start | bytes 786440 | tf_op jit(solution)/shard_map/ppermute | solution.py:432
  34.3 10.8 %collective-permute-start.1 = (bf16[64,2048]{1,0:T(8,128)(2,1)}, bf16[64,2048]{1,0:T(8,128)(2,1)}, u32[]{:S(2)}, u32[]{:S(2)}) collective-permute-start(bf16[64,2048]{1,0:T(8,128)(2,1)} %collective-permute-done.refs_1_), channel_id=1, source_target_pairs={{8,16},{16,24},{9,17},{17,25},{10,18},{18,26},{11,19},{19,27},{12,... | collective-permute-start | bytes 786440 | tf_op jit(solution)/shard_map/ppermute | solution.py:431
  37.8 10.8 %collective-permute-start.4 = (bf16[64,2048]{1,0:T(8,128)(2,1)}, bf16[64,2048]{1,0:T(8,128)(2,1)}, u32[]{:S(2)}, u32[]{:S(2)}) collective-permute-start(bf16[64,2048]{1,0:T(8,128)(2,1)} %collective-permute-done.3.refs_4_), channel_id=1, source_target_pairs={{8,0},{16,8},{9,1},{17,9},{10,2},{18,10},{11,3},{19,11},{12,4},{20... | collective-permute-start | bytes 786440 | tf_op jit(solution)/shard_map/ppermute | solution.py:432
  39.1 10.8 %collective-permute-start.13 = (bf16[64,2048]{1,0:T(8,128)(2,1)S(1)}, bf16[64,2048]{1,0:T(8,128)(2,1)}, u32[]{:S(2)}, u32[]{:S(2)}) collective-permute-start(bf16[64,2048]{1,0:T(8,128)(2,1)S(1)} %collective-permute-done.12.refs_1_), channel_id=1, source_target_pairs={{8,16},{16,24},{9,17},{17,25},{10,18},{18,26},{11,19},{19,27},{12,... | collective-permute-start | bytes 786440 | tf_op jit(solution)/shard_map/ppermute | solution.py:431
  43.0 14.6 %collective-permute-start.16 = (bf16[64,2048]{1,0:T(8,128)(2,1)S(1)}, bf16[64,2048]{1,0:T(8,128)(2,1)}, u32[]{:S(2)}, u32[]{:S(2)}) collective-permute-start(bf16[64,2048]{1,0:T(8,128)(2,1)S(1)} %collective-permute-done.15.refs_4_), channel_id=1, source_target_pairs={{8,0},{16,8},{9,1},{17,9},{10,2},{18,10},{11,3},{19,11},{12,4},{20... | collective-permute-start | bytes 786440 | tf_op jit(solution)/shard_map/ppermute | solution.py:432
  45.0 15.2 %collective-permute-start.2 = (bf16[64,2048]{1,0:T(8,128)(2,1)}, bf16[64,2048]{1,0:T(8,128)(2,1)}, u32[]{:S(2)}, u32[]{:S(2)}) collective-permute-start(bf16[64,2048]{1,0:T(8,128)(2,1)} %collective-permute-done.1.refs_2_), channel_id=1, source_target_pairs={{16,24},{17,25},{18,26},{19,27},{20,28},{21,29},{22,30},{23,31}} | collective-permute-start | bytes 786440 | tf_op jit(solution)/shard_map/ppermute | solution.py:431
  48.6 14.7 %collective-permute-start.5 = (bf16[64,2048]{1,0:T(8,128)(2,1)}, bf16[64,2048]{1,0:T(8,128)(2,1)}, u32[]{:S(2)}, u32[]{:S(2)}) collective-permute-start(bf16[64,2048]{1,0:T(8,128)(2,1)} %collective-permute-done.4.refs_5_), channel_id=1, source_target_pairs={{8,0},{9,1},{10,2},{11,3},{12,4},{13,5},{14,6},{15,7}} | collective-permute-start | bytes 786440 | tf_op jit(solution)/shard_map/ppermute | solution.py:432
  49.9 30.1 %collective-permute-start.14 = (bf16[64,2048]{1,0:T(8,128)(2,1)}, bf16[64,2048]{1,0:T(8,128)(2,1)}, u32[]{:S(2)}, u32[]{:S(2)}) collective-permute-start(bf16[64,2048]{1,0:T(8,128)(2,1)} %collective-permute-done.13.refs_2_), channel_id=1, source_target_pairs={{16,24},{17,25},{18,26},{19,27},{20,28},{21,29},{22,30},{23,31}} | collective-permute-start | bytes 786440 | tf_op jit(solution)/shard_map/ppermute | solution.py:431
  57.6 22.4 %collective-permute-start.17 = (bf16[64,2048]{1,0:T(8,128)(2,1)}, bf16[64,2048]{1,0:T(8,128)(2,1)}, u32[]{:S(2)}, u32[]{:S(2)}) collective-permute-start(bf16[64,2048]{1,0:T(8,128)(2,1)} %collective-permute-done.16.refs_5_), channel_id=1, source_target_pairs={{8,0},{9,1},{10,2},{11,3},{12,4},{13,5},{14,6},{15,7}} | collective-permute-start | bytes 786440 | tf_op jit(solution)/shard_map/ppermute | solution.py:432
  63.2 1.9 %copy-start.1 = (bf16[1,4096,384]{2,1,0:T(8,128)(2,1)S(1)}, bf16[1,4096,384]{2,1,0:T(8,128)(2,1)}, u32[]{:S(2)}) copy-start(bf16[1,4096,384]{2,1,0:T(8,128)(2,1)} %refs_12_.3) | copy-start | bytes 9437188
  67.3 12.7 %copy-start.11 = (bf16[64,2048]{1,0:T(8,128)(2,1)S(1)}, bf16[64,2048]{1,0:T(8,128)(2,1)}, u32[]{:S(2)}) copy-start(bf16[64,2048]{1,0:T(8,128)(2,1)} %copy-done.10) | copy-start | bytes 786436
  67.3 12.7 %copy-start.13 = (bf16[64,2048]{1,0:T(8,128)(2,1)S(1)}, bf16[64,2048]{1,0:T(8,128)(2,1)}, u32[]{:S(2)}) copy-start(bf16[64,2048]{1,0:T(8,128)(2,1)} %copy-done.12) | copy-start | bytes 786436
  80.0 10.7 %copy-start.7 = (bf16[256,2048]{1,0:T(8,128)(2,1)}, bf16[256,2048]{1,0:T(8,128)(2,1)S(1)}, u32[]{:S(2)}) copy-start(bf16[256,2048]{1,0:T(8,128)(2,1)S(1)} %get-tuple-element.32.refs_16_.x_ref) | copy-start | bytes 3145732
  96.7 23.0 %all-to-all-start.4 = ((f32[32,1,129]{2,1,0:T(1,128)}), f32[32,1,129]{2,1,0:T(1,128)S(1)}, u32[]{:S(2)}, u32[]{:S(2)}) async-start(f32[32,1,129]{2,1,0:T(1,128)} %all_to_all.22), calls=%async_computation.4 | async-start | bytes 65536 | tf_op jit(solution)/shard_map/all_to_all | solution.py:480
  99.6 20.8 %collective-permute-start.18 = (bf16[64,2048]{1,0:T(8,128)(2,1)}, bf16[64,2048]{1,0:T(8,128)(2,1)S(1)}, u32[]{:S(2)}, u32[]{:S(2)}) collective-permute-start(bf16[64,2048]{1,0:T(8,128)(2,1)} %copy-done.18), channel_id=1, source_target_pairs={{0,8},{1,9},{2,10},{3,11},{4,12},{5,13},{6,14},{7,15}} | collective-permute-start | bytes 786440 | tf_op jit(solution)/shard_map/ppermute | solution.py:447
  103.3 17.1 %collective-permute-start.21 = (bf16[64,2048]{1,0:T(8,128)(2,1)}, bf16[64,2048]{1,0:T(8,128)(2,1)S(1)}, u32[]{:S(2)}, u32[]{:S(2)}) collective-permute-start(bf16[64,2048]{1,0:T(8,128)(2,1)} %copy-done.22), channel_id=1, source_target_pairs={{24,16},{25,17},{26,18},{27,19},{28,20},{29,21},{30,22},{31,23}} | collective-permute-start | bytes 786440 | tf_op jit(solution)/shard_map/ppermute | solution.py:448
  104.0 18.7 %collective-permute-start.6 = (bf16[64,2048]{1,0:T(8,128)(2,1)}, bf16[64,2048]{1,0:T(8,128)(2,1)S(1)}, u32[]{:S(2)}, u32[]{:S(2)}) collective-permute-start(bf16[64,2048]{1,0:T(8,128)(2,1)} %copy-done.14), channel_id=1, source_target_pairs={{0,8},{1,9},{2,10},{3,11},{4,12},{5,13},{6,14},{7,15}} | collective-permute-start | bytes 786440 | tf_op jit(solution)/shard_map/ppermute | solution.py:447
  105.3 17.3 %collective-permute-start.9 = (bf16[64,2048]{1,0:T(8,128)(2,1)}, bf16[64,2048]{1,0:T(8,128)(2,1)S(1)}, u32[]{:S(2)}, u32[]{:S(2)}) collective-permute-start(bf16[64,2048]{1,0:T(8,128)(2,1)} %copy-done.16), channel_id=1, source_target_pairs={{24,16},{25,17},{26,18},{27,19},{28,20},{29,21},{30,22},{31,23}} | collective-permute-start | bytes 786440 | tf_op jit(solution)/shard_map/ppermute | solution.py:448
  111.4 8.9 %copy-start.25 = (bf16[64,2048]{1,0:T(8,128)(2,1)S(1)}, bf16[64,2048]{1,0:T(8,128)(2,1)}, u32[]{:S(2)}) copy-start(bf16[64,2048]{1,0:T(8,128)(2,1)} %copy-done.24) | copy-start | bytes 786436
  111.4 11.2 %copy-start.21 = (bf16[64,2048]{1,0:T(8,128)(2,1)S(1)}, bf16[64,2048]{1,0:T(8,128)(2,1)}, u32[]{:S(2)}) copy-start(bf16[64,2048]{1,0:T(8,128)(2,1)} %copy-done.20) | copy-start | bytes 786436
  111.4 17.2 %copy-start.23 = (bf16[64,2048]{1,0:T(8,128)(2,1)S(1)}, bf16[64,2048]{1,0:T(8,128)(2,1)}, u32[]{:S(2)}) copy-start(bf16[64,2048]{1,0:T(8,128)(2,1)} %copy-done.22) | copy-start | bytes 786436
  119.7 13.4 %copy-start.19 = (bf16[64,2048]{1,0:T(8,128)(2,1)S(1)}, bf16[64,2048]{1,0:T(8,128)(2,1)}, u32[]{:S(2)}) copy-start(bf16[64,2048]{1,0:T(8,128)(2,1)} %copy-done.18) | copy-start | bytes 786436
  119.7 14.8 %copy-start.17 = (bf16[64,2048]{1,0:T(8,128)(2,1)S(1)}, bf16[64,2048]{1,0:T(8,128)(2,1)}, u32[]{:S(2)}) copy-start(bf16[64,2048]{1,0:T(8,128)(2,1)} %copy-done.16) | copy-start | bytes 786436
  119.7 19.7 %copy-start.15 = (bf16[64,2048]{1,0:T(8,128)(2,1)S(1)}, bf16[64,2048]{1,0:T(8,128)(2,1)}, u32[]{:S(2)}) copy-start(bf16[64,2048]{1,0:T(8,128)(2,1)} %copy-done.14) | copy-start | bytes 786436
  119.7 22.9 %copy-start.29 = (bf16[64,2048]{1,0:T(8,128)(2,1)S(1)}, bf16[64,2048]{1,0:T(8,128)(2,1)}, u32[]{:S(2)}) copy-start(bf16[64,2048]{1,0:T(8,128)(2,1)} %copy-done.28) | copy-start | bytes 786436
  120.5 27.7 %copy-start.27 = (bf16[64,2048]{1,0:T(8,128)(2,1)S(1)}, bf16[64,2048]{1,0:T(8,128)(2,1)}, u32[]{:S(2)}) copy-start(bf16[64,2048]{1,0:T(8,128)(2,1)} %copy-done.26) | copy-start | bytes 786436
  120.5 8.1 %collective-permute-start.19 = (bf16[64,2048]{1,0:T(8,128)(2,1)S(1)}, bf16[64,2048]{1,0:T(8,128)(2,1)S(1)}, u32[]{:S(2)}, u32[]{:S(2)}) collective-permute-start(bf16[64,2048]{1,0:T(8,128)(2,1)S(1)} %get-tuple-element.49), channel_id=1, source_target_pairs={{0,8},{8,16},{1,9},{9,17},{2,10},{10,18},{3,11},{11,19},{4,12},{12... | collective-permute-start | bytes 786440 | tf_op jit(solution)/shard_map/ppermute | solution.py:447
  122.0 11.1 %collective-permute-start.22 = (bf16[64,2048]{1,0:T(8,128)(2,1)S(1)}, bf16[64,2048]{1,0:T(8,128)(2,1)S(1)}, u32[]{:S(2)}, u32[]{:S(2)}) collective-permute-start(bf16[64,2048]{1,0:T(8,128)(2,1)S(1)} %get-tuple-element.50), channel_id=1, source_target_pairs={{16,8},{24,16},{17,9},{25,17},{18,10},{26,18},{19,11},{27,19},{20,... | collective-permute-start | bytes 786440 | tf_op jit(solution)/shard_map/ppermute | solution.py:448
  122.8 11.7 %collective-permute-start.7 = (bf16[64,2048]{1,0:T(8,128)(2,1)S(1)}, bf16[64,2048]{1,0:T(8,128)(2,1)S(1)}, u32[]{:S(2)}, u32[]{:S(2)}) collective-permute-start(bf16[64,2048]{1,0:T(8,128)(2,1)S(1)} %get-tuple-element.51), channel_id=1, source_target_pairs={{0,8},{8,16},{1,9},{9,17},{2,10},{10,18},{3,11},{11,19},{4,12},{12... | collective-permute-start | bytes 786440 | tf_op jit(solution)/shard_map/ppermute | solution.py:447
  126.8 12.6 %collective-permute-start.10 = (bf16[64,2048]{1,0:T(8,128)(2,1)S(1)}, bf16[64,2048]{1,0:T(8,128)(2,1)S(1)}, u32[]{:S(2)}, u32[]{:S(2)}) collective-permute-start(bf16[64,2048]{1,0:T(8,128)(2,1)S(1)} %get-tuple-element.52), channel_id=1, source_target_pairs={{16,8},{24,16},{17,9},{25,17},{18,10},{26,18},{19,11},{27,19},{20,... | collective-permute-start | bytes 786440 | tf_op jit(solution)/shard_map/ppermute | solution.py:448
  128.7 12.1 %collective-permute-start.20 = (bf16[64,2048]{1,0:T(8,128)(2,1)S(1)}, bf16[64,2048]{1,0:T(8,128)(2,1)S(1)}, u32[]{:S(2)}, u32[]{:S(2)}) collective-permute-start(bf16[64,2048]{1,0:T(8,128)(2,1)S(1)} %add_convert_fusion.2), channel_id=1, source_target_pairs={{0,8},{8,16},{16,24},{1,9},{9,17},{17,25},{2,10},{10,18},{18,26},{... | collective-permute-start | bytes 786440 | tf_op jit(solution)/shard_map/ppermute | solution.py:447
  133.2 9.4 %collective-permute-start.23 = (bf16[64,2048]{1,0:T(8,128)(2,1)S(1)}, bf16[64,2048]{1,0:T(8,128)(2,1)S(1)}, u32[]{:S(2)}, u32[]{:S(2)}) collective-permute-start(bf16[64,2048]{1,0:T(8,128)(2,1)S(1)} %add_convert_fusion.1), channel_id=1, source_target_pairs={{8,0},{16,8},{24,16},{9,1},{17,9},{25,17},{10,2},{18,10},{26,18},{... | collective-permute-start | bytes 786440 | tf_op jit(solution)/shard_map/ppermute | solution.py:448
  134.6 12.5 %collective-permute-start.8 = (bf16[64,2048]{1,0:T(8,128)(2,1)S(1)}, bf16[64,2048]{1,0:T(8,128)(2,1)S(1)}, u32[]{:S(2)}, u32[]{:S(2)}) collective-permute-start(bf16[64,2048]{1,0:T(8,128)(2,1)S(1)} %add_convert_fusion.5), channel_id=1, source_target_pairs={{0,8},{8,16},{16,24},{1,9},{9,17},{17,25},{2,10},{10,18},{18,26},{... | collective-permute-start | bytes 786440 | tf_op jit(solution)/shard_map/ppermute | solution.py:447
  139.5 8.7 %collective-permute-start.11 = (bf16[64,2048]{1,0:T(8,128)(2,1)S(1)}, bf16[64,2048]{1,0:T(8,128)(2,1)S(1)}, u32[]{:S(2)}, u32[]{:S(2)}) collective-permute-start(bf16[64,2048]{1,0:T(8,128)(2,1)S(1)} %add_convert_fusion.4), channel_id=1, source_target_pairs={{8,0},{16,8},{24,16},{9,1},{17,9},{25,17},{10,2},{18,10},{26,18},{... | collective-permute-start | bytes 786440 | tf_op jit(solution)/shard_map/ppermute | solution.py:448
  143.4 10.6 %all-to-all-start.3 = ((bf16[8,8,2048]{2,1,0:T(8,128)(2,1)}), bf16[8,8,2048]{2,1,0:T(8,128)(2,1)S(1)}, u32[]{:S(2)}, u32[]{:S(2)}) async-start(bf16[8,8,2048]{2,1,0:T(8,128)(2,1)} %fusion.5), calls=%async_computation.3 | async-start | bytes 524288 | tf_op jit(solution)/shard_map/all_to_all | solution.py:462
  154.0 10.3 %all-to-all-start.1 = ((bf16[8,8,2048]{2,1,0:T(8,128)(2,1)}), bf16[8,8,2048]{2,1,0:T(8,128)(2,1)S(1)}, u32[]{:S(2)}, u32[]{:S(2)}) async-start(bf16[8,8,2048]{2,1,0:T(8,128)(2,1)} %fusion.4), calls=%async_computation.1 | async-start | bytes 524288 | tf_op jit(solution)/shard_map/all_to_all | solution.py:462
  (26 other events, 22.3 us)

commit v3 on v1

v3 whole, which is shorter than its diff:
```python
import jax
import jax.numpy as jnp
from jax import lax
from jax.experimental import pallas as pl
from jax.experimental.pallas import tpu as pltpu
from jax.sharding import PartitionSpec as P

BOTH = ("seq", "exp")
F32 = jnp.float32
BF16 = jnp.bfloat16
ROWS = ((0,), (0,))
LAST = ((1,), (1,))
STEPS = 4
LANES = 128


def mm(a, b, dims=((1,), (0,))):
    return lax.dot_general(a, b, (dims, ((), ())), preferred_element_type=F32)


def limit(mib):
    return pltpu.CompilerParams(vmem_limit_bytes=mib * 2**20)


def cost(flops, moved):
    return pl.CostEstimate(flops=flops, bytes_accessed=moved, transcendentals=0)


def shape(dims, dtype=BF16):
    return jax.ShapeDtypeStruct(dims, dtype)


IN_HBM = pl.BlockSpec(memory_space=pltpu.HBM)
ANYWHERE = pl.BlockSpec(memory_space=pl.ANY)
IN_VMEM = pl.BlockSpec(memory_space=pltpu.VMEM)


def choose_rows(rows, picks, counts, pack, only_live):
    own, features = rows.shape
    slots, experts = picks.shape
    count = experts * pack * slots
    part = features // pack
    width = part // STEPS

    def body(picks_ref, counts_ref, rows_ref, out_ref, hot_ref, picks_s, counts_s, rows_v, sems):
        small = [
            pltpu.make_async_copy(picks_ref, picks_s, sems.at[STEPS]),
            pltpu.make_async_copy(counts_ref, counts_s, sems.at[STEPS + 1]),
        ]
        large = [
            pltpu.make_async_copy(rows_ref.at[:, pl.ds(j * pack * width, pack * width)],
                                  rows_v.at[:, pl.ds(j * pack * width, pack * width)], sems.at[j])
            for j in range(STEPS)
        ]
        for copy in small + large:
            copy.start()
        for copy in small:
            copy.wait()
        dims = (count, own)
        row = lax.broadcasted_iota(jnp.int32, dims, 0)
        token = lax.broadcasted_iota(jnp.int32, dims, 1)
        place = row // (pack * slots) * slots + row % slots
        part_of = (row // slots) % pack
        want = jnp.full(dims, -1, jnp.int32)
        for e in range(experts):
            for k in range(slots):
                pick = picks_s[k, e]
                if only_live:
                    pick = jnp.where(k < counts_s[0, e], pick, -1)
                want = jnp.where(place == e * slots + k, pick, want)
        for h in range(pack):
            hot_ref[h] = jnp.where((want == token) & (part_of == h), 1.0, 0.0).astype(BF16)
        for copy in large:
            copy.wait()
        for j in range(STEPS):
            out_ref[:, j * width : (j + 1) * width] = sum(
                mm(hot_ref[h], rows_v[:, h * part + j * width : h * part + (j + 1) * width]) for h in range(pack)
            ).astype(BF16)

    return pl.pallas_call(
        body,
        in_specs=[IN_HBM] * 3,
        out_specs=[IN_VMEM] * 2,
        out_shape=[shape((count, part)), shape((pack, count, own))],
        scratch_shapes=[
            pltpu.SMEM(picks.shape, jnp.int32),
            pltpu.SMEM(counts.shape, jnp.int32),
            pltpu.VMEM(rows.shape, BF16),
            pltpu.SemaphoreType.DMA((STEPS + 2,)),
        ],
        compiler_params=limit(8),
        cost_estimate=cost(2 * count * own * features, 2 * features * own),
    )(picks, counts, rows)


def scatter_rows(back, hot):
    count, part = back.shape
    pack, _, own = hot.shape
    width = part // 2

    def body(hot_ref, back_ref, out_ref):
        out_ref[...] = mm(hot_ref[...], back_ref[...], ROWS).astype(BF16)

    return pl.pallas_call(
        body,
        grid=(pack, 2),
        in_specs=[
            pl.BlockSpec((None, count, own), lambda h, i: (h, 0, 0)),
            pl.BlockSpec((count, width), lambda h, i: (0, i)),
        ],
        out_specs=pl.BlockSpec((own, width), lambda h, i: (0, h * 2 + i)),
        out_shape=shape((own, part * pack)),
        compiler_params=limit(8),
        cost_estimate=cost(2 * count * own * part * pack, 2 * part * pack * own),
    )(hot, back)


def first_part(rows, pack, slots):
    return (lax.broadcasted_iota(jnp.int32, (rows, 1), 0) // slots) % pack == 0


def fold(parts, slots):
    rows = parts[0].shape[0]
    total = parts[0]
    for h in range(1, len(parts)):
        total = total + pltpu.roll(parts[h], rows - h * slots, 0)
    return total


def spread(value, pack, slots):
    return [value if h == 0 else pltpu.roll(value, h * slots, 0) for h in range(pack)]


class Arrivals:
    def __init__(self, blocks, plan):
        self.blocks, self.plan = blocks, plan

    def start(self, refs, target, sems):
        rows = refs[0].shape[0]
        here = lax.axis_index("seq")
        for k, (a, b, t) in enumerate(self.plan):
            place = target.at[pl.ds(k * rows, rows), :]
            if a == b:
                pltpu.make_async_copy(refs[a], place, sems.at[k]).start()
            else:

                @pl.when(here >= t)
                def _():
                    pltpu.make_async_copy(refs[a], place, sems.at[k]).start()

                @pl.when(here < t)
                def _():
                    pltpu.make_async_copy(refs[b], place, sems.at[k]).start()

    def wait(self, refs, target, sems):
        rows = refs[0].shape[0]
        for k, (a, _, _) in enumerate(self.plan):
            pltpu.make_async_copy(refs[a], target.at[pl.ds(k * rows, rows), :], sems.at[k]).wait()


def side_copies(gate_ref, up_ref, router_ref, side, sems, pack, j, width):
    part = side.shape[0]
    hidden_n = gate_ref.shape[2]
    rows = pl.ds(j * width, width)
    copies = []
    for h in range(pack):
        for n, ref in enumerate((gate_ref, up_ref)):
            columns = pl.ds((2 * h + n) * hidden_n, hidden_n)
            copies.append((ref.at[0, pl.ds(h * part + j * width, width), :], side.at[rows, columns]))
    columns = pl.ds(2 * pack * hidden_n, LANES)
    copies.append((router_ref.at[rows, :], side.at[rows, columns]))
    return [pltpu.make_async_copy(a, b, sems.at[j, n]) for n, (a, b) in enumerate(copies)]


def down_copies(down_ref, stack, sems, pack):
    hidden_n = down_ref.shape[1]
    part = stack.shape[1]
    return [
        pltpu.make_async_copy(
            down_ref.at[0, :, pl.ds(h * part, part)], stack.at[pl.ds(h * hidden_n, hidden_n), :], sems.at[h]
        )
        for h in range(pack)
    ]


def send_blocks(out, out_refs, seq_n, columns):
    rows = out.shape[0] // seq_n
    for k in range(seq_n):
        out_refs[k][:, columns] = out[k * rows : (k + 1) * rows]
    if len(out_refs) > seq_n:
        here = lax.axis_index("seq")

        @pl.when(here == 0)
        def _():
            out_refs[seq_n][:, columns] = out[rows : 2 * rows]

        @pl.when(here > 0)
        def _():
            out_refs[seq_n][:, columns] = out[(seq_n - 1) * rows :]


def sends(seq_n):
    return seq_n + 1 if seq_n == 4 else seq_n


def expert_forward(arrivals, seq_n, slots, experts, pack, router_side, threshold, w_gate, w_up, w_down, hid_scale):
    block_rows, part = arrivals.blocks[0].shape
    rows = block_rows * seq_n
    hidden_n = w_gate.shape[2]
    width = part // STEPS
    total = 2 * pack * hidden_n + LANES
    n_blocks = len(arrivals.blocks)
    n_sends = sends(seq_n)

    def body(*refs):
        blocks = refs[:n_blocks]
        router_ref, gate_ref, up_ref, down_ref, threshold_ref, scale_ref = refs[n_blocks : n_blocks + 6]
        x_ref, pre_ref, hidden_ref = refs[n_blocks + 6 : n_blocks + 9]
        out_refs = refs[n_blocks + 9 : n_blocks + 9 + n_sends]
        side, stack, x_sems, side_sems, stack_sems = refs[n_blocks + 9 + n_sends :]
        arrivals.start(blocks, x_ref, x_sems)
        chunks = [side_copies(gate_ref, up_ref, router_ref, side, side_sems, pack, j, width) for j in range(STEPS)]
        downs = down_copies(down_ref, stack, stack_sems, pack)
        for chunk in chunks:
            for copy in chunk:
                copy.start()
        for copy in downs:
            copy.start()
        arrivals.wait(blocks, x_ref, x_sems)
        for j, chunk in enumerate(chunks):
            for copy in chunk:
                copy.wait()
            y = mm(x_ref[:, j * width : (j + 1) * width], side[j * width : (j + 1) * width, :])
            if j == 0:
                acc = y
            else:
                acc = acc + y
        columns = [acc[:, n * hidden_n : (n + 1) * hidden_n] for n in range(2 * pack)]
        gate = fold(columns[0::2], slots)
        up = fold(columns[1::2], slots)
        scores = acc[:, 2 * pack * hidden_n :]
        lane = lax.broadcasted_iota(jnp.int32, scores.shape, 1)
        expert = lax.axis_index("exp")
        score = fold([jnp.where(lane == h * experts + expert, scores, 0.0) for h in range(pack)], slots)
        lane = lax.broadcasted_iota(jnp.int32, threshold_ref.shape, 1)
        score = score - jnp.where(lane == expert, threshold_ref[...], 0.0)
        g = jax.nn.sigmoid(jnp.sum(score, axis=1, keepdims=True))
        pre_ref[:, :hidden_n] = gate
        pre_ref[:, hidden_n : 2 * hidden_n] = up
        pre_ref[:, 2 * hidden_n :] = jnp.broadcast_to(g, (rows, LANES))
        hidden = gate * jax.nn.sigmoid(gate) * up * scale_ref[...] * g
        hidden = jnp.where(first_part(rows, pack, slots), hidden, 0.0)
        for h, value in enumerate(spread(hidden, pack, slots)):
            hidden_ref[:, h * hidden_n : (h + 1) * hidden_n] = value.astype(BF16)
        for copy in downs:
            copy.wait()
        for j in range(STEPS):
            now = slice(j * width, (j + 1) * width)
            send_blocks(mm(hidden_ref[...], stack[:, now]).astype(BF16), out_refs, seq_n, now)

    padded = jnp.zeros((1, LANES), F32).at[:, :experts].set(threshold[None, :])
    return pl.pallas_call(
        body,
        in_specs=[ANYWHERE] * n_blocks + [IN_HBM] * 4 + [IN_VMEM] * 2,
        out_specs=[IN_VMEM] * (3 + n_sends),
        out_shape=[
            shape((rows, part)),
            shape((rows, 2 * hidden_n + LANES), F32),
            shape((rows, pack * hidden_n)),
        ]
        + [shape((block_rows, part))] * n_sends,
        scratch_shapes=[
            pltpu.VMEM((part, total), BF16),
            pltpu.VMEM((pack * hidden_n, part), BF16),
            pltpu.SemaphoreType.DMA((seq_n,)),
            pltpu.SemaphoreType.DMA((STEPS, 2 * pack + 1)),
            pltpu.SemaphoreType.DMA((pack,)),
        ],
        compiler_params=limit(28),
        cost_estimate=cost(6 * rows * part * pack * hidden_n, 6 * part * pack * hidden_n),
    )(*arrivals.blocks, router_side, w_gate, w_up, w_down, padded, hid_scale)


def split3(v):
    hi = v.astype(BF16)
    rest = v - hi.astype(F32)
    mid = rest.astype(BF16)
    return hi, mid, (rest - mid.astype(F32)).astype(BF16)


def expert_backward(arrivals, seq_n, slots, experts, pack, x, pre, router_side, w_gate, w_up, w_down, hid_scale):
    block_rows, part = arrivals.blocks[0].shape
    rows = block_rows * seq_n
    hidden_n = w_gate.shape[2]
    width = part // STEPS
    total = 2 * pack * hidden_n + LANES
    n_blocks = len(arrivals.blocks)
    n_sends = sends(seq_n)

    def body(*refs):
        blocks = refs[:n_blocks]
        router_ref, gate_ref, up_ref, down_ref, scale_ref, x_ref, pre_ref = refs[n_blocks : n_blocks + 7]
        c_ref, delta_ref, router_out, total_ref = refs[n_blocks + 7 : n_blocks + 11]
        out_refs = refs[n_blocks + 11 : n_blocks + 11 + n_sends]
        side, stack, columns, x_sems, side_sems, stack_sems = refs[n_blocks + 11 + n_sends :]
        arrivals.start(blocks, c_ref, x_sems)
        chunks = [side_copies(gate_ref, up_ref, router_ref, side, side_sems, pack, j, width) for j in range(STEPS)]
        downs = down_copies(down_ref, stack, stack_sems, pack)
        for copy in downs:
            copy.start()
        for chunk in chunks:
            for copy in chunk:
                copy.start()
        arrivals.wait(blocks, c_ref, x_sems)
        parts = []
        for h, copy in enumerate(downs):
            copy.wait()
            parts.append(mm(c_ref[...], stack[h * hidden_n : (h + 1) * hidden_n, :], LAST))
        raw = jnp.where(first_part(rows, pack, slots), fold(parts, slots) * scale_ref[...], 0.0)
        gate = pre_ref[:, :hidden_n]
        up = pre_ref[:, hidden_n : 2 * hidden_n]
        g = pre_ref[:, 2 * hidden_n : 2 * hidden_n + 1]
        sig = jax.nn.sigmoid(gate)
        act = gate * sig
        score = jnp.sum(act * up * raw, axis=1, keepdims=True) * g * (1.0 - g)
        grad = raw * g
        to_gate = spread(grad * up * sig * (1.0 + gate * (1.0 - sig)), pack, slots)
        to_up = spread(grad * act, pack, slots)
        expert = lax.axis_index("exp")
        lane = lax.broadcasted_iota(jnp.int32, (rows, LANES), 1)
        by_expert = jnp.zeros((rows, LANES), F32)
        by_split = jnp.zeros((rows, LANES), F32)
        for h, value in enumerate(spread(jnp.broadcast_to(score, (rows, LANES)), pack, slots)):
            delta_ref[:, 2 * h * hidden_n : (2 * h + 1) * hidden_n] = to_gate[h].astype(BF16)
            delta_ref[:, (2 * h + 1) * hidden_n : (2 * h + 2) * hidden_n] = to_up[h].astype(BF16)
            for n, piece in enumerate(split3(value)):
                piece = piece.astype(F32)
                by_split = jnp.where(lane == 3 * h + n, piece, by_split)
                if n < 2:
                    by_expert = jnp.where(lane == (n * pack + h) * experts + expert, piece, by_expert)
        columns[...] = by_split.astype(BF16)
        delta_ref[:, 2 * pack * hidden_n :] = by_expert.astype(BF16)
        total_ref[...] = jnp.broadcast_to(-jnp.sum(score, axis=0, keepdims=True), total_ref.shape)
        for j, chunk in enumerate(chunks):
            now = slice(j * width, (j + 1) * width)
            for copy in chunk:
                copy.wait()
            send_blocks(mm(delta_ref[...], side[now, :], LAST).astype(BF16), out_refs, seq_n, now)
        for j in range(STEPS):
            now = slice(j * width, (j + 1) * width)
            told = mm(columns[...], x_ref[:, now], ROWS)
            for h in range(pack):
                router_out[h : h + 1, now] = jnp.sum(told[3 * h : 3 * h + 3], axis=0, keepdims=True)

    return pl.pallas_call(
        body,
        in_specs=[ANYWHERE] * n_blocks + [IN_HBM] * 4 + [IN_VMEM] * 3,
        out_specs=[IN_VMEM] * (4 + n_sends),
        out_shape=[
            shape((rows, part)),
            shape((rows, total)),
            shape((pack, part), F32),
            shape((1, LANES), F32),
        ]
        + [shape((block_rows, part))] * n_sends,
        scratch_shapes=[
            pltpu.VMEM((part, total), BF16),
            pltpu.VMEM((pack * hidden_n, part), BF16),
            pltpu.VMEM((rows, LANES), BF16),
            pltpu.SemaphoreType.DMA((seq_n,)),
            pltpu.SemaphoreType.DMA((STEPS, 2 * pack + 1)),
            pltpu.SemaphoreType.DMA((pack,)),
        ],
        compiler_params=limit(28),
        cost_estimate=cost(6 * rows * part * pack * hidden_n, 6 * part * pack * hidden_n),
    )(*arrivals.blocks, router_side, w_gate, w_up, w_down, hid_scale, x, pre)


def side_grads(x, delta, pack, hidden_n):
    rows, part = x.shape
    width = part // STEPS

    def body(x_ref, delta_ref, gate_out, up_out):
        both = mm(x_ref[...], delta_ref[...], ROWS)
        gate_out[...] = both[:, :hidden_n]
        up_out[...] = both[:, hidden_n:]

    tall = pl.BlockSpec((None, width, hidden_n), lambda h, i: (0, h * STEPS + i, 0))
    return pl.pallas_call(
        body,
        grid=(pack, STEPS),
        in_specs=[
            pl.BlockSpec((rows, width), lambda h, i: (0, i)),
            pl.BlockSpec((rows, 2 * hidden_n), lambda h, i: (0, h)),
        ],
        out_specs=[tall, tall],
        out_shape=[shape((1, part * pack, hidden_n), F32)] * 2,
        compiler_params=limit(16),
        cost_estimate=cost(4 * rows * part * pack * hidden_n, 8 * part * pack * hidden_n),
    )(x, delta)


def down_grads(c, hidden, pack, hidden_n):
    rows, part = c.shape
    width = part // 2

    def body(c_ref, hidden_ref, out):
        out[...] = mm(hidden_ref[...], c_ref[...], ROWS)

    return pl.pallas_call(
        body,
        grid=(pack, 2),
        in_specs=[
            pl.BlockSpec((rows, width), lambda h, i: (0, i)),
            pl.BlockSpec((rows, hidden_n), lambda h, i: (0, h)),
        ],
        out_specs=pl.BlockSpec((None, hidden_n, width), lambda h, i: (0, 0, h * 2 + i)),
        out_shape=shape((1, hidden_n, part * pack), F32),
        compiler_params=limit(16),
        cost_estimate=cost(2 * rows * part * pack * hidden_n, 4 * part * pack * hidden_n),
    )(c, hidden)


def up_line(block, n, first=0, last=None):
    last = n - 1 if last is None else last
    return lax.ppermute(block, "seq", [(s, s + 1) for s in range(first, last)])


def down_line(block, n, first=1, last=None):
    last = n if last is None else last
    return lax.ppermute(block, "seq", [(s, s - 1) for s in range(first, last)])


def line_gather(block, n):
    if n == 4:
        far = lax.ppermute(block, "seq", [(s, (s + 2) % 4) for s in range(4)])
        below = up_line(block, n)
        above = down_line(block, n)
        ends = lax.ppermute(far, "seq", [(2, 3), (1, 0)])
        return Arrivals([block, below, above, far, ends], [(0, 0, 0), (1, 4, 1), (3, 3, 0), (4, 2, 3)])
    ups, downs = [], []
    up = down = block
    for j in range(1, n):
        up = up_line(up, n, j - 1)
        down = down_line(down, n, 1, n - j + 1)
        ups.append(up)
        downs.append(down)
    plan = [(0, 0, 0)] + [(k, 2 * n - 1 - k, k) for k in range(1, n)]
    return Arrivals([block] + ups + downs, plan)


def add(*parts):
    return sum(part.astype(F32) for part in parts).astype(BF16)


def line_sum(parts, n):
    if n == 4:
        ends = lax.ppermute(parts[4], "seq", [(3, 2), (0, 1)])
        below = up_line(parts[3], n)
        above = down_line(parts[1], n)
        far = lax.ppermute(add(parts[2], ends), "seq", [(s, (s + 2) % 4) for s in range(4)])
        return add(parts[0], below, above, far), ends
    up, down = parts[1], parts[n - 1]
    first = None
    for j in range(1, n):
        if j > 1:
            up, down = add(parts[j], up), add(parts[n - j], down)
        up = up_line(up, n, 0, j)
        down = down_line(down, n, n - j)
        first = up if first is None else first
    return add(parts[0], up, down), first


def on_device(tokens, cotangent, router, threshold, w_gate, w_up, w_down, hid_scale, picks, counts):
    experts, slots = picks.shape[1:]
    features = tokens.shape[1]
    true_hidden = w_gate.shape[2]
    extra = -true_hidden % LANES
    if extra:
        w_gate, w_up = (jnp.pad(w, ((0, 0), (0, 0), (0, extra))) for w in (w_gate, w_up))
        w_down = jnp.pad(w_down, ((0, 0), (0, extra), (0, 0)))
        hid_scale = jnp.pad(hid_scale, ((0, 0), (0, extra)))
    hidden_n = true_hidden + extra
    seq_n = lax.axis_size("seq")
    everyone = seq_n * lax.axis_size("exp")
    pack = max(1, 8 // slots)
    chosen = picks[0].T

    def to_experts(block):
        block = block.reshape(experts, -1, block.shape[1])
        return lax.all_to_all(block, "exp", split_axis=0, concat_axis=0, tiled=True).reshape(-1, block.shape[2])

    x_rows, _ = choose_rows(tokens, chosen, counts, pack, False)
    c_rows, hot = choose_rows(cotangent, chosen, counts, pack, True)
    x_in = line_gather(to_experts(x_rows), seq_n)
    c_in = line_gather(to_experts(c_rows), seq_n)
    halves = list(router.reshape(pack, features // pack, experts))
    router_side = jnp.concatenate(halves + halves, axis=1)
    router_side = jnp.pad(router_side, ((0, 0), (0, LANES - router_side.shape[1])))

    x, pre, hidden, *out = expert_forward(
        x_in, seq_n, slots, experts, pack, router_side, threshold, w_gate, w_up, w_down, hid_scale
    )
    out, began = line_sum(out, seq_n)
    c_in.blocks[0], _ = lax.optimization_barrier((c_in.blocks[0], began))
    c, delta, router_part, total, *back = expert_backward(
        c_in, seq_n, slots, experts, pack, x, pre, router_side, w_gate, w_up, w_down, hid_scale
    )
    back, began = line_sum(back, seq_n)
    x, c, _ = lax.optimization_barrier((x, c, began))
    down_grad = down_grads(c, hidden, pack, hidden_n)
    gate_grad, up_grad = side_grads(x, delta, pack, hidden_n)
    if extra:
        gate_grad, up_grad = gate_grad[:, :, :true_hidden], up_grad[:, :, :true_hidden]
        down_grad = down_grad[:, :true_hidden]
    mixture = scatter_rows(to_experts(out), hot)
    token_grad = scatter_rows(to_experts(back), hot)

    message = jnp.concatenate(
        [router_part.reshape(everyone, -1), jnp.broadcast_to(total[:, :1], (everyone, 1))], axis=1
    )
    told = lax.all_to_all(message, BOTH, split_axis=0, concat_axis=0, tiled=True)
    told = jnp.sum(told.reshape(seq_n, experts, -1), axis=0)
    return mixture, token_grad, told[:, :-1].T, told[:, -1], gate_grad, up_grad, down_grad


def solution(mesh):
    by_owner = P(BOTH, None)
    columns = P("exp", None, "seq")
    down = P("exp", "seq", None)
    return jax.shard_map(
        on_device,
        mesh=mesh,
        in_specs=(
            by_owner,
            by_owner,
            P(),
            P(),
            columns,
            columns,
            down,
            P("exp", "seq"),
            P(BOTH, None, None),
            by_owner,
        ),
        out_specs=(by_owner, by_owner, by_owner, P(), columns, columns, down),
        check_vma=False,
    )
```

time: 165 us -> 168 us (1.018)
  matrix products: 44.9 us -> 0 us
  starting transfers between devices: 22 us -> 57.5 us
  Pallas kernels: 0 us -> 31.5 us
  waiting for transfers between devices: 66.5 us -> 43.9 us
  other arithmetic: 4.52 us -> 7.51 us
    all_to_all x4, waiting for transfers between devices: 61.5 us -> 8.14 us  [to_experts(): lax.all_to_all(block, 'exp', split_axis=0, concat_axis=0, tiled=True)]
    dot_general x15 -> x0, matrix products: 44.9 us -> none  [mm(): return lax.dot_general(a, b, (dims, ((), ())), preferred_element_type=F32)]
    ppermute x0 -> x16, starting transfers between devices: none -> 36.9 us  [the longest x4 15.7 us: up_line(): return lax.ppermute(block, 'seq', [(s, s + 1) for s in range(first, last)])]
    ppermute x0 -> x16, waiting for transfers between devices: none -> 34.6 us  [the longest x2 20.3 us: line_sum(): lax.ppermute(add(parts[2], ends), 'seq', [(s, (s + 2) % 4) for s in range...]
    pallas_call x0 -> x8, Pallas kernels: none -> 31.5 us  [the longest x1 6.87 us: side_grads(): pl.pallas_call(body, grid=(pack, STEPS), in_specs=[pl.BlockSpec((rows, wi...]
    unnamed x17 -> x60, local copies, waits for them, and re-layouts: 0.81 us -> 19.5 us
    reshape x7 -> x1, local copies, waits for them, and re-layouts: 15.4 us -> 0.02 us  [on_device(): router_part.reshape(everyone, -1)]
    convert_element_type x2 -> x0, local copies, waits for them, and re-layouts: 4.56 us -> none  [the longest x1 2.43 us: on_device(): cots_wide = cots.astype(F32)]
  transfers between devices with their start and end apart: 5 -> 21, of which waited for: 5 -> 8; matrix products, arithmetic and copies ran while one was open for 28% -> 8% of each run, Pallas kernels for 0% -> 16%
where the time goes in v3:
time: 168 us; the launch traced here: 167 us
  starting transfers between devices  57.5 us (34%)
  waiting for transfers between devices  43.9 us (26%)
  Pallas kernels  31.5 us (19%)
  local copies, waits for them, and re-layouts  25.2 us (15%)
  other arithmetic  7.51 us (4%)
    ppermute x2, waiting for transfers between devices, line_sum(): lax.ppermute(add(parts[2], ends), 'seq', [(s, (s + 2) % 4) for s in range...  20.3 us
    unnamed x60, local copies, waits for them, and re-layouts  19.5 us
    ppermute x4, starting transfers between devices, up_line(): return lax.ppermute(block, 'seq', [(s, s + 1) for s in range(first, last)])  15.7 us
    all_to_all x4, starting transfers between devices, to_experts(): lax.all_to_all(block, 'exp', split_axis=0, concat_axis=0, tiled=True)  15.7 us
    all_to_all x4, waiting for transfers between devices, to_experts(): lax.all_to_all(block, 'exp', split_axis=0, concat_axis=0, tiled=True)  8.14 us
    ppermute x2, starting transfers between devices, line_gather(): far = lax.ppermute(block, 'seq', [(s, (s + 2) % 4) for s in range(4)])  7.52 us
    ppermute x2, waiting for transfers between devices, line_gather(): far = lax.ppermute(block, 'seq', [(s, (s + 2) % 4) for s in range(4)])  7.18 us
    pallas_call x1, Pallas kernels, side_grads(): pl.pallas_call(body, grid=(pack, STEPS), in_specs=[pl.BlockSpec((rows, wi...  6.87 us
  transfers between devices with their start and end apart: 21, of which 8 were waited for; matrix products, arithmetic and copies ran while one was open for 8% of the time, Pallas kernels for 16%

profile of v3, /device:TPU:0, one launch (start us, length us, event | category | flops | bytes accessed | tf_op | source)
XLA Modules:
  0.0 166.6 jit_solution(3330078554368034510)
XLA Ops:
  0.7 1.6 copy-done.3
  3.6 1.4 shard_map.154
  5.7 5.2 %all-to-all-start = ((bf16[8,8,2048]{2,1,0:T(8,128)(2,1)}), bf16[8,8,2048]{2,1,0:T(8,128)(2,1)S(1)}, u32[]{:S(2)}, u32[]{:S(2)}) async-start(bf16[8,8,2048]{2,1,0:T(8,128)(2,1)} %bitcast.32), calls=%async_computation | async-start | bytes 524288 | tf_op jit(solution)/shard_map/all_to_all | solution.py:491
  10.8 1.6 copy-done.4
  13.8 1.2 shard_map.153
  15.7 2.1 %all-to-all-done = bf16[8,8,2048]{2,1,0:T(8,128)(2,1)S(1)} async-done(((bf16[8,8,2048]{2,1,0:T(8,128)(2,1)}), bf16[8,8,2048]{2,1,0:T(8,128)(2,1)S(1)}, u32[]{:S(2)}, u32[]{:S(2)}) %all-to-all-start) | async-done | bytes 262176 | tf_op jit(solution)/shard_map/all_to_all | solution.py:491
  18.5 3.4 %all-to-all-start.2 = ((bf16[8,8,2048]{2,1,0:T(8,128)(2,1)}), bf16[8,8,2048]{2,1,0:T(8,128)(2,1)S(1)}, u32[]{:S(2)}, u32[]{:S(2)}) async-start(bf16[8,8,2048]{2,1,0:T(8,128)(2,1)} %bitcast.31), calls=%async_computation.2 | async-start | bytes 524288 | tf_op jit(solution)/shard_map/all_to_all | solution.py:491
  21.9 2.7 %collective-permute-start.2 = (bf16[64,2048]{1,0:T(8,128)(2,1)}, bf16[64,2048]{1,0:T(8,128)(2,1)}, u32[]{:S(2)}, u32[]{:S(2)}) collective-permute-start(bf16[64,2048]{1,0:T(8,128)(2,1)} %bitcast.25), channel_id=1, source_target_pairs={{0,16},{8,24},{16,0},{24,8},{1,17},{9,25},{17,1},{25,9},{2,18},{10... | collective-permute-start | bytes 786440 | tf_op jit(solution)/shard_map/ppermute | solution.py:436
  25.3 4.2 %collective-permute-start = (bf16[64,2048]{1,0:T(8,128)(2,1)}, bf16[64,2048]{1,0:T(8,128)(2,1)}, u32[]{:S(2)}, u32[]{:S(2)}) collective-permute-start(bf16[64,2048]{1,0:T(8,128)(2,1)} %bitcast.26), channel_id=1, source_target_pairs={{0,8},{8,16},{16,24},{1,9},{9,17},{17,25},{2,10},{10,18},{18,26},{... | collective-permute-start | bytes 786440 | tf_op jit(solution)/shard_map/ppermute | solution.py:426
  29.5 1.3 collective-permute-start.1
  30.8 7.2 %collective-permute-done.2.refs_3_ = bf16[64,2048]{1,0:T(8,128)(2,1)} collective-permute-done((bf16[64,2048]{1,0:T(8,128)(2,1)}, bf16[64,2048]{1,0:T(8,128)(2,1)}, u32[]{:S(2)}, u32[]{:S(2)}) %collective-permute-start.2) | collective-permute-done | bytes 262176 | tf_op jit(solution)/shard_map/ppermute | solution.py:436
  38.0 1.3 collective-permute-start.3
  40.6 4.9 %collective-permute-start.10 = (bf16[64,2048]{1,0:T(8,128)(2,1)S(1)}, bf16[64,2048]{1,0:T(8,128)(2,1)}, u32[]{:S(2)}, u32[]{:S(2)}) collective-permute-start(bf16[64,2048]{1,0:T(8,128)(2,1)S(1)} %bitcast.21), channel_id=1, source_target_pairs={{0,16},{8,24},{16,0},{24,8},{1,17},{9,25},{17,1},{25,9},{2,18},{10... | collective-permute-start | bytes 786440 | tf_op jit(solution)/shard_map/ppermute | solution.py:436
  45.4 1.3 fusion.2
  46.7 1.9 %copy.25 = bf16[2048,32]{1,0:T(8,128)(2,1)} copy(bf16[2048,32]{0,1:T(8,128)(2,1)} %pad_maximum_fusion) | data formatting | bytes 262144 | tf_op jit(solution)/shard_map/concatenate | solution.py:498
  48.6 1.1 pad.8.refs_5_
  49.9 1.9 %copy-done.1 = bf16[1,4096,384]{2,1,0:T(8,128)(2,1)S(1)} copy-done((bf16[1,4096,384]{2,1,0:T(8,128)(2,1)S(1)}, bf16[1,4096,384]{2,1,0:T(8,128)(2,1)}, u32[]{:S(2)}) %copy-start.1) | copy-done | bytes 3145752
  51.7 1.9 %copy-done.2 = bf16[1,384,4096]{2,1,0:T(8,128)(2,1)S(1)} copy-done((bf16[1,384,4096]{2,1,0:T(8,128)(2,1)S(1)}, bf16[1,384,4096]{2,1,0:T(8,128)(2,1)}, u32[]{:S(2)}) %copy-start.2) | copy-done | bytes 3145752
  53.6 0.9 copy-done.6
  54.6 6.3 %shard_map.155 = (bf16[256,2048]{1,0:T(8,128)(2,1)S(1)}, f32[256,896]{1,0:T(8,128)S(1)}, bf16[256,768]{1,0:T(8,128)(2,1)S(1)}, bf16[64,2048]{1,0:T(8,128)(2,1)S(...) custom-call(bf16[64,2048]{1,0:T(8,128)(2,1)S(1)} %bitcast.28, ...), custom_call_target="tpu_custom_call" | custom-call | flops 2415919104 | bytes 9437184 | tf_op jit(solution)/shard_map/pallas_call | solution.py:262
  63.1 1.3 collective-permute-start.6
  64.4 1.3 collective-permute-start.8
  65.7 1.3 collective-permute-start.9
  67.0 1.3 collective-permute-start.11
  68.3 6.6 %collective-permute-start.4 = (bf16[64,2048]{1,0:T(8,128)(2,1)}, bf16[64,2048]{1,0:T(8,128)(2,1)}, u32[]{:S(2)}, u32[]{:S(2)}) collective-permute-start(bf16[64,2048]{1,0:T(8,128)(2,1)} %get-tuple-element.47), channel_id=1, source_target_pairs={{0,8},{8,16},{16,24},{1,9},{9,17},{17,25},{2,10},{10,18},{18,26},{... | collective-permute-start | bytes 786440 | tf_op jit(solution)/shard_map/ppermute | solution.py:426
  74.9 1.3 collective-permute-start.5
  76.7 1.4 collective-permute-done.9.refs_2_
  78.1 5.2 %collective-permute-done.11.refs_4_ = bf16[64,2048]{1,0:T(8,128)(2,1)S(1)} collective-permute-done((bf16[64,2048]{1,0:T(8,128)(2,1)}, bf16[64,2048]{1,0:T(8,128)(2,1)S(1)}, u32[]{:S(2)}, u32[]{:S(2)}) %collective-permute-start.11) | collective-permute-done | bytes 262176 | tf_op jit(solution)/shard_map/ppermute | solution.py:439
  83.3 6.7 %shard_map.157 = (bf16[256,2048]{1,0:T(8,128)(2,1)S(1)}, bf16[256,1664]{1,0:T(8,128)(2,1)S(1)}, f32[2,2048]{1,0:T(2,128)S(1)}, f32[1,128]{1,0:T(1,128)S(1)}, bf1...) custom-call(bf16[64,2048]{1,0:T(8,128)(2,1)S(1)} %bitcast.24, ...), custom_call_target="tpu_custom_call" | custom-call | flops 2415919104 | bytes 9437184 | tf_op jit(solution)/shard_map/pallas_call | solution.py:355
  90.0 1.0 copy-done.9
  92.4 0.9 copy-done.25
  94.7 1.7 %collective-permute-start.14 = (bf16[64,2048]{1,0:T(8,128)(2,1)}, bf16[64,2048]{1,0:T(8,128)(2,1)S(1)}, u32[]{:S(2)}, u32[]{:S(2)}) collective-permute-start(bf16[64,2048]{1,0:T(8,128)(2,1)} %get-tuple-element.59), channel_id=1, source_target_pairs={{24,16},{0,8},{25,17},{1,9},{26,18},{2,10},{27,19},{3,11},{28,20},... | collective-permute-start | bytes 786440 | tf_op jit(solution)/shard_map/ppermute | solution.py:458
  97.1 4.9 %all-to-all-start.4 = ((f32[32,1,129]{2,1,0:T(1,128)}), f32[32,1,129]{2,1,0:T(1,128)S(1)}, u32[]{:S(2)}, u32[]{:S(2)}) async-start(f32[32,1,129]{2,1,0:T(1,128)} %all_to_all.22), calls=%async_computation.4 | async-start | bytes 65536 | tf_op jit(solution)/shard_map/all_to_all | solution.py:522
  102.0 3.7 %collective-permute-start.12 = (bf16[64,2048]{1,0:T(8,128)(2,1)}, bf16[64,2048]{1,0:T(8,128)(2,1)S(1)}, u32[]{:S(2)}, u32[]{:S(2)}) collective-permute-start(bf16[64,2048]{1,0:T(8,128)(2,1)} %copy-done.28), channel_id=1, source_target_pairs={{0,8},{8,16},{16,24},{1,9},{9,17},{17,25},{2,10},{10,18},{18,26},{... | collective-permute-start | bytes 786440 | tf_op jit(solution)/shard_map/ppermute | solution.py:426
  105.7 1.3 collective-permute-start.13
  107.0 1.1 add_convert_fusion.3
  108.1 1.1 all-to-all-done.4
  110.4 2.4 %collective-permute-start.7 = (bf16[64,2048]{1,0:T(8,128)(2,1)S(1)}, bf16[64,2048]{1,0:T(8,128)(2,1)S(1)}, u32[]{:S(2)}, u32[]{:S(2)}) collective-permute-start(bf16[64,2048]{1,0:T(8,128)(2,1)S(1)} %add_convert_fusion.3), channel_id=1, source_target_pairs={{0,16},{8,24},{16,0},{24,8},{1,17},{9,25},{17,1},{25,9},{2,18},{10... | collective-permute-start | bytes 786440 | tf_op jit(solution)/shard_map/ppermute | solution.py:461
  112.9 1.0 add_convert_fusion.1
  114.5 20.3 %collective-permute-done.7 = bf16[64,2048]{1,0:T(8,128)(2,1)S(1)} collective-permute-done((bf16[64,2048]{1,0:T(8,128)(2,1)S(1)}, bf16[64,2048]{1,0:T(8,128)(2,1)S(1)}, u32[]{:S(2)}, u32[]{:S(2)}) %collective-permute-start.7) | collective-permute-done | bytes 262176 | tf_op jit(solution)/shard_map/ppermute | solution.py:461
  134.7 1.9 %fusion = bf16[8,8,2048]{2,1,0:T(8,128)(2,1)} fusion(bf16[64,2048]{1,0:T(8,128)(2,1)S(1)} %collective-permute-done.7, bf16[64,2048]{1,0:T(8,128)(2,1)} %collective-permute-done.5, bf16[64,2048]{1,0:T(8,128)(2,1)} %collective-permute-done.4, bf16[64,2048]{1,0:T(8,128)(2,1)} %copy-done.13), kind=kLoop, calls=%fused_computation.4 | loop fusion | flops 1048576 | bytes 1310720 | tf_op jit(solution)/shard_map/reshape | solution.py:490
  136.7 3.7 %all-to-all-start.1 = ((bf16[8,8,2048]{2,1,0:T(8,128)(2,1)}), bf16[8,8,2048]{2,1,0:T(8,128)(2,1)S(1)}, u32[]{:S(2)}, u32[]{:S(2)}) async-start(bf16[8,8,2048]{2,1,0:T(8,128)(2,1)} %fusion), calls=%async_computation.1 | async-start | bytes 524288 | tf_op jit(solution)/shard_map/all_to_all | solution.py:491
  141.2 6.1 %all-to-all-done.1 = bf16[8,8,2048]{2,1,0:T(8,128)(2,1)S(1)} async-done(((bf16[8,8,2048]{2,1,0:T(8,128)(2,1)}), bf16[8,8,2048]{2,1,0:T(8,128)(2,1)S(1)}, u32[]{:S(2)}, u32[]{:S(2)}) %all-to-all-start.1) | async-done | bytes 262176 | tf_op jit(solution)/shard_map/all_to_all | solution.py:491
  147.3 3.4 %all-to-all-start.3 = ((bf16[8,8,2048]{2,1,0:T(8,128)(2,1)}), bf16[8,8,2048]{2,1,0:T(8,128)(2,1)S(1)}, u32[]{:S(2)}, u32[]{:S(2)}) async-start(bf16[8,8,2048]{2,1,0:T(8,128)(2,1)} %fusion.1), calls=%async_computation.3 | async-start | bytes 524288 | tf_op jit(solution)/shard_map/all_to_all | solution.py:491
  150.7 3.8 %shard_map.160 = f32[1,384,4096]{2,1,0:T(8,128)} custom-call(bf16[256,2048]{1,0:T(8,128)(2,1)S(1)} %copy-done.10, bf16[256,768]{1,0:T(8,128)(2,1)S(1)} %copy-done.12), custom_call_target="tpu_custom_call" | custom-call | flops 805306368 | bytes 6291456 | tf_op jit(solution)/shard_map/pallas_call | solution.py:410
  154.5 6.9 %shard_map.159 = (f32[1,4096,384]{2,1,0:T(8,128)}, f32[1,4096,384]{2,1,0:T(8,128)}) custom-call(bf16[256,2048]{1,0:T(8,128)(2,1)S(1)} %copy-done.8, bf16[256,1664]{1,0:T(8,128)(2,1)S(1)} %copy-done.26), custom_call_target="tpu_custom_call" | custom-call | flops 1610612736 | bytes 12582912 | tf_op jit(solution)/shard_map/pallas_call | solution.py:389
  161.4 2.6 %shard_map.156 = bf16[256,4096]{1,0:T(8,128)(2,1)} custom-call(bf16[2,64,256]{2,1,0:T(8,128)(2,1)S(1)} %get-tuple-element.44.hot_ref, bf16[64,2048]{1,0:T(8,128)(2,1)S(1)} %bitcast.29), custom_call_target="tpu_custom_call" | custom-call | flops 134217728 | bytes 2097152 | tf_op jit(solution)/shard_map/pallas_call | solution.py:104
  164.0 2.6 %shard_map.158 = bf16[256,4096]{1,0:T(8,128)(2,1)} custom-call(bf16[2,64,256]{2,1,0:T(8,128)(2,1)S(1)} %get-tuple-element.44.hot_ref, bf16[64,2048]{1,0:T(8,128)(2,1)S(1)} %bitcast.30), custom_call_target="tpu_custom_call" | custom-call | flops 134217728 | bytes 2097152 | tf_op jit(solution)/shard_map/pallas_call | solution.py:104
  (79 shorter events, 15.7 us)
Async XLA Ops:
  0.6 49.2 %copy-start.22 = (f32[1,384]{1,0:T(1,128)S(1)}, f32[1,384]{1,0:T(1,128)}, u32[]{:S(2)}) copy-start(f32[1,384]{1,0:T(1,128)} %refs_9_.1) | copy-start | bytes 4612
  0.6 1.6 copy-start.3
  2.2 0.7 copy-start.20
  3.6 46.3 %copy-start = (bf16[1,4096,384]{2,1,0:T(8,128)(2,1)S(1)}, bf16[1,4096,384]{2,1,0:T(8,128)(2,1)}, u32[]{:S(2)}) copy-start(bf16[1,4096,384]{2,1,0:T(8,128)(2,1)} %refs_6_.3) | copy-start | bytes 9437188
  5.0 0.7 copy-start.19
  5.7 12.1 %all-to-all-start = ((bf16[8,8,2048]{2,1,0:T(8,128)(2,1)}), bf16[8,8,2048]{2,1,0:T(8,128)(2,1)S(1)}, u32[]{:S(2)}, u32[]{:S(2)}) async-start(bf16[8,8,2048]{2,1,0:T(8,128)(2,1)} %bitcast.32), calls=%async_computation | async-start | bytes 524288 | tf_op jit(solution)/shard_map/all_to_all | solution.py:491
  10.8 1.6 copy-start.4
  15.0 0.7 copy-start.18
  17.8 0.7 copy-start.5
  18.5 22.1 %all-to-all-start.2 = ((bf16[8,8,2048]{2,1,0:T(8,128)(2,1)}), bf16[8,8,2048]{2,1,0:T(8,128)(2,1)S(1)}, u32[]{:S(2)}, u32[]{:S(2)}) async-start(bf16[8,8,2048]{2,1,0:T(8,128)(2,1)} %bitcast.31), calls=%async_computation.2 | async-start | bytes 524288 | tf_op jit(solution)/shard_map/all_to_all | solution.py:491
  21.9 16.1 %collective-permute-start.2 = (bf16[64,2048]{1,0:T(8,128)(2,1)}, bf16[64,2048]{1,0:T(8,128)(2,1)}, u32[]{:S(2)}, u32[]{:S(2)}) collective-permute-start(bf16[64,2048]{1,0:T(8,128)(2,1)} %bitcast.25), channel_id=1, source_target_pairs={{0,16},{8,24},{16,0},{24,8},{1,17},{9,25},{17,1},{25,9},{2,18},{10... | collective-permute-start | bytes 786440 | tf_op jit(solution)/shard_map/ppermute | solution.py:436
  25.3 24.5 %collective-permute-start = (bf16[64,2048]{1,0:T(8,128)(2,1)}, bf16[64,2048]{1,0:T(8,128)(2,1)}, u32[]{:S(2)}, u32[]{:S(2)}) collective-permute-start(bf16[64,2048]{1,0:T(8,128)(2,1)} %bitcast.26), channel_id=1, source_target_pairs={{0,8},{8,16},{16,24},{1,9},{9,17},{17,25},{2,10},{10,18},{18,26},{... | collective-permute-start | bytes 786440 | tf_op jit(solution)/shard_map/ppermute | solution.py:426
  29.5 20.3 %collective-permute-start.1 = (bf16[64,2048]{1,0:T(8,128)(2,1)}, bf16[64,2048]{1,0:T(8,128)(2,1)}, u32[]{:S(2)}, u32[]{:S(2)}) collective-permute-start(bf16[64,2048]{1,0:T(8,128)(2,1)} %bitcast.27), channel_id=1, source_target_pairs={{8,0},{16,8},{24,16},{9,1},{17,9},{25,17},{10,2},{18,10},{26,18},{... | collective-permute-start | bytes 786440 | tf_op jit(solution)/shard_map/ppermute | solution.py:431
  38.0 11.9 %collective-permute-start.3 = (bf16[64,2048]{1,0:T(8,128)(2,1)}, bf16[64,2048]{1,0:T(8,128)(2,1)}, u32[]{:S(2)}, u32[]{:S(2)}) collective-permute-start(bf16[64,2048]{1,0:T(8,128)(2,1)} %collective-permute-done.2.refs_3_), channel_id=1, source_target_pairs={{16,24},{8,0},{17,25},{9,1},{18,26},{10,2},{19,27},{11,3},{20,28},... | collective-permute-start | bytes 786440 | tf_op jit(solution)/shard_map/ppermute | solution.py:439
  40.6 26.4 %collective-permute-start.10 = (bf16[64,2048]{1,0:T(8,128)(2,1)S(1)}, bf16[64,2048]{1,0:T(8,128)(2,1)}, u32[]{:S(2)}, u32[]{:S(2)}) collective-permute-start(bf16[64,2048]{1,0:T(8,128)(2,1)S(1)} %bitcast.21), channel_id=1, source_target_pairs={{0,16},{8,24},{16,0},{24,8},{1,17},{9,25},{17,1},{25,9},{2,18},{10... | collective-permute-start | bytes 786440 | tf_op jit(solution)/shard_map/ppermute | solution.py:436
  49.8 1.9 %copy-start.1 = (bf16[1,4096,384]{2,1,0:T(8,128)(2,1)S(1)}, bf16[1,4096,384]{2,1,0:T(8,128)(2,1)}, u32[]{:S(2)}) copy-start(bf16[1,4096,384]{2,1,0:T(8,128)(2,1)} %refs_7_.3) | copy-start | bytes 9437188
  51.7 1.9 %copy-start.2 = (bf16[1,384,4096]{2,1,0:T(8,128)(2,1)S(1)}, bf16[1,384,4096]{2,1,0:T(8,128)(2,1)}, u32[]{:S(2)}) copy-start(bf16[1,384,4096]{2,1,0:T(8,128)(2,1)} %refs_8_.3) | copy-start | bytes 9437188
  53.6 0.9 copy-start.6
  60.9 0.7 copy-start.11
  61.7 0.7 copy-start.13
  62.4 0.7 copy-start.16
  63.1 26.9 %copy-start.7 = (bf16[256,2048]{1,0:T(8,128)(2,1)}, bf16[256,2048]{1,0:T(8,128)(2,1)S(1)}, u32[]{:S(2)}) copy-start(bf16[256,2048]{1,0:T(8,128)(2,1)S(1)} %get-tuple-element.63.refs_10_.x_ref) | copy-start | bytes 3145732
  63.1 11.8 %collective-permute-start.6 = (bf16[64,2048]{1,0:T(8,128)(2,1)S(1)}, bf16[64,2048]{1,0:T(8,128)(2,1)S(1)}, u32[]{:S(2)}, u32[]{:S(2)}) collective-permute-start(bf16[64,2048]{1,0:T(8,128)(2,1)S(1)} %get-tuple-element.50), channel_id=1, source_target_pairs={{24,16},{0,8},{25,17},{1,9},{26,18},{2,10},{27,19},{3,11},{28,20},... | collective-permute-start | bytes 786440 | tf_op jit(solution)/shard_map/ppermute | solution.py:458
  64.4 12.3 %collective-permute-start.8 = (bf16[64,2048]{1,0:T(8,128)(2,1)S(1)}, bf16[64,2048]{1,0:T(8,128)(2,1)S(1)}, u32[]{:S(2)}, u32[]{:S(2)}) collective-permute-start(bf16[64,2048]{1,0:T(8,128)(2,1)S(1)} %bitcast.22), channel_id=1, source_target_pairs={{0,8},{8,16},{16,24},{1,9},{9,17},{17,25},{2,10},{10,18},{18,26},{... | collective-permute-start | bytes 786440 | tf_op jit(solution)/shard_map/ppermute | solution.py:426
  65.7 12.4 %collective-permute-start.9 = (bf16[64,2048]{1,0:T(8,128)(2,1)S(1)}, bf16[64,2048]{1,0:T(8,128)(2,1)S(1)}, u32[]{:S(2)}, u32[]{:S(2)}) collective-permute-start(bf16[64,2048]{1,0:T(8,128)(2,1)S(1)} %bitcast.23), channel_id=1, source_target_pairs={{8,0},{16,8},{24,16},{9,1},{17,9},{25,17},{10,2},{18,10},{26,18},{... | collective-permute-start | bytes 786440 | tf_op jit(solution)/shard_map/ppermute | solution.py:431
  67.0 16.3 %collective-permute-start.11 = (bf16[64,2048]{1,0:T(8,128)(2,1)}, bf16[64,2048]{1,0:T(8,128)(2,1)S(1)}, u32[]{:S(2)}, u32[]{:S(2)}) collective-permute-start(bf16[64,2048]{1,0:T(8,128)(2,1)} %collective-permute-done.10.refs_3_), channel_id=1, source_target_pairs={{16,24},{8,0},{17,25},{9,1},{18,26},{10,2},{19,27},{11,3},{20,28},... | collective-permute-start | bytes 786440 | tf_op jit(solution)/shard_map/ppermute | solution.py:439
  68.3 45.6 %collective-permute-start.4 = (bf16[64,2048]{1,0:T(8,128)(2,1)}, bf16[64,2048]{1,0:T(8,128)(2,1)}, u32[]{:S(2)}, u32[]{:S(2)}) collective-permute-start(bf16[64,2048]{1,0:T(8,128)(2,1)} %get-tuple-element.47), channel_id=1, source_target_pairs={{0,8},{8,16},{16,24},{1,9},{9,17},{17,25},{2,10},{10,18},{18,26},{... | collective-permute-start | bytes 786440 | tf_op jit(solution)/shard_map/ppermute | solution.py:426
  74.9 8.5 %copy-start.29 = (bf16[64,2048]{1,0:T(8,128)(2,1)}, bf16[64,2048]{1,0:T(8,128)(2,1)S(1)}, u32[]{:S(2)}) copy-start(bf16[64,2048]{1,0:T(8,128)(2,1)S(1)} %collective-permute-done.6) | copy-start | bytes 786436
  74.9 39.6 %collective-permute-start.5 = (bf16[64,2048]{1,0:T(8,128)(2,1)}, bf16[64,2048]{1,0:T(8,128)(2,1)}, u32[]{:S(2)}, u32[]{:S(2)}) collective-permute-start(bf16[64,2048]{1,0:T(8,128)(2,1)} %get-tuple-element.48), channel_id=1, source_target_pairs={{8,0},{16,8},{24,16},{9,1},{17,9},{25,17},{10,2},{18,10},{26,18},{... | collective-permute-start | bytes 786440 | tf_op jit(solution)/shard_map/ppermute | solution.py:431
  90.0 1.0 copy-start.9
  91.0 0.7 copy-start.14
  91.7 0.7 copy-start.17
  92.4 0.9 copy-start.25
  93.3 0.7 copy-start.27
  94.0 0.7 copy-start.28
  94.7 56.0 %copy-start.12 = (bf16[256,768]{1,0:T(8,128)(2,1)S(1)}, bf16[256,768]{1,0:T(8,128)(2,1)}, u32[]{:S(2)}) copy-start(bf16[256,768]{1,0:T(8,128)(2,1)} %copy-done.11) | copy-start | bytes 1179652
  94.7 45.7 %copy-start.15 = (bf16[64,2048]{1,0:T(8,128)(2,1)S(1)}, bf16[64,2048]{1,0:T(8,128)(2,1)}, u32[]{:S(2)}) copy-start(bf16[64,2048]{1,0:T(8,128)(2,1)} %copy-done.14) | copy-start | bytes 786436
  94.7 56.0 %copy-start.10 = (bf16[256,2048]{1,0:T(8,128)(2,1)S(1)}, bf16[256,2048]{1,0:T(8,128)(2,1)}, u32[]{:S(2)}) copy-start(bf16[256,2048]{1,0:T(8,128)(2,1)} %copy-done.9) | copy-start | bytes 3145732
  94.7 15.8 %collective-permute-start.14 = (bf16[64,2048]{1,0:T(8,128)(2,1)}, bf16[64,2048]{1,0:T(8,128)(2,1)S(1)}, u32[]{:S(2)}, u32[]{:S(2)}) collective-permute-start(bf16[64,2048]{1,0:T(8,128)(2,1)} %get-tuple-element.59), channel_id=1, source_target_pairs={{24,16},{0,8},{25,17},{1,9},{26,18},{2,10},{27,19},{3,11},{28,20},... | collective-permute-start | bytes 786440 | tf_op jit(solution)/shard_map/ppermute | solution.py:458
  97.1 12.1 %all-to-all-start.4 = ((f32[32,1,129]{2,1,0:T(1,128)}), f32[32,1,129]{2,1,0:T(1,128)S(1)}, u32[]{:S(2)}, u32[]{:S(2)}) async-start(f32[32,1,129]{2,1,0:T(1,128)} %all_to_all.22), calls=%async_computation.4 | async-start | bytes 65536 | tf_op jit(solution)/shard_map/all_to_all | solution.py:522
  102.0 38.4 %collective-permute-start.12 = (bf16[64,2048]{1,0:T(8,128)(2,1)}, bf16[64,2048]{1,0:T(8,128)(2,1)S(1)}, u32[]{:S(2)}, u32[]{:S(2)}) collective-permute-start(bf16[64,2048]{1,0:T(8,128)(2,1)} %copy-done.28), channel_id=1, source_target_pairs={{0,8},{8,16},{16,24},{1,9},{9,17},{17,25},{2,10},{10,18},{18,26},{... | collective-permute-start | bytes 786440 | tf_op jit(solution)/shard_map/ppermute | solution.py:426
  105.7 34.7 %collective-permute-start.13 = (bf16[64,2048]{1,0:T(8,128)(2,1)}, bf16[64,2048]{1,0:T(8,128)(2,1)S(1)}, u32[]{:S(2)}, u32[]{:S(2)}) collective-permute-start(bf16[64,2048]{1,0:T(8,128)(2,1)} %copy-done.27), channel_id=1, source_target_pairs={{8,0},{16,8},{24,16},{9,1},{17,9},{25,17},{10,2},{18,10},{26,18},{... | collective-permute-start | bytes 786440 | tf_op jit(solution)/shard_map/ppermute | solution.py:431
  110.4 24.3 %collective-permute-start.7 = (bf16[64,2048]{1,0:T(8,128)(2,1)S(1)}, bf16[64,2048]{1,0:T(8,128)(2,1)S(1)}, u32[]{:S(2)}, u32[]{:S(2)}) collective-permute-start(bf16[64,2048]{1,0:T(8,128)(2,1)S(1)} %add_convert_fusion.3), channel_id=1, source_target_pairs={{0,16},{8,24},{16,0},{24,8},{1,17},{9,25},{17,1},{25,9},{2,18},{10... | collective-permute-start | bytes 786440 | tf_op jit(solution)/shard_map/ppermute | solution.py:461
  113.9 26.5 %collective-permute-start.15 = (bf16[64,2048]{1,0:T(8,128)(2,1)S(1)}, bf16[64,2048]{1,0:T(8,128)(2,1)S(1)}, u32[]{:S(2)}, u32[]{:S(2)}) collective-permute-start(bf16[64,2048]{1,0:T(8,128)(2,1)S(1)} %add_convert_fusion.1), channel_id=1, source_target_pairs={{0,16},{8,24},{16,0},{24,8},{1,17},{9,25},{17,1},{25,9},{2,18},{10... | collective-permute-start | bytes 786440 | tf_op jit(solution)/shard_map/ppermute | solution.py:461
  136.7 10.6 %all-to-all-start.1 = ((bf16[8,8,2048]{2,1,0:T(8,128)(2,1)}), bf16[8,8,2048]{2,1,0:T(8,128)(2,1)S(1)}, u32[]{:S(2)}, u32[]{:S(2)}) async-start(bf16[8,8,2048]{2,1,0:T(8,128)(2,1)} %fusion), calls=%async_computation.1 | async-start | bytes 524288 | tf_op jit(solution)/shard_map/all_to_all | solution.py:491
  147.3 16.7 %all-to-all-start.3 = ((bf16[8,8,2048]{2,1,0:T(8,128)(2,1)}), bf16[8,8,2048]{2,1,0:T(8,128)(2,1)S(1)}, u32[]{:S(2)}, u32[]{:S(2)}) async-start(bf16[8,8,2048]{2,1,0:T(8,128)(2,1)} %fusion.1), calls=%async_computation.3 | async-start | bytes 524288 | tf_op jit(solution)/shard_map/all_to_all | solution.py:491
  150.7 3.8 %copy-start.8 = (bf16[256,2048]{1,0:T(8,128)(2,1)S(1)}, bf16[256,2048]{1,0:T(8,128)(2,1)}, u32[]{:S(2)}) copy-start(bf16[256,2048]{1,0:T(8,128)(2,1)} %copy-done.7) | copy-start | bytes 3145732
  150.7 3.8 %copy-start.26 = (bf16[256,1664]{1,0:T(8,128)(2,1)S(1)}, bf16[256,1664]{1,0:T(8,128)(2,1)}, u32[]{:S(2)}) copy-start(bf16[256,1664]{1,0:T(8,128)(2,1)} %copy-done.25) | copy-start | bytes 2555908
  (3 other events, 2.0 us)

commit v4 on v3

v4 whole, which is shorter than its diff:
```python
import jax
import jax.numpy as jnp
from jax import lax
from jax.experimental import pallas as pl
from jax.experimental.pallas import tpu as pltpu
from jax.sharding import PartitionSpec as P

BOTH = ("seq", "exp")
F32 = jnp.float32
BF16 = jnp.bfloat16
ROWS = ((0,), (0,))
LAST = ((1,), (1,))
STEPS = 4
LANES = 128


def mm(a, b, dims=((1,), (0,))):
    return lax.dot_general(a, b, (dims, ((), ())), preferred_element_type=F32)


PARAMS = pltpu.CompilerParams(vmem_limit_bytes=56 * 2**20)


def cost(flops, moved):
    return pl.CostEstimate(flops=flops, bytes_accessed=moved, transcendentals=0)


def shape(dims, dtype=BF16):
    return jax.ShapeDtypeStruct(dims, dtype)


ANYWHERE = pl.BlockSpec(memory_space=pl.ANY)
IN_VMEM = pl.BlockSpec(memory_space=pltpu.VMEM)


def choose_rows(tokens, cotangent, picks, counts, pack):
    own, features = tokens.shape
    slots, experts = picks.shape
    count = experts * pack * slots
    part = features // pack
    width = part // STEPS

    def body(picks_ref, counts_ref, c_ref, x_ref, c_out, x_out, hot_ref, picks_s, counts_s, c_v, x_v, hot, sems):
        small = [
            pltpu.make_async_copy(picks_ref, picks_s, sems.at[2 * STEPS]),
            pltpu.make_async_copy(counts_ref, counts_s, sems.at[2 * STEPS + 1]),
        ]
        for copy in small:
            copy.start()
        large = []
        for n, (ref, held) in enumerate(((c_ref, c_v), (x_ref, x_v))):
            for j in range(STEPS):
                now = pl.ds(j * pack * width, pack * width)
                large.append(pltpu.make_async_copy(ref.at[:, now], held.at[:, now], sems.at[n * STEPS + j]))
                large[-1].start()
        for copy in small:
            copy.wait()
        dims = (count, own)
        row = lax.broadcasted_iota(jnp.int32, dims, 0)
        token = lax.broadcasted_iota(jnp.int32, dims, 1)
        place = row // (pack * slots) * slots + row % slots
        part_of = (row // slots) % pack
        want = jnp.full(dims, -1, jnp.int32)
        want_live = want
        for e in range(experts):
            for k in range(slots):
                here = place == e * slots + k
                want = jnp.where(here, picks_s[k, e], want)
                want_live = jnp.where(here, jnp.where(k < counts_s[0, e], picks_s[k, e], -1), want_live)
        for h in range(pack):
            hot[h] = jnp.where((want == token) & (part_of == h), 1.0, 0.0).astype(BF16)
            hot_ref[h] = jnp.where((want_live == token) & (part_of == h), 1.0, 0.0).astype(BF16)
        for n, (chooser, held, out_ref) in enumerate(((hot_ref, c_v, c_out), (hot, x_v, x_out))):
            for copy in large[n * STEPS : (n + 1) * STEPS]:
                copy.wait()
            for j in range(STEPS):
                out_ref[:, j * width : (j + 1) * width] = sum(
                    mm(chooser[h], held[:, h * part + j * width : h * part + (j + 1) * width]) for h in range(pack)
                ).astype(BF16)

    return pl.pallas_call(
        body,
        in_specs=[ANYWHERE] * 4,
        out_specs=[IN_VMEM] * 3,
        out_shape=[shape((count, part))] * 2 + [shape((pack, count, own))],
        scratch_shapes=[
            pltpu.SMEM(picks.shape, jnp.int32),
            pltpu.SMEM(counts.shape, jnp.int32),
            pltpu.VMEM(tokens.shape, BF16),
            pltpu.VMEM(tokens.shape, BF16),
            pltpu.VMEM((pack, count, own), BF16),
            pltpu.SemaphoreType.DMA((2 * STEPS + 2,)),
        ],
        compiler_params=PARAMS,
        cost_estimate=cost(4 * count * own * features, 4 * features * own),
    )(picks, counts, cotangent, tokens)


def by_place(arrivals, seq_n, groups):
    blocks = [block.reshape(groups, -1, block.shape[1]) for block in arrivals.blocks]
    _, rows, part = blocks[0].shape

    def body(*refs):
        out_ref, sems = refs[-2:]
        arrivals.start(refs[:-2], [out_ref.at[:, k] for k in range(seq_n)], sems)
        arrivals.wait(refs[:-2], [out_ref.at[:, k] for k in range(seq_n)], sems)

    return pl.pallas_call(
        body,
        in_specs=[ANYWHERE] * len(blocks),
        out_specs=ANYWHERE,
        out_shape=shape((groups, seq_n, rows, part)),
        scratch_shapes=[pltpu.SemaphoreType.DMA((seq_n,))],
        compiler_params=PARAMS,
        cost_estimate=cost(0, 4 * groups * seq_n * rows * part),
    )(*blocks)


def scatter_rows(back, hot, message=None):
    pack, count, own = hot.shape
    part = back.shape[1] if message is None else message[0]
    width = part // 2

    def body(hot_ref, back_ref, *refs):
        out_ref = refs[-1] if message is None else refs[-3]
        out_ref[...] = mm(hot_ref[...], back_ref[...], ROWS).astype(BF16)
        if message is not None:
            message_refs, router_ref, total_ref = refs[:-3], refs[-2], refs[-1]

            @pl.when((pl.program_id(0) == 0) & (pl.program_id(1) == 0))
            def _():
                experts = router_ref.shape[1]
                group = count // experts
                row = lax.broadcasted_iota(jnp.int32, (count, experts), 0)
                expert = lax.broadcasted_iota(jnp.int32, (count, experts), 1)
                mine = row // group == expert
                even = jnp.where(mine & (row % 2 == 0), 1.0, 0.0).astype(BF16)
                odd = jnp.where(mine & (row % 2 == 1), 1.0, 0.0).astype(BF16)
                router = sum(mm(ref[...], even, ROWS) for ref in message_refs)
                total = sum(mm(ref[...], odd, ROWS) for ref in message_refs)
                router_ref[...] = router[: router_ref.shape[0]]
                total_ref[...] = jnp.sum(total[:3], axis=0, keepdims=True)

    in_specs = [
        pl.BlockSpec((None, count, own), lambda h, i: (h, 0, 0)),
        pl.BlockSpec((count, width), lambda h, i: (0, i)),
    ]
    out_specs = [pl.BlockSpec((own, width), lambda h, i: (0, h * 2 + i))]
    out_shape = [shape((own, part * pack))]
    args = [hot, back]
    if message is not None:
        _, per, experts = message
        for t in range((back.shape[1] - part) // LANES):
            in_specs.append(pl.BlockSpec((count, LANES), lambda h, i, t=t: (0, part // LANES + t)))
            args.append(back)
        out_specs += [
            pl.BlockSpec((per, experts), lambda h, i: (0, 0)),
            pl.BlockSpec((1, experts), lambda h, i: (0, 0)),
        ]
        out_shape += [shape((per, experts), F32), shape((1, experts), F32)]
    return pl.pallas_call(
        body,
        grid=(pack, 2),
        in_specs=in_specs,
        out_specs=out_specs,
        out_shape=out_shape,
        compiler_params=PARAMS,
        cost_estimate=cost(2 * count * own * part * pack, 2 * part * pack * own),
    )(*args)


def regroup(value, group, outer, inner):
    return jnp.concatenate(
        [value[(o * inner + i) * group : (o * inner + i + 1) * group] for i in range(inner) for o in range(outer)]
    )


def first_part(rows, pack, slots):
    return (lax.broadcasted_iota(jnp.int32, (rows, 1), 0) // slots) % pack == 0


def fold(parts, slots):
    rows = parts[0].shape[0]
    total = parts[0]
    for h in range(1, len(parts)):
        total = total + pltpu.roll(parts[h], rows - h * slots, 0)
    return total


def spread(value, pack, slots):
    return [value if h == 0 else pltpu.roll(value, h * slots, 0) for h in range(pack)]


class Arrivals:
    def __init__(self, blocks, plan):
        self.blocks, self.plan = blocks, plan

    def start(self, refs, places, sems):
        here = lax.axis_index("seq")
        for k, (a, b, t) in enumerate(self.plan):
            if a == b:
                pltpu.make_async_copy(refs[a], places[k], sems.at[k]).start()
            else:

                @pl.when(here >= t)
                def _():
                    pltpu.make_async_copy(refs[a], places[k], sems.at[k]).start()

                @pl.when(here < t)
                def _():
                    pltpu.make_async_copy(refs[b], places[k], sems.at[k]).start()

    def wait(self, refs, places, sems):
        for k, (a, _, _) in enumerate(self.plan):
            pltpu.make_async_copy(refs[a], places[k], sems.at[k]).wait()


def side_copies(gate_ref, up_ref, router_ref, side, sems, pack, j, width):
    part = side.shape[0]
    hidden_n = gate_ref.shape[2]
    rows = pl.ds(j * width, width)
    copies = []
    for h in range(pack):
        for n, ref in enumerate((gate_ref, up_ref)):
            columns = pl.ds((2 * h + n) * hidden_n, hidden_n)
            copies.append((ref.at[0, pl.ds(h * part + j * width, width), :], side.at[rows, columns]))
    columns = pl.ds(2 * pack * hidden_n, LANES)
    copies.append((router_ref.at[rows, :], side.at[rows, columns]))
    return [pltpu.make_async_copy(a, b, sems.at[j, n]) for n, (a, b) in enumerate(copies)]


def down_copies(down_ref, stack, sems, pack):
    hidden_n = down_ref.shape[1]
    part = stack.shape[1]
    return [
        pltpu.make_async_copy(
            down_ref.at[0, :, pl.ds(h * part, part)], stack.at[pl.ds(h * hidden_n, hidden_n), :], sems.at[h]
        )
        for h in range(pack)
    ]


def send_blocks(out, out_refs, seq_n, columns):
    rows = out.shape[0] // seq_n
    for k in range(seq_n):
        out_refs[k][:, columns] = out[k * rows : (k + 1) * rows]
    if len(out_refs) > seq_n:
        here = lax.axis_index("seq")

        @pl.when(here == 0)
        def _():
            out_refs[seq_n][:, columns] = out[rows : 2 * rows]

        @pl.when(here > 0)
        def _():
            out_refs[seq_n][:, columns] = out[(seq_n - 1) * rows :]


def sends(seq_n):
    return seq_n + 1 if seq_n == 4 else seq_n


def expert_forward(arrivals, seq_n, slots, experts, pack, router_side, threshold, w_gate, w_up, w_down, hid_scale):
    block_rows, part = arrivals.blocks[0].shape
    rows = block_rows * seq_n
    hidden_n = w_gate.shape[2]
    width = part // STEPS
    total = 2 * pack * hidden_n + LANES
    group = pack * slots
    n_blocks = len(arrivals.blocks)
    n_sends = sends(seq_n)

    def body(*refs):
        blocks = refs[:n_blocks]
        router_ref, gate_ref, up_ref, down_ref, threshold_ref, scale_ref = refs[n_blocks : n_blocks + 6]
        x_ref, pre_ref, hidden_ref = refs[n_blocks + 6 : n_blocks + 9]
        out_refs = refs[n_blocks + 9 : n_blocks + 9 + n_sends]
        held, side, stack, x_sems, side_sems, stack_sems = refs[n_blocks + 9 + n_sends :]
        places = [x_ref.at[pl.ds(k * block_rows, block_rows), :] for k in range(seq_n)]
        arrivals.start(blocks, places, x_sems)
        chunks = [side_copies(gate_ref, up_ref, router_ref, side, side_sems, pack, j, width) for j in range(STEPS)]
        downs = down_copies(down_ref, stack, stack_sems, pack)
        for chunk in chunks:
            for copy in chunk:
                copy.start()
        for copy in downs:
            copy.start()
        arrivals.wait(blocks, places, x_sems)
        for j, chunk in enumerate(chunks):
            for copy in chunk:
                copy.wait()
            y = mm(x_ref[:, j * width : (j + 1) * width], side[j * width : (j + 1) * width, :])
            if j == 0:
                acc = y
            else:
                acc = acc + y
        columns = [acc[:, n * hidden_n : (n + 1) * hidden_n] for n in range(2 * pack)]
        gate = fold(columns[0::2], slots)
        up = fold(columns[1::2], slots)
        scores = acc[:, 2 * pack * hidden_n :]
        lane = lax.broadcasted_iota(jnp.int32, scores.shape, 1)
        expert = lax.axis_index("exp")
        score = fold([jnp.where(lane == h * experts + expert, scores, 0.0) for h in range(pack)], slots)
        lane = lax.broadcasted_iota(jnp.int32, threshold_ref.shape, 1)
        score = score - jnp.where(lane == expert, threshold_ref[...], 0.0)
        g = jax.nn.sigmoid(jnp.sum(score, axis=1, keepdims=True))
        pre_ref[:, :hidden_n] = gate
        pre_ref[:, hidden_n : 2 * hidden_n] = up
        pre_ref[:, 2 * hidden_n :] = jnp.broadcast_to(g, (rows, LANES))
        hidden = gate * jax.nn.sigmoid(gate) * up * scale_ref[...] * g
        hidden = jnp.where(first_part(rows, pack, slots), hidden, 0.0)
        for h, value in enumerate(spread(hidden, pack, slots)):
            now = slice(h * hidden_n, (h + 1) * hidden_n)
            held[:, now] = value.astype(BF16)
            hidden_ref[:, now] = regroup(value, group, seq_n, rows // seq_n // group).astype(BF16)
        for copy in downs:
            copy.wait()
        for j in range(STEPS):
            now = slice(j * width, (j + 1) * width)
            send_blocks(mm(held[...], stack[:, now]).astype(BF16), out_refs, seq_n, now)

    padded = jnp.zeros((1, LANES), F32).at[:, :experts].set(threshold[None, :])
    return pl.pallas_call(
        body,
        in_specs=[ANYWHERE] * n_blocks + [ANYWHERE] * 4 + [IN_VMEM] * 2,
        out_specs=[IN_VMEM] * (3 + n_sends),
        out_shape=[
            shape((rows, part)),
            shape((rows, 2 * hidden_n + LANES), F32),
            shape((rows, pack * hidden_n)),
        ]
        + [shape((block_rows, part))] * n_sends,
        scratch_shapes=[
            pltpu.VMEM((rows, pack * hidden_n), BF16),
            pltpu.VMEM((part, total), BF16),
            pltpu.VMEM((pack * hidden_n, part), BF16),
            pltpu.SemaphoreType.DMA((seq_n,)),
            pltpu.SemaphoreType.DMA((STEPS, 2 * pack + 1)),
            pltpu.SemaphoreType.DMA((pack,)),
        ],
        compiler_params=PARAMS,
        cost_estimate=cost(6 * rows * part * pack * hidden_n, 6 * part * pack * hidden_n),
    )(*arrivals.blocks, router_side, w_gate, w_up, w_down, padded, hid_scale)


def split3(v):
    hi = v.astype(BF16)
    rest = v - hi.astype(F32)
    mid = rest.astype(BF16)
    return hi, mid, (rest - mid.astype(F32)).astype(BF16)


def riding(seq_n, group):
    return LANES * -(-2 * seq_n // group)


def expert_backward(c, seq_n, exp_n, slots, pack, x, pre, router_side, w_gate, w_up, w_down, hid_scale):
    rows, part = x.shape
    block_rows = rows // seq_n
    hidden_n = w_gate.shape[2]
    width = part // STEPS
    total = 2 * pack * hidden_n + LANES
    group = pack * slots
    extra = riding(seq_n, group)
    per = part * pack // (seq_n * exp_n)
    n_sends = sends(seq_n)

    def body(*refs):
        c_ref, router_ref, gate_ref, up_ref, down_ref, x_ref, scale_ref, pre_ref, delta_ref = refs[:9]
        out_refs = refs[9 : 9 + n_sends]
        c_v, x_v, side, stack, columns, message, c_sem, x_sem, side_sems, stack_sems = refs[9 + n_sends :]
        c_copy = pltpu.make_async_copy(c_ref, c_v, c_sem)
        x_copy = pltpu.make_async_copy(x_ref, x_v, x_sem)
        chunks = [side_copies(gate_ref, up_ref, router_ref, side, side_sems, pack, j, width) for j in range(STEPS)]
        downs = down_copies(down_ref, stack, stack_sems, pack)
        c_copy.start()
        for copy in downs:
            copy.start()
        for chunk in chunks:
            for copy in chunk:
                copy.start()
        x_copy.start()
        c_copy.wait()
        parts = []
        for h, copy in enumerate(downs):
            copy.wait()
            parts.append(mm(c_v[...], stack[h * hidden_n : (h + 1) * hidden_n, :], LAST))
        raw = regroup(fold(parts, slots), group, block_rows // group, seq_n)
        raw = jnp.where(first_part(rows, pack, slots), raw * scale_ref[...], 0.0)
        gate = pre_ref[:, :hidden_n]
        up = pre_ref[:, hidden_n : 2 * hidden_n]
        g = pre_ref[:, 2 * hidden_n : 2 * hidden_n + 1]
        sig = jax.nn.sigmoid(gate)
        act = gate * sig
        score = jnp.sum(act * up * raw, axis=1, keepdims=True) * g * (1.0 - g)
        grad = raw * g
        to_gate = spread(grad * up * sig * (1.0 + gate * (1.0 - sig)), pack, slots)
        to_up = spread(grad * act, pack, slots)
        expert = lax.axis_index("exp")
        lane = lax.broadcasted_iota(jnp.int32, (rows, LANES), 1)
        by_expert = jnp.zeros((rows, LANES), F32)
        by_split = jnp.zeros((rows, LANES), F32)
        for h, value in enumerate(spread(jnp.broadcast_to(score, (rows, LANES)), pack, slots)):
            delta_ref[:, 2 * h * hidden_n : (2 * h + 1) * hidden_n] = to_gate[h].astype(BF16)
            delta_ref[:, (2 * h + 1) * hidden_n : (2 * h + 2) * hidden_n] = to_up[h].astype(BF16)
            for n, piece in enumerate(split3(value)):
                piece = piece.astype(F32)
                by_split = jnp.where(lane == 3 * h + n, piece, by_split)
                if n < 2:
                    by_expert = jnp.where(lane == (n * pack + h) * exp_n + expert, piece, by_expert)
        columns[...] = by_split.astype(BF16)
        delta_ref[:, 2 * pack * hidden_n :] = by_expert.astype(BF16)
        for j, chunk in enumerate(chunks):
            now = slice(j * width, (j + 1) * width)
            for copy in chunk:
                copy.wait()
            send_blocks(mm(delta_ref[...], side[now, :], LAST).astype(BF16), out_refs, seq_n, now)

        here = lax.axis_index("seq")
        x_copy.wait()
        told = mm(columns[...], x_v[...], ROWS)
        sub = lax.broadcasted_iota(jnp.int32, (group, LANES), 0)
        lane = lax.broadcasted_iota(jnp.int32, (group, LANES), 1)
        minus = jnp.broadcast_to(-jnp.sum(score, axis=0, keepdims=True), (group, LANES))
        pieces = [piece.astype(F32) for piece in split3(minus)]
        threshold_row = jnp.zeros((group, LANES), F32)
        for n, piece in enumerate(pieces):
            threshold_row = jnp.where(lane == n, piece, threshold_row)
        for owner in range(seq_n * exp_n):
            h, first = divmod(owner * per, part)
            shift = first % LANES
            value = jnp.sum(told[3 * h : 3 * h + 3, first - shift : first - shift + LANES], axis=0, keepdims=True)
            value = jnp.broadcast_to(value, (group, LANES))
            if shift:
                value = pltpu.roll(value, LANES - shift, 1)
            if per < LANES:
                value = jnp.where(lane < per, value, 0.0)
            d, place = divmod(owner, exp_n)
            for t in range(extra // LANES):
                row = sub + t * group
                message[d, place * group : (place + 1) * group, t * LANES : (t + 1) * LANES] = jnp.where(
                    row == 2 * here, value, jnp.where(row == 2 * here + 1, threshold_row, 0.0)
                )
        ride = [message[lax.rem(here - k + seq_n, seq_n)] for k in range(seq_n)]
        send_blocks(jnp.concatenate(ride).astype(BF16), out_refs, seq_n, slice(part, part + extra))

    return pl.pallas_call(
        body,
        in_specs=[ANYWHERE] * 6 + [IN_VMEM] * 2,
        out_specs=[IN_VMEM] * (1 + n_sends),
        out_shape=[shape((rows, total))] + [shape((block_rows, part + extra))] * n_sends,
        scratch_shapes=[
            pltpu.VMEM((rows, part), BF16),
            pltpu.VMEM((rows, part), BF16),
            pltpu.VMEM((part, total), BF16),
            pltpu.VMEM((pack * hidden_n, part), BF16),
            pltpu.VMEM((rows, LANES), BF16),
            pltpu.VMEM((seq_n, block_rows, extra), F32),
            pltpu.SemaphoreType.DMA,
            pltpu.SemaphoreType.DMA,
            pltpu.SemaphoreType.DMA((STEPS, 2 * pack + 1)),
            pltpu.SemaphoreType.DMA((pack,)),
        ],
        compiler_params=PARAMS,
        cost_estimate=cost(6 * rows * part * pack * hidden_n, 6 * part * pack * hidden_n),
    )(c, router_side, w_gate, w_up, w_down, x, hid_scale, pre)


def side_grads(x, delta, pack, hidden_n):
    rows, part = x.shape
    width = part // STEPS

    def body(x_ref, delta_ref, gate_out, up_out):
        both = mm(x_ref[...], delta_ref[...], ROWS)
        gate_out[...] = both[:, :hidden_n]
        up_out[...] = both[:, hidden_n:]

    tall = pl.BlockSpec((None, width, hidden_n), lambda h, i: (0, h * STEPS + i, 0))
    return pl.pallas_call(
        body,
        grid=(pack, STEPS),
        in_specs=[
            pl.BlockSpec((rows, width), lambda h, i: (0, i)),
            pl.BlockSpec((rows, 2 * hidden_n), lambda h, i: (0, h)),
        ],
        out_specs=[tall, tall],
        out_shape=[shape((1, part * pack, hidden_n), F32)] * 2,
        compiler_params=PARAMS,
        cost_estimate=cost(4 * rows * part * pack * hidden_n, 8 * part * pack * hidden_n),
    )(x, delta)


def down_grads(c, hidden, pack, hidden_n):
    rows, part = c.shape
    width = part // 2

    def body(c_ref, hidden_ref, out):
        out[...] = mm(hidden_ref[...], c_ref[...], ROWS)

    return pl.pallas_call(
        body,
        grid=(pack, 2),
        in_specs=[
            pl.BlockSpec((rows, width), lambda h, i: (0, i)),
            pl.BlockSpec((rows, hidden_n), lambda h, i: (0, h)),
        ],
        out_specs=pl.BlockSpec((None, hidden_n, width), lambda h, i: (0, 0, h * 2 + i)),
        out_shape=shape((1, hidden_n, part * pack), F32),
        compiler_params=PARAMS,
        cost_estimate=cost(2 * rows * part * pack * hidden_n, 4 * part * pack * hidden_n),
    )(c, hidden)


def up_line(block, n, first=0, last=None):
    last = n - 1 if last is None else last
    return lax.ppermute(block, "seq", [(s, s + 1) for s in range(first, last)])


def down_line(block, n, first=1, last=None):
    last = n if last is None else last
    return lax.ppermute(block, "seq", [(s, s - 1) for s in range(first, last)])


def line_gather(block, n):
    ups, downs = [], []
    up = down = block
    for j in range(1, n):
        up = up_line(up, n, j - 1)
        down = down_line(down, n, 1, n - j + 1)
        ups.append(up)
        downs.append(down)
    plan = [(0, 0, 0)] + [(k, 2 * n - 1 - k, k) for k in range(1, n)]
    return Arrivals([block] + ups + downs, plan)


def add(*parts):
    return sum(part.astype(F32) for part in parts).astype(BF16)


def after(value, *others):
    return lax.optimization_barrier((value, *others))[0]


def line_begin(parts, n):
    if n == 4:
        return lax.ppermute(parts[4], "seq", [(3, 2), (0, 1)])
    return up_line(parts[1], n, 0, 1)


def line_sum(parts, n, begun, wait_far, wait_sum):
    if n == 4:
        ends = begun
        below = up_line(parts[3], n)
        above = down_line(parts[1], n)
        middle = after(add(parts[2], ends), *wait_far)
        far = lax.ppermute(middle, "seq", [(s, (s + 2) % 4) for s in range(4)])
        return add(parts[0], below, above, after(far, *wait_sum))
    up, down = parts[1], parts[n - 1]
    for j in range(1, n):
        if j > 1:
            up, down = add(parts[j], up), add(parts[n - j], down)
        up = begun if j == 1 else up_line(up, n, 0, j)
        down = down_line(down, n, n - j)
    return add(parts[0], up, down)


def on_device(tokens, cotangent, router, threshold, w_gate, w_up, w_down, hid_scale, picks, counts):
    experts, slots = picks.shape[1:]
    features = tokens.shape[1]
    true_hidden = w_gate.shape[2]
    extra = -true_hidden % LANES
    if extra:
        w_gate, w_up = (jnp.pad(w, ((0, 0), (0, 0), (0, extra))) for w in (w_gate, w_up))
        w_down = jnp.pad(w_down, ((0, 0), (0, extra), (0, 0)))
        hid_scale = jnp.pad(hid_scale, ((0, 0), (0, extra)))
    hidden_n = true_hidden + extra
    seq_n = lax.axis_size("seq")
    exp_n = lax.axis_size("exp")
    everyone = seq_n * exp_n
    pack = max(1, 8 // slots)
    chosen = picks[0].T

    def to_experts(block):
        block = block.reshape(experts, -1, block.shape[1])
        return lax.all_to_all(block, "exp", split_axis=0, concat_axis=0, tiled=True).reshape(-1, block.shape[2])

    c_rows, x_rows, hot = choose_rows(tokens, cotangent, chosen, counts, pack)
    c_in = line_gather(c_rows, seq_n)
    x_in = line_gather(to_experts(x_rows), seq_n)
    c = lax.all_to_all(by_place(c_in, seq_n, experts), "exp", split_axis=0, concat_axis=0, tiled=True)
    c = c.reshape(-1, c.shape[-1])
    halves = list(router.reshape(pack, features // pack, experts))
    router_side = jnp.concatenate(halves + halves, axis=1)
    router_side = jnp.pad(router_side, ((0, 0), (0, LANES - router_side.shape[1])))

    x, pre, hidden, *out = expert_forward(
        x_in, seq_n, slots, experts, pack, router_side, threshold, w_gate, w_up, w_down, hid_scale
    )
    out_begun = line_begin(out, seq_n)
    delta, *back = expert_backward(
        after(c, out_begun), seq_n, exp_n, slots, pack, x, pre, router_side, w_gate, w_up, w_down, hid_scale
    )
    back_begun = line_begin(back, seq_n)
    out = line_sum(out, seq_n, out_begun, (), (delta,))
    back = line_sum(back, seq_n, back_begun, (out,), ())
    x, c, _ = lax.optimization_barrier((x, c, back_begun))
    down_grad = down_grads(c, hidden, pack, hidden_n)
    gate_grad, up_grad = side_grads(x, delta, pack, hidden_n)
    out = to_experts(out)
    back, gate_grad, up_grad, down_grad, out = lax.optimization_barrier((back, gate_grad, up_grad, down_grad, out))
    (mixture,) = scatter_rows(out, hot)
    message = (features // pack, features // everyone, experts)
    token_grad, router_grad, threshold_grad = scatter_rows(to_experts(back), hot, message)
    if extra:
        gate_grad, up_grad = gate_grad[:, :, :true_hidden], up_grad[:, :, :true_hidden]
        down_grad = down_grad[:, :true_hidden]
    return mixture, token_grad, router_grad, threshold_grad[0], gate_grad, up_grad, down_grad


def solution(mesh):
    by_owner = P(BOTH, None)
    columns = P("exp", None, "seq")
    down = P("exp", "seq", None)
    return jax.shard_map(
        on_device,
        mesh=mesh,
        in_specs=(
            by_owner,
            by_owner,
            P(),
            P(),
            columns,
            columns,
            down,
            P("exp", "seq"),
            P(BOTH, None, None),
            by_owner,
        ),
        out_specs=(by_owner, by_owner, by_owner, P(), columns, columns, down),
        check_vma=False,
    )
```

time: 168 us -> 181 us (1.077)
  Pallas kernels: 31.5 us -> 81.9 us
  local copies, waits for them, and re-layouts: 25.2 us -> 6.31 us
  waiting for transfers between devices: 43.9 us -> 25.5 us
  other arithmetic: 7.51 us -> 5.02 us
  starting transfers between devices: 57.5 us -> 59.8 us
    pallas_call x6, Pallas kernels: 20.8 us -> 67.5 us  [the longest x1 32.9 us: by_place(): pl.pallas_call(body, in_specs=[ANYWHERE] * len(blocks), out_specs=ANYWHER...]
    ppermute x8 -> x4, waiting for transfers between devices: 32.6 us -> 10.8 us  [the longest x2 10.8 us: line_begin(): return lax.ppermute(parts[4], 'seq', [(3, 2), (0, 1)])]
    unnamed x60 -> x37, local copies, waits for them, and re-layouts: 19.5 us -> 4.61 us
    ppermute x4 -> x8, waiting for transfers between devices: 1.43 us -> 10.6 us  [down_line(): return lax.ppermute(block, 'seq', [(s, s - 1) for s in range(first, last)])]
    ppermute x4 -> x8, starting transfers between devices: 5.15 us -> 10.3 us  [down_line(): return lax.ppermute(block, 'seq', [(s, s - 1) for s in range(first, last)])]
    all_to_all x4 -> x3, waiting for transfers between devices: 8.14 us -> 4.1 us  [to_experts(): lax.all_to_all(block, 'exp', split_axis=0, concat_axis=0, tiled=True)]
    reshape x2 -> x0, other arithmetic: 2.79 us -> none  [to_experts(): block = block.reshape(experts, -1, block.shape[1])]
    all_to_all x4 -> x3, starting transfers between devices: 15.7 us -> 12.9 us  [to_experts(): lax.all_to_all(block, 'exp', split_axis=0, concat_axis=0, tiled=True)]
  transfers between devices with their start and end apart: 21 -> 24, of which waited for: 8 -> 8; matrix products, arithmetic and copies ran while one was open for 8% -> 3% of each run, Pallas kernels for 16% -> 41%
where the time goes in v4:
time: 181 us; the launch traced here: 180 us
  Pallas kernels  81.9 us (45%)
  starting transfers between devices  59.8 us (33%)
  waiting for transfers between devices  25.5 us (14%)
  local copies, waits for them, and re-layouts  6.31 us (3%)
  other arithmetic  5.02 us (3%)
    pallas_call x1, Pallas kernels, by_place(): pl.pallas_call(body, in_specs=[ANYWHERE] * len(blocks), out_specs=ANYWHER...  32.9 us
    ppermute x8, starting transfers between devices, up_line(): return lax.ppermute(block, 'seq', [(s, s + 1) for s in range(first, last)])  15.6 us
    all_to_all x3, starting transfers between devices, to_experts(): lax.all_to_all(block, 'exp', split_axis=0, concat_axis=0, tiled=True)  12.9 us
    pallas_call x1, Pallas kernels, expert_backward(): pl.pallas_call(body, in_specs=[ANYWHERE] * 6 + [IN_VMEM] * 2, out_specs=[...  11.7 us
    pallas_call x1, Pallas kernels, expert_forward(): pl.pallas_call(body, in_specs=[ANYWHERE] * n_blocks + [ANYWHERE] * 4 + [I...  11.1 us
    ppermute x2, waiting for transfers between devices, line_begin(): return lax.ppermute(parts[4], 'seq', [(3, 2), (0, 1)])  10.8 us
    ppermute x8, waiting for transfers between devices, down_line(): return lax.ppermute(block, 'seq', [(s, s - 1) for s in range(first, last)])  10.6 us
    ppermute x8, starting transfers between devices, down_line(): return lax.ppermute(block, 'seq', [(s, s - 1) for s in range(first, last)])  10.3 us
  transfers between devices with their start and end apart: 24, of which 8 were waited for; matrix products, arithmetic and copies ran while one was open for 3% of the time, Pallas kernels for 41%

profile of v4, /device:TPU:0, one launch (start us, length us, event | category | flops | bytes accessed | tf_op | source)
XLA Modules:
  0.0 179.6 jit_solution(1581831521358747015)
XLA Ops:
  0.7 3.5 %shard_map.153 = (bf16[64,2048]{1,0:T(8,128)(2,1)}, bf16[64,2048]{1,0:T(8,128)(2,1)}, bf16[2,64,256]{2,1,0:T(8,128)(2,1)}) custom-call(s32[4,8]{1,0:T(4,128)} %bitcast.34, s32[1,8]{1,0:T(1,128)} %counts_ref.1, bf16[256,4096]{1,0:T(8,128)(2,1)} %c_ref.1, bf16[256,4096]{1,0:T(8,128)(2,1)} %x_ref.1), custom_call_target="tpu_custom_call" | custom-call | flops 268435456 | bytes 4194304 | tf_op jit(solution)/shard_map/pallas_call | solution.py:81
  4.1 5.2 %all-to-all-start.1 = ((bf16[8,8,2048]{2,1,0:T(8,128)(2,1)}), bf16[8,8,2048]{2,1,0:T(8,128)(2,1)S(1)}, u32[]{:S(2)}, u32[]{:S(2)}) async-start(bf16[8,8,2048]{2,1,0:T(8,128)(2,1)} %bitcast.28), calls=%async_computation.1 | async-start | bytes 524288 | tf_op jit(solution)/shard_map/all_to_all | solution.py:585
  9.3 1.3 collective-permute-start.3
  10.6 4.6 %collective-permute-start = (bf16[64,2048]{1,0:T(8,128)(2,1)}, bf16[64,2048]{1,0:T(8,128)(2,1)S(1)}, u32[]{:S(2)}, u32[]{:S(2)}) collective-permute-start(bf16[64,2048]{1,0:T(8,128)(2,1)} %get-tuple-element.52), channel_id=1, source_target_pairs={{0,8},{8,16},{16,24},{1,9},{9,17},{17,25},{2,10},{10,18},{18,26},{... | collective-permute-start | bytes 786440 | tf_op jit(solution)/shard_map/ppermute | solution.py:516
  15.2 1.1 all-to-all-done.1
  16.2 1.3 collective-permute-start.9
  17.5 4.6 %collective-permute-start.6 = (bf16[64,2048]{1,0:T(8,128)(2,1)S(1)}, bf16[64,2048]{1,0:T(8,128)(2,1)S(1)}, u32[]{:S(2)}, u32[]{:S(2)}) collective-permute-start(bf16[64,2048]{1,0:T(8,128)(2,1)S(1)} %bitcast.25), channel_id=1, source_target_pairs={{0,8},{8,16},{16,24},{1,9},{9,17},{17,25},{2,10},{10,18},{18,26},{... | collective-permute-start | bytes 786440 | tf_op jit(solution)/shard_map/ppermute | solution.py:516
  22.1 1.3 collective-permute-start.4
  24.1 2.0 %collective-permute-done.9.refs_4_ = bf16[64,2048]{1,0:T(8,128)(2,1)S(1)} collective-permute-done((bf16[64,2048]{1,0:T(8,128)(2,1)S(1)}, bf16[64,2048]{1,0:T(8,128)(2,1)S(1)}, u32[]{:S(2)}, u32[]{:S(2)}) %collective-permute-start.9) | collective-permute-done | bytes 262176 | tf_op jit(solution)/shard_map/ppermute | solution.py:521
  26.2 1.3 collective-permute-start.10
  27.5 0.7 collective-permute-start.7
  28.2 4.0 %collective-permute-done.4 = bf16[64,2048]{1,0:T(8,128)(2,1)S(1)} collective-permute-done((bf16[64,2048]{1,0:T(8,128)(2,1)S(1)}, bf16[64,2048]{1,0:T(8,128)(2,1)S(1)}, u32[]{:S(2)}, u32[]{:S(2)}) %collective-permute-start.4) | collective-permute-done | bytes 262176 | tf_op jit(solution)/shard_map/ppermute | solution.py:521
  32.2 1.3 collective-permute-start.5
  33.5 1.4 collective-permute-start.2
  34.9 3.8 %collective-permute-done.10.refs_5_ = bf16[64,2048]{1,0:T(8,128)(2,1)S(1)} collective-permute-done((bf16[64,2048]{1,0:T(8,128)(2,1)S(1)}, bf16[64,2048]{1,0:T(8,128)(2,1)S(1)}, u32[]{:S(2)}, u32[]{:S(2)}) %collective-permute-start.10) | collective-permute-done | bytes 262176 | tf_op jit(solution)/shard_map/ppermute | solution.py:521
  38.7 1.3 collective-permute-start.11
  40.0 0.7 collective-permute-start.8
  42.8 0.9 pad.7.refs_7_.refs_1_
  43.7 0.7 collective-permute-done.5
  44.4 32.9 %shard_map.154 = bf16[8,4,8,2048]{3,2,1,0:T(8,128)(2,1)} custom-call(bf16[8,8,2048]{2,1,0:T(8,128)(2,1)} %bitcast.29, bf16[8,8,2048]{2,1,0:T(8,128)(2,1)} %bitcast.31, bf16[8,8,2048]{2,1,0:T(8,128)(2,1)} %bitcast.33, bf16[8,8,2048]{2,1,0:T(8,128)(2,1)} %bitcast.5.refs_3_, bf16[8,8,2048]{2,1,0:T(8,128)(2,1)} %bitcast.30, bf16[8,8,2048]{2,1,0:T(8,128)(2,1)} %bitcast.32, ...), custom_call_target="tpu_custom_call" | custom-call | bytes 2097152 | tf_op jit(solution)/shard_map/pallas_call | solution.py:108
  77.4 3.6 %all-to-all-start = ((bf16[8,4,8,2048]{3,2,1,0:T(8,128)(2,1)}), bf16[8,4,8,2048]{3,2,1,0:T(8,128)(2,1)S(1)}, u32[]{:S(2)}, u32[]{:S(2)}) async-start(bf16[8,4,8,2048]{3,2,1,0:T(8,128)(2,1)} %shard_map.154), calls=%async_computation | async-start | bytes 2097152 | tf_op jit(solution)/shard_map/all_to_all | solution.py:590
  81.7 0.7 copy-done.11
  82.4 11.1 %shard_map.155 = (bf16[256,2048]{1,0:T(8,128)(2,1)}, f32[256,896]{1,0:T(8,128)}, bf16[256,768]{1,0:T(8,128)(2,1)}, bf16[64,2048]{1,0:T(8,128)(2,1)}, bf16[64,204...) custom-call(bf16[64,2048]{1,0:T(8,128)(2,1)} %bitcast.26, ...), custom_call_target="tpu_custom_call" | custom-call | flops 2415919104 | bytes 9437184 | tf_op jit(solution)/shard_map/pallas_call | solution.py:323
  93.5 3.9 %collective-permute-start.12 = (bf16[64,2048]{1,0:T(8,128)(2,1)}, bf16[64,2048]{1,0:T(8,128)(2,1)S(1)}, u32[]{:S(2)}, u32[]{:S(2)}) collective-permute-start(bf16[64,2048]{1,0:T(8,128)(2,1)} %get-tuple-element.54), channel_id=1, source_target_pairs={{24,16},{0,8},{25,17},{1,9},{26,18},{2,10},{27,19},{3,11},{28,20},... | collective-permute-start | bytes 786440 | tf_op jit(solution)/shard_map/ppermute | solution.py:546
  97.4 6.4 %collective-permute-done.12 = bf16[64,2048]{1,0:T(8,128)(2,1)S(1)} collective-permute-done((bf16[64,2048]{1,0:T(8,128)(2,1)}, bf16[64,2048]{1,0:T(8,128)(2,1)S(1)}, u32[]{:S(2)}, u32[]{:S(2)}) %collective-permute-start.12) | collective-permute-done | bytes 262176 | tf_op jit(solution)/shard_map/ppermute | solution.py:546
  103.8 1.0 add_convert_fusion.3
  104.8 5.9 %collective-permute-start.18 = (bf16[64,2048]{1,0:T(8,128)(2,1)S(1)}, bf16[64,2048]{1,0:T(8,128)(2,1)S(1)}, u32[]{:S(2)}, u32[]{:S(2)}) collective-permute-start(bf16[64,2048]{1,0:T(8,128)(2,1)S(1)} %add_convert_fusion.3), channel_id=1, source_target_pairs={{0,16},{8,24},{16,0},{24,8},{1,17},{9,25},{17,1},{25,9},{2,18},{10... | collective-permute-start | bytes 786440 | tf_op jit(solution)/shard_map/ppermute | solution.py:556
  110.7 1.6 collective-permute-start.16
  112.3 1.3 collective-permute-start.17
  113.6 1.0 copy-done
  114.6 11.7 %shard_map.156 = (bf16[256,1664]{1,0:T(8,128)(2,1)}, bf16[64,2176]{1,0:T(8,128)(2,1)}, bf16[64,2176]{1,0:T(8,128)(2,1)}, bf16[64,2176]{1,0:T(8,128)(2,1)}, bf16[...) custom-call(bf16[256,2048]{1,0:T(8,128)(2,1)} %bitcast.20, bf16[2048,128]{1,0:T(8,128)(2,1)} %pad.7.refs_7_.refs_1_, ...), custom_call_target="tpu_custom_call" | custom-call | flops 2415919104 | bytes 9437184 | tf_op jit(solution)/shard_map/pallas_call | solution.py:447
  126.3 4.6 %collective-permute-start.15 = (bf16[64,2176]{1,0:T(8,128)(2,1)}, bf16[64,2176]{1,0:T(8,128)(2,1)S(1)}, u32[]{:S(2)}, u32[]{:S(2)}) collective-permute-start(bf16[64,2176]{1,0:T(8,128)(2,1)} %get-tuple-element.62), channel_id=1, source_target_pairs={{24,16},{0,8},{25,17},{1,9},{26,18},{2,10},{27,19},{3,11},{28,20},... | collective-permute-start | bytes 835592 | tf_op jit(solution)/shard_map/ppermute | solution.py:546
  130.9 0.8 add_convert_fusion.2
  131.8 4.3 %collective-permute-done.15 = bf16[64,2176]{1,0:T(8,128)(2,1)S(1)} collective-permute-done((bf16[64,2176]{1,0:T(8,128)(2,1)}, bf16[64,2176]{1,0:T(8,128)(2,1)S(1)}, u32[]{:S(2)}, u32[]{:S(2)}) %collective-permute-start.15) | collective-permute-done | bytes 278560 | tf_op jit(solution)/shard_map/ppermute | solution.py:546
  136.1 1.0 add_convert_fusion.1
  137.1 3.1 %collective-permute-start.19 = (bf16[64,2176]{1,0:T(8,128)(2,1)S(1)}, bf16[64,2176]{1,0:T(8,128)(2,1)S(1)}, u32[]{:S(2)}, u32[]{:S(2)}) collective-permute-start(bf16[64,2176]{1,0:T(8,128)(2,1)S(1)} %add_convert_fusion.1), channel_id=1, source_target_pairs={{0,16},{8,24},{16,0},{24,8},{1,17},{9,25},{17,1},{25,9},{2,18},{10... | collective-permute-start | bytes 835592 | tf_op jit(solution)/shard_map/ppermute | solution.py:556
  140.2 1.6 collective-permute-start.13
  141.7 1.3 collective-permute-start.14
  143.0 3.5 %all-to-all-start.2 = ((bf16[8,8,2048]{2,1,0:T(8,128)(2,1)}), bf16[8,8,2048]{2,1,0:T(8,128)(2,1)S(1)}, u32[]{:S(2)}, u32[]{:S(2)}) async-start(bf16[8,8,2048]{2,1,0:T(8,128)(2,1)} %bitcast.13), calls=%async_computation.2 | async-start | bytes 524288 | tf_op jit(solution)/shard_map/all_to_all | solution.py:585
  146.6 5.4 %shard_map.158 = f32[1,384,4096]{2,1,0:T(8,128)} custom-call(bf16[256,2048]{1,0:T(8,128)(2,1)} %bitcast.21, bf16[256,768]{1,0:T(8,128)(2,1)} %get-tuple-element.74.hidden_ref), custom_call_target="tpu_custom_call" | custom-call | flops 805306368 | bytes 6291456 | tf_op jit(solution)/shard_map/pallas_call | solution.py:500
  152.0 8.9 %shard_map.157 = (f32[1,4096,384]{2,1,0:T(8,128)}, f32[1,4096,384]{2,1,0:T(8,128)}) custom-call(bf16[256,2048]{1,0:T(8,128)(2,1)} %get-tuple-element.70.refs_5_.x_ref, bf16[256,1664]{1,0:T(8,128)(2,1)} %get-tuple-element.67.delta_ref), custom_call_target="tpu_custom_call" | custom-call | flops 1610612736 | bytes 12582912 | tf_op jit(solution)/shard_map/pallas_call | solution.py:479
  161.0 0.8 add_convert_fusion
  161.8 4.2 %all-to-all-start.3 = ((bf16[8,8,2176]{2,1,0:T(8,128)(2,1)}), bf16[8,8,2176]{2,1,0:T(8,128)(2,1)S(1)}, u32[]{:S(2)}, u32[]{:S(2)}) async-start(bf16[8,8,2176]{2,1,0:T(8,128)(2,1)} %bitcast.15), calls=%async_computation.3 | async-start | bytes 557056 | tf_op jit(solution)/shard_map/all_to_all | solution.py:585
  166.0 4.1 %shard_map.159 = bf16[256,4096]{1,0:T(8,128)(2,1)} custom-call(bf16[2,64,256]{2,1,0:T(8,128)(2,1)} %get-tuple-element.51.hot_ref, bf16[64,2048]{1,0:T(8,128)(2,1)} %bitcast.27), custom_call_target="tpu_custom_call" | custom-call | flops 134217728 | bytes 2097152 | tf_op jit(solution)/shard_map/pallas_call | solution.py:161
  170.1 3.0 %all-to-all-done.3 = bf16[8,8,2176]{2,1,0:T(8,128)(2,1)S(1)} async-done(((bf16[8,8,2176]{2,1,0:T(8,128)(2,1)}), bf16[8,8,2176]{2,1,0:T(8,128)(2,1)S(1)}, u32[]{:S(2)}, u32[]{:S(2)}) %all-to-all-start.3) | async-done | bytes 278560 | tf_op jit(solution)/shard_map/all_to_all | solution.py:585
  173.1 0.7 copy-done.1
  173.8 4.3 %shard_map.160 = (bf16[256,4096]{1,0:T(8,128)(2,1)}, f32[128,8]{1,0:T(8,128)}, f32[1,8]{1,0:T(1,128)}) custom-call(bf16[2,64,256]{2,1,0:T(8,128)(2,1)} %get-tuple-element.51.hot_ref, bf16[64,2176]{1,0:T(8,128)(2,1)} %bitcast.22, bf16[64,2176]{1,0:T(8,128)(2,1)} %bitcast.23), custom_call_target="tpu_custom_call" | custom-call | flops 134217728 | bytes 2097152 | tf_op jit(solution)/shard_map/pallas_call | solution.py:161
  178.1 1.5 copy.23
  (56 shorter events, 3.6 us)
Async XLA Ops:
  0.6 27.5 %copy-start.16 = (bf16[4096,8]{0,1:T(8,128)(2,1)S(1)}, bf16[4096,8]{0,1:T(8,128)(2,1)}, u32[]{:S(2)}) copy-start(bf16[4096,8]{0,1:T(8,128)(2,1)} %param.14) | copy-start | bytes 196612
  0.6 41.0 %copy-start.17 = (f32[8]{0:T(128)S(1)}, f32[8]{0:T(128)}, u32[]{:S(2)}) copy-start(f32[8]{0:T(128)} %param.15) | copy-start | bytes 100
  4.1 12.1 %all-to-all-start.1 = ((bf16[8,8,2048]{2,1,0:T(8,128)(2,1)}), bf16[8,8,2048]{2,1,0:T(8,128)(2,1)S(1)}, u32[]{:S(2)}, u32[]{:S(2)}) async-start(bf16[8,8,2048]{2,1,0:T(8,128)(2,1)} %bitcast.28), calls=%async_computation.1 | async-start | bytes 524288 | tf_op jit(solution)/shard_map/all_to_all | solution.py:585
  9.3 12.8 %collective-permute-start.3 = (bf16[64,2048]{1,0:T(8,128)(2,1)}, bf16[64,2048]{1,0:T(8,128)(2,1)S(1)}, u32[]{:S(2)}, u32[]{:S(2)}) collective-permute-start(bf16[64,2048]{1,0:T(8,128)(2,1)} %get-tuple-element.52), channel_id=1, source_target_pairs={{8,0},{16,8},{24,16},{9,1},{17,9},{25,17},{10,2},{18,10},{26,18},{... | collective-permute-start | bytes 786440 | tf_op jit(solution)/shard_map/ppermute | solution.py:521
  10.6 12.8 %collective-permute-start = (bf16[64,2048]{1,0:T(8,128)(2,1)}, bf16[64,2048]{1,0:T(8,128)(2,1)S(1)}, u32[]{:S(2)}, u32[]{:S(2)}) collective-permute-start(bf16[64,2048]{1,0:T(8,128)(2,1)} %get-tuple-element.52), channel_id=1, source_target_pairs={{0,8},{8,16},{16,24},{1,9},{9,17},{17,25},{2,10},{10,18},{18,26},{... | collective-permute-start | bytes 786440 | tf_op jit(solution)/shard_map/ppermute | solution.py:516
  16.2 61.1 %copy-start.2 = (bf16[8,8,2048]{2,1,0:T(8,128)(2,1)}, bf16[8,8,2048]{2,1,0:T(8,128)(2,1)S(1)}, u32[]{:S(2)}) copy-start(bf16[8,8,2048]{2,1,0:T(8,128)(2,1)S(1)} %all-to-all-done.1) | copy-start | bytes 786436
  16.2 9.9 %collective-permute-start.9 = (bf16[64,2048]{1,0:T(8,128)(2,1)S(1)}, bf16[64,2048]{1,0:T(8,128)(2,1)S(1)}, u32[]{:S(2)}, u32[]{:S(2)}) collective-permute-start(bf16[64,2048]{1,0:T(8,128)(2,1)S(1)} %bitcast.24), channel_id=1, source_target_pairs={{8,0},{16,8},{24,16},{9,1},{17,9},{25,17},{10,2},{18,10},{26,18},{... | collective-permute-start | bytes 786440 | tf_op jit(solution)/shard_map/ppermute | solution.py:521
  17.5 9.9 %collective-permute-start.6 = (bf16[64,2048]{1,0:T(8,128)(2,1)S(1)}, bf16[64,2048]{1,0:T(8,128)(2,1)S(1)}, u32[]{:S(2)}, u32[]{:S(2)}) collective-permute-start(bf16[64,2048]{1,0:T(8,128)(2,1)S(1)} %bitcast.25), channel_id=1, source_target_pairs={{0,8},{8,16},{16,24},{1,9},{9,17},{17,25},{2,10},{10,18},{18,26},{... | collective-permute-start | bytes 786440 | tf_op jit(solution)/shard_map/ppermute | solution.py:516
  22.1 22.3 %copy-start.12 = (bf16[64,2048]{1,0:T(8,128)(2,1)}, bf16[64,2048]{1,0:T(8,128)(2,1)S(1)}, u32[]{:S(2)}) copy-start(bf16[64,2048]{1,0:T(8,128)(2,1)S(1)} %collective-permute-done.3) | copy-start | bytes 786436
  22.1 10.1 %collective-permute-start.4 = (bf16[64,2048]{1,0:T(8,128)(2,1)S(1)}, bf16[64,2048]{1,0:T(8,128)(2,1)S(1)}, u32[]{:S(2)}, u32[]{:S(2)}) collective-permute-start(bf16[64,2048]{1,0:T(8,128)(2,1)S(1)} %collective-permute-done.3), channel_id=1, source_target_pairs={{8,0},{16,8},{9,1},{17,9},{10,2},{18,10},{11,3},{19,11},{12,4},{20... | collective-permute-start | bytes 786440 | tf_op jit(solution)/shard_map/ppermute | solution.py:521
  23.4 21.0 %copy-start.13 = (bf16[64,2048]{1,0:T(8,128)(2,1)}, bf16[64,2048]{1,0:T(8,128)(2,1)S(1)}, u32[]{:S(2)}) copy-start(bf16[64,2048]{1,0:T(8,128)(2,1)S(1)} %collective-permute-done) | copy-start | bytes 786436
  23.4 10.0 %collective-permute-start.1 = (bf16[64,2048]{1,0:T(8,128)(2,1)S(1)}, bf16[64,2048]{1,0:T(8,128)(2,1)S(1)}, u32[]{:S(2)}, u32[]{:S(2)}) collective-permute-start(bf16[64,2048]{1,0:T(8,128)(2,1)S(1)} %collective-permute-done), channel_id=1, source_target_pairs={{8,16},{16,24},{9,17},{17,25},{10,18},{18,26},{11,19},{19,27},{12,... | collective-permute-start | bytes 786440 | tf_op jit(solution)/shard_map/ppermute | solution.py:516
  26.2 51.2 %copy-start.5 = (bf16[64,2048]{1,0:T(8,128)(2,1)}, bf16[64,2048]{1,0:T(8,128)(2,1)S(1)}, u32[]{:S(2)}) copy-start(bf16[64,2048]{1,0:T(8,128)(2,1)S(1)} %collective-permute-done.9.refs_4_) | copy-start | bytes 786436
  26.2 12.5 %collective-permute-start.10 = (bf16[64,2048]{1,0:T(8,128)(2,1)S(1)}, bf16[64,2048]{1,0:T(8,128)(2,1)S(1)}, u32[]{:S(2)}, u32[]{:S(2)}) collective-permute-start(bf16[64,2048]{1,0:T(8,128)(2,1)S(1)} %collective-permute-done.9.refs_4_), channel_id=1, source_target_pairs={{8,0},{16,8},{9,1},{17,9},{10,2},{18,10},{11,3},{19,11},{12,4},{20... | collective-permute-start | bytes 786440 | tf_op jit(solution)/shard_map/ppermute | solution.py:521
  27.5 49.9 %copy-start.6 = (bf16[64,2048]{1,0:T(8,128)(2,1)}, bf16[64,2048]{1,0:T(8,128)(2,1)S(1)}, u32[]{:S(2)}) copy-start(bf16[64,2048]{1,0:T(8,128)(2,1)S(1)} %collective-permute-done.6.refs_1_) | copy-start | bytes 786436
  27.5 12.5 %collective-permute-start.7 = (bf16[64,2048]{1,0:T(8,128)(2,1)S(1)}, bf16[64,2048]{1,0:T(8,128)(2,1)S(1)}, u32[]{:S(2)}, u32[]{:S(2)}) collective-permute-start(bf16[64,2048]{1,0:T(8,128)(2,1)S(1)} %collective-permute-done.6.refs_1_), channel_id=1, source_target_pairs={{8,16},{16,24},{9,17},{17,25},{10,18},{18,26},{11,19},{19,27},{12,... | collective-permute-start | bytes 786440 | tf_op jit(solution)/shard_map/ppermute | solution.py:516
  32.2 12.2 %copy-start.14 = (bf16[64,2048]{1,0:T(8,128)(2,1)}, bf16[64,2048]{1,0:T(8,128)(2,1)S(1)}, u32[]{:S(2)}) copy-start(bf16[64,2048]{1,0:T(8,128)(2,1)S(1)} %collective-permute-done.4) | copy-start | bytes 786436
  32.2 12.2 %collective-permute-start.5 = (bf16[64,2048]{1,0:T(8,128)(2,1)S(1)}, bf16[64,2048]{1,0:T(8,128)(2,1)}, u32[]{:S(2)}, u32[]{:S(2)}) collective-permute-start(bf16[64,2048]{1,0:T(8,128)(2,1)S(1)} %collective-permute-done.4), channel_id=1, source_target_pairs={{8,0},{9,1},{10,2},{11,3},{12,4},{13,5},{14,6},{15,7}} | collective-permute-start | bytes 786440 | tf_op jit(solution)/shard_map/ppermute | solution.py:521
  33.5 10.9 %copy-start.15 = (bf16[64,2048]{1,0:T(8,128)(2,1)}, bf16[64,2048]{1,0:T(8,128)(2,1)S(1)}, u32[]{:S(2)}) copy-start(bf16[64,2048]{1,0:T(8,128)(2,1)S(1)} %collective-permute-done.1) | copy-start | bytes 786436
  33.5 10.9 %collective-permute-start.2 = (bf16[64,2048]{1,0:T(8,128)(2,1)S(1)}, bf16[64,2048]{1,0:T(8,128)(2,1)}, u32[]{:S(2)}, u32[]{:S(2)}) collective-permute-start(bf16[64,2048]{1,0:T(8,128)(2,1)S(1)} %collective-permute-done.1), channel_id=1, source_target_pairs={{16,24},{17,25},{18,26},{19,27},{20,28},{21,29},{22,30},{23,31}} | collective-permute-start | bytes 786440 | tf_op jit(solution)/shard_map/ppermute | solution.py:516
  38.7 38.7 %copy-start.7 = (bf16[64,2048]{1,0:T(8,128)(2,1)}, bf16[64,2048]{1,0:T(8,128)(2,1)S(1)}, u32[]{:S(2)}) copy-start(bf16[64,2048]{1,0:T(8,128)(2,1)S(1)} %collective-permute-done.10.refs_5_) | copy-start | bytes 786436
  38.7 42.3 %collective-permute-start.11 = (bf16[64,2048]{1,0:T(8,128)(2,1)S(1)}, bf16[64,2048]{1,0:T(8,128)(2,1)S(1)}, u32[]{:S(2)}, u32[]{:S(2)}) collective-permute-start(bf16[64,2048]{1,0:T(8,128)(2,1)S(1)} %collective-permute-done.10.refs_5_), channel_id=1, source_target_pairs={{8,0},{9,1},{10,2},{11,3},{12,4},{13,5},{14,6},{15,7}} | collective-permute-start | bytes 786440 | tf_op jit(solution)/shard_map/ppermute | solution.py:521
  40.0 37.4 %copy-start.8 = (bf16[64,2048]{1,0:T(8,128)(2,1)}, bf16[64,2048]{1,0:T(8,128)(2,1)S(1)}, u32[]{:S(2)}) copy-start(bf16[64,2048]{1,0:T(8,128)(2,1)S(1)} %collective-permute-done.7.refs_2_) | copy-start | bytes 786436
  40.0 41.0 %collective-permute-start.8 = (bf16[64,2048]{1,0:T(8,128)(2,1)S(1)}, bf16[64,2048]{1,0:T(8,128)(2,1)S(1)}, u32[]{:S(2)}, u32[]{:S(2)}) collective-permute-start(bf16[64,2048]{1,0:T(8,128)(2,1)S(1)} %collective-permute-done.7.refs_2_), channel_id=1, source_target_pairs={{16,24},{17,25},{18,26},{19,27},{20,28},{21,29},{22,30},{23,31}} | collective-permute-start | bytes 786440 | tf_op jit(solution)/shard_map/ppermute | solution.py:516
  77.4 36.2 %all-to-all-start = ((bf16[8,4,8,2048]{3,2,1,0:T(8,128)(2,1)}), bf16[8,4,8,2048]{3,2,1,0:T(8,128)(2,1)S(1)}, u32[]{:S(2)}, u32[]{:S(2)}) async-start(bf16[8,4,8,2048]{3,2,1,0:T(8,128)(2,1)} %shard_map.154), calls=%async_computation | async-start | bytes 2097152 | tf_op jit(solution)/shard_map/all_to_all | solution.py:590
  81.0 0.7 copy-start.10
  81.7 0.7 copy-start.11
  93.5 10.3 %collective-permute-start.12 = (bf16[64,2048]{1,0:T(8,128)(2,1)}, bf16[64,2048]{1,0:T(8,128)(2,1)S(1)}, u32[]{:S(2)}, u32[]{:S(2)}) collective-permute-start(bf16[64,2048]{1,0:T(8,128)(2,1)} %get-tuple-element.54), channel_id=1, source_target_pairs={{24,16},{0,8},{25,17},{1,9},{26,18},{2,10},{27,19},{3,11},{28,20},... | collective-permute-start | bytes 786440 | tf_op jit(solution)/shard_map/ppermute | solution.py:546
  104.8 21.5 %collective-permute-start.18 = (bf16[64,2048]{1,0:T(8,128)(2,1)S(1)}, bf16[64,2048]{1,0:T(8,128)(2,1)S(1)}, u32[]{:S(2)}, u32[]{:S(2)}) collective-permute-start(bf16[64,2048]{1,0:T(8,128)(2,1)S(1)} %add_convert_fusion.3), channel_id=1, source_target_pairs={{0,16},{8,24},{16,0},{24,8},{1,17},{9,25},{17,1},{25,9},{2,18},{10... | collective-permute-start | bytes 786440 | tf_op jit(solution)/shard_map/ppermute | solution.py:556
  110.7 20.2 %collective-permute-start.16 = (bf16[64,2048]{1,0:T(8,128)(2,1)}, bf16[64,2048]{1,0:T(8,128)(2,1)S(1)}, u32[]{:S(2)}, u32[]{:S(2)}) collective-permute-start(bf16[64,2048]{1,0:T(8,128)(2,1)} %get-tuple-element.64), channel_id=1, source_target_pairs={{0,8},{8,16},{16,24},{1,9},{9,17},{17,25},{2,10},{10,18},{18,26},{... | collective-permute-start | bytes 786440 | tf_op jit(solution)/shard_map/ppermute | solution.py:516
  112.3 18.6 %collective-permute-start.17 = (bf16[64,2048]{1,0:T(8,128)(2,1)}, bf16[64,2048]{1,0:T(8,128)(2,1)S(1)}, u32[]{:S(2)}, u32[]{:S(2)}) collective-permute-start(bf16[64,2048]{1,0:T(8,128)(2,1)} %get-tuple-element.65), channel_id=1, source_target_pairs={{8,0},{16,8},{24,16},{9,1},{17,9},{25,17},{10,2},{18,10},{26,18},{... | collective-permute-start | bytes 786440 | tf_op jit(solution)/shard_map/ppermute | solution.py:521
  113.6 1.0 copy-start
  114.6 16.3 %copy-start.9 = (bf16[64,2048]{1,0:T(8,128)(2,1)S(1)}, bf16[64,2048]{1,0:T(8,128)(2,1)}, u32[]{:S(2)}) copy-start(bf16[64,2048]{1,0:T(8,128)(2,1)} %get-tuple-element.63) | copy-start | bytes 786436
  126.3 9.8 %collective-permute-start.15 = (bf16[64,2176]{1,0:T(8,128)(2,1)}, bf16[64,2176]{1,0:T(8,128)(2,1)S(1)}, u32[]{:S(2)}, u32[]{:S(2)}) collective-permute-start(bf16[64,2176]{1,0:T(8,128)(2,1)} %get-tuple-element.62), channel_id=1, source_target_pairs={{24,16},{0,8},{25,17},{1,9},{26,18},{2,10},{27,19},{3,11},{28,20},... | collective-permute-start | bytes 835592 | tf_op jit(solution)/shard_map/ppermute | solution.py:546
  137.1 23.8 %collective-permute-start.19 = (bf16[64,2176]{1,0:T(8,128)(2,1)S(1)}, bf16[64,2176]{1,0:T(8,128)(2,1)S(1)}, u32[]{:S(2)}, u32[]{:S(2)}) collective-permute-start(bf16[64,2176]{1,0:T(8,128)(2,1)S(1)} %add_convert_fusion.1), channel_id=1, source_target_pairs={{0,16},{8,24},{16,0},{24,8},{1,17},{9,25},{17,1},{25,9},{2,18},{10... | collective-permute-start | bytes 835592 | tf_op jit(solution)/shard_map/ppermute | solution.py:556
  140.2 20.8 %collective-permute-start.13 = (bf16[64,2176]{1,0:T(8,128)(2,1)}, bf16[64,2176]{1,0:T(8,128)(2,1)S(1)}, u32[]{:S(2)}, u32[]{:S(2)}) collective-permute-start(bf16[64,2176]{1,0:T(8,128)(2,1)} %get-tuple-element.59), channel_id=1, source_target_pairs={{0,8},{8,16},{16,24},{1,9},{9,17},{17,25},{2,10},{10,18},{18,26},{... | collective-permute-start | bytes 835592 | tf_op jit(solution)/shard_map/ppermute | solution.py:516
  141.7 19.2 %collective-permute-start.14 = (bf16[64,2176]{1,0:T(8,128)(2,1)}, bf16[64,2176]{1,0:T(8,128)(2,1)S(1)}, u32[]{:S(2)}, u32[]{:S(2)}) collective-permute-start(bf16[64,2176]{1,0:T(8,128)(2,1)} %get-tuple-element.60), channel_id=1, source_target_pairs={{8,0},{16,8},{24,16},{9,1},{17,9},{25,17},{10,2},{18,10},{26,18},{... | collective-permute-start | bytes 835592 | tf_op jit(solution)/shard_map/ppermute | solution.py:521
  143.0 18.8 %all-to-all-start.2 = ((bf16[8,8,2048]{2,1,0:T(8,128)(2,1)}), bf16[8,8,2048]{2,1,0:T(8,128)(2,1)S(1)}, u32[]{:S(2)}, u32[]{:S(2)}) async-start(bf16[8,8,2048]{2,1,0:T(8,128)(2,1)} %bitcast.13), calls=%async_computation.2 | async-start | bytes 524288 | tf_op jit(solution)/shard_map/all_to_all | solution.py:585
  152.0 8.9 %copy-start.4 = (bf16[64,2176]{1,0:T(8,128)(2,1)S(1)}, bf16[64,2176]{1,0:T(8,128)(2,1)}, u32[]{:S(2)}) copy-start(bf16[64,2176]{1,0:T(8,128)(2,1)} %get-tuple-element.58) | copy-start | bytes 835588
  161.8 4.2 %copy-start.3 = (bf16[8,8,2048]{2,1,0:T(8,128)(2,1)}, bf16[8,8,2048]{2,1,0:T(8,128)(2,1)S(1)}, u32[]{:S(2)}) copy-start(bf16[8,8,2048]{2,1,0:T(8,128)(2,1)S(1)} %all-to-all-done.2) | copy-start | bytes 786436
  161.8 11.3 %all-to-all-start.3 = ((bf16[8,8,2176]{2,1,0:T(8,128)(2,1)}), bf16[8,8,2176]{2,1,0:T(8,128)(2,1)S(1)}, u32[]{:S(2)}, u32[]{:S(2)}) async-start(bf16[8,8,2176]{2,1,0:T(8,128)(2,1)} %bitcast.15), calls=%async_computation.3 | async-start | bytes 557056 | tf_op jit(solution)/shard_map/all_to_all | solution.py:585
  173.1 0.7 copy-start.1

commit v5 on v4

--- a/solution.py
+++ b/solution.py
@@ -18,7 +18,23 @@
     return lax.dot_general(a, b, (dims, ((), ())), preferred_element_type=F32)
 
 
-PARAMS = pltpu.CompilerParams(vmem_limit_bytes=56 * 2**20)
+PARAMS = pltpu.CompilerParams(vmem_limit_bytes=20 * 2**20)
+
+
+def to_vmem(x):
+    return pltpu.with_memory_space_constraint(x, pltpu.VMEM)
+
+
+def to_hbm(x):
+    return pltpu.with_memory_space_constraint(x, pltpu.HBM)
+
+
+def held(dims, dtype=BF16):
+    return pltpu.VMEM(dims, dtype)
+
+
+def sent(dims, dtype=BF16):
+    return pltpu.HBM(dims, dtype)
 
 
 def cost(flops, moved):
@@ -82,7 +98,7 @@
         body,
         in_specs=[ANYWHERE] * 4,
         out_specs=[IN_VMEM] * 3,
-        out_shape=[shape((count, part))] * 2 + [shape((pack, count, own))],
+        out_shape=[sent((count, part))] * 2 + [held((pack, count, own))],
         scratch_shapes=[
             pltpu.SMEM(picks.shape, jnp.int32),
             pltpu.SMEM(counts.shape, jnp.int32),
@@ -93,7 +109,7 @@
         ],
         compiler_params=PARAMS,
         cost_estimate=cost(4 * count * own * features, 4 * features * own),
-    )(picks, counts, cotangent, tokens)
+    )(*(to_hbm(x) for x in (picks, counts, cotangent, tokens)))
 
 
 def by_place(arrivals, seq_n, groups):
@@ -108,8 +124,8 @@
     return pl.pallas_call(
         body,
         in_specs=[ANYWHERE] * len(blocks),
-        out_specs=ANYWHERE,
-        out_shape=shape((groups, seq_n, rows, part)),
+        out_specs=IN_VMEM,
+        out_shape=sent((groups, seq_n, rows, part)),
         scratch_shapes=[pltpu.SemaphoreType.DMA((seq_n,))],
         compiler_params=PARAMS,
         cost_estimate=cost(0, 4 * groups * seq_n * rows * part),
@@ -129,16 +145,16 @@
 
             @pl.when((pl.program_id(0) == 0) & (pl.program_id(1) == 0))
             def _():
-                experts = router_ref.shape[1]
+                experts = router_ref.shape[0]
                 group = count // experts
                 row = lax.broadcasted_iota(jnp.int32, (count, experts), 0)
                 expert = lax.broadcasted_iota(jnp.int32, (count, experts), 1)
                 mine = row // group == expert
                 even = jnp.where(mine & (row % 2 == 0), 1.0, 0.0).astype(BF16)
                 odd = jnp.where(mine & (row % 2 == 1), 1.0, 0.0).astype(BF16)
-                router = sum(mm(ref[...], even, ROWS) for ref in message_refs)
+                router = sum(mm(even, ref[...], ROWS) for ref in message_refs)
                 total = sum(mm(ref[...], odd, ROWS) for ref in message_refs)
-                router_ref[...] = router[: router_ref.shape[0]]
+                router_ref[...] = router[:, : router_ref.shape[1]]
                 total_ref[...] = jnp.sum(total[:3], axis=0, keepdims=True)
 
     in_specs = [
@@ -147,17 +163,17 @@
     ]
     out_specs = [pl.BlockSpec((own, width), lambda h, i: (0, h * 2 + i))]
     out_shape = [shape((own, part * pack))]
-    args = [hot, back]
+    args = [to_vmem(hot), back]
     if message is not None:
         _, per, experts = message
         for t in range((back.shape[1] - part) // LANES):
             in_specs.append(pl.BlockSpec((count, LANES), lambda h, i, t=t: (0, part // LANES + t)))
             args.append(back)
         out_specs += [
-            pl.BlockSpec((per, experts), lambda h, i: (0, 0)),
+            pl.BlockSpec((experts, per), lambda h, i: (0, 0)),
             pl.BlockSpec((1, experts), lambda h, i: (0, 0)),
         ]
-        out_shape += [shape((per, experts), F32), shape((1, experts), F32)]
+        out_shape += [shape((experts, per), F32), shape((1, experts), F32)]
     return pl.pallas_call(
         body,
         grid=(pack, 2),
@@ -215,29 +231,43 @@
             pltpu.make_async_copy(refs[a], places[k], sems.at[k]).wait()
 
 
-def side_copies(gate_ref, up_ref, router_ref, side, sems, pack, j, width):
-    part = side.shape[0]
-    hidden_n = gate_ref.shape[2]
-    rows = pl.ds(j * width, width)
-    copies = []
-    for h in range(pack):
-        for n, ref in enumerate((gate_ref, up_ref)):
-            columns = pl.ds((2 * h + n) * hidden_n, hidden_n)
-            copies.append((ref.at[0, pl.ds(h * part + j * width, width), :], side.at[rows, columns]))
-    columns = pl.ds(2 * pack * hidden_n, LANES)
-    copies.append((router_ref.at[rows, :], side.at[rows, columns]))
-    return [pltpu.make_async_copy(a, b, sems.at[j, n]) for n, (a, b) in enumerate(copies)]
-
-
-def down_copies(down_ref, stack, sems, pack):
-    hidden_n = down_ref.shape[1]
-    part = stack.shape[1]
-    return [
-        pltpu.make_async_copy(
-            down_ref.at[0, :, pl.ds(h * part, part)], stack.at[pl.ds(h * hidden_n, hidden_n), :], sems.at[h]
-        )
-        for h in range(pack)
-    ]
+def hold_weights(router, w_gate, w_up, w_down, pack):
+    features, experts = router.shape
+    part = features // pack
+    hidden_n = w_gate.shape[2]
+    total = 2 * pack * hidden_n + LANES
+
+    def body(router_ref, gate_ref, up_ref, down_ref, side, stack, router_v, sems):
+        copies = [pltpu.make_async_copy(router_ref, router_v, sems.at[0])]
+        for h in range(pack):
+            now = pl.ds(h * part, part)
+            for n, ref in enumerate((gate_ref, up_ref)):
+                columns = pl.ds((2 * h + n) * hidden_n, hidden_n)
+                copies.append(pltpu.make_async_copy(ref.at[0, now, :], side.at[:, columns], sems.at[len(copies)]))
+            rows = pl.ds(h * hidden_n, hidden_n)
+            copies.append(pltpu.make_async_copy(down_ref.at[0, :, now], stack.at[rows, :], sems.at[len(copies)]))
+        for copy in copies:
+            copy.start()
+        copies[0].wait()
+        row = lax.broadcasted_iota(jnp.int32, (experts, LANES), 0)
+        lane = lax.broadcasted_iota(jnp.int32, (experts, LANES), 1)
+        columns = jnp.zeros((part, LANES), F32)
+        for h in range(pack):
+            place = (lane == h * experts + row) | (lane == (pack + h) * experts + row)
+            columns = columns + mm(router_v[h * part : (h + 1) * part, :], jnp.where(place, 1.0, 0.0).astype(BF16))
+        side[:, 2 * pack * hidden_n :] = columns.astype(BF16)
+        for copy in copies[1:]:
+            copy.wait()
+
+    return pl.pallas_call(
+        body,
+        in_specs=[ANYWHERE] * 4,
+        out_specs=[IN_VMEM] * 2,
+        out_shape=[held((part, total)), held((pack * hidden_n, part))],
+        scratch_shapes=[pltpu.VMEM(router.shape, BF16), pltpu.SemaphoreType.DMA((3 * pack + 1,))],
+        compiler_params=PARAMS,
+        cost_estimate=cost(0, 12 * features * hidden_n),
+    )(*(to_hbm(x) for x in (router, w_gate, w_up, w_down)))
 
 
 def send_blocks(out, out_refs, seq_n, columns):
@@ -260,87 +290,67 @@
     return seq_n + 1 if seq_n == 4 else seq_n
 
 
-def expert_forward(arrivals, seq_n, slots, experts, pack, router_side, threshold, w_gate, w_up, w_down, hid_scale):
+def expert_forward(arrivals, seq_n, slots, experts, pack, side, stack, threshold, hid_scale):
     block_rows, part = arrivals.blocks[0].shape
     rows = block_rows * seq_n
-    hidden_n = w_gate.shape[2]
+    hidden_n = hid_scale.shape[1]
     width = part // STEPS
-    total = 2 * pack * hidden_n + LANES
     group = pack * slots
     n_blocks = len(arrivals.blocks)
     n_sends = sends(seq_n)
 
     def body(*refs):
         blocks = refs[:n_blocks]
-        router_ref, gate_ref, up_ref, down_ref, threshold_ref, scale_ref = refs[n_blocks : n_blocks + 6]
-        x_ref, pre_ref, hidden_ref = refs[n_blocks + 6 : n_blocks + 9]
-        out_refs = refs[n_blocks + 9 : n_blocks + 9 + n_sends]
-        held, side, stack, x_sems, side_sems, stack_sems = refs[n_blocks + 9 + n_sends :]
+        side_ref, stack_ref, threshold_ref, scale_ref, x_ref, pre_ref, hidden_ref = refs[n_blocks : n_blocks + 7]
+        out_refs = refs[n_blocks + 7 : n_blocks + 7 + n_sends]
+        here, sems = refs[n_blocks + 7 + n_sends :]
         places = [x_ref.at[pl.ds(k * block_rows, block_rows), :] for k in range(seq_n)]
-        arrivals.start(blocks, places, x_sems)
-        chunks = [side_copies(gate_ref, up_ref, router_ref, side, side_sems, pack, j, width) for j in range(STEPS)]
-        downs = down_copies(down_ref, stack, stack_sems, pack)
-        for chunk in chunks:
-            for copy in chunk:
-                copy.start()
-        for copy in downs:
-            copy.start()
-        arrivals.wait(blocks, places, x_sems)
-        for j, chunk in enumerate(chunks):
-            for copy in chunk:
-                copy.wait()
-            y = mm(x_ref[:, j * width : (j + 1) * width], side[j * width : (j + 1) * width, :])
-            if j == 0:
-                acc = y
-            else:
-                acc = acc + y
-        columns = [acc[:, n * hidden_n : (n + 1) * hidden_n] for n in range(2 * pack)]
+        arrivals.start(blocks, places, sems)
+        arrivals.wait(blocks, places, sems)
+        both = 2 * hidden_n
+        columns = []
+        for h in range(pack):
+            y = mm(x_ref[...], side_ref[:, h * both : (h + 1) * both])
+            columns += [y[:, :hidden_n], y[:, hidden_n:]]
+        scores = mm(x_ref[...], side_ref[:, pack * both :])
         gate = fold(columns[0::2], slots)
         up = fold(columns[1::2], slots)
-        scores = acc[:, 2 * pack * hidden_n :]
         lane = lax.broadcasted_iota(jnp.int32, scores.shape, 1)
         expert = lax.axis_index("exp")
         score = fold([jnp.where(lane == h * experts + expert, scores, 0.0) for h in range(pack)], slots)
         lane = lax.broadcasted_iota(jnp.int32, threshold_ref.shape, 1)
-        score = score - jnp.where(lane == expert, threshold_ref[...], 0.0)
-        g = jax.nn.sigmoid(jnp.sum(score, axis=1, keepdims=True))
+        cut = jnp.sum(jnp.where(lane == expert, threshold_ref[...], 0.0), axis=1, keepdims=True)
+        g = jax.nn.sigmoid(jnp.sum(score, axis=1, keepdims=True) - cut)
         pre_ref[:, :hidden_n] = gate
-        pre_ref[:, hidden_n : 2 * hidden_n] = up
-        pre_ref[:, 2 * hidden_n :] = jnp.broadcast_to(g, (rows, LANES))
+        pre_ref[:, hidden_n:both] = up
+        pre_ref[:, both:] = jnp.broadcast_to(g, (rows, LANES))
         hidden = gate * jax.nn.sigmoid(gate) * up * scale_ref[...] * g
         hidden = jnp.where(first_part(rows, pack, slots), hidden, 0.0)
         for h, value in enumerate(spread(hidden, pack, slots)):
             now = slice(h * hidden_n, (h + 1) * hidden_n)
-            held[:, now] = value.astype(BF16)
-            hidden_ref[:, now] = regroup(value, group, seq_n, rows // seq_n // group).astype(BF16)
-        for copy in downs:
-            copy.wait()
+            here[:, now] = value.astype(BF16)
+            hidden_ref[:, now] = regroup(value, group, seq_n, block_rows // group).astype(BF16)
         for j in range(STEPS):
             now = slice(j * width, (j + 1) * width)
-            send_blocks(mm(held[...], stack[:, now]).astype(BF16), out_refs, seq_n, now)
-
-    padded = jnp.zeros((1, LANES), F32).at[:, :experts].set(threshold[None, :])
+            send_blocks(mm(here[...], stack_ref[:, now]).astype(BF16), out_refs, seq_n, now)
+
     return pl.pallas_call(
         body,
-        in_specs=[ANYWHERE] * n_blocks + [ANYWHERE] * 4 + [IN_VMEM] * 2,
+        in_specs=[ANYWHERE] * n_blocks + [IN_VMEM] * 4,
         out_specs=[IN_VMEM] * (3 + n_sends),
         out_shape=[
-            shape((rows, part)),
-            shape((rows, 2 * hidden_n + LANES), F32),
-            shape((rows, pack * hidden_n)),
+            held((rows, part)),
+            held((rows, 2 * hidden_n + LANES), F32),
+            held((rows, pack * hidden_n)),
         ]
-        + [shape((block_rows, part))] * n_sends,
+        + [sent((block_rows, part))] * n_sends,
         scratch_shapes=[
             pltpu.VMEM((rows, pack * hidden_n), BF16),
-            pltpu.VMEM((part, total), BF16),
-            pltpu.VMEM((pack * hidden_n, part), BF16),
             pltpu.SemaphoreType.DMA((seq_n,)),
-            pltpu.SemaphoreType.DMA((STEPS, 2 * pack + 1)),
-            pltpu.SemaphoreType.DMA((pack,)),
         ],
         compiler_params=PARAMS,
         cost_estimate=cost(6 * rows * part * pack * hidden_n, 6 * part * pack * hidden_n),
-    )(*arrivals.blocks, router_side, w_gate, w_up, w_down, padded, hid_scale)
+    )(*arrivals.blocks, to_vmem(side), to_vmem(stack), threshold.reshape(1, -1), hid_scale)
 
 
 def split3(v):
@@ -354,10 +364,10 @@
     return LANES * -(-2 * seq_n // group)
 
 
-def expert_backward(c, seq_n, exp_n, slots, pack, x, pre, router_side, w_gate, w_up, w_down, hid_scale):
+def expert_backward(c, seq_n, exp_n, slots, pack, x, pre, side, stack, hid_scale):
     rows, part = x.shape
     block_rows = rows // seq_n
-    hidden_n = w_gate.shape[2]
+    hidden_n = hid_scale.shape[1]
     width = part // STEPS
     total = 2 * pack * hidden_n + LANES
     group = pack * slots
@@ -366,25 +376,14 @@
     n_sends = sends(seq_n)
 
     def body(*refs):
-        c_ref, router_ref, gate_ref, up_ref, down_ref, x_ref, scale_ref, pre_ref, delta_ref = refs[:9]
-        out_refs = refs[9 : 9 + n_sends]
-        c_v, x_v, side, stack, columns, message, c_sem, x_sem, side_sems, stack_sems = refs[9 + n_sends :]
+        c_ref, side_ref, stack_ref, x_ref, scale_ref, pre_ref, delta_ref = refs[:7]
+        out_refs = refs[7 : 7 + n_sends]
+        c_v, columns, message, c_sem = refs[7 + n_sends :]
         c_copy = pltpu.make_async_copy(c_ref, c_v, c_sem)
-        x_copy = pltpu.make_async_copy(x_ref, x_v, x_sem)
-        chunks = [side_copies(gate_ref, up_ref, router_ref, side, side_sems, pack, j, width) for j in range(STEPS)]
-        downs = down_copies(down_ref, stack, stack_sems, pack)
         c_copy.start()
-        for copy in downs:
-            copy.start()
-        for chunk in chunks:
-            for copy in chunk:
-                copy.start()
-        x_copy.start()
         c_copy.wait()
-        parts = []
-        for h, copy in enumerate(downs):
-            copy.wait()
-            parts.append(mm(c_v[...], stack[h * hidden_n : (h + 1) * hidden_n, :], LAST))
+        both = mm(c_v[...], stack_ref[...], LAST)
+        parts = [both[:, h * hidden_n : (h + 1) * hidden_n] for h in range(pack)]
         raw = regroup(fold(parts, slots), group, block_rows // group, seq_n)
         raw = jnp.where(first_part(rows, pack, slots), raw * scale_ref[...], 0.0)
         gate = pre_ref[:, :hidden_n]
@@ -410,15 +409,12 @@
                     by_expert = jnp.where(lane == (n * pack + h) * exp_n + expert, piece, by_expert)
         columns[...] = by_split.astype(BF16)
         delta_ref[:, 2 * pack * hidden_n :] = by_expert.astype(BF16)
-        for j, chunk in enumerate(chunks):
+        for j in range(STEPS):
             now = slice(j * width, (j + 1) * width)
-            for copy in chunk:
-                copy.wait()
-            send_blocks(mm(delta_ref[...], side[now, :], LAST).astype(BF16), out_refs, seq_n, now)
+            send_blocks(mm(delta_ref[...], side_ref[now, :], LAST).astype(BF16), out_refs, seq_n, now)
 
         here = lax.axis_index("seq")
-        x_copy.wait()
-        told = mm(columns[...], x_v[...], ROWS)
+        told = mm(columns[...], x_ref[...], ROWS)
         sub = lax.broadcasted_iota(jnp.int32, (group, LANES), 0)
         lane = lax.broadcasted_iota(jnp.int32, (group, LANES), 1)
         minus = jnp.broadcast_to(-jnp.sum(score, axis=0, keepdims=True), (group, LANES))
@@ -446,24 +442,18 @@
 
     return pl.pallas_call(
         body,
-        in_specs=[ANYWHERE] * 6 + [IN_VMEM] * 2,
+        in_specs=[ANYWHERE] + [IN_VMEM] * 5,
         out_specs=[IN_VMEM] * (1 + n_sends),
-        out_shape=[shape((rows, total))] + [shape((block_rows, part + extra))] * n_sends,
+        out_shape=[held((rows, total))] + [sent((block_rows, part + extra))] * n_sends,
         scratch_shapes=[
             pltpu.VMEM((rows, part), BF16),
-            pltpu.VMEM((rows, part), BF16),
-            pltpu.VMEM((part, total), BF16),
-            pltpu.VMEM((pack * hidden_n, part), BF16),
             pltpu.VMEM((rows, LANES), BF16),
             pltpu.VMEM((seq_n, block_rows, extra), F32),
             pltpu.SemaphoreType.DMA,
-            pltpu.SemaphoreType.DMA,
-            pltpu.SemaphoreType.DMA((STEPS, 2 * pack + 1)),
-            pltpu.SemaphoreType.DMA((pack,)),
         ],
         compiler_params=PARAMS,
         cost_estimate=cost(6 * rows * part * pack * hidden_n, 6 * part * pack * hidden_n),
-    )(c, router_side, w_gate, w_up, w_down, x, hid_scale, pre)
+    )(c, to_vmem(side), to_vmem(stack), to_vmem(x), hid_scale, to_vmem(pre))
 
 
 def side_grads(x, delta, pack, hidden_n):
@@ -471,23 +461,25 @@
     width = part // STEPS
 
     def body(x_ref, delta_ref, gate_out, up_out):
-        both = mm(x_ref[...], delta_ref[...], ROWS)
-        gate_out[...] = both[:, :hidden_n]
-        up_out[...] = both[:, hidden_n:]
-
-    tall = pl.BlockSpec((None, width, hidden_n), lambda h, i: (0, h * STEPS + i, 0))
-    return pl.pallas_call(
-        body,
-        grid=(pack, STEPS),
+        for h in range(pack):
+            both = mm(x_ref[...], delta_ref[:, 2 * h * hidden_n : 2 * (h + 1) * hidden_n], ROWS)
+            gate_out[h] = both[:, :hidden_n]
+            up_out[h] = both[:, hidden_n:]
+
+    tall = pl.BlockSpec((pack, width, hidden_n), lambda i: (0, i, 0))
+    gate, up = pl.pallas_call(
+        body,
+        grid=(STEPS,),
         in_specs=[
-            pl.BlockSpec((rows, width), lambda h, i: (0, i)),
-            pl.BlockSpec((rows, 2 * hidden_n), lambda h, i: (0, h)),
+            pl.BlockSpec((rows, width), lambda i: (0, i)),
+            pl.BlockSpec(delta.shape, lambda i: (0, 0)),
         ],
         out_specs=[tall, tall],
-        out_shape=[shape((1, part * pack, hidden_n), F32)] * 2,
+        out_shape=[shape((pack, part, hidden_n), F32)] * 2,
         compiler_params=PARAMS,
         cost_estimate=cost(4 * rows * part * pack * hidden_n, 8 * part * pack * hidden_n),
-    )(x, delta)
+    )(to_vmem(x), to_vmem(delta))
+    return gate.reshape(1, part * pack, hidden_n), up.reshape(1, part * pack, hidden_n)
 
 
 def down_grads(c, hidden, pack, hidden_n):
@@ -508,7 +500,7 @@
         out_shape=shape((1, hidden_n, part * pack), F32),
         compiler_params=PARAMS,
         cost_estimate=cost(2 * rows * part * pack * hidden_n, 4 * part * pack * hidden_n),
-    )(c, hidden)
+    )(c, to_vmem(hidden))
 
 
 def up_line(block, n, first=0, last=None):
@@ -589,16 +581,13 @@
     x_in = line_gather(to_experts(x_rows), seq_n)
     c = lax.all_to_all(by_place(c_in, seq_n, experts), "exp", split_axis=0, concat_axis=0, tiled=True)
     c = c.reshape(-1, c.shape[-1])
-    halves = list(router.reshape(pack, features // pack, experts))
-    router_side = jnp.concatenate(halves + halves, axis=1)
-    router_side = jnp.pad(router_side, ((0, 0), (0, LANES - router_side.shape[1])))
-
-    x, pre, hidden, *out = expert_forward(
-        x_in, seq_n, slots, experts, pack, router_side, threshold, w_gate, w_up, w_down, hid_scale
-    )
+    w_down, w_gate, w_up, _ = lax.optimization_barrier((w_down, w_gate, w_up, c_in.blocks[1]))
+    side, stack = hold_weights(router, w_gate, w_up, w_down, pack)
+
+    x, pre, hidden, *out = expert_forward(x_in, seq_n, slots, experts, pack, side, stack, threshold, hid_scale)
     out_begun = line_begin(out, seq_n)
     delta, *back = expert_backward(
-        after(c, out_begun), seq_n, exp_n, slots, pack, x, pre, router_side, w_gate, w_up, w_down, hid_scale
+        after(c, out_begun), seq_n, exp_n, slots, pack, x, pre, side, stack, hid_scale
     )
     back_begun = line_begin(back, seq_n)
     out = line_sum(out, seq_n, out_begun, (), (delta,))
@@ -614,7 +603,7 @@
     if extra:
         gate_grad, up_grad = gate_grad[:, :, :true_hidden], up_grad[:, :, :true_hidden]
         down_grad = down_grad[:, :true_hidden]
-    return mixture, token_grad, router_grad, threshold_grad[0], gate_grad, up_grad, down_grad
+    return mixture, token_grad, router_grad.T, threshold_grad[0], gate_grad, up_grad, down_grad
 
 
 def solution(mesh):

time: 181 us -> 156 us (0.86)
  Pallas kernels: 81.9 us -> 39.5 us
  local copies, waits for them, and re-layouts: 6.31 us -> 21.2 us
  starting transfers between devices: 59.8 us -> 66.3 us
  waiting for transfers between devices: 25.5 us -> 21 us
    pallas_call x4 -> x5, Pallas kernels: 64.6 us -> 25 us  [the longest x1 7.39 us: expert_backward(): pl.pallas_call(body, in_specs=[ANYWHERE] + [IN_VMEM] * 5, out_specs=[IN_V...]
    unnamed x37 -> x57, local copies, waits for them, and re-layouts: 4.61 us -> 21.2 us
    ppermute x8, waiting for transfers between devices: 10.6 us -> 5.97 us  [down_line(): return lax.ppermute(block, 'seq', [(s, s - 1) for s in range(first, last)])]
    ppermute x2, starting transfers between devices: 8.45 us -> 12.6 us  [line_begin(): return lax.ppermute(parts[4], 'seq', [(3, 2), (0, 1)])]
    ppermute x8, starting transfers between devices: 15.6 us -> 18.9 us  [up_line(): return lax.ppermute(block, 'seq', [(s, s + 1) for s in range(first, last)])]
    pallas_call x2, Pallas kernels: 8.34 us -> 5.54 us  [scatter_rows(): pl.pallas_call(body, grid=(pack, 2), in_specs=in_specs, out_specs=out_spe...]
    convert_element_type x4, other arithmetic: 3.72 us -> 5.56 us  [add(): return sum((part.astype(F32) for part in parts)).astype(BF16)]
  transfers between devices with their start and end apart: 24 -> 24, of which waited for: 8 -> 6; matrix products, arithmetic and copies ran while one was open for 3% -> 4% of each run, Pallas kernels for 41% -> 21%
where the time goes in v5:
time: 156 us; the launch traced here: 155 us
  starting transfers between devices  66.3 us (42%)
  Pallas kernels  39.5 us (25%)
  local copies, waits for them, and re-layouts  21.2 us (14%)
  waiting for transfers between devices  21 us (13%)
  other arithmetic  5.56 us (4%)
    unnamed x57, local copies, waits for them, and re-layouts  21.2 us
    ppermute x8, starting transfers between devices, up_line(): return lax.ppermute(block, 'seq', [(s, s + 1) for s in range(first, last)])  18.9 us
    all_to_all x3, starting transfers between devices, to_experts(): lax.all_to_all(block, 'exp', split_axis=0, concat_axis=0, tiled=True)  13 us
    ppermute x2, starting transfers between devices, line_begin(): return lax.ppermute(parts[4], 'seq', [(3, 2), (0, 1)])  12.6 us
    ppermute x8, starting transfers between devices, down_line(): return lax.ppermute(block, 'seq', [(s, s - 1) for s in range(first, last)])  10.3 us
    ppermute x2, waiting for transfers between devices, line_begin(): return lax.ppermute(parts[4], 'seq', [(3, 2), (0, 1)])  9.45 us
    pallas_call x1, Pallas kernels, expert_backward(): pl.pallas_call(body, in_specs=[ANYWHERE] + [IN_VMEM] * 5, out_specs=[IN_V...  7.39 us
    ppermute x2, starting transfers between devices, line_sum(): far = lax.ppermute(middle, 'seq', [(s, (s + 2) % 4) for s in range(4)])  7.29 us
  transfers between devices with their start and end apart: 24, of which 6 were waited for; matrix products, arithmetic and copies ran while one was open for 4% of the time, Pallas kernels for 21%

profile of v5, /device:TPU:0, one launch (start us, length us, event | category | flops | bytes accessed | tf_op | source)
XLA Modules:
  0.0 154.6 jit_solution(11933593595170099239)
XLA Ops:
  0.6 3.5 %shard_map.153 = (bf16[64,2048]{1,0:T(8,128)(2,1)}, bf16[64,2048]{1,0:T(8,128)(2,1)}, bf16[2,64,256]{2,1,0:T(8,128)(2,1)S(1)}) custom-call(s32[4,8]{1,0:T(4,128)} %bitcast.33, s32[1,8]{1,0:T(1,128)} %counts_ref.1, bf16[256,4096]{1,0:T(8,128)(2,1)} %c_ref.1, bf16[256,4096]{1,0:T(8,128)(2,1)} %x_ref.1), custom_call_target="tpu_custom_call" | custom-call | flops 268435456 | bytes 4194304 | tf_op jit(solution)/shard_map/pallas_call | solution.py:97
  4.7 5.2 %all-to-all-start.1 = ((bf16[8,8,2048]{2,1,0:T(8,128)(2,1)}), bf16[8,8,2048]{2,1,0:T(8,128)(2,1)S(1)}, u32[]{:S(2)}, u32[]{:S(2)}) async-start(bf16[8,8,2048]{2,1,0:T(8,128)(2,1)} %bitcast.32), calls=%async_computation.1 | async-start | bytes 524288 | tf_op jit(solution)/shard_map/all_to_all | solution.py:577
  9.9 1.3 collective-permute-start.3
  11.2 4.6 %collective-permute-start = (bf16[64,2048]{1,0:T(8,128)(2,1)}, bf16[64,2048]{1,0:T(8,128)(2,1)S(1)}, u32[]{:S(2)}, u32[]{:S(2)}) collective-permute-start(bf16[64,2048]{1,0:T(8,128)(2,1)} %get-tuple-element.45), channel_id=1, source_target_pairs={{0,8},{8,16},{16,24},{1,9},{9,17},{17,25},{2,10},{10,18},{18,26},{... | collective-permute-start | bytes 786440 | tf_op jit(solution)/shard_map/ppermute | solution.py:508
  15.8 1.1 all-to-all-done.1
  16.8 1.3 collective-permute-start.9
  18.1 4.6 %collective-permute-start.6 = (bf16[64,2048]{1,0:T(8,128)(2,1)S(1)}, bf16[64,2048]{1,0:T(8,128)(2,1)S(1)}, u32[]{:S(2)}, u32[]{:S(2)}) collective-permute-start(bf16[64,2048]{1,0:T(8,128)(2,1)S(1)} %bitcast.25), channel_id=1, source_target_pairs={{0,8},{8,16},{16,24},{1,9},{9,17},{17,25},{2,10},{10,18},{18,26},{... | collective-permute-start | bytes 786440 | tf_op jit(solution)/shard_map/ppermute | solution.py:508
  22.7 1.3 collective-permute-start.4
  24.7 1.4 collective-permute-start.1
  26.8 1.3 collective-permute-start.10
  28.8 1.4 collective-permute-start.7
  30.9 1.2 collective-permute-done.4
  32.1 1.3 collective-permute-start.5
  33.4 1.4 collective-permute-start.2
  34.7 4.8 %collective-permute-done.10.refs_5_ = bf16[64,2048]{1,0:T(8,128)(2,1)} collective-permute-done((bf16[64,2048]{1,0:T(8,128)(2,1)S(1)}, bf16[64,2048]{1,0:T(8,128)(2,1)}, u32[]{:S(2)}, u32[]{:S(2)}) %collective-permute-start.10) | collective-permute-done | bytes 262176 | tf_op jit(solution)/shard_map/ppermute | solution.py:513
  39.5 1.3 collective-permute-start.11
  40.8 1.4 collective-permute-start.8
  42.2 1.3 copy.17.router_ref
  43.5 4.2 %shard_map.155 = (bf16[2048,1664]{1,0:T(8,128)(2,1)S(1)}, bf16[768,2048]{1,0:T(8,128)(2,1)S(1)}) custom-call(bf16[4096,8]{1,0:T(8,128)(2,1)} %copy.17.router_ref, bf16[1,4096,384]{2,1,0:T(8,128)(2,1)} %gate_ref, bf16[1,4096,384]{2,1,0:T(8,128)(2,1)} %up_ref, bf16[1,384,4096]{2,1,0:T(8,128)(2,1)} %down_ref), custom_call_target="tpu_custom_call" | custom-call | bytes 18874368 | tf_op jit(solution)/shard_map/pallas_call | solution.py:262
  47.7 2.8 %copy-done = bf16[2048,1664]{1,0:T(8,128)(2,1)} copy-done((bf16[2048,1664]{1,0:T(8,128)(2,1)}, bf16[2048,1664]{1,0:T(8,128)(2,1)S(1)}, u32[]{:S(2)}) %copy-start) | copy-done | bytes 6815768
  50.5 2.1 %shard_map.154 = bf16[8,4,8,2048]{3,2,1,0:T(8,128)(2,1)} custom-call(bf16[8,8,2048]{2,1,0:T(8,128)(2,1)S(1)} %bitcast.28, bf16[8,8,2048]{2,1,0:T(8,128)(2,1)S(1)} %bitcast.30, bf16[8,8,2048]{2,1,0:T(8,128)(2,1)} %bitcast.4.refs_2_, bf16[8,8,2048]{2,1,0:T(8,128)(2,1)} %bitcast.5.refs_3_, bf16[8,8,2048]{2,1,0:T(8,128)(2,1)S(1)} %bitcast.29, ...), custom_call_target="tpu_custom_call" | custom-call | bytes 2097152 | tf_op jit(solution)/shard_map/pallas_call | solution.py:124
  52.5 4.3 %all-to-all-start = ((bf16[8,4,8,2048]{3,2,1,0:T(8,128)(2,1)}), bf16[8,4,8,2048]{3,2,1,0:T(8,128)(2,1)}, u32[]{:S(2)}, u32[]{:S(2)}) async-start(bf16[8,4,8,2048]{3,2,1,0:T(8,128)(2,1)} %shard_map.154), calls=%async_computation | async-start | bytes 2097152 | tf_op jit(solution)/shard_map/all_to_all | solution.py:582
  56.9 2.9 %copy-done.1 = bf16[2048,1664]{1,0:T(8,128)(2,1)S(1)} copy-done((bf16[2048,1664]{1,0:T(8,128)(2,1)S(1)}, bf16[2048,1664]{1,0:T(8,128)(2,1)}, u32[]{:S(2)}) %copy-start.1) | copy-done | bytes 6815768
  61.7 5.8 %shard_map.156 = (bf16[256,2048]{1,0:T(8,128)(2,1)S(1)}, f32[256,896]{1,0:T(8,128)S(1)}, bf16[256,768]{1,0:T(8,128)(2,1)S(1)}, bf16[64,2048]{1,0:T(8,128)(2,1)},...) custom-call(bf16[64,2048]{1,0:T(8,128)(2,1)S(1)} %bitcast.26, ...), custom_call_target="tpu_custom_call" | custom-call | flops 2415919104 | bytes 9437184 | tf_op jit(solution)/shard_map/pallas_call | solution.py:337
  70.1 8.0 %collective-permute-start.12 = (bf16[64,2048]{1,0:T(8,128)(2,1)}, bf16[64,2048]{1,0:T(8,128)(2,1)S(1)}, u32[]{:S(2)}, u32[]{:S(2)}) collective-permute-start(bf16[64,2048]{1,0:T(8,128)(2,1)} %get-tuple-element.52), channel_id=1, source_target_pairs={{24,16},{0,8},{25,17},{1,9},{26,18},{2,10},{27,19},{3,11},{28,20},... | collective-permute-start | bytes 786440 | tf_op jit(solution)/shard_map/ppermute | solution.py:538
  78.2 6.4 %collective-permute-done.12 = bf16[64,2048]{1,0:T(8,128)(2,1)S(1)} collective-permute-done((bf16[64,2048]{1,0:T(8,128)(2,1)}, bf16[64,2048]{1,0:T(8,128)(2,1)S(1)}, u32[]{:S(2)}, u32[]{:S(2)}) %collective-permute-start.12) | collective-permute-done | bytes 262176 | tf_op jit(solution)/shard_map/ppermute | solution.py:538
  84.5 1.7 %add_convert_fusion.3 = bf16[64,2048]{1,0:T(8,128)(2,1)} fusion(bf16[64,2048]{1,0:T(8,128)(2,1)S(1)} %collective-permute-done.12, bf16[64,2048]{1,0:T(8,128)(2,1)} %get-tuple-element.64), kind=kLoop, calls=%fused_computation.3 | loop fusion | flops 524288 | bytes 786432 | tf_op jit(solution)/shard_map/convert_element_type | solution.py:529
  86.2 4.9 %collective-permute-start.18 = (bf16[64,2048]{1,0:T(8,128)(2,1)}, bf16[64,2048]{1,0:T(8,128)(2,1)}, u32[]{:S(2)}, u32[]{:S(2)}) collective-permute-start(bf16[64,2048]{1,0:T(8,128)(2,1)} %add_convert_fusion.3), channel_id=1, source_target_pairs={{0,16},{8,24},{16,0},{24,8},{1,17},{9,25},{17,1},{25,9},{2,18},{10... | collective-permute-start | bytes 786440 | tf_op jit(solution)/shard_map/ppermute | solution.py:548
  91.2 2.3 %collective-permute-start.16 = (bf16[64,2048]{1,0:T(8,128)(2,1)}, bf16[64,2048]{1,0:T(8,128)(2,1)}, u32[]{:S(2)}, u32[]{:S(2)}) collective-permute-start(bf16[64,2048]{1,0:T(8,128)(2,1)} %get-tuple-element.62), channel_id=1, source_target_pairs={{0,8},{8,16},{16,24},{1,9},{9,17},{17,25},{2,10},{10,18},{18,26},{... | collective-permute-start | bytes 786440 | tf_op jit(solution)/shard_map/ppermute | solution.py:508
  93.4 1.3 collective-permute-start.17
  94.7 2.9 %copy-done.2 = bf16[2048,1664]{1,0:T(8,128)(2,1)S(1)} copy-done((bf16[2048,1664]{1,0:T(8,128)(2,1)S(1)}, bf16[2048,1664]{1,0:T(8,128)(2,1)}, u32[]{:S(2)}) %copy-start.2) | copy-done | bytes 6815768
  97.7 1.2 copy-done.4
  98.9 1.2 copy-done.7
  100.1 7.4 %shard_map.157 = (bf16[256,1664]{1,0:T(8,128)(2,1)S(1)}, bf16[64,2176]{1,0:T(8,128)(2,1)}, bf16[64,2176]{1,0:T(8,128)(2,1)}, bf16[64,2176]{1,0:T(8,128)(2,1)}, b...) custom-call(bf16[256,2048]{1,0:T(8,128)(2,1)} %bitcast.9.refs_0_.c_ref, bf16[2048,1664]{1,0:T(8,128)(2,1)S(1)} %copy-done.2, ...), custom_call_target="tpu_custom_call" | custom-call | flops 2415919104 | bytes 9437184 | tf_op jit(solution)/shard_map/pallas_call | solution.py:443
  108.4 4.6 %collective-permute-start.15 = (bf16[64,2176]{1,0:T(8,128)(2,1)}, bf16[64,2176]{1,0:T(8,128)(2,1)S(1)}, u32[]{:S(2)}, u32[]{:S(2)}) collective-permute-start(bf16[64,2176]{1,0:T(8,128)(2,1)} %get-tuple-element.60), channel_id=1, source_target_pairs={{24,16},{0,8},{25,17},{1,9},{26,18},{2,10},{27,19},{3,11},{28,20},... | collective-permute-start | bytes 835592 | tf_op jit(solution)/shard_map/ppermute | solution.py:538
  113.0 2.0 %add_convert_fusion.2 = bf16[64,2048]{1,0:T(8,128)(2,1)} fusion(bf16[64,2048]{1,0:T(8,128)(2,1)} %collective-permute-done.18, bf16[64,2048]{1,0:T(8,128)(2,1)} %collective-permute-done.17, bf16[64,2048]{1,0:T(8,128)(2,1)} %collective-permute-done.16, bf16[64,2048]{1,0:T(8,128)(2,1)S(1)} %copy-done.26), kind=kLoop, calls=%fused_computation.2 | loop fusion | flops 1048576 | bytes 1310720 | tf_op jit(solution)/shard_map/convert_element_type | solution.py:529
  114.9 3.1 %collective-permute-done.15 = bf16[64,2176]{1,0:T(8,128)(2,1)S(1)} collective-permute-done((bf16[64,2176]{1,0:T(8,128)(2,1)}, bf16[64,2176]{1,0:T(8,128)(2,1)S(1)}, u32[]{:S(2)}, u32[]{:S(2)}) %collective-permute-start.15) | collective-permute-done | bytes 278560 | tf_op jit(solution)/shard_map/ppermute | solution.py:538
  118.0 1.0 add_convert_fusion.1
  119.1 2.4 %collective-permute-start.19 = (bf16[64,2176]{1,0:T(8,128)(2,1)S(1)}, bf16[64,2176]{1,0:T(8,128)(2,1)S(1)}, u32[]{:S(2)}, u32[]{:S(2)}) collective-permute-start(bf16[64,2176]{1,0:T(8,128)(2,1)S(1)} %add_convert_fusion.1), channel_id=1, source_target_pairs={{0,16},{8,24},{16,0},{24,8},{1,17},{9,25},{17,1},{25,9},{2,18},{10... | collective-permute-start | bytes 835592 | tf_op jit(solution)/shard_map/ppermute | solution.py:548
  121.4 2.0 %collective-permute-start.13 = (bf16[64,2176]{1,0:T(8,128)(2,1)}, bf16[64,2176]{1,0:T(8,128)(2,1)S(1)}, u32[]{:S(2)}, u32[]{:S(2)}) collective-permute-start(bf16[64,2176]{1,0:T(8,128)(2,1)} %get-tuple-element.57), channel_id=1, source_target_pairs={{0,8},{8,16},{16,24},{1,9},{9,17},{17,25},{2,10},{10,18},{18,26},{... | collective-permute-start | bytes 835592 | tf_op jit(solution)/shard_map/ppermute | solution.py:508
  123.4 1.3 collective-permute-start.14
  124.7 3.6 %all-to-all-start.2 = ((bf16[8,8,2048]{2,1,0:T(8,128)(2,1)}), bf16[8,8,2048]{2,1,0:T(8,128)(2,1)S(1)}, u32[]{:S(2)}, u32[]{:S(2)}) async-start(bf16[8,8,2048]{2,1,0:T(8,128)(2,1)} %bitcast.15), calls=%async_computation.2 | async-start | bytes 524288 | tf_op jit(solution)/shard_map/all_to_all | solution.py:577
  128.4 5.5 %shard_map.159 = f32[1,384,4096]{2,1,0:T(8,128)} custom-call(bf16[256,2048]{1,0:T(8,128)(2,1)} %bitcast.9.refs_0_.c_ref, bf16[256,768]{1,0:T(8,128)(2,1)S(1)} %copy-done.9), custom_call_target="tpu_custom_call" | custom-call | flops 805306368 | bytes 6291456 | tf_op jit(solution)/shard_map/pallas_call | solution.py:492
  133.9 5.6 %shard_map.158 = (f32[2,2048,384]{2,1,0:T(8,128)}, f32[2,2048,384]{2,1,0:T(8,128)}) custom-call(bf16[256,2048]{1,0:T(8,128)(2,1)S(1)} %copy-done.5, bf16[256,1664]{1,0:T(8,128)(2,1)S(1)} %copy-done.24), custom_call_target="tpu_custom_call" | custom-call | flops 1610612736 | bytes 12582912 | tf_op jit(solution)/shard_map/pallas_call | solution.py:470
  140.4 4.2 %all-to-all-start.3 = ((bf16[8,8,2176]{2,1,0:T(8,128)(2,1)}), bf16[8,8,2176]{2,1,0:T(8,128)(2,1)S(1)}, u32[]{:S(2)}, u32[]{:S(2)}) async-start(bf16[8,8,2176]{2,1,0:T(8,128)(2,1)} %bitcast.17), calls=%async_computation.3 | async-start | bytes 557056 | tf_op jit(solution)/shard_map/all_to_all | solution.py:577
  144.6 2.6 %shard_map.160 = bf16[256,4096]{1,0:T(8,128)(2,1)} custom-call(bf16[2,64,256]{2,1,0:T(8,128)(2,1)S(1)} %copy-done.15, bf16[64,2048]{1,0:T(8,128)(2,1)S(1)} %bitcast.27), custom_call_target="tpu_custom_call" | custom-call | flops 134217728 | bytes 2097152 | tf_op jit(solution)/shard_map/pallas_call | solution.py:177
  147.2 4.5 %all-to-all-done.3 = bf16[8,8,2176]{2,1,0:T(8,128)(2,1)S(1)} async-done(((bf16[8,8,2176]{2,1,0:T(8,128)(2,1)}), bf16[8,8,2176]{2,1,0:T(8,128)(2,1)S(1)}, u32[]{:S(2)}, u32[]{:S(2)}) %all-to-all-start.3) | async-done | bytes 278560 | tf_op jit(solution)/shard_map/all_to_all | solution.py:577
  151.7 2.9 %shard_map.161 = (bf16[256,4096]{1,0:T(8,128)(2,1)}, f32[8,128]{1,0:T(8,128)}, f32[1,8]{1,0:T(1,128)}) custom-call(bf16[2,64,256]{2,1,0:T(8,128)(2,1)S(1)} %copy-done.15, bf16[64,2176]{1,0:T(8,128)(2,1)S(1)} %bitcast.22, bf16[64,2176]{1,0:T(8,128)(2,1)S(1)} %bitcast.23), custom_call_target="tpu_custom_call" | custom-call | flops 134217728 | bytes 2097152 | tf_op jit(solution)/shard_map/pallas_call | solution.py:177
  (70 shorter events, 9.8 us)
Async XLA Ops:
  0.6 41.5 %copy-start.27 = (bf16[4096,8]{0,1:T(8,128)(2,1)S(1)}, bf16[4096,8]{0,1:T(8,128)(2,1)}, u32[]{:S(2)}) copy-start(bf16[4096,8]{0,1:T(8,128)(2,1)} %param.12) | copy-start | bytes 196612
  4.7 12.1 %all-to-all-start.1 = ((bf16[8,8,2048]{2,1,0:T(8,128)(2,1)}), bf16[8,8,2048]{2,1,0:T(8,128)(2,1)S(1)}, u32[]{:S(2)}, u32[]{:S(2)}) async-start(bf16[8,8,2048]{2,1,0:T(8,128)(2,1)} %bitcast.32), calls=%async_computation.1 | async-start | bytes 524288 | tf_op jit(solution)/shard_map/all_to_all | solution.py:577
  9.9 12.8 %collective-permute-start.3 = (bf16[64,2048]{1,0:T(8,128)(2,1)}, bf16[64,2048]{1,0:T(8,128)(2,1)S(1)}, u32[]{:S(2)}, u32[]{:S(2)}) collective-permute-start(bf16[64,2048]{1,0:T(8,128)(2,1)} %get-tuple-element.45), channel_id=1, source_target_pairs={{8,0},{16,8},{24,16},{9,1},{17,9},{25,17},{10,2},{18,10},{26,18},{... | collective-permute-start | bytes 786440 | tf_op jit(solution)/shard_map/ppermute | solution.py:513
  11.2 13.5 %collective-permute-start = (bf16[64,2048]{1,0:T(8,128)(2,1)}, bf16[64,2048]{1,0:T(8,128)(2,1)S(1)}, u32[]{:S(2)}, u32[]{:S(2)}) collective-permute-start(bf16[64,2048]{1,0:T(8,128)(2,1)} %get-tuple-element.45), channel_id=1, source_target_pairs={{0,8},{8,16},{16,24},{1,9},{9,17},{17,25},{2,10},{10,18},{18,26},{... | collective-permute-start | bytes 786440 | tf_op jit(solution)/shard_map/ppermute | solution.py:508
  16.8 9.9 %collective-permute-start.9 = (bf16[64,2048]{1,0:T(8,128)(2,1)S(1)}, bf16[64,2048]{1,0:T(8,128)(2,1)S(1)}, u32[]{:S(2)}, u32[]{:S(2)}) collective-permute-start(bf16[64,2048]{1,0:T(8,128)(2,1)S(1)} %bitcast.24), channel_id=1, source_target_pairs={{8,0},{16,8},{24,16},{9,1},{17,9},{25,17},{10,2},{18,10},{26,18},{... | collective-permute-start | bytes 786440 | tf_op jit(solution)/shard_map/ppermute | solution.py:513
  18.1 10.7 %collective-permute-start.6 = (bf16[64,2048]{1,0:T(8,128)(2,1)S(1)}, bf16[64,2048]{1,0:T(8,128)(2,1)S(1)}, u32[]{:S(2)}, u32[]{:S(2)}) collective-permute-start(bf16[64,2048]{1,0:T(8,128)(2,1)S(1)} %bitcast.25), channel_id=1, source_target_pairs={{0,8},{8,16},{16,24},{1,9},{9,17},{17,25},{2,10},{10,18},{18,26},{... | collective-permute-start | bytes 786440 | tf_op jit(solution)/shard_map/ppermute | solution.py:508
  22.7 9.3 %collective-permute-start.4 = (bf16[64,2048]{1,0:T(8,128)(2,1)S(1)}, bf16[64,2048]{1,0:T(8,128)(2,1)}, u32[]{:S(2)}, u32[]{:S(2)}) collective-permute-start(bf16[64,2048]{1,0:T(8,128)(2,1)S(1)} %collective-permute-done.3), channel_id=1, source_target_pairs={{8,0},{16,8},{9,1},{17,9},{10,2},{18,10},{11,3},{19,11},{12,4},{20... | collective-permute-start | bytes 786440 | tf_op jit(solution)/shard_map/ppermute | solution.py:513
  24.7 8.6 %collective-permute-start.1 = (bf16[64,2048]{1,0:T(8,128)(2,1)S(1)}, bf16[64,2048]{1,0:T(8,128)(2,1)}, u32[]{:S(2)}, u32[]{:S(2)}) collective-permute-start(bf16[64,2048]{1,0:T(8,128)(2,1)S(1)} %collective-permute-done), channel_id=1, source_target_pairs={{8,16},{16,24},{9,17},{17,25},{10,18},{18,26},{11,19},{19,27},{12,... | collective-permute-start | bytes 786440 | tf_op jit(solution)/shard_map/ppermute | solution.py:508
  26.8 12.7 %collective-permute-start.10 = (bf16[64,2048]{1,0:T(8,128)(2,1)S(1)}, bf16[64,2048]{1,0:T(8,128)(2,1)}, u32[]{:S(2)}, u32[]{:S(2)}) collective-permute-start(bf16[64,2048]{1,0:T(8,128)(2,1)S(1)} %collective-permute-done.9.refs_4_), channel_id=1, source_target_pairs={{8,0},{16,8},{9,1},{17,9},{10,2},{18,10},{11,3},{19,11},{12,4},{20... | collective-permute-start | bytes 786440 | tf_op jit(solution)/shard_map/ppermute | solution.py:513
  28.1 0.7 copy-start.10
  28.8 12.0 %collective-permute-start.7 = (bf16[64,2048]{1,0:T(8,128)(2,1)S(1)}, bf16[64,2048]{1,0:T(8,128)(2,1)}, u32[]{:S(2)}, u32[]{:S(2)}) collective-permute-start(bf16[64,2048]{1,0:T(8,128)(2,1)S(1)} %collective-permute-done.6.refs_1_), channel_id=1, source_target_pairs={{8,16},{16,24},{9,17},{17,25},{10,18},{18,26},{11,19},{19,27},{12,... | collective-permute-start | bytes 786440 | tf_op jit(solution)/shard_map/ppermute | solution.py:508
  32.1 18.4 %collective-permute-start.5 = (bf16[64,2048]{1,0:T(8,128)(2,1)}, bf16[64,2048]{1,0:T(8,128)(2,1)}, u32[]{:S(2)}, u32[]{:S(2)}) collective-permute-start(bf16[64,2048]{1,0:T(8,128)(2,1)} %collective-permute-done.4), channel_id=1, source_target_pairs={{8,0},{9,1},{10,2},{11,3},{12,4},{13,5},{14,6},{15,7}} | collective-permute-start | bytes 786440 | tf_op jit(solution)/shard_map/ppermute | solution.py:513
  33.4 17.1 %collective-permute-start.2 = (bf16[64,2048]{1,0:T(8,128)(2,1)}, bf16[64,2048]{1,0:T(8,128)(2,1)}, u32[]{:S(2)}, u32[]{:S(2)}) collective-permute-start(bf16[64,2048]{1,0:T(8,128)(2,1)} %collective-permute-done.1), channel_id=1, source_target_pairs={{16,24},{17,25},{18,26},{19,27},{20,28},{21,29},{22,30},{23,31}} | collective-permute-start | bytes 786440 | tf_op jit(solution)/shard_map/ppermute | solution.py:508
  39.5 17.3 %collective-permute-start.11 = (bf16[64,2048]{1,0:T(8,128)(2,1)}, bf16[64,2048]{1,0:T(8,128)(2,1)}, u32[]{:S(2)}, u32[]{:S(2)}) collective-permute-start(bf16[64,2048]{1,0:T(8,128)(2,1)} %collective-permute-done.10.refs_5_), channel_id=1, source_target_pairs={{8,0},{9,1},{10,2},{11,3},{12,4},{13,5},{14,6},{15,7}} | collective-permute-start | bytes 786440 | tf_op jit(solution)/shard_map/ppermute | solution.py:513
  40.8 16.0 %collective-permute-start.8 = (bf16[64,2048]{1,0:T(8,128)(2,1)}, bf16[64,2048]{1,0:T(8,128)(2,1)}, u32[]{:S(2)}, u32[]{:S(2)}) collective-permute-start(bf16[64,2048]{1,0:T(8,128)(2,1)} %collective-permute-done.7.refs_2_), channel_id=1, source_target_pairs={{16,24},{17,25},{18,26},{19,27},{20,28},{21,29},{22,30},{23,31}} | collective-permute-start | bytes 786440 | tf_op jit(solution)/shard_map/ppermute | solution.py:508
  43.5 7.0 %copy-start.16 = (bf16[64,2048]{1,0:T(8,128)(2,1)S(1)}, bf16[64,2048]{1,0:T(8,128)(2,1)}, u32[]{:S(2)}) copy-start(bf16[64,2048]{1,0:T(8,128)(2,1)} %get-tuple-element.45) | copy-start | bytes 786436
  43.5 7.0 %copy-start.18 = (bf16[64,2048]{1,0:T(8,128)(2,1)S(1)}, bf16[64,2048]{1,0:T(8,128)(2,1)}, u32[]{:S(2)}) copy-start(bf16[64,2048]{1,0:T(8,128)(2,1)} %copy-done.17) | copy-start | bytes 786436
  43.5 7.0 %copy-start.20 = (bf16[64,2048]{1,0:T(8,128)(2,1)S(1)}, bf16[64,2048]{1,0:T(8,128)(2,1)}, u32[]{:S(2)}) copy-start(bf16[64,2048]{1,0:T(8,128)(2,1)} %copy-done.19) | copy-start | bytes 786436
  47.6 2.8 %copy-start = (bf16[2048,1664]{1,0:T(8,128)(2,1)}, bf16[2048,1664]{1,0:T(8,128)(2,1)S(1)}, u32[]{:S(2)}) copy-start(bf16[2048,1664]{1,0:T(8,128)(2,1)S(1)} %get-tuple-element.50.refs_7_.refs_1_) | copy-start | bytes 20447236
  50.4 6.4 %copy-start.21 = (f32[1,384]{1,0:T(1,128)S(1)}, f32[1,384]{1,0:T(1,128)}, u32[]{:S(2)}) copy-start(f32[1,384]{1,0:T(1,128)} %refs_4_.1) | copy-start | bytes 4612
  50.4 6.4 %copy-start.22 = (f32[8]{0:T(128)S(1)}, f32[8]{0:T(128)}, u32[]{:S(2)}) copy-start(f32[8]{0:T(128)} %param.13) | copy-start | bytes 100
  52.5 42.2 %all-to-all-start = ((bf16[8,4,8,2048]{3,2,1,0:T(8,128)(2,1)}), bf16[8,4,8,2048]{3,2,1,0:T(8,128)(2,1)}, u32[]{:S(2)}, u32[]{:S(2)}) async-start(bf16[8,4,8,2048]{3,2,1,0:T(8,128)(2,1)} %shard_map.154), calls=%async_computation | async-start | bytes 2097152 | tf_op jit(solution)/shard_map/all_to_all | solution.py:582
  56.8 2.9 %copy-start.1 = (bf16[2048,1664]{1,0:T(8,128)(2,1)S(1)}, bf16[2048,1664]{1,0:T(8,128)(2,1)}, u32[]{:S(2)}) copy-start(bf16[2048,1664]{1,0:T(8,128)(2,1)} %copy-done) | copy-start | bytes 20447236
  59.8 0.9 copy-start.11
  60.7 0.9 copy-start.13
  67.5 1.0 copy-start.3
  68.5 0.9 copy-start.6
  69.4 0.7 copy-start.8
  70.1 14.4 %collective-permute-start.12 = (bf16[64,2048]{1,0:T(8,128)(2,1)}, bf16[64,2048]{1,0:T(8,128)(2,1)S(1)}, u32[]{:S(2)}, u32[]{:S(2)}) collective-permute-start(bf16[64,2048]{1,0:T(8,128)(2,1)} %get-tuple-element.52), channel_id=1, source_target_pairs={{24,16},{0,8},{25,17},{1,9},{26,18},{2,10},{27,19},{3,11},{28,20},... | collective-permute-start | bytes 786440 | tf_op jit(solution)/shard_map/ppermute | solution.py:538
  86.2 22.1 %collective-permute-start.18 = (bf16[64,2048]{1,0:T(8,128)(2,1)}, bf16[64,2048]{1,0:T(8,128)(2,1)}, u32[]{:S(2)}, u32[]{:S(2)}) collective-permute-start(bf16[64,2048]{1,0:T(8,128)(2,1)} %add_convert_fusion.3), channel_id=1, source_target_pairs={{0,16},{8,24},{16,0},{24,8},{1,17},{9,25},{17,1},{25,9},{2,18},{10... | collective-permute-start | bytes 786440 | tf_op jit(solution)/shard_map/ppermute | solution.py:548
  91.2 21.8 %collective-permute-start.16 = (bf16[64,2048]{1,0:T(8,128)(2,1)}, bf16[64,2048]{1,0:T(8,128)(2,1)}, u32[]{:S(2)}, u32[]{:S(2)}) collective-permute-start(bf16[64,2048]{1,0:T(8,128)(2,1)} %get-tuple-element.62), channel_id=1, source_target_pairs={{0,8},{8,16},{16,24},{1,9},{9,17},{17,25},{2,10},{10,18},{18,26},{... | collective-permute-start | bytes 786440 | tf_op jit(solution)/shard_map/ppermute | solution.py:508
  93.4 19.5 %collective-permute-start.17 = (bf16[64,2048]{1,0:T(8,128)(2,1)}, bf16[64,2048]{1,0:T(8,128)(2,1)}, u32[]{:S(2)}, u32[]{:S(2)}) collective-permute-start(bf16[64,2048]{1,0:T(8,128)(2,1)} %get-tuple-element.63), channel_id=1, source_target_pairs={{8,0},{16,8},{24,16},{9,1},{17,9},{25,17},{10,2},{18,10},{26,18},{... | collective-permute-start | bytes 786440 | tf_op jit(solution)/shard_map/ppermute | solution.py:513
  94.7 2.9 %copy-start.2 = (bf16[2048,1664]{1,0:T(8,128)(2,1)S(1)}, bf16[2048,1664]{1,0:T(8,128)(2,1)}, u32[]{:S(2)}) copy-start(bf16[2048,1664]{1,0:T(8,128)(2,1)} %copy-done) | copy-start | bytes 20447236
  97.7 1.2 copy-start.4
  98.9 1.2 copy-start.7
  100.1 12.9 %copy-start.26 = (bf16[64,2048]{1,0:T(8,128)(2,1)S(1)}, bf16[64,2048]{1,0:T(8,128)(2,1)}, u32[]{:S(2)}) copy-start(bf16[64,2048]{1,0:T(8,128)(2,1)} %get-tuple-element.61) | copy-start | bytes 786436
  100.1 28.3 %copy-start.9 = (bf16[256,768]{1,0:T(8,128)(2,1)S(1)}, bf16[256,768]{1,0:T(8,128)(2,1)}, u32[]{:S(2)}) copy-start(bf16[256,768]{1,0:T(8,128)(2,1)} %copy-done.8) | copy-start | bytes 1179652
  107.5 0.9 copy-start.23
  108.4 9.7 %collective-permute-start.15 = (bf16[64,2176]{1,0:T(8,128)(2,1)}, bf16[64,2176]{1,0:T(8,128)(2,1)S(1)}, u32[]{:S(2)}, u32[]{:S(2)}) collective-permute-start(bf16[64,2176]{1,0:T(8,128)(2,1)} %get-tuple-element.60), channel_id=1, source_target_pairs={{24,16},{0,8},{25,17},{1,9},{26,18},{2,10},{27,19},{3,11},{28,20},... | collective-permute-start | bytes 835592 | tf_op jit(solution)/shard_map/ppermute | solution.py:538
  119.1 20.4 %collective-permute-start.19 = (bf16[64,2176]{1,0:T(8,128)(2,1)S(1)}, bf16[64,2176]{1,0:T(8,128)(2,1)S(1)}, u32[]{:S(2)}, u32[]{:S(2)}) collective-permute-start(bf16[64,2176]{1,0:T(8,128)(2,1)S(1)} %add_convert_fusion.1), channel_id=1, source_target_pairs={{0,16},{8,24},{16,0},{24,8},{1,17},{9,25},{17,1},{25,9},{2,18},{10... | collective-permute-start | bytes 835592 | tf_op jit(solution)/shard_map/ppermute | solution.py:548
  121.4 18.1 %collective-permute-start.13 = (bf16[64,2176]{1,0:T(8,128)(2,1)}, bf16[64,2176]{1,0:T(8,128)(2,1)S(1)}, u32[]{:S(2)}, u32[]{:S(2)}) collective-permute-start(bf16[64,2176]{1,0:T(8,128)(2,1)} %get-tuple-element.57), channel_id=1, source_target_pairs={{0,8},{8,16},{16,24},{1,9},{9,17},{17,25},{2,10},{10,18},{18,26},{... | collective-permute-start | bytes 835592 | tf_op jit(solution)/shard_map/ppermute | solution.py:508
  123.4 16.1 %collective-permute-start.14 = (bf16[64,2176]{1,0:T(8,128)(2,1)}, bf16[64,2176]{1,0:T(8,128)(2,1)S(1)}, u32[]{:S(2)}, u32[]{:S(2)}) collective-permute-start(bf16[64,2176]{1,0:T(8,128)(2,1)} %get-tuple-element.58), channel_id=1, source_target_pairs={{8,0},{16,8},{24,16},{9,1},{17,9},{25,17},{10,2},{18,10},{26,18},{... | collective-permute-start | bytes 835592 | tf_op jit(solution)/shard_map/ppermute | solution.py:513
  124.7 15.6 %all-to-all-start.2 = ((bf16[8,8,2048]{2,1,0:T(8,128)(2,1)}), bf16[8,8,2048]{2,1,0:T(8,128)(2,1)S(1)}, u32[]{:S(2)}, u32[]{:S(2)}) async-start(bf16[8,8,2048]{2,1,0:T(8,128)(2,1)} %bitcast.15), calls=%async_computation.2 | async-start | bytes 524288 | tf_op jit(solution)/shard_map/all_to_all | solution.py:577
  128.4 5.5 %copy-start.5 = (bf16[256,2048]{1,0:T(8,128)(2,1)S(1)}, bf16[256,2048]{1,0:T(8,128)(2,1)}, u32[]{:S(2)}) copy-start(bf16[256,2048]{1,0:T(8,128)(2,1)} %copy-done.3) | copy-start | bytes 3145732
  128.4 5.5 %copy-start.24 = (bf16[256,1664]{1,0:T(8,128)(2,1)S(1)}, bf16[256,1664]{1,0:T(8,128)(2,1)}, u32[]{:S(2)}) copy-start(bf16[256,1664]{1,0:T(8,128)(2,1)} %copy-done.23) | copy-start | bytes 2555908
  133.9 5.6 %copy-start.25 = (bf16[64,2176]{1,0:T(8,128)(2,1)S(1)}, bf16[64,2176]{1,0:T(8,128)(2,1)}, u32[]{:S(2)}) copy-start(bf16[64,2176]{1,0:T(8,128)(2,1)} %get-tuple-element.56) | copy-start | bytes 835588
  133.9 10.7 %copy-start.15 = (bf16[2,64,256]{2,1,0:T(8,128)(2,1)S(1)}, bf16[2,64,256]{2,1,0:T(8,128)(2,1)}, u32[]{:S(2)}) copy-start(bf16[2,64,256]{2,1,0:T(8,128)(2,1)} %copy-done.14) | copy-start | bytes 196612
  140.4 11.3 %all-to-all-start.3 = ((bf16[8,8,2176]{2,1,0:T(8,128)(2,1)}), bf16[8,8,2176]{2,1,0:T(8,128)(2,1)S(1)}, u32[]{:S(2)}, u32[]{:S(2)}) async-start(bf16[8,8,2176]{2,1,0:T(8,128)(2,1)} %bitcast.17), calls=%async_computation.3 | async-start | bytes 557056 | tf_op jit(solution)/shard_map/all_to_all | solution.py:577
  (4 other events, 2.7 us)

commit v6 on v4

v6 whole, which is shorter than its diff:
```python
import jax
import jax.numpy as jnp
from jax import lax
from jax.experimental import pallas as pl
from jax.experimental.pallas import tpu as pltpu
from jax.sharding import PartitionSpec as P

BOTH = ("seq", "exp")
F32 = jnp.float32
BF16 = jnp.bfloat16
ROWS = ((0,), (0,))
LAST = ((1,), (1,))
STEPS = 4
LANES = 128


def mm(a, b, dims=((1,), (0,))):
    return lax.dot_general(a, b, (dims, ((), ())), preferred_element_type=F32)


PARAMS = pltpu.CompilerParams(vmem_limit_bytes=56 * 2**20)


def cost(flops, moved):
    return pl.CostEstimate(flops=flops, bytes_accessed=moved, transcendentals=0)


def shape(dims, dtype=BF16):
    return jax.ShapeDtypeStruct(dims, dtype)


ANYWHERE = pl.BlockSpec(memory_space=pl.ANY)
IN_VMEM = pl.BlockSpec(memory_space=pltpu.VMEM)


def choose_rows(tokens, cotangent, picks, counts, pack):
    own, features = tokens.shape
    slots, experts = picks.shape
    count = experts * pack * slots
    part = features // pack
    width = part // STEPS

    def body(picks_ref, counts_ref, c_ref, x_ref, c_out, x_out, hot_ref, picks_s, counts_s, c_v, x_v, hot, sems):
        small = [
            pltpu.make_async_copy(picks_ref, picks_s, sems.at[2 * STEPS]),
            pltpu.make_async_copy(counts_ref, counts_s, sems.at[2 * STEPS + 1]),
        ]
        for copy in small:
            copy.start()
        large = []
        for n, (ref, held) in enumerate(((c_ref, c_v), (x_ref, x_v))):
            for j in range(STEPS):
                now = pl.ds(j * pack * width, pack * width)
                large.append(pltpu.make_async_copy(ref.at[:, now], held.at[:, now], sems.at[n * STEPS + j]))
                large[-1].start()
        for copy in small:
            copy.wait()
        dims = (count, own)
        row = lax.broadcasted_iota(jnp.int32, dims, 0)
        token = lax.broadcasted_iota(jnp.int32, dims, 1)
        place = row // (pack * slots) * slots + row % slots
        part_of = (row // slots) % pack
        want = jnp.full(dims, -1, jnp.int32)
        want_live = want
        for e in range(experts):
            for k in range(slots):
                here = place == e * slots + k
                want = jnp.where(here, picks_s[k, e], want)
                want_live = jnp.where(here, jnp.where(k < counts_s[0, e], picks_s[k, e], -1), want_live)
        for h in range(pack):
            hot[h] = jnp.where((want == token) & (part_of == h), 1.0, 0.0).astype(BF16)
            hot_ref[h] = jnp.where((want_live == token) & (part_of == h), 1.0, 0.0).astype(BF16)
        for n, (chooser, held, out_ref) in enumerate(((hot_ref, c_v, c_out), (hot, x_v, x_out))):
            for copy in large[n * STEPS : (n + 1) * STEPS]:
                copy.wait()
            for j in range(STEPS):
                out_ref[:, j * width : (j + 1) * width] = sum(
                    mm(chooser[h], held[:, h * part + j * width : h * part + (j + 1) * width]) for h in range(pack)
                ).astype(BF16)

    return pl.pallas_call(
        body,
        in_specs=[ANYWHERE] * 4,
        out_specs=[IN_VMEM] * 3,
        out_shape=[shape((count, part))] * 2 + [shape((pack, count, own))],
        scratch_shapes=[
            pltpu.SMEM(picks.shape, jnp.int32),
            pltpu.SMEM(counts.shape, jnp.int32),
            pltpu.VMEM(tokens.shape, BF16),
            pltpu.VMEM(tokens.shape, BF16),
            pltpu.VMEM((pack, count, own), BF16),
            pltpu.SemaphoreType.DMA((2 * STEPS + 2,)),
        ],
        compiler_params=PARAMS,
        cost_estimate=cost(4 * count * own * features, 4 * features * own),
    )(picks, counts, cotangent, tokens)


def scatter_rows(back, hot, seq_n, message=None):
    pack, count, own = hot.shape
    rows = back.shape[0]
    extra = 0 if message is None else riding(seq_n, count // message[1])
    part = back.shape[1] - extra
    width = part // 2

    def body(hot_ref, back_ref, *refs):
        out_ref = refs[-1] if message is None else refs[-3]
        chooser = jnp.concatenate([hot_ref[...]] * seq_n, axis=0)
        out_ref[...] = mm(chooser, back_ref[...], ROWS).astype(BF16)
        if message is not None:
            message_refs, router_ref, total_ref = refs[:-3], refs[-2], refs[-1]

            @pl.when((pl.program_id(0) == 0) & (pl.program_id(1) == 0))
            def _():
                experts, per = router_ref.shape
                group = count // experts
                row = lax.broadcasted_iota(jnp.int32, (rows, experts), 0)
                expert = lax.broadcasted_iota(jnp.int32, (rows, experts), 1)
                mine = row % count // group == expert
                even = jnp.where(mine & (row % 2 == 0), 1.0, 0.0).astype(BF16)
                odd = jnp.where(mine & (row % 2 == 1), 1.0, 0.0).astype(BF16)
                router = sum(mm(even, ref[...], ROWS) for ref in message_refs)
                total = sum(mm(ref[...], odd, ROWS) for ref in message_refs)
                router_ref[...] = router[:, :per]
                total_ref[...] = jnp.sum(total[:3], axis=0, keepdims=True)

    in_specs = [
        pl.BlockSpec((None, count, own), lambda h, i: (h, 0, 0)),
        pl.BlockSpec((rows, width), lambda h, i: (0, i)),
    ]
    out_specs = [pl.BlockSpec((own, width), lambda h, i: (0, h * 2 + i))]
    out_shape = [shape((own, part * pack))]
    args = [hot, back]
    if message is not None:
        per, experts = message
        for t in range(extra // LANES):
            in_specs.append(pl.BlockSpec((rows, LANES), lambda h, i, t=t: (0, part // LANES + t)))
            args.append(back)
        out_specs += [
            pl.BlockSpec((experts, per), lambda h, i: (0, 0)),
            pl.BlockSpec((1, experts), lambda h, i: (0, 0)),
        ]
        out_shape += [shape((experts, per), F32), shape((1, experts), F32)]
    return pl.pallas_call(
        body,
        grid=(pack, 2),
        in_specs=in_specs,
        out_specs=out_specs,
        out_shape=out_shape,
        compiler_params=PARAMS,
        cost_estimate=cost(2 * rows * own * part * pack, 2 * part * pack * own),
    )(*args)


def first_part(rows, pack, slots):
    return (lax.broadcasted_iota(jnp.int32, (rows, 1), 0) // slots) % pack == 0


def fold(parts, slots):
    rows = parts[0].shape[0]
    total = parts[0]
    for h in range(1, len(parts)):
        total = total + pltpu.roll(parts[h], rows - h * slots, 0)
    return total


def spread(value, pack, slots):
    return [value if h == 0 else pltpu.roll(value, h * slots, 0) for h in range(pack)]


class Arrivals:
    def __init__(self, blocks, plan):
        self.blocks, self.plan = blocks, plan

    def start(self, refs, places, sems):
        here = lax.axis_index("seq")
        for k, (a, b, t) in enumerate(self.plan):
            if a == b:
                pltpu.make_async_copy(refs[a], places[k], sems.at[k]).start()
            else:

                @pl.when(here >= t)
                def _():
                    pltpu.make_async_copy(refs[a], places[k], sems.at[k]).start()

                @pl.when(here < t)
                def _():
                    pltpu.make_async_copy(refs[b], places[k], sems.at[k]).start()

    def wait(self, refs, places, sems):
        for k, (a, _, _) in enumerate(self.plan):
            pltpu.make_async_copy(refs[a], places[k], sems.at[k]).wait()


def side_copies(gate_ref, up_ref, router_ref, side, sems, pack, j, width):
    part = side.shape[0]
    hidden_n = gate_ref.shape[2]
    rows = pl.ds(j * width, width)
    copies = []
    for h in range(pack):
        for n, ref in enumerate((gate_ref, up_ref)):
            columns = pl.ds((2 * h + n) * hidden_n, hidden_n)
            copies.append((ref.at[0, pl.ds(h * part + j * width, width), :], side.at[rows, columns]))
    copies.append((router_ref.at[rows, :], side.at[rows, pl.ds(2 * pack * hidden_n, LANES)]))
    return [pltpu.make_async_copy(a, b, sems.at[j, n]) for n, (a, b) in enumerate(copies)]


def down_copies(down_ref, stack, sems, pack):
    hidden_n = down_ref.shape[1]
    part = stack.shape[1]
    return [
        pltpu.make_async_copy(
            down_ref.at[0, :, pl.ds(h * part, part)], stack.at[pl.ds(h * hidden_n, hidden_n), :], sems.at[h]
        )
        for h in range(pack)
    ]


def put_blocks(out, target, columns):
    seq_n, rows, _ = target.shape
    here = lax.axis_index("seq")
    for k in range(seq_n):
        target[lax.rem(here - k + seq_n, seq_n), :, columns] = out[k * rows : (k + 1) * rows]


def expert_forward(arrivals, seq_n, slots, experts, pack, router_side, threshold, w_gate, w_up, w_down, hid_scale):
    block_rows, part = arrivals.blocks[0].shape
    rows = block_rows * seq_n
    hidden_n = w_gate.shape[2]
    both = 2 * hidden_n
    width = part // STEPS
    total = pack * both + LANES
    n_blocks = len(arrivals.blocks)

    def body(*refs):
        blocks = refs[:n_blocks]
        router_ref, gate_ref, up_ref, down_ref, threshold_ref, scale_ref = refs[n_blocks : n_blocks + 6]
        x_ref, out_ref, pre_ref, hidden_ref = refs[n_blocks + 6 : n_blocks + 10]
        x_v, out_v, side, stack, x_sems, side_sems, stack_sems, out_sems = refs[n_blocks + 10 :]
        places = [x_v.at[pl.ds(k * block_rows, block_rows), :] for k in range(seq_n)]
        arrivals.start(blocks, places, x_sems)
        chunks = [side_copies(gate_ref, up_ref, router_ref, side, side_sems, pack, j, width) for j in range(STEPS)]
        downs = down_copies(down_ref, stack, stack_sems, pack)
        for copy in sum(chunks, []) + downs:
            copy.start()
        arrivals.wait(blocks, places, x_sems)
        leaving = [pltpu.make_async_copy(x_v, x_ref, out_sems.at[STEPS])]
        leaving[0].start()
        sums = [0.0] * (pack + 1)
        for j, chunk in enumerate(chunks):
            for copy in chunk:
                copy.wait()
            now = slice(j * width, (j + 1) * width)
            for n in range(pack + 1):
                sums[n] = sums[n] + mm(x_v[:, now], side[now, n * both : min((n + 1) * both, total)])
        gate = fold([y[:, :hidden_n] for y in sums[:pack]], slots)
        up = fold([y[:, hidden_n:] for y in sums[:pack]], slots)
        scores = sums[pack]
        lane = lax.broadcasted_iota(jnp.int32, scores.shape, 1)
        expert = lax.axis_index("exp")
        score = fold([jnp.where(lane == h * experts + expert, scores, 0.0) for h in range(pack)], slots)
        lane = lax.broadcasted_iota(jnp.int32, threshold_ref.shape, 1)
        cut = jnp.sum(jnp.where(lane == expert, threshold_ref[...], 0.0), axis=1, keepdims=True)
        g = jax.nn.sigmoid(jnp.sum(score, axis=1, keepdims=True) - cut)
        hidden = gate * jax.nn.sigmoid(gate) * up * scale_ref[...] * g
        hidden = jnp.where(first_part(rows, pack, slots), hidden, 0.0)
        for h, value in enumerate(spread(hidden, pack, slots)):
            hidden_ref[:, h * hidden_n : (h + 1) * hidden_n] = value.astype(BF16)
        for copy in downs:
            copy.wait()
        for j in range(STEPS):
            now = slice(j * width, (j + 1) * width)
            put_blocks(mm(hidden_ref[...], stack[:, now]).astype(BF16), out_v, now)
            columns = pl.ds(j * width, width)
            leaving.append(pltpu.make_async_copy(out_v.at[:, :, columns], out_ref.at[:, :, columns], out_sems.at[j]))
            leaving[-1].start()
        pre_ref[:, :hidden_n] = gate
        pre_ref[:, hidden_n:both] = up
        pre_ref[:, both:] = jnp.broadcast_to(g, (rows, LANES))
        for copy in leaving:
            copy.wait()

    return pl.pallas_call(
        body,
        in_specs=[ANYWHERE] * (n_blocks + 4) + [IN_VMEM] * 2,
        out_specs=[ANYWHERE] * 2 + [IN_VMEM] * 2,
        out_shape=[
            shape((rows, part)),
            shape((seq_n, block_rows, part)),
            shape((rows, both + LANES), F32),
            shape((rows, pack * hidden_n)),
        ],
        scratch_shapes=[
            pltpu.VMEM((rows, part), BF16),
            pltpu.VMEM((seq_n, block_rows, part), BF16),
            pltpu.VMEM((part, total), BF16),
            pltpu.VMEM((pack * hidden_n, part), BF16),
            pltpu.SemaphoreType.DMA((seq_n,)),
            pltpu.SemaphoreType.DMA((STEPS, 2 * pack + 1)),
            pltpu.SemaphoreType.DMA((pack,)),
            pltpu.SemaphoreType.DMA((STEPS + 1,)),
        ],
        compiler_params=PARAMS,
        cost_estimate=cost(6 * rows * part * pack * hidden_n, 6 * part * pack * hidden_n),
    )(*arrivals.blocks, router_side, w_gate, w_up, w_down, threshold.reshape(1, -1), hid_scale)


def split3(v):
    hi = v.astype(BF16)
    rest = v - hi.astype(F32)
    mid = rest.astype(BF16)
    return hi, mid, (rest - mid.astype(F32)).astype(BF16)


def riding(seq_n, group):
    return LANES * -(-2 * seq_n // group)


def expert_backward(arrivals, seq_n, exp_n, slots, pack, x, pre, router_side, w_gate, w_up, w_down, hid_scale):
    block_rows, part = arrivals.blocks[0].shape
    rows = block_rows * seq_n
    hidden_n = w_gate.shape[2]
    width = part // STEPS
    total = 2 * pack * hidden_n + LANES
    group = pack * slots
    extra = riding(seq_n, group)
    per = part * pack // (seq_n * exp_n)
    n_blocks = len(arrivals.blocks)

    def body(*refs):
        blocks = refs[:n_blocks]
        router_ref, gate_ref, up_ref, down_ref, x_ref, pre_ref, scale_ref = refs[n_blocks : n_blocks + 7]
        c_ref, out_ref, delta_ref = refs[n_blocks + 7 : n_blocks + 10]
        c_v, x_v, pre_v, out_v, side, stack, columns, c_sems, x_sems, side_sems, stack_sems, out_sems = refs[
            n_blocks + 10 :
        ]
        places = [c_v.at[pl.ds(k * block_rows, block_rows), :] for k in range(seq_n)]
        arrivals.start(blocks, places, c_sems)
        chunks = [side_copies(gate_ref, up_ref, router_ref, side, side_sems, pack, j, width) for j in range(STEPS)]
        downs = down_copies(down_ref, stack, stack_sems, pack)
        x_copy = pltpu.make_async_copy(x_ref, x_v, x_sems.at[0])
        pre_copy = pltpu.make_async_copy(pre_ref, pre_v, x_sems.at[1])
        for copy in downs + [pre_copy] + sum(chunks, []) + [x_copy]:
            copy.start()
        arrivals.wait(blocks, places, c_sems)
        leaving = [pltpu.make_async_copy(c_v, c_ref, out_sems.at[STEPS])]
        leaving[0].start()
        for copy in downs:
            copy.wait()
        both = mm(c_v[...], stack[...], LAST)
        parts = [both[:, h * hidden_n : (h + 1) * hidden_n] for h in range(pack)]
        pre_copy.wait()
        raw = jnp.where(first_part(rows, pack, slots), fold(parts, slots) * scale_ref[...], 0.0)
        gate = pre_v[:, :hidden_n]
        up = pre_v[:, hidden_n : 2 * hidden_n]
        g = pre_v[:, 2 * hidden_n : 2 * hidden_n + 1]
        sig = jax.nn.sigmoid(gate)
        act = gate * sig
        score = jnp.sum(act * up * raw, axis=1, keepdims=True) * g * (1.0 - g)
        grad = raw * g
        to_gate = spread(grad * up * sig * (1.0 + gate * (1.0 - sig)), pack, slots)
        to_up = spread(grad * act, pack, slots)
        expert = lax.axis_index("exp")
        lane = lax.broadcasted_iota(jnp.int32, (rows, LANES), 1)
        by_expert = jnp.zeros((rows, LANES), F32)
        by_split = jnp.zeros((rows, LANES), F32)
        for h, value in enumerate(spread(jnp.broadcast_to(score, (rows, LANES)), pack, slots)):
            delta_ref[:, 2 * h * hidden_n : (2 * h + 1) * hidden_n] = to_gate[h].astype(BF16)
            delta_ref[:, (2 * h + 1) * hidden_n : (2 * h + 2) * hidden_n] = to_up[h].astype(BF16)
            for n, piece in enumerate(split3(value)):
                piece = piece.astype(F32)
                by_split = jnp.where(lane == 3 * h + n, piece, by_split)
                if n < 2:
                    by_expert = jnp.where(lane == (n * pack + h) * exp_n + expert, piece, by_expert)
        columns[...] = by_split.astype(BF16)
        delta_ref[:, 2 * pack * hidden_n :] = by_expert.astype(BF16)
        for j, chunk in enumerate(chunks):
            for copy in chunk:
                copy.wait()
            now = slice(j * width, (j + 1) * width)
            put_blocks(mm(delta_ref[...], side[now, :], LAST).astype(BF16), out_v, now)
            if j + 1 < STEPS:
                now = pl.ds(j * width, width)
                leaving.append(pltpu.make_async_copy(out_v.at[:, :, now], out_ref.at[:, :, now], out_sems.at[j]))
                leaving[-1].start()

        here = lax.axis_index("seq")
        x_copy.wait()
        told = mm(columns[...], x_v[...], ROWS)
        sub = lax.broadcasted_iota(jnp.int32, (group, LANES), 0)
        lane = lax.broadcasted_iota(jnp.int32, (group, LANES), 1)
        minus = jnp.broadcast_to(-jnp.sum(score, axis=0, keepdims=True), (group, LANES))
        pieces = [piece.astype(F32) for piece in split3(minus)]
        threshold_row = jnp.zeros((group, LANES), F32)
        for n, piece in enumerate(pieces):
            threshold_row = jnp.where(lane == n, piece, threshold_row)
        for owner in range(seq_n * exp_n):
            h, first = divmod(owner * per, part)
            shift = first % LANES
            value = jnp.sum(told[3 * h : 3 * h + 3, first - shift : first - shift + LANES], axis=0, keepdims=True)
            value = jnp.broadcast_to(value, (group, LANES))
            if shift:
                value = pltpu.roll(value, LANES - shift, 1)
            if per < LANES:
                value = jnp.where(lane < per, value, 0.0)
            d, place = divmod(owner, exp_n)
            for t in range(extra // LANES):
                row = sub + t * group
                now = slice(part + t * LANES, part + (t + 1) * LANES)
                out_v[d, place * group : (place + 1) * group, now] = jnp.where(
                    row == 2 * here, value, jnp.where(row == 2 * here + 1, threshold_row, 0.0)
                ).astype(BF16)
        now = pl.ds((STEPS - 1) * width, width + extra)
        leaving.append(pltpu.make_async_copy(out_v.at[:, :, now], out_ref.at[:, :, now], out_sems.at[STEPS - 1]))
        leaving[-1].start()
        for copy in leaving:
            copy.wait()

    return pl.pallas_call(
        body,
        in_specs=[ANYWHERE] * (n_blocks + 6) + [IN_VMEM],
        out_specs=[ANYWHERE] * 2 + [IN_VMEM],
        out_shape=[
            shape((rows, part)),
            shape((seq_n, block_rows, part + extra)),
            shape((rows, total)),
        ],
        scratch_shapes=[
            pltpu.VMEM((rows, part), BF16),
            pltpu.VMEM((rows, part), BF16),
            pltpu.VMEM(pre.shape, F32),
            pltpu.VMEM((seq_n, block_rows, part + extra), BF16),
            pltpu.VMEM((part, total), BF16),
            pltpu.VMEM((pack * hidden_n, part), BF16),
            pltpu.VMEM((rows, LANES), BF16),
            pltpu.SemaphoreType.DMA((seq_n,)),
            pltpu.SemaphoreType.DMA((2,)),
            pltpu.SemaphoreType.DMA((STEPS, 2 * pack + 1)),
            pltpu.SemaphoreType.DMA((pack,)),
            pltpu.SemaphoreType.DMA((STEPS + 1,)),
        ],
        compiler_params=PARAMS,
        cost_estimate=cost(6 * rows * part * pack * hidden_n, 6 * part * pack * hidden_n),
    )(*arrivals.blocks, router_side, w_gate, w_up, w_down, x, pre, hid_scale)


def side_grads(x, delta, pack, hidden_n):
    rows, part = x.shape
    width = part // STEPS

    def body(x_ref, delta_ref, gate_out, up_out):
        for h in range(pack):
            both = mm(x_ref[...], delta_ref[:, 2 * h * hidden_n : 2 * (h + 1) * hidden_n], ROWS)
            gate_out[h] = both[:, :hidden_n]
            up_out[h] = both[:, hidden_n:]

    tall = pl.BlockSpec((pack, width, hidden_n), lambda i: (0, i, 0))
    gate, up = pl.pallas_call(
        body,
        grid=(STEPS,),
        in_specs=[
            pl.BlockSpec((rows, width), lambda i: (0, i)),
            pl.BlockSpec(delta.shape, lambda i: (0, 0)),
        ],
        out_specs=[tall, tall],
        out_shape=[shape((pack, part, hidden_n), F32)] * 2,
        compiler_params=PARAMS,
        cost_estimate=cost(4 * rows * part * pack * hidden_n, 8 * part * pack * hidden_n),
    )(x, delta)
    return gate.reshape(1, part * pack, hidden_n), up.reshape(1, part * pack, hidden_n)


def down_grads(c, hidden, pack, hidden_n):
    rows, part = c.shape
    width = part // 2

    def body(c_ref, hidden_ref, out):
        out[...] = mm(hidden_ref[...], c_ref[...], ROWS)

    return pl.pallas_call(
        body,
        grid=(pack, 2),
        in_specs=[
            pl.BlockSpec((rows, width), lambda h, i: (0, i)),
            pl.BlockSpec((rows, hidden_n), lambda h, i: (0, h)),
        ],
        out_specs=pl.BlockSpec((None, hidden_n, width), lambda h, i: (0, 0, h * 2 + i)),
        out_shape=shape((1, hidden_n, part * pack), F32),
        compiler_params=PARAMS,
        cost_estimate=cost(2 * rows * part * pack * hidden_n, 4 * part * pack * hidden_n),
    )(c, hidden)


def up_line(block, n, first=0, last=None):
    last = n - 1 if last is None else last
    return lax.ppermute(block, "seq", [(s, s + 1) for s in range(first, last)])


def down_line(block, n, first=1, last=None):
    last = n if last is None else last
    return lax.ppermute(block, "seq", [(s, s - 1) for s in range(first, last)])


def line_gather(block, n):
    ups, downs = [], []
    up = down = block
    for j in range(1, n):
        up = up_line(up, n, j - 1)
        down = down_line(down, n, 1, n - j + 1)
        ups.append(up)
        downs.append(down)
    plan = [(0, 0, 0)] + [(k, 2 * n - 1 - k, k) for k in range(1, n)]
    return Arrivals([block] + ups + downs, plan)


def after(value, *others):
    return lax.optimization_barrier((value, *others))[0]


def on_device(tokens, cotangent, router, threshold, w_gate, w_up, w_down, hid_scale, picks, counts):
    experts, slots = picks.shape[1:]
    features = tokens.shape[1]
    true_hidden = w_gate.shape[2]
    extra = -true_hidden % LANES
    if extra:
        w_gate, w_up = (jnp.pad(w, ((0, 0), (0, 0), (0, extra))) for w in (w_gate, w_up))
        w_down = jnp.pad(w_down, ((0, 0), (0, extra), (0, 0)))
        hid_scale = jnp.pad(hid_scale, ((0, 0), (0, extra)))
    hidden_n = true_hidden + extra
    seq_n = lax.axis_size("seq")
    exp_n = lax.axis_size("exp")
    everyone = seq_n * exp_n
    pack = max(1, 8 // slots)
    chosen = picks[0].T

    def to_experts(block):
        block = block.reshape(experts, -1, block.shape[1])
        return lax.all_to_all(block, "exp", split_axis=0, concat_axis=0, tiled=True).reshape(-1, block.shape[2])

    def to_owners(parts):
        parts = parts.reshape(everyone, -1, parts.shape[2])
        return lax.all_to_all(parts, BOTH, split_axis=0, concat_axis=0, tiled=True).reshape(-1, parts.shape[2])

    c_rows, x_rows, hot = choose_rows(tokens, cotangent, chosen, counts, pack)
    x_in = line_gather(to_experts(x_rows), seq_n)
    c_in = line_gather(to_experts(after(c_rows, x_in.blocks[1])), seq_n)
    halves = list(router.reshape(pack, features // pack, experts))
    router_side = jnp.concatenate(halves + halves, axis=1)
    router_side = jnp.pad(router_side, ((0, 0), (0, LANES - router_side.shape[1])))

    x_in.blocks[0] = after(x_in.blocks[0], c_in.blocks[1])
    x, out, pre, hidden = expert_forward(
        x_in, seq_n, slots, experts, pack, router_side, threshold, w_gate, w_up, w_down, hid_scale
    )
    out = to_owners(out)
    c, back, delta = expert_backward(
        c_in, seq_n, exp_n, slots, pack, x, pre, router_side, w_gate, w_up, w_down, hid_scale
    )
    back = to_owners(back)
    down_grad = down_grads(c, hidden, pack, hidden_n)
    gate_grad, up_grad = side_grads(x, delta, pack, hidden_n)
    (mixture,) = scatter_rows(out, hot, seq_n)
    token_grad, router_grad, threshold_grad = scatter_rows(back, hot, seq_n, (features // everyone, experts))
    if extra:
        gate_grad, up_grad = gate_grad[:, :, :true_hidden], up_grad[:, :, :true_hidden]
        down_grad = down_grad[:, :true_hidden]
    return mixture, token_grad, router_grad.T, threshold_grad[0], gate_grad, up_grad, down_grad


def solution(mesh):
    by_owner = P(BOTH, None)
    columns = P("exp", None, "seq")
    down = P("exp", "seq", None)
    return jax.shard_map(
        on_device,
        mesh=mesh,
        in_specs=(
            by_owner,
            by_owner,
            P(),
            P(),
            columns,
            columns,
            down,
            P("exp", "seq"),
            P(BOTH, None, None),
            by_owner,
        ),
        out_specs=(by_owner, by_owner, by_owner, P(), columns, columns, down),
        check_vma=False,
    )
```

time: 181 us -> 170 us (0.939)
  waiting for transfers between devices: 25.5 us -> 68.7 us
  Pallas kernels: 81.9 us -> 47.4 us
  starting transfers between devices: 59.8 us -> 26.2 us
  blocking collectives: 0 us -> 22.4 us
  other arithmetic: 5.02 us -> 0.01 us
  local copies, waits for them, and re-layouts: 6.31 us -> 3.6 us
    ppermute x8 -> x6, waiting for transfers between devices: 10.6 us -> 52.6 us  [down_line(): return lax.ppermute(block, 'seq', [(s, s - 1) for s in range(first, last)])]
    pallas_call x4 -> x3, Pallas kernels: 64.6 us -> 29.5 us  [the longest x1 12.5 us: expert_backward(): pl.pallas_call(body, in_specs=[ANYWHERE] * (n_blocks + 6) + [IN_VMEM], ou...]
    all_to_all x0 -> x2, blocking collectives: none -> 22.4 us  [to_experts(): lax.all_to_all(block, 'exp', split_axis=0, concat_axis=0, tiled=True)]
    ppermute x4 -> x0, starting transfers between devices: 17.4 us -> none  [the longest x2 8.98 us: line_sum(): far = lax.ppermute(middle, 'seq', [(s, (s + 2) % 4) for s in range(4)])]
    ppermute x4 -> x0, waiting for transfers between devices: 10.8 us -> none  [the longest x2 10.8 us: line_begin(): return lax.ppermute(parts[4], 'seq', [(3, 2), (0, 1)])]
    all_to_all x4 -> x2, starting transfers between devices: 16.5 us -> 7.71 us  [to_owners(): lax.all_to_all(parts, BOTH, split_axis=0, concat_axis=0, tiled=True)]
    all_to_all x4 -> x2, waiting for transfers between devices: 4.1 us -> 10.9 us  [to_owners(): lax.all_to_all(parts, BOTH, split_axis=0, concat_axis=0, tiled=True)]
    ppermute x8 -> x6, waiting for transfers between devices: 0.02 us -> 5.21 us  [up_line(): return lax.ppermute(block, 'seq', [(s, s + 1) for s in range(first, last)])]
  transfers between devices with their start and end apart: 24 -> 14, of which waited for: 8 -> 8; matrix products, arithmetic and copies ran while one was open for 3% -> 1% of each run, Pallas kernels for 41% -> 17%
where the time goes in v6:
time: 170 us; the launch traced here: 169 us
  waiting for transfers between devices  68.7 us (40%)
  Pallas kernels  47.4 us (28%)
  starting transfers between devices  26.2 us (15%)
  blocking collectives  22.4 us (13%)
  local copies, waits for them, and re-layouts  3.6 us (2%)
    ppermute x6, waiting for transfers between devices, down_line(): return lax.ppermute(block, 'seq', [(s, s - 1) for s in range(first, last)])  52.6 us
    all_to_all x2, blocking collectives, to_experts(): lax.all_to_all(block, 'exp', split_axis=0, concat_axis=0, tiled=True)  22.4 us
    pallas_call x1, Pallas kernels, expert_backward(): pl.pallas_call(body, in_specs=[ANYWHERE] * (n_blocks + 6) + [IN_VMEM], ou...  12.5 us
    all_to_all x2, waiting for transfers between devices, to_owners(): lax.all_to_all(parts, BOTH, split_axis=0, concat_axis=0, tiled=True)  10.9 us
    ppermute x6, starting transfers between devices, up_line(): return lax.ppermute(block, 'seq', [(s, s + 1) for s in range(first, last)])  10.7 us
    pallas_call x1, Pallas kernels, expert_forward(): pl.pallas_call(body, in_specs=[ANYWHERE] * (n_blocks + 4) + [IN_VMEM] * 2...  10.1 us
    pallas_call x2, Pallas kernels, scatter_rows(): pl.pallas_call(body, grid=(pack, 2), in_specs=in_specs, out_specs=out_spe...  9 us
    ppermute x6, starting transfers between devices, down_line(): return lax.ppermute(block, 'seq', [(s, s - 1) for s in range(first, last)])  7.72 us
  transfers between devices with their start and end apart: 14, of which 8 were waited for; matrix products, arithmetic and copies ran while one was open for 1% of the time, Pallas kernels for 17%

profile of v6, /device:TPU:0, one launch (start us, length us, event | category | flops | bytes accessed | tf_op | source)
XLA Modules:
  0.0 169.2 jit_solution(4433877524403592728)
XLA Ops:
  0.6 0.0 copy-start.16
  0.6 3.5 %shard_map.153 = (bf16[64,2048]{1,0:T(8,128)(2,1)}, bf16[64,2048]{1,0:T(8,128)(2,1)}, bf16[2,64,256]{2,1,0:T(8,128)(2,1)}) custom-call(s32[4,8]{1,0:T(4,128)} %bitcast.29, s32[1,8]{1,0:T(1,128)} %counts_ref.1, bf16[256,4096]{1,0:T(8,128)(2,1)} %c_ref.1, bf16[256,4096]{1,0:T(8,128)(2,1)} %x_ref.1), custom_call_target="tpu_custom_call" | custom-call | flops 268435456 | bytes 4194304 | tf_op jit(solution)/shard_map/pallas_call | solution.py:81
  4.1 12.1 %all_to_all.20 = bf16[8,8,2048]{2,1,0:T(8,128)(2,1)S(1)} all-to-all(bf16[8,8,2048]{2,1,0:T(8,128)(2,1)} %bitcast.28), channel_id=1, replica_groups=mesh['seq'=4,'exp'=8] {'exp'}, dimensions={0} | all-to-all | bytes 524288 | tf_op jit(solution)/shard_map/all_to_all | solution.py:538
  16.2 3.5 %collective-permute-start = (bf16[64,2048]{1,0:T(8,128)(2,1)S(1)}, bf16[64,2048]{1,0:T(8,128)(2,1)S(1)}, u32[]{:S(2)}, u32[]{:S(2)}) collective-permute-start(bf16[64,2048]{1,0:T(8,128)(2,1)S(1)} %bitcast.23), channel_id=1, source_target_pairs={{0,8},{8,16},{16,24},{1,9},{9,17},{17,25},{2,10},{10,18},{18,26},{... | collective-permute-start | bytes 786440 | tf_op jit(solution)/shard_map/ppermute | solution.py:496
  19.7 1.3 collective-permute-start.4
  21.0 3.6 %collective-permute-done.refs_1_ = bf16[64,2048]{1,0:T(8,128)(2,1)S(1)} collective-permute-done((bf16[64,2048]{1,0:T(8,128)(2,1)S(1)}, bf16[64,2048]{1,0:T(8,128)(2,1)S(1)}, u32[]{:S(2)}, u32[]{:S(2)}) %collective-permute-start) | collective-permute-done | bytes 262176 | tf_op jit(solution)/shard_map/ppermute | solution.py:496
  24.6 0.7 collective-permute-start.2
  25.3 3.5 %collective-permute-done.4.refs_4_ = bf16[64,2048]{1,0:T(8,128)(2,1)S(1)} collective-permute-done((bf16[64,2048]{1,0:T(8,128)(2,1)S(1)}, bf16[64,2048]{1,0:T(8,128)(2,1)S(1)}, u32[]{:S(2)}, u32[]{:S(2)}) %collective-permute-start.4) | collective-permute-done | bytes 262176 | tf_op jit(solution)/shard_map/ppermute | solution.py:501
  28.7 1.3 collective-permute-start.5
  30.0 10.3 %all_to_all.21 = bf16[8,8,2048]{2,1,0:T(8,128)(2,1)S(1)} all-to-all(bf16[8,8,2048]{2,1,0:T(8,128)(2,1)} %bitcast.27), channel_id=1, replica_groups=mesh['seq'=4,'exp'=8] {'exp'}, dimensions={0} | all-to-all | bytes 524288 | tf_op jit(solution)/shard_map/all_to_all | solution.py:538
  40.3 4.6 %collective-permute-start.1 = (bf16[64,2048]{1,0:T(8,128)(2,1)S(1)}, bf16[64,2048]{1,0:T(8,128)(2,1)S(1)}, u32[]{:S(2)}, u32[]{:S(2)}) collective-permute-start(bf16[64,2048]{1,0:T(8,128)(2,1)S(1)} %bitcast.20), channel_id=1, source_target_pairs={{0,8},{8,16},{16,24},{1,9},{9,17},{17,25},{2,10},{10,18},{18,26},{... | collective-permute-start | bytes 786440 | tf_op jit(solution)/shard_map/ppermute | solution.py:496
  44.8 0.0 collective-permute-done.2.refs_2_
  44.9 0.0 copy-start.7
  44.9 0.7 collective-permute-start.3
  45.6 0.0 collective-permute-done.5.refs_5_
  45.6 1.3 collective-permute-start.6
  46.9 0.3 copy.21
  47.2 0.9 pad.4.refs_7_
  48.1 1.6 collective-permute-done.1.refs_1_
  49.7 0.0 collective-permute-done.3.refs_3_
  49.7 4.8 %collective-permute-done.6.refs_6_ = bf16[64,2048]{1,0:T(8,128)(2,1)S(1)} collective-permute-done((bf16[64,2048]{1,0:T(8,128)(2,1)S(1)}, bf16[64,2048]{1,0:T(8,128)(2,1)S(1)}, u32[]{:S(2)}, u32[]{:S(2)}) %collective-permute-start.6) | collective-permute-done | bytes 262176 | tf_op jit(solution)/shard_map/ppermute | solution.py:501
  54.6 0.0 copy-done.5
  54.6 0.0 copy-done.7
  54.6 0.0 copy-done.8
  54.6 0.0 copy-done.10
  54.6 0.7 copy-done.12
  55.3 10.1 %shard_map.154 = (bf16[256,2048]{1,0:T(8,128)(2,1)}, bf16[4,64,2048]{2,1,0:T(8,128)(2,1)}, f32[256,896]{1,0:T(8,128)}, bf16[256,768]{1,0:T(8,128)(2,1)}) custom-call(bf16[64,2048]{1,0:T(8,128)(2,1)} %bitcast.25, bf16[64,2048]{1,0:T(8,128)(2,1)} %copy-done.5, bf16[64,2048]{1,0:T(8,128)(2,1)} %copy-done.7, bf16[64,2048]{1,0:T(8,128)(2,1)} %copy-done.10, ...), custom_call_target="tpu_custom_call" | custom-call | flops 2415919104 | bytes 9437184 | tf_op jit(solution)/shard_map/pallas_call | solution.py:283
  65.4 4.9 %all-to-all-start.2 = ((bf16[32,8,2048]{2,1,0:T(8,128)(2,1)}), bf16[32,8,2048]{2,1,0:T(8,128)(2,1)S(1)}, u32[]{:S(2)}, u32[]{:S(2)}) async-start(bf16[32,8,2048]{2,1,0:T(8,128)(2,1)} %bitcast.26), calls=%async_computation.2 | async-start | bytes 2097152 | tf_op jit(solution)/shard_map/all_to_all | solution.py:542
  70.3 1.3 collective-permute-start.9
  71.6 0.7 collective-permute-start.7
  72.3 21.9 %collective-permute-done.9.refs_4_ = bf16[64,2048]{1,0:T(8,128)(2,1)S(1)} collective-permute-done((bf16[64,2048]{1,0:T(8,128)(2,1)S(1)}, bf16[64,2048]{1,0:T(8,128)(2,1)S(1)}, u32[]{:S(2)}, u32[]{:S(2)}) %collective-permute-start.9) | collective-permute-done | bytes 262176 | tf_op jit(solution)/shard_map/ppermute | solution.py:501
  94.3 1.3 collective-permute-start.10
  95.5 0.0 collective-permute-done.7.refs_2_
  95.6 0.7 collective-permute-start.8
  96.3 14.5 %collective-permute-done.10.refs_5_ = bf16[64,2048]{1,0:T(8,128)(2,1)S(1)} collective-permute-done((bf16[64,2048]{1,0:T(8,128)(2,1)S(1)}, bf16[64,2048]{1,0:T(8,128)(2,1)S(1)}, u32[]{:S(2)}, u32[]{:S(2)}) %collective-permute-start.10) | collective-permute-done | bytes 262176 | tf_op jit(solution)/shard_map/ppermute | solution.py:501
  110.8 1.3 collective-permute-start.11
  112.0 0.0 collective-permute-done.8.refs_3_
  112.1 7.8 %collective-permute-done.11.refs_6_ = bf16[64,2048]{1,0:T(8,128)(2,1)S(1)} collective-permute-done((bf16[64,2048]{1,0:T(8,128)(2,1)S(1)}, bf16[64,2048]{1,0:T(8,128)(2,1)S(1)}, u32[]{:S(2)}, u32[]{:S(2)}) %collective-permute-start.11) | collective-permute-done | bytes 262176 | tf_op jit(solution)/shard_map/ppermute | solution.py:501
  119.9 0.7 copy-done.15
  120.6 12.5 %shard_map.156 = (bf16[256,2048]{1,0:T(8,128)(2,1)}, bf16[4,64,2176]{2,1,0:T(8,128)(2,1)}, bf16[256,1664]{1,0:T(8,128)(2,1)}) custom-call(bf16[64,2048]{1,0:T(8,128)(2,1)} %bitcast.22, bf16[64,2048]{1,0:T(8,128)(2,1)} %copy-done.4, bf16[64,2048]{1,0:T(8,128)(2,1)} %copy-done.11, bf16[64,2048]{1,0:T(8,128)(2,1)} %copy-done.14, bf16[64,2048]{1,0:T(8,128)(2,1)} %copy-done.9, ...), custom_call_target="tpu_custom_call" | custom-call | flops 2415919104 | bytes 9437184 | tf_op jit(solution)/shard_map/pallas_call | solution.py:419
  133.1 0.0 all-to-all-done.2
  133.2 2.8 %all-to-all-start.3 = ((bf16[32,8,2176]{2,1,0:T(8,128)(2,1)}), bf16[32,8,2176]{2,1,0:T(8,128)(2,1)S(1)}, u32[]{:S(2)}, u32[]{:S(2)}) async-start(bf16[32,8,2176]{2,1,0:T(8,128)(2,1)} %bitcast.19), calls=%async_computation.3 | async-start | bytes 2228224 | tf_op jit(solution)/shard_map/all_to_all | solution.py:542
  135.9 5.5 %shard_map.159 = f32[1,384,4096]{2,1,0:T(8,128)} custom-call(bf16[256,2048]{1,0:T(8,128)(2,1)} %get-tuple-element.39.c_ref, bf16[256,768]{1,0:T(8,128)(2,1)} %get-tuple-element.40.hidden_ref), custom_call_target="tpu_custom_call" | custom-call | flops 805306368 | bytes 6291456 | tf_op jit(solution)/shard_map/pallas_call | solution.py:480
  141.4 6.9 %shard_map.158 = (f32[2,2048,384]{2,1,0:T(8,128)}, f32[2,2048,384]{2,1,0:T(8,128)}) custom-call(bf16[256,2048]{1,0:T(8,128)(2,1)} %get-tuple-element.30.refs_11_.x_ref, bf16[256,1664]{1,0:T(8,128)(2,1)} %get-tuple-element.36.delta_ref), custom_call_target="tpu_custom_call" | custom-call | flops 1610612736 | bytes 12582912 | tf_op jit(solution)/shard_map/pallas_call | solution.py:458
  148.3 4.4 %shard_map.155 = bf16[256,4096]{1,0:T(8,128)(2,1)} custom-call(bf16[2,64,256]{2,1,0:T(8,128)(2,1)} %get-tuple-element.24.hot_ref, bf16[256,2048]{1,0:T(8,128)(2,1)} %bitcast.18), custom_call_target="tpu_custom_call" | custom-call | flops 536870912 | bytes 2097152 | tf_op jit(solution)/shard_map/pallas_call | solution.py:144
  152.6 10.9 %all-to-all-done.3 = bf16[32,8,2176]{2,1,0:T(8,128)(2,1)S(1)} async-done(((bf16[32,8,2176]{2,1,0:T(8,128)(2,1)}), bf16[32,8,2176]{2,1,0:T(8,128)(2,1)S(1)}, u32[]{:S(2)}, u32[]{:S(2)}) %all-to-all-start.3) | async-done | bytes 1114144 | tf_op jit(solution)/shard_map/all_to_all | solution.py:542
  163.6 1.0 copy-done
  164.6 4.6 %shard_map.157 = (bf16[256,4096]{1,0:T(8,128)(2,1)}, f32[8,128]{1,0:T(8,128)}, f32[1,8]{1,0:T(1,128)}) custom-call(bf16[2,64,256]{2,1,0:T(8,128)(2,1)} %get-tuple-element.24.hot_ref, bf16[256,2176]{1,0:T(8,128)(2,1)} %bitcast.16, bf16[256,2176]{1,0:T(8,128)(2,1)} %bitcast.17), custom_call_target="tpu_custom_call" | custom-call | flops 536870912 | bytes 2097152 | tf_op jit(solution)/shard_map/pallas_call | solution.py:144
  (27 shorter events, 0.1 us)
Async XLA Ops:
  0.6 46.2 %copy-start.16 = (bf16[4096,8]{0,1:T(8,128)(2,1)S(1)}, bf16[4096,8]{0,1:T(8,128)(2,1)}, u32[]{:S(2)}) copy-start(bf16[4096,8]{0,1:T(8,128)(2,1)} %param.12) | copy-start | bytes 196612
  16.2 38.4 %copy-start.3 = (bf16[8,8,2048]{2,1,0:T(8,128)(2,1)}, bf16[8,8,2048]{2,1,0:T(8,128)(2,1)S(1)}, u32[]{:S(2)}) copy-start(bf16[8,8,2048]{2,1,0:T(8,128)(2,1)S(1)} %all_to_all.20) | copy-start | bytes 786436
  16.2 8.4 %collective-permute-start = (bf16[64,2048]{1,0:T(8,128)(2,1)S(1)}, bf16[64,2048]{1,0:T(8,128)(2,1)S(1)}, u32[]{:S(2)}, u32[]{:S(2)}) collective-permute-start(bf16[64,2048]{1,0:T(8,128)(2,1)S(1)} %bitcast.23), channel_id=1, source_target_pairs={{0,8},{8,16},{16,24},{1,9},{9,17},{17,25},{2,10},{10,18},{18,26},{... | collective-permute-start | bytes 786440 | tf_op jit(solution)/shard_map/ppermute | solution.py:496
  19.7 9.0 %collective-permute-start.4 = (bf16[64,2048]{1,0:T(8,128)(2,1)S(1)}, bf16[64,2048]{1,0:T(8,128)(2,1)S(1)}, u32[]{:S(2)}, u32[]{:S(2)}) collective-permute-start(bf16[64,2048]{1,0:T(8,128)(2,1)S(1)} %bitcast.24), channel_id=1, source_target_pairs={{8,0},{16,8},{24,16},{9,1},{17,9},{25,17},{10,2},{18,10},{26,18},{... | collective-permute-start | bytes 786440 | tf_op jit(solution)/shard_map/ppermute | solution.py:501
  24.6 30.0 %copy-start.5 = (bf16[64,2048]{1,0:T(8,128)(2,1)}, bf16[64,2048]{1,0:T(8,128)(2,1)S(1)}, u32[]{:S(2)}) copy-start(bf16[64,2048]{1,0:T(8,128)(2,1)S(1)} %collective-permute-done.refs_1_) | copy-start | bytes 786436
  24.6 20.2 %collective-permute-start.2 = (bf16[64,2048]{1,0:T(8,128)(2,1)S(1)}, bf16[64,2048]{1,0:T(8,128)(2,1)S(1)}, u32[]{:S(2)}, u32[]{:S(2)}) collective-permute-start(bf16[64,2048]{1,0:T(8,128)(2,1)S(1)} %collective-permute-done.refs_1_), channel_id=1, source_target_pairs={{8,16},{16,24},{9,17},{17,25},{10,18},{18,26},{11,19},{19,27},{12,... | collective-permute-start | bytes 786440 | tf_op jit(solution)/shard_map/ppermute | solution.py:496
  28.7 25.9 %copy-start.6 = (bf16[64,2048]{1,0:T(8,128)(2,1)}, bf16[64,2048]{1,0:T(8,128)(2,1)S(1)}, u32[]{:S(2)}) copy-start(bf16[64,2048]{1,0:T(8,128)(2,1)S(1)} %collective-permute-done.4.refs_4_) | copy-start | bytes 786436
  28.7 16.8 %collective-permute-start.5 = (bf16[64,2048]{1,0:T(8,128)(2,1)S(1)}, bf16[64,2048]{1,0:T(8,128)(2,1)S(1)}, u32[]{:S(2)}, u32[]{:S(2)}) collective-permute-start(bf16[64,2048]{1,0:T(8,128)(2,1)S(1)} %collective-permute-done.4.refs_4_), channel_id=1, source_target_pairs={{8,0},{16,8},{9,1},{17,9},{10,2},{18,10},{11,3},{19,11},{12,4},{20... | collective-permute-start | bytes 786440 | tf_op jit(solution)/shard_map/ppermute | solution.py:501
  40.3 30.0 %copy-start.2 = (bf16[8,8,2048]{2,1,0:T(8,128)(2,1)}, bf16[8,8,2048]{2,1,0:T(8,128)(2,1)S(1)}, u32[]{:S(2)}) copy-start(bf16[8,8,2048]{2,1,0:T(8,128)(2,1)S(1)} %all_to_all.21) | copy-start | bytes 786436
  40.3 9.4 %collective-permute-start.1 = (bf16[64,2048]{1,0:T(8,128)(2,1)S(1)}, bf16[64,2048]{1,0:T(8,128)(2,1)S(1)}, u32[]{:S(2)}, u32[]{:S(2)}) collective-permute-start(bf16[64,2048]{1,0:T(8,128)(2,1)S(1)} %bitcast.20), channel_id=1, source_target_pairs={{0,8},{8,16},{16,24},{1,9},{9,17},{17,25},{2,10},{10,18},{18,26},{... | collective-permute-start | bytes 786440 | tf_op jit(solution)/shard_map/ppermute | solution.py:496
  44.9 9.7 %copy-start.7 = (bf16[64,2048]{1,0:T(8,128)(2,1)}, bf16[64,2048]{1,0:T(8,128)(2,1)S(1)}, u32[]{:S(2)}) copy-start(bf16[64,2048]{1,0:T(8,128)(2,1)S(1)} %collective-permute-done.2.refs_2_) | copy-start | bytes 786436
  44.9 4.9 %collective-permute-start.3 = (bf16[64,2048]{1,0:T(8,128)(2,1)S(1)}, bf16[64,2048]{1,0:T(8,128)(2,1)S(1)}, u32[]{:S(2)}, u32[]{:S(2)}) collective-permute-start(bf16[64,2048]{1,0:T(8,128)(2,1)S(1)} %collective-permute-done.2.refs_2_), channel_id=1, source_target_pairs={{16,24},{17,25},{18,26},{19,27},{20,28},{21,29},{22,30},{23,31}} | collective-permute-start | bytes 786440 | tf_op jit(solution)/shard_map/ppermute | solution.py:496
  45.6 9.0 %copy-start.8 = (bf16[64,2048]{1,0:T(8,128)(2,1)}, bf16[64,2048]{1,0:T(8,128)(2,1)S(1)}, u32[]{:S(2)}) copy-start(bf16[64,2048]{1,0:T(8,128)(2,1)S(1)} %collective-permute-done.5.refs_5_) | copy-start | bytes 786436
  45.6 9.0 %collective-permute-start.6 = (bf16[64,2048]{1,0:T(8,128)(2,1)S(1)}, bf16[64,2048]{1,0:T(8,128)(2,1)S(1)}, u32[]{:S(2)}, u32[]{:S(2)}) collective-permute-start(bf16[64,2048]{1,0:T(8,128)(2,1)S(1)} %collective-permute-done.5.refs_5_), channel_id=1, source_target_pairs={{8,0},{9,1},{10,2},{11,3},{12,4},{13,5},{14,6},{15,7}} | collective-permute-start | bytes 786440 | tf_op jit(solution)/shard_map/ppermute | solution.py:501
  49.7 21.9 %copy-start.4 = (bf16[64,2048]{1,0:T(8,128)(2,1)}, bf16[64,2048]{1,0:T(8,128)(2,1)S(1)}, u32[]{:S(2)}) copy-start(bf16[64,2048]{1,0:T(8,128)(2,1)S(1)} %collective-permute-done.1.refs_1_) | copy-start | bytes 786436
  49.7 4.9 %copy-start.10 = (bf16[64,2048]{1,0:T(8,128)(2,1)}, bf16[64,2048]{1,0:T(8,128)(2,1)S(1)}, u32[]{:S(2)}) copy-start(bf16[64,2048]{1,0:T(8,128)(2,1)S(1)} %collective-permute-done.3.refs_3_) | copy-start | bytes 786436
  54.6 0.7 copy-start.12
  65.4 67.8 %all-to-all-start.2 = ((bf16[32,8,2048]{2,1,0:T(8,128)(2,1)}), bf16[32,8,2048]{2,1,0:T(8,128)(2,1)S(1)}, u32[]{:S(2)}, u32[]{:S(2)}) async-start(bf16[32,8,2048]{2,1,0:T(8,128)(2,1)} %bitcast.26), calls=%async_computation.2 | async-start | bytes 2097152 | tf_op jit(solution)/shard_map/all_to_all | solution.py:542
  70.3 23.9 %collective-permute-start.9 = (bf16[64,2048]{1,0:T(8,128)(2,1)S(1)}, bf16[64,2048]{1,0:T(8,128)(2,1)S(1)}, u32[]{:S(2)}, u32[]{:S(2)}) collective-permute-start(bf16[64,2048]{1,0:T(8,128)(2,1)S(1)} %bitcast.21), channel_id=1, source_target_pairs={{8,0},{16,8},{24,16},{9,1},{17,9},{25,17},{10,2},{18,10},{26,18},{... | collective-permute-start | bytes 786440 | tf_op jit(solution)/shard_map/ppermute | solution.py:501
  71.6 23.9 %collective-permute-start.7 = (bf16[64,2048]{1,0:T(8,128)(2,1)S(1)}, bf16[64,2048]{1,0:T(8,128)(2,1)S(1)}, u32[]{:S(2)}, u32[]{:S(2)}) collective-permute-start(bf16[64,2048]{1,0:T(8,128)(2,1)S(1)} %collective-permute-done.1.refs_1_), channel_id=1, source_target_pairs={{8,16},{16,24},{9,17},{17,25},{10,18},{18,26},{11,19},{19,27},{12,... | collective-permute-start | bytes 786440 | tf_op jit(solution)/shard_map/ppermute | solution.py:496
  94.3 25.6 %copy-start.9 = (bf16[64,2048]{1,0:T(8,128)(2,1)}, bf16[64,2048]{1,0:T(8,128)(2,1)S(1)}, u32[]{:S(2)}) copy-start(bf16[64,2048]{1,0:T(8,128)(2,1)S(1)} %collective-permute-done.9.refs_4_) | copy-start | bytes 786436
  94.3 16.5 %collective-permute-start.10 = (bf16[64,2048]{1,0:T(8,128)(2,1)S(1)}, bf16[64,2048]{1,0:T(8,128)(2,1)S(1)}, u32[]{:S(2)}, u32[]{:S(2)}) collective-permute-start(bf16[64,2048]{1,0:T(8,128)(2,1)S(1)} %collective-permute-done.9.refs_4_), channel_id=1, source_target_pairs={{8,0},{16,8},{9,1},{17,9},{10,2},{18,10},{11,3},{19,11},{12,4},{20... | collective-permute-start | bytes 786440 | tf_op jit(solution)/shard_map/ppermute | solution.py:501
  95.6 24.3 %copy-start.11 = (bf16[64,2048]{1,0:T(8,128)(2,1)}, bf16[64,2048]{1,0:T(8,128)(2,1)S(1)}, u32[]{:S(2)}) copy-start(bf16[64,2048]{1,0:T(8,128)(2,1)S(1)} %collective-permute-done.7.refs_2_) | copy-start | bytes 786436
  95.6 16.5 %collective-permute-start.8 = (bf16[64,2048]{1,0:T(8,128)(2,1)S(1)}, bf16[64,2048]{1,0:T(8,128)(2,1)S(1)}, u32[]{:S(2)}, u32[]{:S(2)}) collective-permute-start(bf16[64,2048]{1,0:T(8,128)(2,1)S(1)} %collective-permute-done.7.refs_2_), channel_id=1, source_target_pairs={{16,24},{17,25},{18,26},{19,27},{20,28},{21,29},{22,30},{23,31}} | collective-permute-start | bytes 786440 | tf_op jit(solution)/shard_map/ppermute | solution.py:496
  110.7 9.2 %copy-start.13 = (bf16[64,2048]{1,0:T(8,128)(2,1)}, bf16[64,2048]{1,0:T(8,128)(2,1)S(1)}, u32[]{:S(2)}) copy-start(bf16[64,2048]{1,0:T(8,128)(2,1)S(1)} %collective-permute-done.10.refs_5_) | copy-start | bytes 786436
  110.8 9.1 %collective-permute-start.11 = (bf16[64,2048]{1,0:T(8,128)(2,1)S(1)}, bf16[64,2048]{1,0:T(8,128)(2,1)S(1)}, u32[]{:S(2)}, u32[]{:S(2)}) collective-permute-start(bf16[64,2048]{1,0:T(8,128)(2,1)S(1)} %collective-permute-done.10.refs_5_), channel_id=1, source_target_pairs={{8,0},{9,1},{10,2},{11,3},{12,4},{13,5},{14,6},{15,7}} | collective-permute-start | bytes 786440 | tf_op jit(solution)/shard_map/ppermute | solution.py:501
  112.0 7.9 %copy-start.14 = (bf16[64,2048]{1,0:T(8,128)(2,1)}, bf16[64,2048]{1,0:T(8,128)(2,1)S(1)}, u32[]{:S(2)}) copy-start(bf16[64,2048]{1,0:T(8,128)(2,1)S(1)} %collective-permute-done.8.refs_3_) | copy-start | bytes 786436
  119.9 0.7 copy-start.15
  133.2 8.2 %copy-start.1 = (bf16[32,8,2048]{2,1,0:T(8,128)(2,1)}, bf16[32,8,2048]{2,1,0:T(8,128)(2,1)S(1)}, u32[]{:S(2)}) copy-start(bf16[32,8,2048]{2,1,0:T(8,128)(2,1)S(1)} %all-to-all-done.2) | copy-start | bytes 3145732
  133.2 30.4 %all-to-all-start.3 = ((bf16[32,8,2176]{2,1,0:T(8,128)(2,1)}), bf16[32,8,2176]{2,1,0:T(8,128)(2,1)S(1)}, u32[]{:S(2)}, u32[]{:S(2)}) async-start(bf16[32,8,2176]{2,1,0:T(8,128)(2,1)} %bitcast.19), calls=%async_computation.3 | async-start | bytes 2228224 | tf_op jit(solution)/shard_map/all_to_all | solution.py:542
  163.6 1.0 copy-start

commit v7 on v6

--- a/solution.py
+++ b/solution.py
@@ -19,6 +19,10 @@
 
 
 PARAMS = pltpu.CompilerParams(vmem_limit_bytes=56 * 2**20)
+
+
+def to_hbm(*arrays):
+    return [pltpu.with_memory_space_constraint(x, pltpu.HBM) for x in arrays]
 
 
 def cost(flops, moved):
@@ -93,7 +97,27 @@
         ],
         compiler_params=PARAMS,
         cost_estimate=cost(4 * count * own * features, 4 * features * own),
-    )(picks, counts, cotangent, tokens)
+    )(*to_hbm(picks, counts, cotangent, tokens))
+
+
+def by_place(arrivals, seq_n, groups):
+    blocks = [block.reshape(groups, -1, block.shape[1]) for block in arrivals.blocks]
+    _, rows, part = blocks[0].shape
+
+    def body(*refs):
+        out_ref, sems = refs[-2:]
+        arrivals.start(refs[:-2], [out_ref.at[:, k] for k in range(seq_n)], sems)
+        arrivals.wait(refs[:-2], [out_ref.at[:, k] for k in range(seq_n)], sems)
+
+    return pl.pallas_call(
+        body,
+        in_specs=[ANYWHERE] * len(blocks),
+        out_specs=IN_VMEM,
+        out_shape=shape((groups, seq_n, rows, part)),
+        scratch_shapes=[pltpu.SemaphoreType.DMA((seq_n,))],
+        compiler_params=PARAMS,
+        cost_estimate=cost(0, 4 * groups * seq_n * rows * part),
+    )(*to_hbm(*blocks))
 
 
 def scatter_rows(back, hot, seq_n, message=None):
@@ -101,55 +125,75 @@
     rows = back.shape[0]
     extra = 0 if message is None else riding(seq_n, count // message[1])
     part = back.shape[1] - extra
-    width = part // 2
+    width = part // STEPS
 
     def body(hot_ref, back_ref, *refs):
-        out_ref = refs[-1] if message is None else refs[-3]
-        chooser = jnp.concatenate([hot_ref[...]] * seq_n, axis=0)
-        out_ref[...] = mm(chooser, back_ref[...], ROWS).astype(BF16)
+        hot_v, back_v, out_v, hot_sem, in_sems, out_sems = refs[-6:]
+        out_ref = refs[0]
+        hot_copy = pltpu.make_async_copy(hot_ref, hot_v, hot_sem)
+        hot_copy.start()
+        arriving = []
+        for i in range(STEPS):
+            now = pl.ds(i * width, width + (extra if i + 1 == STEPS else 0))
+            arriving.append(pltpu.make_async_copy(back_ref.at[:, now], back_v.at[:, now], in_sems.at[i]))
+            arriving[-1].start()
+        hot_copy.wait()
+        choosers = [jnp.concatenate([hot_v[h]] * seq_n, axis=0) for h in range(pack)]
+        leaving = []
+        for i in range(STEPS):
+            arriving[i].wait()
+            for h in range(pack):
+                first = h * part + i * width
+                rows_now = back_v[:, i * width : (i + 1) * width]
+                out_v[:, first : first + width] = mm(choosers[h], rows_now, ROWS).astype(BF16)
+                now = pl.ds(first, width)
+                leaving.append(pltpu.make_async_copy(out_v.at[:, now], out_ref.at[:, now], out_sems.at[h, i]))
+                leaving[-1].start()
         if message is not None:
-            message_refs, router_ref, total_ref = refs[:-3], refs[-2], refs[-1]
-
-            @pl.when((pl.program_id(0) == 0) & (pl.program_id(1) == 0))
-            def _():
-                experts, per = router_ref.shape
-                group = count // experts
-                row = lax.broadcasted_iota(jnp.int32, (rows, experts), 0)
-                expert = lax.broadcasted_iota(jnp.int32, (rows, experts), 1)
-                mine = row % count // group == expert
-                even = jnp.where(mine & (row % 2 == 0), 1.0, 0.0).astype(BF16)
-                odd = jnp.where(mine & (row % 2 == 1), 1.0, 0.0).astype(BF16)
-                router = sum(mm(even, ref[...], ROWS) for ref in message_refs)
-                total = sum(mm(ref[...], odd, ROWS) for ref in message_refs)
-                router_ref[...] = router[:, :per]
-                total_ref[...] = jnp.sum(total[:3], axis=0, keepdims=True)
-
-    in_specs = [
-        pl.BlockSpec((None, count, own), lambda h, i: (h, 0, 0)),
-        pl.BlockSpec((rows, width), lambda h, i: (0, i)),
-    ]
-    out_specs = [pl.BlockSpec((own, width), lambda h, i: (0, h * 2 + i))]
+            router_ref, total_ref = refs[1], refs[2]
+            experts, per = router_ref.shape
+            group = count // experts
+            row = lax.broadcasted_iota(jnp.int32, (rows, experts), 0)
+            expert = lax.broadcasted_iota(jnp.int32, (rows, experts), 1)
+            mine = row % count // group == expert
+            even = jnp.where(mine & (row % 2 == 0), 1.0, 0.0).astype(BF16)
+            odd = jnp.where(mine & (row % 2 == 1), 1.0, 0.0).astype(BF16)
+            rides = [back_v[:, part + t * LANES : part + (t + 1) * LANES] for t in range(extra // LANES)]
+            router = sum(mm(even, ride, ROWS) for ride in rides)
+            total = sum(mm(ride, odd, ROWS) for ride in rides)
+            router_ref[...] = router[:, :per]
+            total_ref[...] = jnp.sum(total[:3], axis=0, keepdims=True)
+        for copy in leaving:
+            copy.wait()
+
+    out_specs = [ANYWHERE]
     out_shape = [shape((own, part * pack))]
-    args = [hot, back]
     if message is not None:
         per, experts = message
-        for t in range(extra // LANES):
-            in_specs.append(pl.BlockSpec((rows, LANES), lambda h, i, t=t: (0, part // LANES + t)))
-            args.append(back)
-        out_specs += [
-            pl.BlockSpec((experts, per), lambda h, i: (0, 0)),
-            pl.BlockSpec((1, experts), lambda h, i: (0, 0)),
-        ]
+        out_specs += [IN_VMEM] * 2
         out_shape += [shape((experts, per), F32), shape((1, experts), F32)]
     return pl.pallas_call(
         body,
-        grid=(pack, 2),
-        in_specs=in_specs,
+        in_specs=[ANYWHERE] * 2,
         out_specs=out_specs,
         out_shape=out_shape,
+        scratch_shapes=[
+            pltpu.VMEM(hot.shape, BF16),
+            pltpu.VMEM(back.shape, BF16),
+            pltpu.VMEM((own, part * pack), BF16),
+            pltpu.SemaphoreType.DMA,
+            pltpu.SemaphoreType.DMA((STEPS,)),
+            pltpu.SemaphoreType.DMA((pack, STEPS)),
+        ],
         compiler_params=PARAMS,
         cost_estimate=cost(2 * rows * own * part * pack, 2 * part * pack * own),
-    )(*args)
+    )(*to_hbm(hot, back))
+
+
+def regroup(value, group, outer, inner):
+    return jnp.concatenate(
+        [value[(o * inner + i) * group : (o * inner + i + 1) * group] for i in range(inner) for o in range(outer)]
+    )
 
 
 def first_part(rows, pack, slots):
@@ -228,6 +272,7 @@
     rows = block_rows * seq_n
     hidden_n = w_gate.shape[2]
     both = 2 * hidden_n
+    group = pack * slots
     width = part // STEPS
     total = pack * both + LANES
     n_blocks = len(arrivals.blocks)
@@ -236,7 +281,7 @@
         blocks = refs[:n_blocks]
         router_ref, gate_ref, up_ref, down_ref, threshold_ref, scale_ref = refs[n_blocks : n_blocks + 6]
         x_ref, out_ref, pre_ref, hidden_ref = refs[n_blocks + 6 : n_blocks + 10]
-        x_v, out_v, side, stack, x_sems, side_sems, stack_sems, out_sems = refs[n_blocks + 10 :]
+        pre_v, hidden_v, other_v, x_v, out_v, side, stack, x_sems, side_sems, stack_sems, out_sems = refs[n_blocks + 10 :]
         places = [x_v.at[pl.ds(k * block_rows, block_rows), :] for k in range(seq_n)]
         arrivals.start(blocks, places, x_sems)
         chunks = [side_copies(gate_ref, up_ref, router_ref, side, side_sems, pack, j, width) for j in range(STEPS)]
@@ -265,25 +310,31 @@
         hidden = gate * jax.nn.sigmoid(gate) * up * scale_ref[...] * g
         hidden = jnp.where(first_part(rows, pack, slots), hidden, 0.0)
         for h, value in enumerate(spread(hidden, pack, slots)):
-            hidden_ref[:, h * hidden_n : (h + 1) * hidden_n] = value.astype(BF16)
+            now = slice(h * hidden_n, (h + 1) * hidden_n)
+            hidden_v[:, now] = value.astype(BF16)
+            other_v[:, now] = regroup(value, group, seq_n, block_rows // group).astype(BF16)
+        pre_v[:, :hidden_n] = gate
+        pre_v[:, hidden_n:both] = up
+        pre_v[:, both:] = jnp.broadcast_to(g, (rows, LANES))
+        leaving.append(pltpu.make_async_copy(pre_v, pre_ref, out_sems.at[STEPS + 1]))
+        leaving.append(pltpu.make_async_copy(other_v, hidden_ref, out_sems.at[STEPS + 2]))
+        for copy in leaving[1:]:
+            copy.start()
         for copy in downs:
             copy.wait()
         for j in range(STEPS):
             now = slice(j * width, (j + 1) * width)
-            put_blocks(mm(hidden_ref[...], stack[:, now]).astype(BF16), out_v, now)
+            put_blocks(mm(hidden_v[...], stack[:, now]).astype(BF16), out_v, now)
             columns = pl.ds(j * width, width)
             leaving.append(pltpu.make_async_copy(out_v.at[:, :, columns], out_ref.at[:, :, columns], out_sems.at[j]))
             leaving[-1].start()
-        pre_ref[:, :hidden_n] = gate
-        pre_ref[:, hidden_n:both] = up
-        pre_ref[:, both:] = jnp.broadcast_to(g, (rows, LANES))
         for copy in leaving:
             copy.wait()
 
     return pl.pallas_call(
         body,
         in_specs=[ANYWHERE] * (n_blocks + 4) + [IN_VMEM] * 2,
-        out_specs=[ANYWHERE] * 2 + [IN_VMEM] * 2,
+        out_specs=[ANYWHERE] * 4,
         out_shape=[
             shape((rows, part)),
             shape((seq_n, block_rows, part)),
@@ -291,6 +342,9 @@
             shape((rows, pack * hidden_n)),
         ],
         scratch_shapes=[
+            pltpu.VMEM((rows, both + LANES), F32),
+            pltpu.VMEM((rows, pack * hidden_n), BF16),
+            pltpu.VMEM((rows, pack * hidden_n), BF16),
             pltpu.VMEM((rows, part), BF16),
             pltpu.VMEM((seq_n, block_rows, part), BF16),
             pltpu.VMEM((part, total), BF16),
@@ -298,11 +352,11 @@
             pltpu.SemaphoreType.DMA((seq_n,)),
             pltpu.SemaphoreType.DMA((STEPS, 2 * pack + 1)),
             pltpu.SemaphoreType.DMA((pack,)),
-            pltpu.SemaphoreType.DMA((STEPS + 1,)),
+            pltpu.SemaphoreType.DMA((STEPS + 3,)),
         ],
         compiler_params=PARAMS,
-        cost_estimate=cost(6 * rows * part * pack * hidden_n, 6 * part * pack * hidden_n),
-    )(*arrivals.blocks, router_side, w_gate, w_up, w_down, threshold.reshape(1, -1), hid_scale)
+        cost_estimate=cost(rows * part, rows * part),
+    )(*to_hbm(*arrivals.blocks, router_side, w_gate, w_up, w_down), threshold.reshape(1, -1), hid_scale)
 
 
 def split3(v):
@@ -316,41 +370,36 @@
     return LANES * -(-2 * seq_n // group)
 
 
-def expert_backward(arrivals, seq_n, exp_n, slots, pack, x, pre, router_side, w_gate, w_up, w_down, hid_scale):
-    block_rows, part = arrivals.blocks[0].shape
-    rows = block_rows * seq_n
+def expert_backward(c, seq_n, exp_n, slots, pack, x, pre, router_side, w_gate, w_up, w_down, hid_scale):
+    rows, part = c.shape
+    block_rows = rows // seq_n
     hidden_n = w_gate.shape[2]
     width = part // STEPS
     total = 2 * pack * hidden_n + LANES
     group = pack * slots
     extra = riding(seq_n, group)
     per = part * pack // (seq_n * exp_n)
-    n_blocks = len(arrivals.blocks)
 
     def body(*refs):
-        blocks = refs[:n_blocks]
-        router_ref, gate_ref, up_ref, down_ref, x_ref, pre_ref, scale_ref = refs[n_blocks : n_blocks + 7]
-        c_ref, out_ref, delta_ref = refs[n_blocks + 7 : n_blocks + 10]
-        c_v, x_v, pre_v, out_v, side, stack, columns, c_sems, x_sems, side_sems, stack_sems, out_sems = refs[
-            n_blocks + 10 :
-        ]
-        places = [c_v.at[pl.ds(k * block_rows, block_rows), :] for k in range(seq_n)]
-        arrivals.start(blocks, places, c_sems)
+        c_ref, router_ref, gate_ref, up_ref, down_ref, x_ref, pre_ref, scale_ref, out_ref, delta_ref = refs[:10]
+        c_v, x_v, pre_v, out_v, side, stack, columns, x_sems, side_sems, stack_sems, out_sems = refs[10:]
+        c_copy = pltpu.make_async_copy(c_ref, c_v, x_sems.at[2])
+        c_copy.start()
         chunks = [side_copies(gate_ref, up_ref, router_ref, side, side_sems, pack, j, width) for j in range(STEPS)]
         downs = down_copies(down_ref, stack, stack_sems, pack)
         x_copy = pltpu.make_async_copy(x_ref, x_v, x_sems.at[0])
         pre_copy = pltpu.make_async_copy(pre_ref, pre_v, x_sems.at[1])
         for copy in downs + [pre_copy] + sum(chunks, []) + [x_copy]:
             copy.start()
-        arrivals.wait(blocks, places, c_sems)
-        leaving = [pltpu.make_async_copy(c_v, c_ref, out_sems.at[STEPS])]
-        leaving[0].start()
+        c_copy.wait()
+        leaving = []
         for copy in downs:
             copy.wait()
         both = mm(c_v[...], stack[...], LAST)
         parts = [both[:, h * hidden_n : (h + 1) * hidden_n] for h in range(pack)]
         pre_copy.wait()
-        raw = jnp.where(first_part(rows, pack, slots), fold(parts, slots) * scale_ref[...], 0.0)
+        raw = regroup(fold(parts, slots), group, block_rows // group, seq_n)
+        raw = jnp.where(first_part(rows, pack, slots), raw * scale_ref[...], 0.0)
         gate = pre_v[:, :hidden_n]
         up = pre_v[:, hidden_n : 2 * hidden_n]
         g = pre_v[:, 2 * hidden_n : 2 * hidden_n + 1]
@@ -418,10 +467,9 @@
 
     return pl.pallas_call(
         body,
-        in_specs=[ANYWHERE] * (n_blocks + 6) + [IN_VMEM],
-        out_specs=[ANYWHERE] * 2 + [IN_VMEM],
+        in_specs=[ANYWHERE] * 7 + [IN_VMEM],
+        out_specs=[ANYWHERE, IN_VMEM],
         out_shape=[
-            shape((rows, part)),
             shape((seq_n, block_rows, part + extra)),
             shape((rows, total)),
         ],
@@ -433,15 +481,14 @@
             pltpu.VMEM((part, total), BF16),
             pltpu.VMEM((pack * hidden_n, part), BF16),
             pltpu.VMEM((rows, LANES), BF16),
-            pltpu.SemaphoreType.DMA((seq_n,)),
-            pltpu.SemaphoreType.DMA((2,)),
+            pltpu.SemaphoreType.DMA((3,)),
             pltpu.SemaphoreType.DMA((STEPS, 2 * pack + 1)),
             pltpu.SemaphoreType.DMA((pack,)),
-            pltpu.SemaphoreType.DMA((STEPS + 1,)),
+            pltpu.SemaphoreType.DMA((STEPS,)),
         ],
         compiler_params=PARAMS,
         cost_estimate=cost(6 * rows * part * pack * hidden_n, 6 * part * pack * hidden_n),
-    )(*arrivals.blocks, router_side, w_gate, w_up, w_down, x, pre, hid_scale)
+    )(*to_hbm(c, router_side, w_gate, w_up, w_down, x, pre), hid_scale)
 
 
 def side_grads(x, delta, pack, hidden_n):
@@ -466,7 +513,7 @@
         out_shape=[shape((pack, part, hidden_n), F32)] * 2,
         compiler_params=PARAMS,
         cost_estimate=cost(4 * rows * part * pack * hidden_n, 8 * part * pack * hidden_n),
-    )(x, delta)
+    )(*to_hbm(x, delta))
     return gate.reshape(1, part * pack, hidden_n), up.reshape(1, part * pack, hidden_n)
 
 
@@ -488,7 +535,7 @@
         out_shape=shape((1, hidden_n, part * pack), F32),
         compiler_params=PARAMS,
         cost_estimate=cost(2 * rows * part * pack * hidden_n, 4 * part * pack * hidden_n),
-    )(c, hidden)
+    )(*to_hbm(c, hidden))
 
 
 def up_line(block, n, first=0, last=None):
@@ -501,20 +548,18 @@
     return lax.ppermute(block, "seq", [(s, s - 1) for s in range(first, last)])
 
 
-def line_gather(block, n):
+def line_gather(block, n, hold=()):
     ups, downs = [], []
     up = down = block
     for j in range(1, n):
         up = up_line(up, n, j - 1)
         down = down_line(down, n, 1, n - j + 1)
+        if j == 1 and hold:
+            up, down, *_ = lax.optimization_barrier((up, down, *hold))
         ups.append(up)
         downs.append(down)
     plan = [(0, 0, 0)] + [(k, 2 * n - 1 - k, k) for k in range(1, n)]
     return Arrivals([block] + ups + downs, plan)
-
-
-def after(value, *others):
-    return lax.optimization_barrier((value, *others))[0]
 
 
 def on_device(tokens, cotangent, router, threshold, w_gate, w_up, w_down, hid_scale, picks, counts):
@@ -542,20 +587,23 @@
         return lax.all_to_all(parts, BOTH, split_axis=0, concat_axis=0, tiled=True).reshape(-1, parts.shape[2])
 
     c_rows, x_rows, hot = choose_rows(tokens, cotangent, chosen, counts, pack)
-    x_in = line_gather(to_experts(x_rows), seq_n)
-    c_in = line_gather(to_experts(after(c_rows, x_in.blocks[1])), seq_n)
+    c_in = line_gather(c_rows, seq_n)
+    c_sent = by_place(c_in, seq_n, experts)
+    x_in = line_gather(to_experts(x_rows), seq_n, (c_sent,))
+    c = lax.all_to_all(c_sent, "exp", split_axis=0, concat_axis=0, tiled=True)
+    c = c.reshape(-1, c.shape[-1])
     halves = list(router.reshape(pack, features // pack, experts))
     router_side = jnp.concatenate(halves + halves, axis=1)
     router_side = jnp.pad(router_side, ((0, 0), (0, LANES - router_side.shape[1])))
 
-    x_in.blocks[0] = after(x_in.blocks[0], c_in.blocks[1])
     x, out, pre, hidden = expert_forward(
         x_in, seq_n, slots, experts, pack, router_side, threshold, w_gate, w_up, w_down, hid_scale
     )
     out = to_owners(out)
-    c, back, delta = expert_backward(
-        c_in, seq_n, exp_n, slots, pack, x, pre, router_side, w_gate, w_up, w_down, hid_scale
+    back, delta = expert_backward(
+        c, seq_n, exp_n, slots, pack, x, pre, router_side, w_gate, w_up, w_down, hid_scale
     )
+    back, out = lax.optimization_barrier((back, out))
     back = to_owners(back)
     down_grad = down_grads(c, hidden, pack, hidden_n)
     gate_grad, up_grad = side_grads(x, delta, pack, hidden_n)

time: 170 us -> 141 us (0.83)
  blocking collectives: 22.4 us -> 0 us
  waiting for transfers between devices: 68.7 us -> 53.9 us
  starting transfers between devices: 26.2 us -> 34.4 us
    ppermute x6, waiting for transfers between devices: 52.6 us -> 21.4 us  [down_line(): return lax.ppermute(block, 'seq', [(s, s - 1) for s in range(first, last)])]
    all_to_all x2 -> x0, blocking collectives: 22.4 us -> none  [to_experts(): lax.all_to_all(block, 'exp', split_axis=0, concat_axis=0, tiled=True)]
    all_to_all x2, waiting for transfers between devices: 10.9 us -> 25.7 us  [to_owners(): lax.all_to_all(parts, BOTH, split_axis=0, concat_axis=0, tiled=True)]
    all_to_all x0 -> x2, starting transfers between devices: none -> 7.31 us  [the longest x1 3.73 us: to_experts(): lax.all_to_all(block, 'exp', split_axis=0, concat_axis=0, tiled=True)]
    all_to_all x0 -> x2, waiting for transfers between devices: none -> 1.75 us  [the longest x1 1.75 us: to_experts(): lax.all_to_all(block, 'exp', split_axis=0, concat_axis=0, tiled=True)]
    pallas_call x3 -> x4, Pallas kernels: 21.5 us -> 21.6 us  [the longest x1 12.5 us: expert_backward(): pl.pallas_call(body, in_specs=[ANYWHERE] * 7 + [IN_VMEM], out_specs=[ANYW...]
  transfers between devices with their start and end apart: 14 -> 16, of which waited for: 8 -> 10; matrix products, arithmetic and copies ran while one was open for 1% -> 1% of each run, Pallas kernels for 17% -> 28%
where the time goes in v7:
time: 141 us; the launch traced here: 140 us
  waiting for transfers between devices  53.9 us (38%)
  Pallas kernels  46.4 us (33%)
  starting transfers between devices  34.4 us (24%)
  local copies, waits for them, and re-layouts  3.79 us (3%)
    all_to_all x2, waiting for transfers between devices, to_owners(): lax.all_to_all(parts, BOTH, split_axis=0, concat_axis=0, tiled=True)  25.7 us
    ppermute x6, waiting for transfers between devices, down_line(): return lax.ppermute(block, 'seq', [(s, s - 1) for s in range(first, last)])  21.4 us
    pallas_call x1, Pallas kernels, expert_backward(): pl.pallas_call(body, in_specs=[ANYWHERE] * 7 + [IN_VMEM], out_specs=[ANYW...  12.5 us
    ppermute x6, starting transfers between devices, up_line(): return lax.ppermute(block, 'seq', [(s, s + 1) for s in range(first, last)])  12.3 us
    pallas_call x1, Pallas kernels, expert_forward(): pl.pallas_call(body, in_specs=[ANYWHERE] * (n_blocks + 4) + [IN_VMEM] * 2...  9.01 us
    ppermute x6, starting transfers between devices, down_line(): return lax.ppermute(block, 'seq', [(s, s - 1) for s in range(first, last)])  7.71 us
    all_to_all x2, starting transfers between devices, to_owners(): lax.all_to_all(parts, BOTH, split_axis=0, concat_axis=0, tiled=True)  7.1 us
    pallas_call x2, Pallas kernels, scatter_rows(): pl.pallas_call(body, in_specs=[ANYWHERE] * 2, out_specs=out_specs, out_sh...  6.91 us
  transfers between devices with their start and end apart: 16, of which 10 were waited for; matrix products, arithmetic and copies ran while one was open for 1% of the time, Pallas kernels for 28%

profile of v7, /device:TPU:0, one launch (start us, length us, event | category | flops | bytes accessed | tf_op | source)
XLA Modules:
  0.0 139.7 jit_solution(9649427895543769280)
XLA Ops:
  0.6 3.4 %shard_map.153 = (bf16[64,2048]{1,0:T(8,128)(2,1)}, bf16[64,2048]{1,0:T(8,128)(2,1)}, bf16[2,64,256]{2,1,0:T(8,128)(2,1)}) custom-call(s32[4,8]{1,0:T(4,128)} %bitcast.39, s32[1,8]{1,0:T(1,128)} %counts_ref.1, bf16[256,4096]{1,0:T(8,128)(2,1)} %c_ref.1, bf16[256,4096]{1,0:T(8,128)(2,1)} %x_ref.1), custom_call_target="tpu_custom_call" | custom-call | flops 268435456 | bytes 4194304 | tf_op jit(solution)/shard_map/pallas_call | solution.py:85
  4.1 0.0 copy-start.16
  4.1 5.1 %collective-permute-start = (bf16[64,2048]{1,0:T(8,128)(2,1)}, bf16[64,2048]{1,0:T(8,128)(2,1)S(1)}, u32[]{:S(2)}, u32[]{:S(2)}) collective-permute-start(bf16[64,2048]{1,0:T(8,128)(2,1)} %get-tuple-element.26), channel_id=1, source_target_pairs={{0,8},{8,16},{16,24},{1,9},{9,17},{17,25},{2,10},{10,18},{18,26},{... | collective-permute-start | bytes 786440 | tf_op jit(solution)/shard_map/ppermute | solution.py:543
  9.2 1.3 collective-permute-start.3
  10.5 4.5 %collective-permute-done = bf16[64,2048]{1,0:T(8,128)(2,1)S(1)} collective-permute-done((bf16[64,2048]{1,0:T(8,128)(2,1)}, bf16[64,2048]{1,0:T(8,128)(2,1)S(1)}, u32[]{:S(2)}, u32[]{:S(2)}) %collective-permute-start) | collective-permute-done | bytes 262176 | tf_op jit(solution)/shard_map/ppermute | solution.py:543
  15.0 0.7 collective-permute-start.1
  15.7 3.3 %collective-permute-done.3 = bf16[64,2048]{1,0:T(8,128)(2,1)S(1)} collective-permute-done((bf16[64,2048]{1,0:T(8,128)(2,1)}, bf16[64,2048]{1,0:T(8,128)(2,1)S(1)}, u32[]{:S(2)}, u32[]{:S(2)}) %collective-permute-start.3) | collective-permute-done | bytes 262176 | tf_op jit(solution)/shard_map/ppermute | solution.py:548
  19.1 1.3 collective-permute-start.4
  20.3 3.7 %all-to-all-start.1 = ((bf16[8,8,2048]{2,1,0:T(8,128)(2,1)}), bf16[8,8,2048]{2,1,0:T(8,128)(2,1)S(1)}, u32[]{:S(2)}, u32[]{:S(2)}) async-start(bf16[8,8,2048]{2,1,0:T(8,128)(2,1)} %bitcast.31), calls=%async_computation.1 | async-start | bytes 524288 | tf_op jit(solution)/shard_map/all_to_all | solution.py:583
  24.1 0.0 copy-start.12
  24.1 0.7 collective-permute-start.2
  24.8 3.2 %collective-permute-done.4 = bf16[64,2048]{1,0:T(8,128)(2,1)S(1)} collective-permute-done((bf16[64,2048]{1,0:T(8,128)(2,1)S(1)}, bf16[64,2048]{1,0:T(8,128)(2,1)S(1)}, u32[]{:S(2)}, u32[]{:S(2)}) %collective-permute-start.4) | collective-permute-done | bytes 262176 | tf_op jit(solution)/shard_map/ppermute | solution.py:548
  28.0 1.3 collective-permute-start.5
  29.3 1.7 %all-to-all-done.1 = bf16[8,8,2048]{2,1,0:T(8,128)(2,1)S(1)} async-done(((bf16[8,8,2048]{2,1,0:T(8,128)(2,1)}), bf16[8,8,2048]{2,1,0:T(8,128)(2,1)S(1)}, u32[]{:S(2)}, u32[]{:S(2)}) %all-to-all-start.1) | async-done | bytes 262176 | tf_op jit(solution)/shard_map/all_to_all | solution.py:583
  31.0 4.6 %collective-permute-start.6 = (bf16[64,2048]{1,0:T(8,128)(2,1)S(1)}, bf16[64,2048]{1,0:T(8,128)(2,1)S(1)}, u32[]{:S(2)}, u32[]{:S(2)}) collective-permute-start(bf16[64,2048]{1,0:T(8,128)(2,1)S(1)} %bitcast.27), channel_id=1, source_target_pairs={{0,8},{8,16},{16,24},{1,9},{9,17},{17,25},{2,10},{10,18},{18,26},{... | collective-permute-start | bytes 786440 | tf_op jit(solution)/shard_map/ppermute | solution.py:543
  35.6 1.3 collective-permute-start.7
  36.9 0.0 collective-permute-done.2
  36.9 0.0 collective-permute-done.5
  37.0 0.6 copy-done.14
  37.6 0.1 copy-done.15
  37.7 2.2 %shard_map.154 = bf16[8,4,8,2048]{3,2,1,0:T(8,128)(2,1)} custom-call(bf16[8,8,2048]{2,1,0:T(8,128)(2,1)} %bitcast.32, bf16[8,8,2048]{2,1,0:T(8,128)(2,1)} %bitcast.33, bf16[8,8,2048]{2,1,0:T(8,128)(2,1)} %bitcast.35, bf16[8,8,2048]{2,1,0:T(8,128)(2,1)} %bitcast.37, bf16[8,8,2048]{2,1,0:T(8,128)(2,1)} %bitcast.34, bf16[8,8,2048]{2,1,0:T(8,128)(2,1)} %bitcast.36, ...), custom_call_target="tpu_custom_call" | custom-call | bytes 2097152 | tf_op jit(solution)/shard_map/pallas_call | solution.py:112
  39.9 0.6 collective-permute-done.6.refs_1_
  40.5 4.3 %collective-permute-done.7.refs_4_ = bf16[64,2048]{1,0:T(8,128)(2,1)S(1)} collective-permute-done((bf16[64,2048]{1,0:T(8,128)(2,1)S(1)}, bf16[64,2048]{1,0:T(8,128)(2,1)S(1)}, u32[]{:S(2)}, u32[]{:S(2)}) %collective-permute-start.7) | collective-permute-done | bytes 262176 | tf_op jit(solution)/shard_map/ppermute | solution.py:548
  44.7 1.3 collective-permute-start.10
  46.0 0.7 collective-permute-start.8
  46.7 3.6 %all-to-all-start = ((bf16[8,4,8,2048]{3,2,1,0:T(8,128)(2,1)}), bf16[8,4,8,2048]{3,2,1,0:T(8,128)(2,1)S(1)}, u32[]{:S(2)}, u32[]{:S(2)}) async-start(bf16[8,4,8,2048]{3,2,1,0:T(8,128)(2,1)} %shard_map.154), calls=%async_computation | async-start | bytes 2097152 | tf_op jit(solution)/shard_map/all_to_all | solution.py:593
  50.3 2.7 %collective-permute-done.10.refs_5_ = bf16[64,2048]{1,0:T(8,128)(2,1)S(1)} collective-permute-done((bf16[64,2048]{1,0:T(8,128)(2,1)S(1)}, bf16[64,2048]{1,0:T(8,128)(2,1)S(1)}, u32[]{:S(2)}, u32[]{:S(2)}) %collective-permute-start.10) | collective-permute-done | bytes 262176 | tf_op jit(solution)/shard_map/ppermute | solution.py:548
  53.0 1.3 collective-permute-start.11
  54.3 0.0 collective-permute-done.8.refs_2_
  54.3 0.7 collective-permute-start.9
  55.0 0.3 copy.21
  55.3 0.9 pad.4.refs_7_.refs_1_
  56.2 7.9 %collective-permute-done.11.refs_6_ = bf16[64,2048]{1,0:T(8,128)(2,1)S(1)} collective-permute-done((bf16[64,2048]{1,0:T(8,128)(2,1)S(1)}, bf16[64,2048]{1,0:T(8,128)(2,1)S(1)}, u32[]{:S(2)}, u32[]{:S(2)}) %collective-permute-start.11) | collective-permute-done | bytes 262176 | tf_op jit(solution)/shard_map/ppermute | solution.py:548
  64.1 0.0 collective-permute-done.9.refs_3_
  64.1 0.7 copy-done.8
  64.8 0.1 copy-done.9
  64.9 9.0 %shard_map.155 = (bf16[256,2048]{1,0:T(8,128)(2,1)}, bf16[4,64,2048]{2,1,0:T(8,128)(2,1)}, f32[256,896]{1,0:T(8,128)}, bf16[256,768]{1,0:T(8,128)(2,1)}) custom-call(bf16[64,2048]{1,0:T(8,128)(2,1)} %bitcast.29, bf16[64,2048]{1,0:T(8,128)(2,1)} %copy-done.4, bf16[64,2048]{1,0:T(8,128)(2,1)} %copy-done.7, bf16[64,2048]{1,0:T(8,128)(2,1)} %copy-done.9, ...), custom_call_target="tpu_custom_call" | custom-call | flops 524288 | bytes 524288 | tf_op jit(solution)/shard_map/pallas_call | solution.py:334
  73.9 0.0 copy-start
  74.0 3.3 %all-to-all-start.2 = ((bf16[32,8,2048]{2,1,0:T(8,128)(2,1)}), bf16[32,8,2048]{2,1,0:T(8,128)(2,1)S(1)}, u32[]{:S(2)}, u32[]{:S(2)}) async-start(bf16[32,8,2048]{2,1,0:T(8,128)(2,1)} %bitcast.30), calls=%async_computation.2 | async-start | bytes 2097152 | tf_op jit(solution)/shard_map/all_to_all | solution.py:587
  77.3 12.5 %shard_map.156 = (bf16[4,64,2176]{2,1,0:T(8,128)(2,1)}, bf16[256,1664]{1,0:T(8,128)(2,1)}) custom-call(bf16[256,2048]{1,0:T(8,128)(2,1)} %bitcast.22, bf16[2048,128]{1,0:T(8,128)(2,1)} %pad.4.refs_7_.refs_1_, bf16[1,4096,384]{2,1,0:T(8,128)(2,1)} %refs_2_.1, bf16[1,4096,384]{2,1,0:T(8,128)(2,1)} %refs_3_.1, bf16[1,384,4096]{2,1,0:T(8,128)(2,1)} %refs_4_.1, ...), custom_call_target="tpu_custom_call" | custom-call | flops 2415919104 | bytes 9437184 | tf_op jit(solution)/shard_map/pallas_call | solution.py:468
  89.8 13.7 %all-to-all-done.2 = bf16[32,8,2048]{2,1,0:T(8,128)(2,1)S(1)} async-done(((bf16[32,8,2048]{2,1,0:T(8,128)(2,1)}), bf16[32,8,2048]{2,1,0:T(8,128)(2,1)S(1)}, u32[]{:S(2)}, u32[]{:S(2)}) %all-to-all-start.2) | async-done | bytes 1048608 | tf_op jit(solution)/shard_map/all_to_all | solution.py:587
  103.5 3.8 %all-to-all-start.3 = ((bf16[32,8,2176]{2,1,0:T(8,128)(2,1)}), bf16[32,8,2176]{2,1,0:T(8,128)(2,1)S(1)}, u32[]{:S(2)}, u32[]{:S(2)}) async-start(bf16[32,8,2176]{2,1,0:T(8,128)(2,1)} %bitcast.26), calls=%async_computation.3 | async-start | bytes 2228224 | tf_op jit(solution)/shard_map/all_to_all | solution.py:587
  107.3 5.5 %shard_map.160 = f32[1,384,4096]{2,1,0:T(8,128)} custom-call(bf16[256,2048]{1,0:T(8,128)(2,1)} %bitcast.23, bf16[256,768]{1,0:T(8,128)(2,1)} %get-tuple-element.42.hidden_ref), custom_call_target="tpu_custom_call" | custom-call | flops 805306368 | bytes 6291456 | tf_op jit(solution)/shard_map/pallas_call | solution.py:527
  112.8 6.9 %shard_map.159 = (f32[2,2048,384]{2,1,0:T(8,128)}, f32[2,2048,384]{2,1,0:T(8,128)}) custom-call(bf16[256,2048]{1,0:T(8,128)(2,1)} %get-tuple-element.30.refs_5_.x_ref, bf16[256,1664]{1,0:T(8,128)(2,1)} %get-tuple-element.39.delta_ref), custom_call_target="tpu_custom_call" | custom-call | flops 1610612736 | bytes 12582912 | tf_op jit(solution)/shard_map/pallas_call | solution.py:505
  119.7 3.2 %shard_map.157 = bf16[256,4096]{1,0:T(8,128)(2,1)} custom-call(bf16[2,64,256]{2,1,0:T(8,128)(2,1)} %get-tuple-element.25.hot_ref, bf16[256,2048]{1,0:T(8,128)(2,1)} %bitcast.24), custom_call_target="tpu_custom_call" | custom-call | flops 536870912 | bytes 2097152 | tf_op jit(solution)/shard_map/pallas_call | solution.py:175
  122.8 12.0 %all-to-all-done.3 = bf16[32,8,2176]{2,1,0:T(8,128)(2,1)S(1)} async-done(((bf16[32,8,2176]{2,1,0:T(8,128)(2,1)}), bf16[32,8,2176]{2,1,0:T(8,128)(2,1)S(1)}, u32[]{:S(2)}, u32[]{:S(2)}) %all-to-all-start.3) | async-done | bytes 1114144 | tf_op jit(solution)/shard_map/all_to_all | solution.py:587
  134.8 1.0 copy-done.2
  135.8 3.8 %shard_map.158 = (bf16[256,4096]{1,0:T(8,128)(2,1)}, f32[8,128]{1,0:T(8,128)}, f32[1,8]{1,0:T(1,128)}) custom-call(bf16[2,64,256]{2,1,0:T(8,128)(2,1)} %get-tuple-element.25.hot_ref, bf16[256,2176]{1,0:T(8,128)(2,1)} %bitcast.25), custom_call_target="tpu_custom_call" | custom-call | flops 536870912 | bytes 2097152 | tf_op jit(solution)/shard_map/pallas_call | solution.py:175
  (30 shorter events, 0.1 us)
Async XLA Ops:
  4.1 50.9 %copy-start.16 = (bf16[4096,8]{0,1:T(8,128)(2,1)S(1)}, bf16[4096,8]{0,1:T(8,128)(2,1)}, u32[]{:S(2)}) copy-start(bf16[4096,8]{0,1:T(8,128)(2,1)} %param.12) | copy-start | bytes 196612
  4.1 10.9 %collective-permute-start = (bf16[64,2048]{1,0:T(8,128)(2,1)}, bf16[64,2048]{1,0:T(8,128)(2,1)S(1)}, u32[]{:S(2)}, u32[]{:S(2)}) collective-permute-start(bf16[64,2048]{1,0:T(8,128)(2,1)} %get-tuple-element.26), channel_id=1, source_target_pairs={{0,8},{8,16},{16,24},{1,9},{9,17},{17,25},{2,10},{10,18},{18,26},{... | collective-permute-start | bytes 786440 | tf_op jit(solution)/shard_map/ppermute | solution.py:543
  9.2 9.9 %collective-permute-start.3 = (bf16[64,2048]{1,0:T(8,128)(2,1)}, bf16[64,2048]{1,0:T(8,128)(2,1)S(1)}, u32[]{:S(2)}, u32[]{:S(2)}) collective-permute-start(bf16[64,2048]{1,0:T(8,128)(2,1)} %get-tuple-element.26), channel_id=1, source_target_pairs={{8,0},{16,8},{24,16},{9,1},{17,9},{25,17},{10,2},{18,10},{26,18},{... | collective-permute-start | bytes 786440 | tf_op jit(solution)/shard_map/ppermute | solution.py:548
  15.0 21.9 %copy-start.10 = (bf16[64,2048]{1,0:T(8,128)(2,1)}, bf16[64,2048]{1,0:T(8,128)(2,1)S(1)}, u32[]{:S(2)}) copy-start(bf16[64,2048]{1,0:T(8,128)(2,1)S(1)} %collective-permute-done) | copy-start | bytes 786436
  15.0 9.0 %collective-permute-start.1 = (bf16[64,2048]{1,0:T(8,128)(2,1)S(1)}, bf16[64,2048]{1,0:T(8,128)(2,1)S(1)}, u32[]{:S(2)}, u32[]{:S(2)}) collective-permute-start(bf16[64,2048]{1,0:T(8,128)(2,1)S(1)} %collective-permute-done), channel_id=1, source_target_pairs={{8,16},{16,24},{9,17},{17,25},{10,18},{18,26},{11,19},{19,27},{12,... | collective-permute-start | bytes 786440 | tf_op jit(solution)/shard_map/ppermute | solution.py:543
  19.0 17.9 %copy-start.11 = (bf16[64,2048]{1,0:T(8,128)(2,1)}, bf16[64,2048]{1,0:T(8,128)(2,1)S(1)}, u32[]{:S(2)}) copy-start(bf16[64,2048]{1,0:T(8,128)(2,1)S(1)} %collective-permute-done.3) | copy-start | bytes 786436
  19.1 8.9 %collective-permute-start.4 = (bf16[64,2048]{1,0:T(8,128)(2,1)S(1)}, bf16[64,2048]{1,0:T(8,128)(2,1)S(1)}, u32[]{:S(2)}, u32[]{:S(2)}) collective-permute-start(bf16[64,2048]{1,0:T(8,128)(2,1)S(1)} %collective-permute-done.3), channel_id=1, source_target_pairs={{8,0},{16,8},{9,1},{17,9},{10,2},{18,10},{11,3},{19,11},{12,4},{20... | collective-permute-start | bytes 786440 | tf_op jit(solution)/shard_map/ppermute | solution.py:548
  20.3 10.7 %all-to-all-start.1 = ((bf16[8,8,2048]{2,1,0:T(8,128)(2,1)}), bf16[8,8,2048]{2,1,0:T(8,128)(2,1)S(1)}, u32[]{:S(2)}, u32[]{:S(2)}) async-start(bf16[8,8,2048]{2,1,0:T(8,128)(2,1)} %bitcast.31), calls=%async_computation.1 | async-start | bytes 524288 | tf_op jit(solution)/shard_map/all_to_all | solution.py:583
  24.1 12.9 %copy-start.12 = (bf16[64,2048]{1,0:T(8,128)(2,1)}, bf16[64,2048]{1,0:T(8,128)(2,1)S(1)}, u32[]{:S(2)}) copy-start(bf16[64,2048]{1,0:T(8,128)(2,1)S(1)} %collective-permute-done.1) | copy-start | bytes 786436
  24.1 12.8 %collective-permute-start.2 = (bf16[64,2048]{1,0:T(8,128)(2,1)S(1)}, bf16[64,2048]{1,0:T(8,128)(2,1)S(1)}, u32[]{:S(2)}, u32[]{:S(2)}) collective-permute-start(bf16[64,2048]{1,0:T(8,128)(2,1)S(1)} %collective-permute-done.1), channel_id=1, source_target_pairs={{16,24},{17,25},{18,26},{19,27},{20,28},{21,29},{22,30},{23,31}} | collective-permute-start | bytes 786440 | tf_op jit(solution)/shard_map/ppermute | solution.py:543
  28.0 9.0 %copy-start.13 = (bf16[64,2048]{1,0:T(8,128)(2,1)}, bf16[64,2048]{1,0:T(8,128)(2,1)S(1)}, u32[]{:S(2)}) copy-start(bf16[64,2048]{1,0:T(8,128)(2,1)S(1)} %collective-permute-done.4) | copy-start | bytes 786436
  28.0 8.9 %collective-permute-start.5 = (bf16[64,2048]{1,0:T(8,128)(2,1)S(1)}, bf16[64,2048]{1,0:T(8,128)(2,1)S(1)}, u32[]{:S(2)}, u32[]{:S(2)}) collective-permute-start(bf16[64,2048]{1,0:T(8,128)(2,1)S(1)} %collective-permute-done.4), channel_id=1, source_target_pairs={{8,0},{9,1},{10,2},{11,3},{12,4},{13,5},{14,6},{15,7}} | collective-permute-start | bytes 786440 | tf_op jit(solution)/shard_map/ppermute | solution.py:548
  31.0 25.2 %copy-start.3 = (bf16[8,8,2048]{2,1,0:T(8,128)(2,1)}, bf16[8,8,2048]{2,1,0:T(8,128)(2,1)S(1)}, u32[]{:S(2)}) copy-start(bf16[8,8,2048]{2,1,0:T(8,128)(2,1)S(1)} %all-to-all-done.1) | copy-start | bytes 786436
  31.0 9.4 %collective-permute-start.6 = (bf16[64,2048]{1,0:T(8,128)(2,1)S(1)}, bf16[64,2048]{1,0:T(8,128)(2,1)S(1)}, u32[]{:S(2)}, u32[]{:S(2)}) collective-permute-start(bf16[64,2048]{1,0:T(8,128)(2,1)S(1)} %bitcast.27), channel_id=1, source_target_pairs={{0,8},{8,16},{16,24},{1,9},{9,17},{17,25},{2,10},{10,18},{18,26},{... | collective-permute-start | bytes 786440 | tf_op jit(solution)/shard_map/ppermute | solution.py:543
  35.6 9.2 %collective-permute-start.7 = (bf16[64,2048]{1,0:T(8,128)(2,1)S(1)}, bf16[64,2048]{1,0:T(8,128)(2,1)S(1)}, u32[]{:S(2)}, u32[]{:S(2)}) collective-permute-start(bf16[64,2048]{1,0:T(8,128)(2,1)S(1)} %bitcast.28), channel_id=1, source_target_pairs={{8,0},{16,8},{24,16},{9,1},{17,9},{25,17},{10,2},{18,10},{26,18},{... | collective-permute-start | bytes 786440 | tf_op jit(solution)/shard_map/ppermute | solution.py:548
  36.9 0.7 copy-start.14
  36.9 0.8 copy-start.15
  40.5 23.6 %copy-start.4 = (bf16[64,2048]{1,0:T(8,128)(2,1)}, bf16[64,2048]{1,0:T(8,128)(2,1)S(1)}, u32[]{:S(2)}) copy-start(bf16[64,2048]{1,0:T(8,128)(2,1)S(1)} %collective-permute-done.6.refs_1_) | copy-start | bytes 786436
  44.7 19.4 %copy-start.5 = (bf16[64,2048]{1,0:T(8,128)(2,1)}, bf16[64,2048]{1,0:T(8,128)(2,1)S(1)}, u32[]{:S(2)}) copy-start(bf16[64,2048]{1,0:T(8,128)(2,1)S(1)} %collective-permute-done.7.refs_4_) | copy-start | bytes 786436
  44.7 8.3 %collective-permute-start.10 = (bf16[64,2048]{1,0:T(8,128)(2,1)S(1)}, bf16[64,2048]{1,0:T(8,128)(2,1)S(1)}, u32[]{:S(2)}, u32[]{:S(2)}) collective-permute-start(bf16[64,2048]{1,0:T(8,128)(2,1)S(1)} %collective-permute-done.7.refs_4_), channel_id=1, source_target_pairs={{8,0},{16,8},{9,1},{17,9},{10,2},{18,10},{11,3},{19,11},{12,4},{20... | collective-permute-start | bytes 786440 | tf_op jit(solution)/shard_map/ppermute | solution.py:548
  46.0 8.3 %collective-permute-start.8 = (bf16[64,2048]{1,0:T(8,128)(2,1)S(1)}, bf16[64,2048]{1,0:T(8,128)(2,1)S(1)}, u32[]{:S(2)}, u32[]{:S(2)}) collective-permute-start(bf16[64,2048]{1,0:T(8,128)(2,1)S(1)} %collective-permute-done.6.refs_1_), channel_id=1, source_target_pairs={{8,16},{16,24},{9,17},{17,25},{10,18},{18,26},{11,19},{19,27},{12,... | collective-permute-start | bytes 786440 | tf_op jit(solution)/shard_map/ppermute | solution.py:543
  46.7 27.2 %all-to-all-start = ((bf16[8,4,8,2048]{3,2,1,0:T(8,128)(2,1)}), bf16[8,4,8,2048]{3,2,1,0:T(8,128)(2,1)S(1)}, u32[]{:S(2)}, u32[]{:S(2)}) async-start(bf16[8,4,8,2048]{3,2,1,0:T(8,128)(2,1)} %shard_map.154), calls=%async_computation | async-start | bytes 2097152 | tf_op jit(solution)/shard_map/all_to_all | solution.py:593
  53.0 11.1 %copy-start.6 = (bf16[64,2048]{1,0:T(8,128)(2,1)}, bf16[64,2048]{1,0:T(8,128)(2,1)S(1)}, u32[]{:S(2)}) copy-start(bf16[64,2048]{1,0:T(8,128)(2,1)S(1)} %collective-permute-done.10.refs_5_) | copy-start | bytes 786436
  53.0 11.1 %collective-permute-start.11 = (bf16[64,2048]{1,0:T(8,128)(2,1)S(1)}, bf16[64,2048]{1,0:T(8,128)(2,1)S(1)}, u32[]{:S(2)}, u32[]{:S(2)}) collective-permute-start(bf16[64,2048]{1,0:T(8,128)(2,1)S(1)} %collective-permute-done.10.refs_5_), channel_id=1, source_target_pairs={{8,0},{9,1},{10,2},{11,3},{12,4},{13,5},{14,6},{15,7}} | collective-permute-start | bytes 786440 | tf_op jit(solution)/shard_map/ppermute | solution.py:548
  54.3 9.8 %copy-start.7 = (bf16[64,2048]{1,0:T(8,128)(2,1)}, bf16[64,2048]{1,0:T(8,128)(2,1)S(1)}, u32[]{:S(2)}) copy-start(bf16[64,2048]{1,0:T(8,128)(2,1)S(1)} %collective-permute-done.8.refs_2_) | copy-start | bytes 786436
  54.3 9.8 %collective-permute-start.9 = (bf16[64,2048]{1,0:T(8,128)(2,1)S(1)}, bf16[64,2048]{1,0:T(8,128)(2,1)S(1)}, u32[]{:S(2)}, u32[]{:S(2)}) collective-permute-start(bf16[64,2048]{1,0:T(8,128)(2,1)S(1)} %collective-permute-done.8.refs_2_), channel_id=1, source_target_pairs={{16,24},{17,25},{18,26},{19,27},{20,28},{21,29},{22,30},{23,31}} | collective-permute-start | bytes 786440 | tf_op jit(solution)/shard_map/ppermute | solution.py:543
  64.1 0.7 copy-start.8
  64.1 0.8 copy-start.9
  73.9 3.3 %copy-start = (bf16[8,4,8,2048]{3,2,1,0:T(8,128)(2,1)}, bf16[8,4,8,2048]{3,2,1,0:T(8,128)(2,1)S(1)}, u32[]{:S(2)}) copy-start(bf16[8,4,8,2048]{3,2,1,0:T(8,128)(2,1)S(1)} %all-to-all-done) | copy-start | bytes 3145732
  74.0 29.5 %all-to-all-start.2 = ((bf16[32,8,2048]{2,1,0:T(8,128)(2,1)}), bf16[32,8,2048]{2,1,0:T(8,128)(2,1)S(1)}, u32[]{:S(2)}, u32[]{:S(2)}) async-start(bf16[32,8,2048]{2,1,0:T(8,128)(2,1)} %bitcast.30), calls=%async_computation.2 | async-start | bytes 2097152 | tf_op jit(solution)/shard_map/all_to_all | solution.py:587
  103.5 9.3 %copy-start.1 = (bf16[32,8,2048]{2,1,0:T(8,128)(2,1)}, bf16[32,8,2048]{2,1,0:T(8,128)(2,1)S(1)}, u32[]{:S(2)}) copy-start(bf16[32,8,2048]{2,1,0:T(8,128)(2,1)S(1)} %all-to-all-done.2) | copy-start | bytes 3145732
  103.5 31.3 %all-to-all-start.3 = ((bf16[32,8,2176]{2,1,0:T(8,128)(2,1)}), bf16[32,8,2176]{2,1,0:T(8,128)(2,1)S(1)}, u32[]{:S(2)}, u32[]{:S(2)}) async-start(bf16[32,8,2176]{2,1,0:T(8,128)(2,1)} %bitcast.26), calls=%async_computation.3 | async-start | bytes 2228224 | tf_op jit(solution)/shard_map/all_to_all | solution.py:587
  134.8 1.0 copy-start.2

commit v8 on v7

--- a/solution.py
+++ b/solution.py
@@ -19,6 +19,7 @@
 
 
 PARAMS = pltpu.CompilerParams(vmem_limit_bytes=56 * 2**20)
+SMALL = pltpu.CompilerParams(vmem_limit_bytes=12 * 2**20)
 
 
 def to_hbm(*arrays):
@@ -185,9 +186,9 @@
             pltpu.SemaphoreType.DMA((STEPS,)),
             pltpu.SemaphoreType.DMA((pack, STEPS)),
         ],
-        compiler_params=PARAMS,
+        compiler_params=SMALL,
         cost_estimate=cost(2 * rows * own * part * pack, 2 * part * pack * own),
-    )(*to_hbm(hot, back))
+    )(*to_hbm(hot), back)
 
 
 def regroup(value, group, outer, inner):
@@ -548,14 +549,14 @@
     return lax.ppermute(block, "seq", [(s, s - 1) for s in range(first, last)])
 
 
-def line_gather(block, n, hold=()):
+def line_gather(block, n, hold, step):
     ups, downs = [], []
     up = down = block
     for j in range(1, n):
+        if j == step:
+            up, down, _ = lax.optimization_barrier((up, down, hold))
         up = up_line(up, n, j - 1)
         down = down_line(down, n, 1, n - j + 1)
-        if j == 1 and hold:
-            up, down, *_ = lax.optimization_barrier((up, down, *hold))
         ups.append(up)
         downs.append(down)
     plan = [(0, 0, 0)] + [(k, 2 * n - 1 - k, k) for k in range(1, n)]
@@ -587,9 +588,10 @@
         return lax.all_to_all(parts, BOTH, split_axis=0, concat_axis=0, tiled=True).reshape(-1, parts.shape[2])
 
     c_rows, x_rows, hot = choose_rows(tokens, cotangent, chosen, counts, pack)
-    c_in = line_gather(c_rows, seq_n)
+    x_rows = to_experts(x_rows)
+    c_in = line_gather(c_rows, seq_n, x_rows, 2)
     c_sent = by_place(c_in, seq_n, experts)
-    x_in = line_gather(to_experts(x_rows), seq_n, (c_sent,))
+    x_in = line_gather(x_rows, seq_n, c_sent, 3)
     c = lax.all_to_all(c_sent, "exp", split_axis=0, concat_axis=0, tiled=True)
     c = c.reshape(-1, c.shape[-1])
     halves = list(router.reshape(pack, features // pack, experts))

time: 141 us -> 140 us (level)
  blocking collectives: 0 us -> 10.7 us
  waiting for transfers between devices: 53.9 us -> 43.5 us
    all_to_all x0 -> x1, blocking collectives: none -> 10.7 us  [to_experts(): lax.all_to_all(block, 'exp', split_axis=0, concat_axis=0, tiled=True)]
    ppermute x6, waiting for transfers between devices: 21.4 us -> 16.5 us  [down_line(): return lax.ppermute(block, 'seq', [(s, s - 1) for s in range(first, last)])]
    ppermute x6, waiting for transfers between devices: 5.13 us -> 1 us  [up_line(): return lax.ppermute(block, 'seq', [(s, s + 1) for s in range(first, last)])]
    ppermute x6, starting transfers between devices: 12.3 us -> 16.2 us  [up_line(): return lax.ppermute(block, 'seq', [(s, s + 1) for s in range(first, last)])]
    all_to_all x1 -> x0, starting transfers between devices: 3.73 us -> none  [to_experts(): lax.all_to_all(block, 'exp', split_axis=0, concat_axis=0, tiled=True)]
    all_to_all x1 -> x0, waiting for transfers between devices: 1.75 us -> none  [to_experts(): lax.all_to_all(block, 'exp', split_axis=0, concat_axis=0, tiled=True)]
  transfers between devices with their start and end apart: 16 -> 15, of which waited for: 10 -> 6; matrix products, arithmetic and copies ran while one was open for 1% -> 1% of each run, Pallas kernels for 28% -> 28%
where the time goes in v8:
time: 140 us; the launch traced here: 139 us
  Pallas kernels  45.9 us (33%)
  waiting for transfers between devices  43.5 us (31%)
  starting transfers between devices  35 us (25%)
  blocking collectives  10.7 us (8%)
  local copies, waits for them, and re-layouts  2.75 us (2%)
    all_to_all x2, waiting for transfers between devices, to_owners(): lax.all_to_all(parts, BOTH, split_axis=0, concat_axis=0, tiled=True)  25.9 us
    ppermute x6, waiting for transfers between devices, down_line(): return lax.ppermute(block, 'seq', [(s, s - 1) for s in range(first, last)])  16.5 us
    ppermute x6, starting transfers between devices, up_line(): return lax.ppermute(block, 'seq', [(s, s + 1) for s in range(first, last)])  16.2 us
    pallas_call x1, Pallas kernels, expert_backward(): pl.pallas_call(body, in_specs=[ANYWHERE] * 7 + [IN_VMEM], out_specs=[ANYW...  12.5 us
    all_to_all x1, blocking collectives, to_experts(): lax.all_to_all(block, 'exp', split_axis=0, concat_axis=0, tiled=True)  10.7 us
    pallas_call x1, Pallas kernels, expert_forward(): pl.pallas_call(body, in_specs=[ANYWHERE] * (n_blocks + 4) + [IN_VMEM] * 2...  9.01 us
    ppermute x6, starting transfers between devices, down_line(): return lax.ppermute(block, 'seq', [(s, s - 1) for s in range(first, last)])  7.74 us
    all_to_all x2, starting transfers between devices, to_owners(): lax.all_to_all(parts, BOTH, split_axis=0, concat_axis=0, tiled=True)  7.45 us
  transfers between devices with their start and end apart: 15, of which 6 were waited for; matrix products, arithmetic and copies ran while one was open for 1% of the time, Pallas kernels for 28%

profile of v8, /device:TPU:0, one launch (start us, length us, event | category | flops | bytes accessed | tf_op | source)
XLA Modules:
  0.0 138.9 jit_solution(9559836157831915824)
XLA Ops:
  0.6 3.4 %shard_map.153 = (bf16[64,2048]{1,0:T(8,128)(2,1)}, bf16[64,2048]{1,0:T(8,128)(2,1)}, bf16[2,64,256]{2,1,0:T(8,128)(2,1)}) custom-call(s32[4,8]{1,0:T(4,128)} %bitcast.39, s32[1,8]{1,0:T(1,128)} %counts_ref.1, bf16[256,4096]{1,0:T(8,128)(2,1)} %c_ref.1, bf16[256,4096]{1,0:T(8,128)(2,1)} %x_ref.1), custom_call_target="tpu_custom_call" | custom-call | flops 268435456 | bytes 4194304 | tf_op jit(solution)/shard_map/pallas_call | solution.py:86
  4.1 0.0 copy-start.14
  4.1 5.1 %collective-permute-start = (bf16[64,2048]{1,0:T(8,128)(2,1)}, bf16[64,2048]{1,0:T(8,128)(2,1)S(1)}, u32[]{:S(2)}, u32[]{:S(2)}) collective-permute-start(bf16[64,2048]{1,0:T(8,128)(2,1)} %get-tuple-element.28), channel_id=1, source_target_pairs={{0,8},{8,16},{16,24},{1,9},{9,17},{17,25},{2,10},{10,18},{18,26},{... | collective-permute-start | bytes 786440 | tf_op jit(solution)/shard_map/ppermute | solution.py:544
  9.2 1.3 collective-permute-start.1
  10.5 10.7 %all_to_all.20 = bf16[8,8,2048]{2,1,0:T(8,128)(2,1)S(1)} all-to-all(bf16[8,8,2048]{2,1,0:T(8,128)(2,1)} %bitcast.31), channel_id=1, replica_groups=mesh['seq'=4,'exp'=8] {'exp'}, dimensions={0} | all-to-all | bytes 524288 | tf_op jit(solution)/shard_map/all_to_all | solution.py:584
  21.1 0.0 collective-permute-done
  21.2 0.0 collective-permute-done.1
  21.2 1.3 collective-permute-start.4
  22.5 0.7 collective-permute-start.2
  23.2 8.5 %collective-permute-start.6 = (bf16[64,2048]{1,0:T(8,128)(2,1)S(1)}, bf16[64,2048]{1,0:T(8,128)(2,1)S(1)}, u32[]{:S(2)}, u32[]{:S(2)}) collective-permute-start(bf16[64,2048]{1,0:T(8,128)(2,1)S(1)} %bitcast.27), channel_id=1, source_target_pairs={{0,8},{8,16},{16,24},{1,9},{9,17},{17,25},{2,10},{10,18},{18,26},{... | collective-permute-start | bytes 786440 | tf_op jit(solution)/shard_map/ppermute | solution.py:544
  31.6 1.3 collective-permute-start.8
  32.9 0.0 collective-permute-done.4
  32.9 1.3 collective-permute-start.5
  34.2 0.0 collective-permute-done.2
  34.3 0.0 copy-start.11
  34.3 0.7 collective-permute-start.3
  34.9 1.0 collective-permute-done.6.refs_1_
  35.9 0.7 collective-permute-start.7
  36.6 6.1 %collective-permute-done.8.refs_4_ = bf16[64,2048]{1,0:T(8,128)(2,1)S(1)} collective-permute-done((bf16[64,2048]{1,0:T(8,128)(2,1)S(1)}, bf16[64,2048]{1,0:T(8,128)(2,1)S(1)}, u32[]{:S(2)}, u32[]{:S(2)}) %collective-permute-start.8) | collective-permute-done | bytes 262176 | tf_op jit(solution)/shard_map/ppermute | solution.py:549
  42.8 1.3 collective-permute-start.9
  44.0 2.5 %collective-permute-done.5 = bf16[64,2048]{1,0:T(8,128)(2,1)S(1)} collective-permute-done((bf16[64,2048]{1,0:T(8,128)(2,1)S(1)}, bf16[64,2048]{1,0:T(8,128)(2,1)S(1)}, u32[]{:S(2)}, u32[]{:S(2)}) %collective-permute-start.5) | collective-permute-done | bytes 262176 | tf_op jit(solution)/shard_map/ppermute | solution.py:549
  46.5 0.0 collective-permute-done.3
  46.6 0.7 copy-done.12
  47.2 0.1 copy-done.13
  47.3 2.2 %shard_map.154 = bf16[8,4,8,2048]{3,2,1,0:T(8,128)(2,1)} custom-call(bf16[8,8,2048]{2,1,0:T(8,128)(2,1)} %bitcast.32, bf16[8,8,2048]{2,1,0:T(8,128)(2,1)} %bitcast.33, bf16[8,8,2048]{2,1,0:T(8,128)(2,1)} %bitcast.36, bf16[8,8,2048]{2,1,0:T(8,128)(2,1)} %bitcast.38, bf16[8,8,2048]{2,1,0:T(8,128)(2,1)} %bitcast.34, bf16[8,8,2048]{2,1,0:T(8,128)(2,1)} %bitcast.35, ...), custom_call_target="tpu_custom_call" | custom-call | bytes 2097152 | tf_op jit(solution)/shard_map/pallas_call | solution.py:113
  49.5 3.6 %all-to-all-start.1 = ((bf16[8,4,8,2048]{3,2,1,0:T(8,128)(2,1)}), bf16[8,4,8,2048]{3,2,1,0:T(8,128)(2,1)S(1)}, u32[]{:S(2)}, u32[]{:S(2)}) async-start(bf16[8,4,8,2048]{3,2,1,0:T(8,128)(2,1)} %shard_map.154), calls=%async_computation.1 | async-start | bytes 2097152 | tf_op jit(solution)/shard_map/all_to_all | solution.py:595
  53.1 0.0 collective-permute-done.7.refs_2_
  53.1 0.0 collective-permute-done.9.refs_5_
  53.1 0.0 copy-start.5
  53.1 0.7 collective-permute-start.10
  53.8 1.3 collective-permute-start.11
  55.2 0.3 copy.21
  55.4 0.9 pad.4.refs_7_.refs_1_
  56.4 0.0 collective-permute-done.10.refs_3_
  56.4 7.9 %collective-permute-done.11.refs_6_ = bf16[64,2048]{1,0:T(8,128)(2,1)S(1)} collective-permute-done((bf16[64,2048]{1,0:T(8,128)(2,1)S(1)}, bf16[64,2048]{1,0:T(8,128)(2,1)S(1)}, u32[]{:S(2)}, u32[]{:S(2)}) %collective-permute-start.11) | collective-permute-done | bytes 262176 | tf_op jit(solution)/shard_map/ppermute | solution.py:549
  64.3 0.7 copy-done.7
  65.0 9.0 %shard_map.155 = (bf16[256,2048]{1,0:T(8,128)(2,1)}, bf16[4,64,2048]{2,1,0:T(8,128)(2,1)}, f32[256,896]{1,0:T(8,128)}, bf16[256,768]{1,0:T(8,128)(2,1)}) custom-call(bf16[64,2048]{1,0:T(8,128)(2,1)} %bitcast.29, bf16[64,2048]{1,0:T(8,128)(2,1)} %copy-done.2, bf16[64,2048]{1,0:T(8,128)(2,1)} %copy-done.4, bf16[64,2048]{1,0:T(8,128)(2,1)} %copy-done.6, ...), custom_call_target="tpu_custom_call" | custom-call | flops 524288 | bytes 524288 | tf_op jit(solution)/shard_map/pallas_call | solution.py:335
  74.1 0.0 all-to-all-done.1
  74.1 0.0 copy-start
  74.1 3.7 %all-to-all-start.2 = ((bf16[32,8,2048]{2,1,0:T(8,128)(2,1)}), bf16[32,8,2048]{2,1,0:T(8,128)(2,1)S(1)}, u32[]{:S(2)}, u32[]{:S(2)}) async-start(bf16[32,8,2048]{2,1,0:T(8,128)(2,1)} %bitcast.30), calls=%async_computation.2 | async-start | bytes 2097152 | tf_op jit(solution)/shard_map/all_to_all | solution.py:588
  77.7 12.5 %shard_map.156 = (bf16[4,64,2176]{2,1,0:T(8,128)(2,1)}, bf16[256,1664]{1,0:T(8,128)(2,1)}) custom-call(bf16[256,2048]{1,0:T(8,128)(2,1)} %bitcast.24, bf16[2048,128]{1,0:T(8,128)(2,1)} %pad.4.refs_7_.refs_1_, bf16[1,4096,384]{2,1,0:T(8,128)(2,1)} %refs_2_.1, bf16[1,4096,384]{2,1,0:T(8,128)(2,1)} %refs_3_.1, bf16[1,384,4096]{2,1,0:T(8,128)(2,1)} %refs_4_.1, ...), custom_call_target="tpu_custom_call" | custom-call | flops 2415919104 | bytes 9437184 | tf_op jit(solution)/shard_map/pallas_call | solution.py:469
  90.3 13.7 %all-to-all-done.2 = bf16[32,8,2048]{2,1,0:T(8,128)(2,1)S(1)} async-done(((bf16[32,8,2048]{2,1,0:T(8,128)(2,1)}), bf16[32,8,2048]{2,1,0:T(8,128)(2,1)S(1)}, u32[]{:S(2)}, u32[]{:S(2)}) %all-to-all-start.2) | async-done | bytes 1048608 | tf_op jit(solution)/shard_map/all_to_all | solution.py:588
  104.0 3.8 %all-to-all-start.3 = ((bf16[32,8,2176]{2,1,0:T(8,128)(2,1)}), bf16[32,8,2176]{2,1,0:T(8,128)(2,1)S(1)}, u32[]{:S(2)}, u32[]{:S(2)}) async-start(bf16[32,8,2176]{2,1,0:T(8,128)(2,1)} %bitcast.26), calls=%async_computation.3 | async-start | bytes 2228224 | tf_op jit(solution)/shard_map/all_to_all | solution.py:588
  107.8 5.5 %shard_map.160 = f32[1,384,4096]{2,1,0:T(8,128)} custom-call(bf16[256,2048]{1,0:T(8,128)(2,1)} %bitcast.25, bf16[256,768]{1,0:T(8,128)(2,1)} %get-tuple-element.46.hidden_ref), custom_call_target="tpu_custom_call" | custom-call | flops 805306368 | bytes 6291456 | tf_op jit(solution)/shard_map/pallas_call | solution.py:528
  113.2 6.9 %shard_map.159 = (f32[2,2048,384]{2,1,0:T(8,128)}, f32[2,2048,384]{2,1,0:T(8,128)}) custom-call(bf16[256,2048]{1,0:T(8,128)(2,1)} %get-tuple-element.34.refs_5_.x_ref, bf16[256,1664]{1,0:T(8,128)(2,1)} %get-tuple-element.43.delta_ref), custom_call_target="tpu_custom_call" | custom-call | flops 1610612736 | bytes 12582912 | tf_op jit(solution)/shard_map/pallas_call | solution.py:506
  120.1 2.9 %shard_map.157 = bf16[256,4096]{1,0:T(8,128)(2,1)} custom-call(bf16[2,64,256]{2,1,0:T(8,128)(2,1)} %get-tuple-element.27.hot_ref, bf16[256,2048]{1,0:T(8,128)(2,1)S(1)} %bitcast.22), custom_call_target="tpu_custom_call" | custom-call | flops 536870912 | bytes 2097152 | tf_op jit(solution)/shard_map/pallas_call | solution.py:176
  123.0 12.2 %all-to-all-done.3 = bf16[32,8,2176]{2,1,0:T(8,128)(2,1)S(1)} async-done(((bf16[32,8,2176]{2,1,0:T(8,128)(2,1)}), bf16[32,8,2176]{2,1,0:T(8,128)(2,1)S(1)}, u32[]{:S(2)}, u32[]{:S(2)}) %all-to-all-start.3) | async-done | bytes 1114144 | tf_op jit(solution)/shard_map/all_to_all | solution.py:588
  135.2 3.5 %shard_map.158 = (bf16[256,4096]{1,0:T(8,128)(2,1)}, f32[8,128]{1,0:T(8,128)}, f32[1,8]{1,0:T(1,128)}) custom-call(bf16[2,64,256]{2,1,0:T(8,128)(2,1)} %get-tuple-element.27.hot_ref, bf16[256,2176]{1,0:T(8,128)(2,1)S(1)} %bitcast.23), custom_call_target="tpu_custom_call" | custom-call | flops 536870912 | bytes 2097152 | tf_op jit(solution)/shard_map/pallas_call | solution.py:176
  (25 shorter events, 0.1 us)
Async XLA Ops:
  4.1 51.0 %copy-start.14 = (bf16[4096,8]{0,1:T(8,128)(2,1)S(1)}, bf16[4096,8]{0,1:T(8,128)(2,1)}, u32[]{:S(2)}) copy-start(bf16[4096,8]{0,1:T(8,128)(2,1)} %param.12) | copy-start | bytes 196612
  4.1 17.1 %collective-permute-start = (bf16[64,2048]{1,0:T(8,128)(2,1)}, bf16[64,2048]{1,0:T(8,128)(2,1)S(1)}, u32[]{:S(2)}, u32[]{:S(2)}) collective-permute-start(bf16[64,2048]{1,0:T(8,128)(2,1)} %get-tuple-element.28), channel_id=1, source_target_pairs={{0,8},{8,16},{16,24},{1,9},{9,17},{17,25},{2,10},{10,18},{18,26},{... | collective-permute-start | bytes 786440 | tf_op jit(solution)/shard_map/ppermute | solution.py:544
  9.2 12.0 %collective-permute-start.1 = (bf16[64,2048]{1,0:T(8,128)(2,1)}, bf16[64,2048]{1,0:T(8,128)(2,1)S(1)}, u32[]{:S(2)}, u32[]{:S(2)}) collective-permute-start(bf16[64,2048]{1,0:T(8,128)(2,1)} %get-tuple-element.28), channel_id=1, source_target_pairs={{8,0},{16,8},{24,16},{9,1},{17,9},{25,17},{10,2},{18,10},{26,18},{... | collective-permute-start | bytes 786440 | tf_op jit(solution)/shard_map/ppermute | solution.py:549
  21.1 35.2 %copy-start.1 = (bf16[8,8,2048]{2,1,0:T(8,128)(2,1)}, bf16[8,8,2048]{2,1,0:T(8,128)(2,1)S(1)}, u32[]{:S(2)}) copy-start(bf16[8,8,2048]{2,1,0:T(8,128)(2,1)S(1)} %all_to_all.20) | copy-start | bytes 786436
  21.1 25.4 %copy-start.8 = (bf16[64,2048]{1,0:T(8,128)(2,1)}, bf16[64,2048]{1,0:T(8,128)(2,1)S(1)}, u32[]{:S(2)}) copy-start(bf16[64,2048]{1,0:T(8,128)(2,1)S(1)} %collective-permute-done) | copy-start | bytes 786436
  21.2 25.4 %copy-start.9 = (bf16[64,2048]{1,0:T(8,128)(2,1)}, bf16[64,2048]{1,0:T(8,128)(2,1)S(1)}, u32[]{:S(2)}) copy-start(bf16[64,2048]{1,0:T(8,128)(2,1)S(1)} %collective-permute-done.1) | copy-start | bytes 786436
  21.2 11.8 %collective-permute-start.4 = (bf16[64,2048]{1,0:T(8,128)(2,1)S(1)}, bf16[64,2048]{1,0:T(8,128)(2,1)S(1)}, u32[]{:S(2)}, u32[]{:S(2)}) collective-permute-start(bf16[64,2048]{1,0:T(8,128)(2,1)S(1)} %collective-permute-done.1), channel_id=1, source_target_pairs={{8,0},{16,8},{9,1},{17,9},{10,2},{18,10},{11,3},{19,11},{12,4},{20... | collective-permute-start | bytes 786440 | tf_op jit(solution)/shard_map/ppermute | solution.py:549
  22.5 11.8 %collective-permute-start.2 = (bf16[64,2048]{1,0:T(8,128)(2,1)S(1)}, bf16[64,2048]{1,0:T(8,128)(2,1)S(1)}, u32[]{:S(2)}, u32[]{:S(2)}) collective-permute-start(bf16[64,2048]{1,0:T(8,128)(2,1)S(1)} %collective-permute-done), channel_id=1, source_target_pairs={{8,16},{16,24},{9,17},{17,25},{10,18},{18,26},{11,19},{19,27},{12,... | collective-permute-start | bytes 786440 | tf_op jit(solution)/shard_map/ppermute | solution.py:544
  23.2 12.8 %collective-permute-start.6 = (bf16[64,2048]{1,0:T(8,128)(2,1)S(1)}, bf16[64,2048]{1,0:T(8,128)(2,1)S(1)}, u32[]{:S(2)}, u32[]{:S(2)}) collective-permute-start(bf16[64,2048]{1,0:T(8,128)(2,1)S(1)} %bitcast.27), channel_id=1, source_target_pairs={{0,8},{8,16},{16,24},{1,9},{9,17},{17,25},{2,10},{10,18},{18,26},{... | collective-permute-start | bytes 786440 | tf_op jit(solution)/shard_map/ppermute | solution.py:544
  31.6 11.1 %collective-permute-start.8 = (bf16[64,2048]{1,0:T(8,128)(2,1)S(1)}, bf16[64,2048]{1,0:T(8,128)(2,1)S(1)}, u32[]{:S(2)}, u32[]{:S(2)}) collective-permute-start(bf16[64,2048]{1,0:T(8,128)(2,1)S(1)} %bitcast.28), channel_id=1, source_target_pairs={{8,0},{16,8},{24,16},{9,1},{17,9},{25,17},{10,2},{18,10},{26,18},{... | collective-permute-start | bytes 786440 | tf_op jit(solution)/shard_map/ppermute | solution.py:549
  32.9 13.6 %copy-start.10 = (bf16[64,2048]{1,0:T(8,128)(2,1)}, bf16[64,2048]{1,0:T(8,128)(2,1)S(1)}, u32[]{:S(2)}) copy-start(bf16[64,2048]{1,0:T(8,128)(2,1)S(1)} %collective-permute-done.4) | copy-start | bytes 786436
  32.9 13.6 %collective-permute-start.5 = (bf16[64,2048]{1,0:T(8,128)(2,1)S(1)}, bf16[64,2048]{1,0:T(8,128)(2,1)S(1)}, u32[]{:S(2)}, u32[]{:S(2)}) collective-permute-start(bf16[64,2048]{1,0:T(8,128)(2,1)S(1)} %collective-permute-done.4), channel_id=1, source_target_pairs={{8,0},{9,1},{10,2},{11,3},{12,4},{13,5},{14,6},{15,7}} | collective-permute-start | bytes 786440 | tf_op jit(solution)/shard_map/ppermute | solution.py:549
  34.3 12.3 %copy-start.11 = (bf16[64,2048]{1,0:T(8,128)(2,1)}, bf16[64,2048]{1,0:T(8,128)(2,1)S(1)}, u32[]{:S(2)}) copy-start(bf16[64,2048]{1,0:T(8,128)(2,1)S(1)} %collective-permute-done.2) | copy-start | bytes 786436
  34.3 12.3 %collective-permute-start.3 = (bf16[64,2048]{1,0:T(8,128)(2,1)S(1)}, bf16[64,2048]{1,0:T(8,128)(2,1)S(1)}, u32[]{:S(2)}, u32[]{:S(2)}) collective-permute-start(bf16[64,2048]{1,0:T(8,128)(2,1)S(1)} %collective-permute-done.2), channel_id=1, source_target_pairs={{16,24},{17,25},{18,26},{19,27},{20,28},{21,29},{22,30},{23,31}} | collective-permute-start | bytes 786440 | tf_op jit(solution)/shard_map/ppermute | solution.py:544
  35.9 20.5 %copy-start.2 = (bf16[64,2048]{1,0:T(8,128)(2,1)}, bf16[64,2048]{1,0:T(8,128)(2,1)S(1)}, u32[]{:S(2)}) copy-start(bf16[64,2048]{1,0:T(8,128)(2,1)S(1)} %collective-permute-done.6.refs_1_) | copy-start | bytes 786436
  35.9 17.2 %collective-permute-start.7 = (bf16[64,2048]{1,0:T(8,128)(2,1)S(1)}, bf16[64,2048]{1,0:T(8,128)(2,1)S(1)}, u32[]{:S(2)}, u32[]{:S(2)}) collective-permute-start(bf16[64,2048]{1,0:T(8,128)(2,1)S(1)} %collective-permute-done.6.refs_1_), channel_id=1, source_target_pairs={{8,16},{16,24},{9,17},{17,25},{10,18},{18,26},{11,19},{19,27},{12,... | collective-permute-start | bytes 786440 | tf_op jit(solution)/shard_map/ppermute | solution.py:544
  42.8 13.6 %copy-start.3 = (bf16[64,2048]{1,0:T(8,128)(2,1)}, bf16[64,2048]{1,0:T(8,128)(2,1)S(1)}, u32[]{:S(2)}) copy-start(bf16[64,2048]{1,0:T(8,128)(2,1)S(1)} %collective-permute-done.8.refs_4_) | copy-start | bytes 786436
  42.8 10.4 %collective-permute-start.9 = (bf16[64,2048]{1,0:T(8,128)(2,1)S(1)}, bf16[64,2048]{1,0:T(8,128)(2,1)S(1)}, u32[]{:S(2)}, u32[]{:S(2)}) collective-permute-start(bf16[64,2048]{1,0:T(8,128)(2,1)S(1)} %collective-permute-done.8.refs_4_), channel_id=1, source_target_pairs={{8,0},{16,8},{9,1},{17,9},{10,2},{18,10},{11,3},{19,11},{12,4},{20... | collective-permute-start | bytes 786440 | tf_op jit(solution)/shard_map/ppermute | solution.py:549
  46.5 0.7 copy-start.12
  46.5 0.8 copy-start.13
  49.5 24.5 %all-to-all-start.1 = ((bf16[8,4,8,2048]{3,2,1,0:T(8,128)(2,1)}), bf16[8,4,8,2048]{3,2,1,0:T(8,128)(2,1)S(1)}, u32[]{:S(2)}, u32[]{:S(2)}) async-start(bf16[8,4,8,2048]{3,2,1,0:T(8,128)(2,1)} %shard_map.154), calls=%async_computation.1 | async-start | bytes 2097152 | tf_op jit(solution)/shard_map/all_to_all | solution.py:595
  53.1 11.2 %copy-start.4 = (bf16[64,2048]{1,0:T(8,128)(2,1)}, bf16[64,2048]{1,0:T(8,128)(2,1)S(1)}, u32[]{:S(2)}) copy-start(bf16[64,2048]{1,0:T(8,128)(2,1)S(1)} %collective-permute-done.7.refs_2_) | copy-start | bytes 786436
  53.1 11.2 %copy-start.5 = (bf16[64,2048]{1,0:T(8,128)(2,1)}, bf16[64,2048]{1,0:T(8,128)(2,1)S(1)}, u32[]{:S(2)}) copy-start(bf16[64,2048]{1,0:T(8,128)(2,1)S(1)} %collective-permute-done.9.refs_5_) | copy-start | bytes 786436
  53.1 3.3 %collective-permute-start.10 = (bf16[64,2048]{1,0:T(8,128)(2,1)S(1)}, bf16[64,2048]{1,0:T(8,128)(2,1)S(1)}, u32[]{:S(2)}, u32[]{:S(2)}) collective-permute-start(bf16[64,2048]{1,0:T(8,128)(2,1)S(1)} %collective-permute-done.7.refs_2_), channel_id=1, source_target_pairs={{16,24},{17,25},{18,26},{19,27},{20,28},{21,29},{22,30},{23,31}} | collective-permute-start | bytes 786440 | tf_op jit(solution)/shard_map/ppermute | solution.py:544
  53.8 10.5 %collective-permute-start.11 = (bf16[64,2048]{1,0:T(8,128)(2,1)S(1)}, bf16[64,2048]{1,0:T(8,128)(2,1)S(1)}, u32[]{:S(2)}, u32[]{:S(2)}) collective-permute-start(bf16[64,2048]{1,0:T(8,128)(2,1)S(1)} %collective-permute-done.9.refs_5_), channel_id=1, source_target_pairs={{8,0},{9,1},{10,2},{11,3},{12,4},{13,5},{14,6},{15,7}} | collective-permute-start | bytes 786440 | tf_op jit(solution)/shard_map/ppermute | solution.py:549
  56.4 7.9 %copy-start.6 = (bf16[64,2048]{1,0:T(8,128)(2,1)}, bf16[64,2048]{1,0:T(8,128)(2,1)S(1)}, u32[]{:S(2)}) copy-start(bf16[64,2048]{1,0:T(8,128)(2,1)S(1)} %collective-permute-done.10.refs_3_) | copy-start | bytes 786436
  64.3 0.7 copy-start.7
  74.1 3.7 %copy-start = (bf16[8,4,8,2048]{3,2,1,0:T(8,128)(2,1)}, bf16[8,4,8,2048]{3,2,1,0:T(8,128)(2,1)S(1)}, u32[]{:S(2)}) copy-start(bf16[8,4,8,2048]{3,2,1,0:T(8,128)(2,1)S(1)} %all-to-all-done.1) | copy-start | bytes 3145732
  74.1 29.9 %all-to-all-start.2 = ((bf16[32,8,2048]{2,1,0:T(8,128)(2,1)}), bf16[32,8,2048]{2,1,0:T(8,128)(2,1)S(1)}, u32[]{:S(2)}, u32[]{:S(2)}) async-start(bf16[32,8,2048]{2,1,0:T(8,128)(2,1)} %bitcast.30), calls=%async_computation.2 | async-start | bytes 2097152 | tf_op jit(solution)/shard_map/all_to_all | solution.py:588
  104.0 31.3 %all-to-all-start.3 = ((bf16[32,8,2176]{2,1,0:T(8,128)(2,1)}), bf16[32,8,2176]{2,1,0:T(8,128)(2,1)S(1)}, u32[]{:S(2)}, u32[]{:S(2)}) async-start(bf16[32,8,2176]{2,1,0:T(8,128)(2,1)} %bitcast.26), calls=%async_computation.3 | async-start | bytes 2228224 | tf_op jit(solution)/shard_map/all_to_all | solution.py:588

commit v9 on v8

--- a/solution.py
+++ b/solution.py
@@ -41,11 +41,12 @@
 def choose_rows(tokens, cotangent, picks, counts, pack):
     own, features = tokens.shape
     slots, experts = picks.shape
-    count = experts * pack * slots
+    group = pack * slots
+    count = 2 * experts * group
     part = features // pack
     width = part // STEPS
 
-    def body(picks_ref, counts_ref, c_ref, x_ref, c_out, x_out, hot_ref, picks_s, counts_s, c_v, x_v, hot, sems):
+    def body(picks_ref, counts_ref, c_ref, x_ref, out_ref, hot_ref, picks_s, counts_s, c_v, x_v, out_v, sems, out_sems):
         small = [
             pltpu.make_async_copy(picks_ref, picks_s, sems.at[2 * STEPS]),
             pltpu.make_async_copy(counts_ref, counts_s, sems.at[2 * STEPS + 1]),
@@ -53,72 +54,68 @@
         for copy in small:
             copy.start()
         large = []
-        for n, (ref, held) in enumerate(((c_ref, c_v), (x_ref, x_v))):
-            for j in range(STEPS):
-                now = pl.ds(j * pack * width, pack * width)
-                large.append(pltpu.make_async_copy(ref.at[:, now], held.at[:, now], sems.at[n * STEPS + j]))
-                large[-1].start()
+        for j in range(STEPS):
+            now = pl.ds(j * pack * width, pack * width)
+            large.append(pltpu.make_async_copy(x_ref.at[:, now], x_v.at[:, now], sems.at[2 * j]))
+            large.append(pltpu.make_async_copy(c_ref.at[:, now], c_v.at[:, now], sems.at[2 * j + 1]))
+        for copy in large:
+            copy.start()
         for copy in small:
             copy.wait()
         dims = (count, own)
         row = lax.broadcasted_iota(jnp.int32, dims, 0)
         token = lax.broadcasted_iota(jnp.int32, dims, 1)
-        place = row // (pack * slots) * slots + row % slots
-        part_of = (row // slots) % pack
+        second = (row // group) % 2
+        place = (row // (2 * group) * slots + row % slots) * 2 + second
         want = jnp.full(dims, -1, jnp.int32)
-        want_live = want
         for e in range(experts):
             for k in range(slots):
-                here = place == e * slots + k
-                want = jnp.where(here, picks_s[k, e], want)
-                want_live = jnp.where(here, jnp.where(k < counts_s[0, e], picks_s[k, e], -1), want_live)
+                index = (e * slots + k) * 2
+                want = jnp.where(place == index, picks_s[k, e], want)
+                live = jnp.where(k < counts_s[0, e], picks_s[k, e], -1)
+                want = jnp.where(place == index + 1, live, want)
+        found = (want == token) & (second == 0)
+        found_live = (want == token) & (second == 1)
+        part_of = (row // slots) % pack
+        chosen = [jnp.where(found & (part_of == h), 1.0, 0.0).astype(BF16) for h in range(pack)]
+        live = [jnp.where(found_live & (part_of == h), 1.0, 0.0) for h in range(pack)]
         for h in range(pack):
-            hot[h] = jnp.where((want == token) & (part_of == h), 1.0, 0.0).astype(BF16)
-            hot_ref[h] = jnp.where((want_live == token) & (part_of == h), 1.0, 0.0).astype(BF16)
-        for n, (chooser, held, out_ref) in enumerate(((hot_ref, c_v, c_out), (hot, x_v, x_out))):
-            for copy in large[n * STEPS : (n + 1) * STEPS]:
-                copy.wait()
-            for j in range(STEPS):
-                out_ref[:, j * width : (j + 1) * width] = sum(
-                    mm(chooser[h], held[:, h * part + j * width : h * part + (j + 1) * width]) for h in range(pack)
-                ).astype(BF16)
+            hot_ref[h] = jnp.concatenate(
+                [live[h][(2 * e + 1) * group : (2 * e + 2) * group] for e in range(experts)]
+            ).astype(BF16)
+        live = [value.astype(BF16) for value in live]
+        for copy in large:
+            copy.wait()
+        leaving = []
+        for j in range(STEPS):
+            total = 0.0
+            for h in range(pack):
+                now = slice(h * part + j * width, h * part + (j + 1) * width)
+                total = total + mm(chosen[h], x_v[:, now]) + mm(live[h], c_v[:, now])
+            out_v[:, j * width : (j + 1) * width] = total.astype(BF16)
+            now = pl.ds(j * width, width)
+            leaving.append(pltpu.make_async_copy(out_v.at[:, now], out_ref.at[:, now], out_sems.at[j]))
+            leaving[-1].start()
+        for copy in leaving:
+            copy.wait()
 
     return pl.pallas_call(
         body,
         in_specs=[ANYWHERE] * 4,
-        out_specs=[IN_VMEM] * 3,
-        out_shape=[shape((count, part))] * 2 + [shape((pack, count, own))],
+        out_specs=[ANYWHERE, IN_VMEM],
+        out_shape=[shape((count, part)), shape((pack, count // 2, own))],
         scratch_shapes=[
             pltpu.SMEM(picks.shape, jnp.int32),
             pltpu.SMEM(counts.shape, jnp.int32),
             pltpu.VMEM(tokens.shape, BF16),
             pltpu.VMEM(tokens.shape, BF16),
-            pltpu.VMEM((pack, count, own), BF16),
+            pltpu.VMEM((count, part), BF16),
             pltpu.SemaphoreType.DMA((2 * STEPS + 2,)),
+            pltpu.SemaphoreType.DMA((STEPS,)),
         ],
         compiler_params=PARAMS,
         cost_estimate=cost(4 * count * own * features, 4 * features * own),
     )(*to_hbm(picks, counts, cotangent, tokens))
-
-
-def by_place(arrivals, seq_n, groups):
-    blocks = [block.reshape(groups, -1, block.shape[1]) for block in arrivals.blocks]
-    _, rows, part = blocks[0].shape
-
-    def body(*refs):
-        out_ref, sems = refs[-2:]
-        arrivals.start(refs[:-2], [out_ref.at[:, k] for k in range(seq_n)], sems)
-        arrivals.wait(refs[:-2], [out_ref.at[:, k] for k in range(seq_n)], sems)
-
-    return pl.pallas_call(
-        body,
-        in_specs=[ANYWHERE] * len(blocks),
-        out_specs=IN_VMEM,
-        out_shape=shape((groups, seq_n, rows, part)),
-        scratch_shapes=[pltpu.SemaphoreType.DMA((seq_n,))],
-        compiler_params=PARAMS,
-        cost_estimate=cost(0, 4 * groups * seq_n * rows * part),
-    )(*to_hbm(*blocks))
 
 
 def scatter_rows(back, hot, seq_n, message=None):
@@ -191,12 +188,6 @@
     )(*to_hbm(hot), back)
 
 
-def regroup(value, group, outer, inner):
-    return jnp.concatenate(
-        [value[(o * inner + i) * group : (o * inner + i + 1) * group] for i in range(inner) for o in range(outer)]
-    )
-
-
 def first_part(rows, pack, slots):
     return (lax.broadcasted_iota(jnp.int32, (rows, 1), 0) // slots) % pack == 0
 
@@ -273,7 +264,6 @@
     rows = block_rows * seq_n
     hidden_n = w_gate.shape[2]
     both = 2 * hidden_n
-    group = pack * slots
     width = part // STEPS
     total = pack * both + LANES
     n_blocks = len(arrivals.blocks)
@@ -282,7 +272,7 @@
         blocks = refs[:n_blocks]
         router_ref, gate_ref, up_ref, down_ref, threshold_ref, scale_ref = refs[n_blocks : n_blocks + 6]
         x_ref, out_ref, pre_ref, hidden_ref = refs[n_blocks + 6 : n_blocks + 10]
-        pre_v, hidden_v, other_v, x_v, out_v, side, stack, x_sems, side_sems, stack_sems, out_sems = refs[n_blocks + 10 :]
+        pre_v, hidden_v, x_v, out_v, side, stack, x_sems, side_sems, stack_sems, out_sems = refs[n_blocks + 10 :]
         places = [x_v.at[pl.ds(k * block_rows, block_rows), :] for k in range(seq_n)]
         arrivals.start(blocks, places, x_sems)
         chunks = [side_copies(gate_ref, up_ref, router_ref, side, side_sems, pack, j, width) for j in range(STEPS)]
@@ -313,12 +303,11 @@
         for h, value in enumerate(spread(hidden, pack, slots)):
             now = slice(h * hidden_n, (h + 1) * hidden_n)
             hidden_v[:, now] = value.astype(BF16)
-            other_v[:, now] = regroup(value, group, seq_n, block_rows // group).astype(BF16)
         pre_v[:, :hidden_n] = gate
         pre_v[:, hidden_n:both] = up
         pre_v[:, both:] = jnp.broadcast_to(g, (rows, LANES))
         leaving.append(pltpu.make_async_copy(pre_v, pre_ref, out_sems.at[STEPS + 1]))
-        leaving.append(pltpu.make_async_copy(other_v, hidden_ref, out_sems.at[STEPS + 2]))
+        leaving.append(pltpu.make_async_copy(hidden_v, hidden_ref, out_sems.at[STEPS + 2]))
         for copy in leaving[1:]:
             copy.start()
         for copy in downs:
@@ -345,7 +334,6 @@
         scratch_shapes=[
             pltpu.VMEM((rows, both + LANES), F32),
             pltpu.VMEM((rows, pack * hidden_n), BF16),
-            pltpu.VMEM((rows, pack * hidden_n), BF16),
             pltpu.VMEM((rows, part), BF16),
             pltpu.VMEM((seq_n, block_rows, part), BF16),
             pltpu.VMEM((part, total), BF16),
@@ -356,7 +344,7 @@
             pltpu.SemaphoreType.DMA((STEPS + 3,)),
         ],
         compiler_params=PARAMS,
-        cost_estimate=cost(rows * part, rows * part),
+        cost_estimate=cost(6 * rows * part * pack * hidden_n, 12 * part * pack * hidden_n),
     )(*to_hbm(*arrivals.blocks, router_side, w_gate, w_up, w_down), threshold.reshape(1, -1), hid_scale)
 
 
@@ -371,36 +359,41 @@
     return LANES * -(-2 * seq_n // group)
 
 
-def expert_backward(c, seq_n, exp_n, slots, pack, x, pre, router_side, w_gate, w_up, w_down, hid_scale):
-    rows, part = c.shape
-    block_rows = rows // seq_n
+def expert_backward(arrivals, seq_n, exp_n, slots, pack, x, pre, router_side, w_gate, w_up, w_down, hid_scale):
+    block_rows, part = arrivals.blocks[0].shape
+    rows = block_rows * seq_n
     hidden_n = w_gate.shape[2]
     width = part // STEPS
     total = 2 * pack * hidden_n + LANES
     group = pack * slots
     extra = riding(seq_n, group)
     per = part * pack // (seq_n * exp_n)
+    n_blocks = len(arrivals.blocks)
 
     def body(*refs):
-        c_ref, router_ref, gate_ref, up_ref, down_ref, x_ref, pre_ref, scale_ref, out_ref, delta_ref = refs[:10]
-        c_v, x_v, pre_v, out_v, side, stack, columns, x_sems, side_sems, stack_sems, out_sems = refs[10:]
-        c_copy = pltpu.make_async_copy(c_ref, c_v, x_sems.at[2])
-        c_copy.start()
+        blocks = refs[:n_blocks]
+        router_ref, gate_ref, up_ref, down_ref, x_ref, pre_ref, scale_ref = refs[n_blocks : n_blocks + 7]
+        c_ref, out_ref, delta_ref = refs[n_blocks + 7 : n_blocks + 10]
+        c_v, x_v, pre_v, out_v, side, stack, columns, c_sems, x_sems, side_sems, stack_sems, out_sems = refs[
+            n_blocks + 10 :
+        ]
+        places = [c_v.at[pl.ds(k * block_rows, block_rows), :] for k in range(seq_n)]
+        arrivals.start(blocks, places, c_sems)
         chunks = [side_copies(gate_ref, up_ref, router_ref, side, side_sems, pack, j, width) for j in range(STEPS)]
         downs = down_copies(down_ref, stack, stack_sems, pack)
         x_copy = pltpu.make_async_copy(x_ref, x_v, x_sems.at[0])
         pre_copy = pltpu.make_async_copy(pre_ref, pre_v, x_sems.at[1])
         for copy in downs + [pre_copy] + sum(chunks, []) + [x_copy]:
             copy.start()
-        c_copy.wait()
-        leaving = []
+        arrivals.wait(blocks, places, c_sems)
+        leaving = [pltpu.make_async_copy(c_v, c_ref, out_sems.at[STEPS])]
+        leaving[0].start()
         for copy in downs:
             copy.wait()
         both = mm(c_v[...], stack[...], LAST)
         parts = [both[:, h * hidden_n : (h + 1) * hidden_n] for h in range(pack)]
         pre_copy.wait()
-        raw = regroup(fold(parts, slots), group, block_rows // group, seq_n)
-        raw = jnp.where(first_part(rows, pack, slots), raw * scale_ref[...], 0.0)
+        raw = jnp.where(first_part(rows, pack, slots), fold(parts, slots) * scale_ref[...], 0.0)
         gate = pre_v[:, :hidden_n]
         up = pre_v[:, hidden_n : 2 * hidden_n]
         g = pre_v[:, 2 * hidden_n : 2 * hidden_n + 1]
@@ -468,9 +461,10 @@
 
     return pl.pallas_call(
         body,
-        in_specs=[ANYWHERE] * 7 + [IN_VMEM],
-        out_specs=[ANYWHERE, IN_VMEM],
+        in_specs=[ANYWHERE] * (n_blocks + 6) + [IN_VMEM],
+        out_specs=[ANYWHERE] * 2 + [IN_VMEM],
         out_shape=[
+            shape((rows, part)),
             shape((seq_n, block_rows, part + extra)),
             shape((rows, total)),
         ],
@@ -482,14 +476,15 @@
             pltpu.VMEM((part, total), BF16),
             pltpu.VMEM((pack * hidden_n, part), BF16),
             pltpu.VMEM((rows, LANES), BF16),
-            pltpu.SemaphoreType.DMA((3,)),
+            pltpu.SemaphoreType.DMA((seq_n,)),
+            pltpu.SemaphoreType.DMA((2,)),
             pltpu.SemaphoreType.DMA((STEPS, 2 * pack + 1)),
             pltpu.SemaphoreType.DMA((pack,)),
-            pltpu.SemaphoreType.DMA((STEPS,)),
+            pltpu.SemaphoreType.DMA((STEPS + 1,)),
         ],
         compiler_params=PARAMS,
-        cost_estimate=cost(6 * rows * part * pack * hidden_n, 6 * part * pack * hidden_n),
-    )(*to_hbm(c, router_side, w_gate, w_up, w_down, x, pre), hid_scale)
+        cost_estimate=cost(100 * rows * part * pack * hidden_n, 100 * part * pack * hidden_n),
+    )(*to_hbm(*arrivals.blocks, router_side, w_gate, w_up, w_down, x, pre), hid_scale)
 
 
 def side_grads(x, delta, pack, hidden_n):
@@ -549,12 +544,10 @@
     return lax.ppermute(block, "seq", [(s, s - 1) for s in range(first, last)])
 
 
-def line_gather(block, n, hold, step):
+def line_gather(block, n):
     ups, downs = [], []
     up = down = block
     for j in range(1, n):
-        if j == step:
-            up, down, _ = lax.optimization_barrier((up, down, hold))
         up = up_line(up, n, j - 1)
         down = down_line(down, n, 1, n - j + 1)
         ups.append(up)
@@ -579,21 +572,14 @@
     pack = max(1, 8 // slots)
     chosen = picks[0].T
 
-    def to_experts(block):
-        block = block.reshape(experts, -1, block.shape[1])
-        return lax.all_to_all(block, "exp", split_axis=0, concat_axis=0, tiled=True).reshape(-1, block.shape[2])
-
     def to_owners(parts):
         parts = parts.reshape(everyone, -1, parts.shape[2])
         return lax.all_to_all(parts, BOTH, split_axis=0, concat_axis=0, tiled=True).reshape(-1, parts.shape[2])
 
-    c_rows, x_rows, hot = choose_rows(tokens, cotangent, chosen, counts, pack)
-    x_rows = to_experts(x_rows)
-    c_in = line_gather(c_rows, seq_n, x_rows, 2)
-    c_sent = by_place(c_in, seq_n, experts)
-    x_in = line_gather(x_rows, seq_n, c_sent, 3)
-    c = lax.all_to_all(c_sent, "exp", split_axis=0, concat_axis=0, tiled=True)
-    c = c.reshape(-1, c.shape[-1])
+    sent, hot = choose_rows(tokens, cotangent, chosen, counts, pack)
+    sent = sent.reshape(experts, 2, -1, sent.shape[1])
+    here = lax.all_to_all(sent, "exp", split_axis=0, concat_axis=0, tiled=True)
+    x_in, c_in = (line_gather(here[:, n].reshape(-1, here.shape[3]), seq_n) for n in range(2))
     halves = list(router.reshape(pack, features // pack, experts))
     router_side = jnp.concatenate(halves + halves, axis=1)
     router_side = jnp.pad(router_side, ((0, 0), (0, LANES - router_side.shape[1])))
@@ -602,8 +588,8 @@
         x_in, seq_n, slots, experts, pack, router_side, threshold, w_gate, w_up, w_down, hid_scale
     )
     out = to_owners(out)
-    back, delta = expert_backward(
-        c, seq_n, exp_n, slots, pack, x, pre, router_side, w_gate, w_up, w_down, hid_scale
+    c, back, delta = expert_backward(
+        c_in, seq_n, exp_n, slots, pack, x, pre, router_side, w_gate, w_up, w_down, hid_scale
     )
     back, out = lax.optimization_barrier((back, out))
     back = to_owners(back)

time: 140 us -> 132 us (0.943)
  starting transfers between devices: 35 us -> 25.6 us
  blocking collectives: 10.7 us -> 14.9 us
    ppermute x6, starting transfers between devices: 16.2 us -> 11.4 us  [up_line(): return lax.ppermute(block, 'seq', [(s, s + 1) for s in range(first, last)])]
    all_to_all x1, blocking collectives: 10.7 us -> 14.9 us  [on_device(): here = lax.all_to_all(sent, 'exp', split_axis=0, concat_axis=0, tiled=True)]
    all_to_all x1 -> x0, starting transfers between devices: 3.57 us -> none  [on_device(): c = lax.all_to_all(c_sent, 'exp', split_axis=0, concat_axis=0, tiled=True)]
    ppermute x6, waiting for transfers between devices: 16.5 us -> 13.5 us  [down_line(): return lax.ppermute(block, 'seq', [(s, s - 1) for s in range(first, last)])]
    ppermute x6, waiting for transfers between devices: 1 us -> 3.44 us  [up_line(): return lax.ppermute(block, 'seq', [(s, s + 1) for s in range(first, last)])]
    pallas_call x3 -> x2, Pallas kernels: 18.1 us -> 16.9 us  [the longest x1 12.6 us: expert_backward(): pl.pallas_call(body, in_specs=[ANYWHERE] * (n_blocks + 6) + [IN_VMEM], ou...]
  transfers between devices with their start and end apart: 15 -> 14, of which waited for: 6 -> 8; matrix products, arithmetic and copies ran while one was open for 1% -> 1% of each run, Pallas kernels for 28% -> 28%
where the time goes in v9:
time: 132 us; the launch traced here: 131 us
  Pallas kernels  44.6 us (34%)
  waiting for transfers between devices  42.8 us (32%)
  starting transfers between devices  25.6 us (19%)
  blocking collectives  14.9 us (11%)
  local copies, waits for them, and re-layouts  2.01 us (2%)
    all_to_all x2, waiting for transfers between devices, to_owners(): lax.all_to_all(parts, BOTH, split_axis=0, concat_axis=0, tiled=True)  25.8 us
    all_to_all x1, blocking collectives, on_device(): here = lax.all_to_all(sent, 'exp', split_axis=0, concat_axis=0, tiled=True)  14.9 us
    ppermute x6, waiting for transfers between devices, down_line(): return lax.ppermute(block, 'seq', [(s, s - 1) for s in range(first, last)])  13.5 us
    pallas_call x1, Pallas kernels, expert_backward(): pl.pallas_call(body, in_specs=[ANYWHERE] * (n_blocks + 6) + [IN_VMEM], ou...  12.6 us
    ppermute x6, starting transfers between devices, up_line(): return lax.ppermute(block, 'seq', [(s, s + 1) for s in range(first, last)])  11.4 us
    pallas_call x1, Pallas kernels, expert_forward(): pl.pallas_call(body, in_specs=[ANYWHERE] * (n_blocks + 4) + [IN_VMEM] * 2...  9.01 us
    ppermute x6, starting transfers between devices, down_line(): return lax.ppermute(block, 'seq', [(s, s - 1) for s in range(first, last)])  7.72 us
    pallas_call x1, Pallas kernels, side_grads(): pl.pallas_call(body, grid=(STEPS,), in_specs=[pl.BlockSpec((rows, width),...  6.87 us
  transfers between devices with their start and end apart: 14, of which 8 were waited for; matrix products, arithmetic and copies ran while one was open for 1% of the time, Pallas kernels for 28%

profile of v9, /device:TPU:0, one launch (start us, length us, event | category | flops | bytes accessed | tf_op | source)
XLA Modules:
  0.0 131.0 jit_solution(2953024495773588404)
XLA Ops:
  0.6 0.0 copy-start.8
  0.6 4.3 %shard_map.153 = (bf16[128,2048]{1,0:T(8,128)(2,1)}, bf16[2,64,256]{2,1,0:T(8,128)(2,1)}) custom-call(s32[4,8]{1,0:T(4,128)} %bitcast.22, s32[1,8]{1,0:T(1,128)} %counts_ref.1, bf16[256,4096]{1,0:T(8,128)(2,1)} %c_ref.1, bf16[256,4096]{1,0:T(8,128)(2,1)} %x_ref.1), custom_call_target="tpu_custom_call" | custom-call | flops 536870912 | bytes 4194304 | tf_op jit(solution)/shard_map/pallas_call | solution.py:102
  5.0 14.9 %all_to_all.15 = bf16[8,2,8,2048]{3,2,1,0:T(8,128)(2,1)S(1)} all-to-all(bf16[8,2,8,2048]{3,2,1,0:T(8,128)(2,1)} %bitcast.21), channel_id=1, replica_groups=mesh['seq'=4,'exp'=8] {'exp'}, dimensions={0} | all-to-all | bytes 1048576 | tf_op jit(solution)/shard_map/all_to_all | solution.py:581
  19.9 0.0 copy-start
  20.0 1.3 collective-permute-start.9
  21.3 4.6 %collective-permute-start.6 = (bf16[64,2048]{1,0:T(8,128)(2,1)S(1)}, bf16[64,2048]{1,0:T(8,128)(2,1)S(1)}, u32[]{:S(2)}, u32[]{:S(2)}) collective-permute-start(bf16[64,2048]{1,0:T(8,128)(2,1)S(1)} %get-tuple-element.39.refs_0_), channel_id=1, source_target_pairs={{0,8},{8,16},{16,24},{1,9},{9,17},{17,25},{2,10},{10,18},{18,26},{... | collective-permute-start | bytes 786440 | tf_op jit(solution)/shard_map/ppermute | solution.py:539
  25.8 3.5 %collective-permute-start = (bf16[64,2048]{1,0:T(8,128)(2,1)S(1)}, bf16[64,2048]{1,0:T(8,128)(2,1)S(1)}, u32[]{:S(2)}, u32[]{:S(2)}) collective-permute-start(bf16[64,2048]{1,0:T(8,128)(2,1)S(1)} %get-tuple-element.40.refs_0_), channel_id=1, source_target_pairs={{0,8},{8,16},{16,24},{1,9},{9,17},{17,25},{2,10},{10,18},{18,26},{... | collective-permute-start | bytes 786440 | tf_op jit(solution)/shard_map/ppermute | solution.py:539
  29.3 1.3 collective-permute-start.3
  30.6 0.0 collective-permute-done.9.refs_4_
  30.6 1.3 collective-permute-start.10
  31.9 0.6 collective-permute-done.6.refs_1_
  32.6 0.7 collective-permute-start.7
  33.2 2.8 %collective-permute-done.refs_1_ = bf16[64,2048]{1,0:T(8,128)(2,1)S(1)} collective-permute-done((bf16[64,2048]{1,0:T(8,128)(2,1)S(1)}, bf16[64,2048]{1,0:T(8,128)(2,1)S(1)}, u32[]{:S(2)}, u32[]{:S(2)}) %collective-permute-start) | collective-permute-done | bytes 262176 | tf_op jit(solution)/shard_map/ppermute | solution.py:539
  36.0 0.7 collective-permute-start.1
  36.7 3.7 %collective-permute-done.3.refs_4_ = bf16[64,2048]{1,0:T(8,128)(2,1)S(1)} collective-permute-done((bf16[64,2048]{1,0:T(8,128)(2,1)S(1)}, bf16[64,2048]{1,0:T(8,128)(2,1)S(1)}, u32[]{:S(2)}, u32[]{:S(2)}) %collective-permute-start.3) | collective-permute-done | bytes 262176 | tf_op jit(solution)/shard_map/ppermute | solution.py:544
  40.5 1.3 collective-permute-start.4
  41.7 2.5 %collective-permute-done.10.refs_5_ = bf16[64,2048]{1,0:T(8,128)(2,1)S(1)} collective-permute-done((bf16[64,2048]{1,0:T(8,128)(2,1)S(1)}, bf16[64,2048]{1,0:T(8,128)(2,1)S(1)}, u32[]{:S(2)}, u32[]{:S(2)}) %collective-permute-start.10) | collective-permute-done | bytes 262176 | tf_op jit(solution)/shard_map/ppermute | solution.py:544
  44.2 1.3 collective-permute-start.11
  45.5 0.0 collective-permute-done.7.refs_2_
  45.5 0.7 collective-permute-start.8
  46.2 0.0 copy-done.8
  46.2 0.0 collective-permute-done.1.refs_2_
  46.2 0.0 copy-start.11
  46.2 1.4 %collective-permute-start.2 = (bf16[64,2048]{1,0:T(8,128)(2,1)S(1)}, bf16[64,2048]{1,0:T(8,128)(2,1)}, u32[]{:S(2)}, u32[]{:S(2)}) collective-permute-start(bf16[64,2048]{1,0:T(8,128)(2,1)S(1)} %collective-permute-done.1.refs_2_), channel_id=1, source_target_pairs={{16,24},{17,25},{18,26},{19,27},{20,28},{21,29},{22,30},{23,31}} | collective-permute-start | bytes 786440 | tf_op jit(solution)/shard_map/ppermute | solution.py:539
  47.6 4.5 %collective-permute-done.4.refs_5_ = bf16[64,2048]{1,0:T(8,128)(2,1)} collective-permute-done((bf16[64,2048]{1,0:T(8,128)(2,1)S(1)}, bf16[64,2048]{1,0:T(8,128)(2,1)}, u32[]{:S(2)}, u32[]{:S(2)}) %collective-permute-start.4) | collective-permute-done | bytes 262176 | tf_op jit(solution)/shard_map/ppermute | solution.py:544
  52.2 1.3 collective-permute-start.5
  53.5 0.3 copy.22
  53.8 0.9 pad.4.refs_7_
  54.7 2.8 %collective-permute-done.11.refs_6_ = bf16[64,2048]{1,0:T(8,128)(2,1)S(1)} collective-permute-done((bf16[64,2048]{1,0:T(8,128)(2,1)S(1)}, bf16[64,2048]{1,0:T(8,128)(2,1)S(1)}, u32[]{:S(2)}, u32[]{:S(2)}) %collective-permute-start.11) | collective-permute-done | bytes 262176 | tf_op jit(solution)/shard_map/ppermute | solution.py:544
  57.4 0.0 collective-permute-done.8.refs_3_
  57.4 0.0 copy-done.1
  57.5 0.0 copy-done.2
  57.5 0.0 copy-done.3
  57.5 0.0 copy-done.4
  57.5 0.7 copy-done.5
  58.1 0.1 copy-done.6
  58.2 9.0 %shard_map.154 = (bf16[256,2048]{1,0:T(8,128)(2,1)}, bf16[4,64,2048]{2,1,0:T(8,128)(2,1)}, f32[256,896]{1,0:T(8,128)}, bf16[256,768]{1,0:T(8,128)(2,1)}) custom-call(bf16[64,2048]{1,0:T(8,128)(2,1)} %copy-done, bf16[64,2048]{1,0:T(8,128)(2,1)} %copy-done.2, bf16[64,2048]{1,0:T(8,128)(2,1)} %copy-done.4, bf16[64,2048]{1,0:T(8,128)(2,1)} %copy-done.6, ...), custom_call_target="tpu_custom_call" | custom-call | flops 2415919104 | bytes 18874368 | tf_op jit(solution)/shard_map/pallas_call | solution.py:324
  67.3 2.7 %all-to-all-start.1 = ((bf16[32,8,2048]{2,1,0:T(8,128)(2,1)}), bf16[32,8,2048]{2,1,0:T(8,128)(2,1)S(1)}, u32[]{:S(2)}, u32[]{:S(2)}) async-start(bf16[32,8,2048]{2,1,0:T(8,128)(2,1)} %bitcast.20), calls=%async_computation.1 | async-start | bytes 2097152 | tf_op jit(solution)/shard_map/all_to_all | solution.py:577
  69.9 0.0 collective-permute-done.2.refs_3_
  69.9 0.0 collective-permute-done.5.refs_6_
  70.0 12.6 %shard_map.155 = (bf16[256,2048]{1,0:T(8,128)(2,1)}, bf16[4,64,2176]{2,1,0:T(8,128)(2,1)}, bf16[256,1664]{1,0:T(8,128)(2,1)}) custom-call(bf16[64,2048]{1,0:T(8,128)(2,1)} %copy-done.7, bf16[64,2048]{1,0:T(8,128)(2,1)} %copy-done.9, bf16[64,2048]{1,0:T(8,128)(2,1)} %copy-done.11, bf16[64,2048]{1,0:T(8,128)(2,1)} %collective-permute-done.2.refs_3_, ...), custom_call_target="tpu_custom_call" | custom-call | flops 40265318400 | bytes 157286400 | tf_op jit(solution)/shard_map/pallas_call | solution.py:462
  82.5 13.6 %all-to-all-done.1 = bf16[32,8,2048]{2,1,0:T(8,128)(2,1)S(1)} async-done(((bf16[32,8,2048]{2,1,0:T(8,128)(2,1)}), bf16[32,8,2048]{2,1,0:T(8,128)(2,1)S(1)}, u32[]{:S(2)}, u32[]{:S(2)}) %all-to-all-start.1) | async-done | bytes 1048608 | tf_op jit(solution)/shard_map/all_to_all | solution.py:577
  96.1 3.8 %all-to-all-start.2 = ((bf16[32,8,2176]{2,1,0:T(8,128)(2,1)}), bf16[32,8,2176]{2,1,0:T(8,128)(2,1)S(1)}, u32[]{:S(2)}, u32[]{:S(2)}) async-start(bf16[32,8,2176]{2,1,0:T(8,128)(2,1)} %bitcast.19), calls=%async_computation.2 | async-start | bytes 2228224 | tf_op jit(solution)/shard_map/all_to_all | solution.py:577
  99.9 5.5 %shard_map.159 = f32[1,384,4096]{2,1,0:T(8,128)} custom-call(bf16[256,2048]{1,0:T(8,128)(2,1)} %get-tuple-element.37.c_ref, bf16[256,768]{1,0:T(8,128)(2,1)} %get-tuple-element.38.hidden_ref), custom_call_target="tpu_custom_call" | custom-call | flops 805306368 | bytes 6291456 | tf_op jit(solution)/shard_map/pallas_call | solution.py:523
  105.4 6.9 %shard_map.158 = (f32[2,2048,384]{2,1,0:T(8,128)}, f32[2,2048,384]{2,1,0:T(8,128)}) custom-call(bf16[256,2048]{1,0:T(8,128)(2,1)} %get-tuple-element.25.refs_11_.x_ref, bf16[256,1664]{1,0:T(8,128)(2,1)} %get-tuple-element.34.delta_ref), custom_call_target="tpu_custom_call" | custom-call | flops 1610612736 | bytes 12582912 | tf_op jit(solution)/shard_map/pallas_call | solution.py:501
  112.2 2.9 %shard_map.156 = bf16[256,4096]{1,0:T(8,128)(2,1)} custom-call(bf16[2,64,256]{2,1,0:T(8,128)(2,1)} %get-tuple-element.23.hot_ref, bf16[256,2048]{1,0:T(8,128)(2,1)S(1)} %bitcast.17), custom_call_target="tpu_custom_call" | custom-call | flops 536870912 | bytes 2097152 | tf_op jit(solution)/shard_map/pallas_call | solution.py:173
  115.2 12.2 %all-to-all-done.2 = bf16[32,8,2176]{2,1,0:T(8,128)(2,1)S(1)} async-done(((bf16[32,8,2176]{2,1,0:T(8,128)(2,1)}), bf16[32,8,2176]{2,1,0:T(8,128)(2,1)S(1)}, u32[]{:S(2)}, u32[]{:S(2)}) %all-to-all-start.2) | async-done | bytes 1114144 | tf_op jit(solution)/shard_map/all_to_all | solution.py:577
  127.4 3.5 %shard_map.157 = (bf16[256,4096]{1,0:T(8,128)(2,1)}, f32[8,128]{1,0:T(8,128)}, f32[1,8]{1,0:T(1,128)}) custom-call(bf16[2,64,256]{2,1,0:T(8,128)(2,1)} %get-tuple-element.23.hot_ref, bf16[256,2176]{1,0:T(8,128)(2,1)S(1)} %bitcast.18), custom_call_target="tpu_custom_call" | custom-call | flops 536870912 | bytes 2097152 | tf_op jit(solution)/shard_map/pallas_call | solution.py:173
  (17 shorter events, 0.1 us)
Async XLA Ops:
  0.6 45.6 %copy-start.8 = (bf16[4096,8]{0,1:T(8,128)(2,1)S(1)}, bf16[4096,8]{0,1:T(8,128)(2,1)}, u32[]{:S(2)}) copy-start(bf16[4096,8]{0,1:T(8,128)(2,1)} %param.12) | copy-start | bytes 196612
  19.9 37.5 %copy-start = (bf16[64,2048]{1,0:T(8,128)(2,1)}, bf16[64,2048]{1,0:T(8,128)(2,1)S(1)}, u32[]{:S(2)}) copy-start(bf16[64,2048]{1,0:T(8,128)(2,1)S(1)} %get-tuple-element.39.refs_0_) | copy-start | bytes 786436
  19.9 47.3 %copy-start.7 = (bf16[64,2048]{1,0:T(8,128)(2,1)}, bf16[64,2048]{1,0:T(8,128)(2,1)S(1)}, u32[]{:S(2)}) copy-start(bf16[64,2048]{1,0:T(8,128)(2,1)S(1)} %get-tuple-element.40.refs_0_) | copy-start | bytes 786436
  20.0 10.7 %collective-permute-start.9 = (bf16[64,2048]{1,0:T(8,128)(2,1)S(1)}, bf16[64,2048]{1,0:T(8,128)(2,1)S(1)}, u32[]{:S(2)}, u32[]{:S(2)}) collective-permute-start(bf16[64,2048]{1,0:T(8,128)(2,1)S(1)} %get-tuple-element.39.refs_0_), channel_id=1, source_target_pairs={{8,0},{16,8},{24,16},{9,1},{17,9},{25,17},{10,2},{18,10},{26,18},{... | collective-permute-start | bytes 786440 | tf_op jit(solution)/shard_map/ppermute | solution.py:544
  21.3 11.3 %collective-permute-start.6 = (bf16[64,2048]{1,0:T(8,128)(2,1)S(1)}, bf16[64,2048]{1,0:T(8,128)(2,1)S(1)}, u32[]{:S(2)}, u32[]{:S(2)}) collective-permute-start(bf16[64,2048]{1,0:T(8,128)(2,1)S(1)} %get-tuple-element.39.refs_0_), channel_id=1, source_target_pairs={{0,8},{8,16},{16,24},{1,9},{9,17},{17,25},{2,10},{10,18},{18,26},{... | collective-permute-start | bytes 786440 | tf_op jit(solution)/shard_map/ppermute | solution.py:539
  25.8 10.2 %collective-permute-start = (bf16[64,2048]{1,0:T(8,128)(2,1)S(1)}, bf16[64,2048]{1,0:T(8,128)(2,1)S(1)}, u32[]{:S(2)}, u32[]{:S(2)}) collective-permute-start(bf16[64,2048]{1,0:T(8,128)(2,1)S(1)} %get-tuple-element.40.refs_0_), channel_id=1, source_target_pairs={{0,8},{8,16},{16,24},{1,9},{9,17},{17,25},{2,10},{10,18},{18,26},{... | collective-permute-start | bytes 786440 | tf_op jit(solution)/shard_map/ppermute | solution.py:539
  29.3 11.1 %collective-permute-start.3 = (bf16[64,2048]{1,0:T(8,128)(2,1)S(1)}, bf16[64,2048]{1,0:T(8,128)(2,1)S(1)}, u32[]{:S(2)}, u32[]{:S(2)}) collective-permute-start(bf16[64,2048]{1,0:T(8,128)(2,1)S(1)} %get-tuple-element.40.refs_0_), channel_id=1, source_target_pairs={{8,0},{16,8},{24,16},{9,1},{17,9},{25,17},{10,2},{18,10},{26,18},{... | collective-permute-start | bytes 786440 | tf_op jit(solution)/shard_map/ppermute | solution.py:544
  30.6 26.8 %copy-start.1 = (bf16[64,2048]{1,0:T(8,128)(2,1)}, bf16[64,2048]{1,0:T(8,128)(2,1)S(1)}, u32[]{:S(2)}) copy-start(bf16[64,2048]{1,0:T(8,128)(2,1)S(1)} %collective-permute-done.9.refs_4_) | copy-start | bytes 786436
  30.6 13.6 %collective-permute-start.10 = (bf16[64,2048]{1,0:T(8,128)(2,1)S(1)}, bf16[64,2048]{1,0:T(8,128)(2,1)S(1)}, u32[]{:S(2)}, u32[]{:S(2)}) collective-permute-start(bf16[64,2048]{1,0:T(8,128)(2,1)S(1)} %collective-permute-done.9.refs_4_), channel_id=1, source_target_pairs={{8,0},{16,8},{9,1},{17,9},{10,2},{18,10},{11,3},{19,11},{12,4},{20... | collective-permute-start | bytes 786440 | tf_op jit(solution)/shard_map/ppermute | solution.py:544
  32.6 24.9 %copy-start.2 = (bf16[64,2048]{1,0:T(8,128)(2,1)}, bf16[64,2048]{1,0:T(8,128)(2,1)S(1)}, u32[]{:S(2)}) copy-start(bf16[64,2048]{1,0:T(8,128)(2,1)S(1)} %collective-permute-done.6.refs_1_) | copy-start | bytes 786436
  32.6 12.9 %collective-permute-start.7 = (bf16[64,2048]{1,0:T(8,128)(2,1)S(1)}, bf16[64,2048]{1,0:T(8,128)(2,1)S(1)}, u32[]{:S(2)}, u32[]{:S(2)}) collective-permute-start(bf16[64,2048]{1,0:T(8,128)(2,1)S(1)} %collective-permute-done.6.refs_1_), channel_id=1, source_target_pairs={{8,16},{16,24},{9,17},{17,25},{10,18},{18,26},{11,19},{19,27},{12,... | collective-permute-start | bytes 786440 | tf_op jit(solution)/shard_map/ppermute | solution.py:539
  36.0 31.2 %copy-start.9 = (bf16[64,2048]{1,0:T(8,128)(2,1)}, bf16[64,2048]{1,0:T(8,128)(2,1)S(1)}, u32[]{:S(2)}) copy-start(bf16[64,2048]{1,0:T(8,128)(2,1)S(1)} %collective-permute-done.refs_1_) | copy-start | bytes 786436
  36.0 10.2 %collective-permute-start.1 = (bf16[64,2048]{1,0:T(8,128)(2,1)S(1)}, bf16[64,2048]{1,0:T(8,128)(2,1)S(1)}, u32[]{:S(2)}, u32[]{:S(2)}) collective-permute-start(bf16[64,2048]{1,0:T(8,128)(2,1)S(1)} %collective-permute-done.refs_1_), channel_id=1, source_target_pairs={{8,16},{16,24},{9,17},{17,25},{10,18},{18,26},{11,19},{19,27},{12,... | collective-permute-start | bytes 786440 | tf_op jit(solution)/shard_map/ppermute | solution.py:539
  40.5 29.5 %copy-start.10 = (bf16[64,2048]{1,0:T(8,128)(2,1)}, bf16[64,2048]{1,0:T(8,128)(2,1)S(1)}, u32[]{:S(2)}) copy-start(bf16[64,2048]{1,0:T(8,128)(2,1)S(1)} %collective-permute-done.3.refs_4_) | copy-start | bytes 786436
  40.5 11.7 %collective-permute-start.4 = (bf16[64,2048]{1,0:T(8,128)(2,1)S(1)}, bf16[64,2048]{1,0:T(8,128)(2,1)}, u32[]{:S(2)}, u32[]{:S(2)}) collective-permute-start(bf16[64,2048]{1,0:T(8,128)(2,1)S(1)} %collective-permute-done.3.refs_4_), channel_id=1, source_target_pairs={{8,0},{16,8},{9,1},{17,9},{10,2},{18,10},{11,3},{19,11},{12,4},{20... | collective-permute-start | bytes 786440 | tf_op jit(solution)/shard_map/ppermute | solution.py:544
  44.2 13.3 %copy-start.3 = (bf16[64,2048]{1,0:T(8,128)(2,1)}, bf16[64,2048]{1,0:T(8,128)(2,1)S(1)}, u32[]{:S(2)}) copy-start(bf16[64,2048]{1,0:T(8,128)(2,1)S(1)} %collective-permute-done.10.refs_5_) | copy-start | bytes 786436
  44.2 13.2 %collective-permute-start.11 = (bf16[64,2048]{1,0:T(8,128)(2,1)S(1)}, bf16[64,2048]{1,0:T(8,128)(2,1)S(1)}, u32[]{:S(2)}, u32[]{:S(2)}) collective-permute-start(bf16[64,2048]{1,0:T(8,128)(2,1)S(1)} %collective-permute-done.10.refs_5_), channel_id=1, source_target_pairs={{8,0},{9,1},{10,2},{11,3},{12,4},{13,5},{14,6},{15,7}} | collective-permute-start | bytes 786440 | tf_op jit(solution)/shard_map/ppermute | solution.py:544
  45.5 12.0 %copy-start.4 = (bf16[64,2048]{1,0:T(8,128)(2,1)}, bf16[64,2048]{1,0:T(8,128)(2,1)S(1)}, u32[]{:S(2)}) copy-start(bf16[64,2048]{1,0:T(8,128)(2,1)S(1)} %collective-permute-done.7.refs_2_) | copy-start | bytes 786436
  45.5 11.9 %collective-permute-start.8 = (bf16[64,2048]{1,0:T(8,128)(2,1)S(1)}, bf16[64,2048]{1,0:T(8,128)(2,1)S(1)}, u32[]{:S(2)}, u32[]{:S(2)}) collective-permute-start(bf16[64,2048]{1,0:T(8,128)(2,1)S(1)} %collective-permute-done.7.refs_2_), channel_id=1, source_target_pairs={{16,24},{17,25},{18,26},{19,27},{20,28},{21,29},{22,30},{23,31}} | collective-permute-start | bytes 786440 | tf_op jit(solution)/shard_map/ppermute | solution.py:539
  46.2 23.7 %copy-start.11 = (bf16[64,2048]{1,0:T(8,128)(2,1)}, bf16[64,2048]{1,0:T(8,128)(2,1)S(1)}, u32[]{:S(2)}) copy-start(bf16[64,2048]{1,0:T(8,128)(2,1)S(1)} %collective-permute-done.1.refs_2_) | copy-start | bytes 786436
  46.2 23.7 %collective-permute-start.2 = (bf16[64,2048]{1,0:T(8,128)(2,1)S(1)}, bf16[64,2048]{1,0:T(8,128)(2,1)}, u32[]{:S(2)}, u32[]{:S(2)}) collective-permute-start(bf16[64,2048]{1,0:T(8,128)(2,1)S(1)} %collective-permute-done.1.refs_2_), channel_id=1, source_target_pairs={{16,24},{17,25},{18,26},{19,27},{20,28},{21,29},{22,30},{23,31}} | collective-permute-start | bytes 786440 | tf_op jit(solution)/shard_map/ppermute | solution.py:539
  52.2 17.8 %collective-permute-start.5 = (bf16[64,2048]{1,0:T(8,128)(2,1)}, bf16[64,2048]{1,0:T(8,128)(2,1)}, u32[]{:S(2)}, u32[]{:S(2)}) collective-permute-start(bf16[64,2048]{1,0:T(8,128)(2,1)} %collective-permute-done.4.refs_5_), channel_id=1, source_target_pairs={{8,0},{9,1},{10,2},{11,3},{12,4},{13,5},{14,6},{15,7}} | collective-permute-start | bytes 786440 | tf_op jit(solution)/shard_map/ppermute | solution.py:544
  57.4 0.7 copy-start.5
  57.4 0.8 copy-start.6
  67.3 28.9 %all-to-all-start.1 = ((bf16[32,8,2048]{2,1,0:T(8,128)(2,1)}), bf16[32,8,2048]{2,1,0:T(8,128)(2,1)S(1)}, u32[]{:S(2)}, u32[]{:S(2)}) async-start(bf16[32,8,2048]{2,1,0:T(8,128)(2,1)} %bitcast.20), calls=%async_computation.1 | async-start | bytes 2097152 | tf_op jit(solution)/shard_map/all_to_all | solution.py:577
  96.1 31.2 %all-to-all-start.2 = ((bf16[32,8,2176]{2,1,0:T(8,128)(2,1)}), bf16[32,8,2176]{2,1,0:T(8,128)(2,1)S(1)}, u32[]{:S(2)}, u32[]{:S(2)}) async-start(bf16[32,8,2176]{2,1,0:T(8,128)(2,1)} %bitcast.19), calls=%async_computation.2 | async-start | bytes 2228224 | tf_op jit(solution)/shard_map/all_to_all | solution.py:577

commit v10 on v9

--- a/solution.py
+++ b/solution.py
@@ -48,16 +48,17 @@
 
     def body(picks_ref, counts_ref, c_ref, x_ref, out_ref, hot_ref, picks_s, counts_s, c_v, x_v, out_v, sems, out_sems):
         small = [
-            pltpu.make_async_copy(picks_ref, picks_s, sems.at[2 * STEPS]),
-            pltpu.make_async_copy(counts_ref, counts_s, sems.at[2 * STEPS + 1]),
+            pltpu.make_async_copy(picks_ref, picks_s, sems.at[STEPS, 0]),
+            pltpu.make_async_copy(counts_ref, counts_s, sems.at[STEPS, 1]),
         ]
         for copy in small:
             copy.start()
         large = []
         for j in range(STEPS):
-            now = pl.ds(j * pack * width, pack * width)
-            large.append(pltpu.make_async_copy(x_ref.at[:, now], x_v.at[:, now], sems.at[2 * j]))
-            large.append(pltpu.make_async_copy(c_ref.at[:, now], c_v.at[:, now], sems.at[2 * j + 1]))
+            for h in range(pack):
+                now = pl.ds(h * part + j * width, width)
+                for n, (ref, held) in enumerate(((x_ref, x_v), (c_ref, c_v))):
+                    large.append(pltpu.make_async_copy(ref.at[:, now], held.at[:, now], sems.at[j, 2 * h + n]))
         for copy in large:
             copy.start()
         for copy in small:
@@ -84,10 +85,10 @@
                 [live[h][(2 * e + 1) * group : (2 * e + 2) * group] for e in range(experts)]
             ).astype(BF16)
         live = [value.astype(BF16) for value in live]
-        for copy in large:
-            copy.wait()
         leaving = []
         for j in range(STEPS):
+            for copy in large[2 * pack * j : 2 * pack * (j + 1)]:
+                copy.wait()
             total = 0.0
             for h in range(pack):
                 now = slice(h * part + j * width, h * part + (j + 1) * width)
@@ -110,7 +111,7 @@
             pltpu.VMEM(tokens.shape, BF16),
             pltpu.VMEM(tokens.shape, BF16),
             pltpu.VMEM((count, part), BF16),
-            pltpu.SemaphoreType.DMA((2 * STEPS + 2,)),
+            pltpu.SemaphoreType.DMA((STEPS + 1, 2 * pack)),
             pltpu.SemaphoreType.DMA((STEPS,)),
         ],
         compiler_params=PARAMS,
@@ -207,6 +208,9 @@
 class Arrivals:
     def __init__(self, blocks, plan):
         self.blocks, self.plan = blocks, plan
+
+    def near(self, step):
+        return self.blocks[step], self.blocks[len(self.blocks) // 2 + step]
 
     def start(self, refs, places, sems):
         here = lax.axis_index("seq")
@@ -544,16 +548,29 @@
     return lax.ppermute(block, "seq", [(s, s - 1) for s in range(first, last)])
 
 
-def line_gather(block, n):
+def line_gather(block, n, pause=None):
     ups, downs = [], []
-    up = down = block
-    for j in range(1, n):
-        up = up_line(up, n, j - 1)
-        down = down_line(down, n, 1, n - j + 1)
-        ups.append(up)
-        downs.append(down)
     plan = [(0, 0, 0)] + [(k, 2 * n - 1 - k, k) for k in range(1, n)]
-    return Arrivals([block] + ups + downs, plan)
+
+    def go(up, down, first, last):
+        for j in range(first, last):
+            up = up_line(up, n, j - 1)
+            down = down_line(down, n, 1, n - j + 1)
+            ups.append(up)
+            downs.append(down)
+        return Arrivals([block] + ups + downs, plan)
+
+    if pause is None:
+        return go(block, block, 1, n)
+
+    def finish(value):
+        return go(behind(ups[-1], value), behind(downs[-1], value), pause + 1, n)
+
+    return go(block, block, 1, pause + 1), finish
+
+
+def behind(value, *others):
+    return lax.optimization_barrier((value, *others))[0]
 
 
 def on_device(tokens, cotangent, router, threshold, w_gate, w_up, w_down, hid_scale, picks, counts):
@@ -579,14 +596,19 @@
     sent, hot = choose_rows(tokens, cotangent, chosen, counts, pack)
     sent = sent.reshape(experts, 2, -1, sent.shape[1])
     here = lax.all_to_all(sent, "exp", split_axis=0, concat_axis=0, tiled=True)
-    x_in, c_in = (line_gather(here[:, n].reshape(-1, here.shape[3]), seq_n) for n in range(2))
+    x_rows, c_rows = (here[:, n].reshape(-1, here.shape[3]) for n in range(2))
+    x_in = line_gather(x_rows, seq_n)
+    c_rows = behind(c_rows, *(x_in.near(min(2, seq_n - 1))))
+    c_in, finish = line_gather(c_rows, seq_n, seq_n - 2)
     halves = list(router.reshape(pack, features // pack, experts))
     router_side = jnp.concatenate(halves + halves, axis=1)
     router_side = jnp.pad(router_side, ((0, 0), (0, LANES - router_side.shape[1])))
 
+    x_in.blocks[0] = behind(x_in.blocks[0], *c_in.near(1))
     x, out, pre, hidden = expert_forward(
         x_in, seq_n, slots, experts, pack, router_side, threshold, w_gate, w_up, w_down, hid_scale
     )
+    c_in = finish(pre)
     out = to_owners(out)
     c, back, delta = expert_backward(
         c_in, seq_n, exp_n, slots, pack, x, pre, router_side, w_gate, w_up, w_down, hid_scale

time: 132 us -> 139 us (1.053)
  waiting for transfers between devices: 42.8 us -> 46.9 us
  starting transfers between devices: 25.6 us -> 27.6 us
    ppermute x6, waiting for transfers between devices: 13.5 us -> 19.5 us  [down_line(): return lax.ppermute(block, 'seq', [(s, s - 1) for s in range(first, last)])]
    all_to_all x2, starting transfers between devices: 6.43 us -> 9.22 us  [to_owners(): lax.all_to_all(parts, BOTH, split_axis=0, concat_axis=0, tiled=True)]
    all_to_all x2, waiting for transfers between devices: 25.8 us -> 23.8 us  [to_owners(): lax.all_to_all(parts, BOTH, split_axis=0, concat_axis=0, tiled=True)]
  transfers between devices with their start and end apart: 14 -> 14, of which waited for: 8 -> 8; matrix products, arithmetic and copies ran while one was open for 1% -> 1% of each run, Pallas kernels for 28% -> 27%
where the time goes in v10:
time: 139 us; the launch traced here: 138 us
  waiting for transfers between devices  46.9 us (34%)
  Pallas kernels  44.3 us (32%)
  starting transfers between devices  27.6 us (20%)
  blocking collectives  14.9 us (11%)
  local copies, waits for them, and re-layouts  2.73 us (2%)
    all_to_all x2, waiting for transfers between devices, to_owners(): lax.all_to_all(parts, BOTH, split_axis=0, concat_axis=0, tiled=True)  23.8 us
    ppermute x6, waiting for transfers between devices, down_line(): return lax.ppermute(block, 'seq', [(s, s - 1) for s in range(first, last)])  19.5 us
    all_to_all x1, blocking collectives, on_device(): here = lax.all_to_all(sent, 'exp', split_axis=0, concat_axis=0, tiled=True)  14.9 us
    pallas_call x1, Pallas kernels, expert_backward(): pl.pallas_call(body, in_specs=[ANYWHERE] * (n_blocks + 6) + [IN_VMEM], ou...  12.5 us
    ppermute x6, starting transfers between devices, up_line(): return lax.ppermute(block, 'seq', [(s, s + 1) for s in range(first, last)])  10.7 us
    all_to_all x2, starting transfers between devices, to_owners(): lax.all_to_all(parts, BOTH, split_axis=0, concat_axis=0, tiled=True)  9.22 us
    pallas_call x1, Pallas kernels, expert_forward(): pl.pallas_call(body, in_specs=[ANYWHERE] * (n_blocks + 4) + [IN_VMEM] * 2...  9.05 us
    ppermute x6, starting transfers between devices, down_line(): return lax.ppermute(block, 'seq', [(s, s - 1) for s in range(first, last)])  7.73 us
  transfers between devices with their start and end apart: 14, of which 8 were waited for; matrix products, arithmetic and copies ran while one was open for 1% of the time, Pallas kernels for 27%

profile of v10, /device:TPU:0, one launch (start us, length us, event | category | flops | bytes accessed | tf_op | source)
XLA Modules:
  0.0 137.7 jit_solution(17393550662766099770)
XLA Ops:
  0.6 0.0 copy-start.8
  0.6 4.0 %shard_map.153 = (bf16[128,2048]{1,0:T(8,128)(2,1)}, bf16[2,64,256]{2,1,0:T(8,128)(2,1)}) custom-call(s32[4,8]{1,0:T(4,128)} %bitcast.22, s32[1,8]{1,0:T(1,128)} %counts_ref.1, bf16[256,4096]{1,0:T(8,128)(2,1)} %c_ref.1, bf16[256,4096]{1,0:T(8,128)(2,1)} %x_ref.1), custom_call_target="tpu_custom_call" | custom-call | flops 536870912 | bytes 4194304 | tf_op jit(solution)/shard_map/pallas_call | solution.py:103
  4.7 14.9 %all_to_all.15 = bf16[8,2,8,2048]{3,2,1,0:T(8,128)(2,1)S(1)} all-to-all(bf16[8,2,8,2048]{3,2,1,0:T(8,128)(2,1)} %bitcast.21), channel_id=1, replica_groups=mesh['seq'=4,'exp'=8] {'exp'}, dimensions={0} | all-to-all | bytes 1048576 | tf_op jit(solution)/shard_map/all_to_all | solution.py:598
  19.6 0.0 copy-start
  19.6 3.5 %collective-permute-start = (bf16[64,2048]{1,0:T(8,128)(2,1)S(1)}, bf16[64,2048]{1,0:T(8,128)(2,1)S(1)}, u32[]{:S(2)}, u32[]{:S(2)}) collective-permute-start(bf16[64,2048]{1,0:T(8,128)(2,1)S(1)} %get-tuple-element.30.refs_0_), channel_id=1, source_target_pairs={{0,8},{8,16},{16,24},{1,9},{9,17},{17,25},{2,10},{10,18},{18,26},{... | collective-permute-start | bytes 786440 | tf_op jit(solution)/shard_map/ppermute | solution.py:543
  23.2 1.3 collective-permute-start.2
  24.5 3.6 %collective-permute-done.refs_1_ = bf16[64,2048]{1,0:T(8,128)(2,1)S(1)} collective-permute-done((bf16[64,2048]{1,0:T(8,128)(2,1)S(1)}, bf16[64,2048]{1,0:T(8,128)(2,1)S(1)}, u32[]{:S(2)}, u32[]{:S(2)}) %collective-permute-start) | collective-permute-done | bytes 262176 | tf_op jit(solution)/shard_map/ppermute | solution.py:543
  28.0 0.7 collective-permute-start.1
  28.7 3.5 %collective-permute-done.2.refs_4_ = bf16[64,2048]{1,0:T(8,128)(2,1)S(1)} collective-permute-done((bf16[64,2048]{1,0:T(8,128)(2,1)S(1)}, bf16[64,2048]{1,0:T(8,128)(2,1)S(1)}, u32[]{:S(2)}, u32[]{:S(2)}) %collective-permute-start.2) | collective-permute-done | bytes 262176 | tf_op jit(solution)/shard_map/ppermute | solution.py:548
  32.2 1.3 collective-permute-start.3
  33.5 0.0 collective-permute-done.1.refs_2_
  33.5 6.9 %collective-permute-done.3.refs_5_ = bf16[64,2048]{1,0:T(8,128)(2,1)S(1)} collective-permute-done((bf16[64,2048]{1,0:T(8,128)(2,1)S(1)}, bf16[64,2048]{1,0:T(8,128)(2,1)S(1)}, u32[]{:S(2)}, u32[]{:S(2)}) %collective-permute-start.3) | collective-permute-done | bytes 262176 | tf_op jit(solution)/shard_map/ppermute | solution.py:548
  40.4 3.8 %collective-permute-start.4 = (bf16[64,2048]{1,0:T(8,128)(2,1)S(1)}, bf16[64,2048]{1,0:T(8,128)(2,1)S(1)}, u32[]{:S(2)}, u32[]{:S(2)}) collective-permute-start(bf16[64,2048]{1,0:T(8,128)(2,1)S(1)} %get-tuple-element.29.refs_0_), channel_id=1, source_target_pairs={{0,8},{8,16},{16,24},{1,9},{9,17},{17,25},{2,10},{10,18},{18,26},{... | collective-permute-start | bytes 786440 | tf_op jit(solution)/shard_map/ppermute | solution.py:543
  44.2 1.3 collective-permute-start.6
  45.5 0.7 collective-permute-start.7
  46.2 1.3 collective-permute-start.8
  47.5 7.4 %collective-permute-done.6.refs_4_ = bf16[64,2048]{1,0:T(8,128)(2,1)S(1)} collective-permute-done((bf16[64,2048]{1,0:T(8,128)(2,1)S(1)}, bf16[64,2048]{1,0:T(8,128)(2,1)S(1)}, u32[]{:S(2)}, u32[]{:S(2)}) %collective-permute-start.6) | collective-permute-done | bytes 262176 | tf_op jit(solution)/shard_map/ppermute | solution.py:548
  54.9 1.3 collective-permute-start.10
  56.2 0.0 collective-permute-done.4.refs_1_
  56.2 0.0 copy-start.9
  56.2 1.4 %collective-permute-start.5 = (bf16[64,2048]{1,0:T(8,128)(2,1)S(1)}, bf16[64,2048]{1,0:T(8,128)(2,1)}, u32[]{:S(2)}, u32[]{:S(2)}) collective-permute-start(bf16[64,2048]{1,0:T(8,128)(2,1)S(1)} %collective-permute-done.4.refs_1_), channel_id=1, source_target_pairs={{8,16},{16,24},{9,17},{17,25},{10,18},{18,26},{11,19},{19,27},{12,... | collective-permute-start | bytes 786440 | tf_op jit(solution)/shard_map/ppermute | solution.py:543
  57.7 0.3 copy.22
  57.9 0.9 pad.4.refs_7_
  58.8 0.0 collective-permute-done.7.refs_3_
  58.8 0.5 collective-permute-done.8.refs_6_
  59.3 0.0 copy-done
  59.3 0.2 copy-done.5
  59.5 0.4 copy-done.6
  60.0 9.1 %shard_map.154 = (bf16[256,2048]{1,0:T(8,128)(2,1)}, bf16[4,64,2048]{2,1,0:T(8,128)(2,1)}, f32[256,896]{1,0:T(8,128)}, bf16[256,768]{1,0:T(8,128)(2,1)}) custom-call(bf16[64,2048]{1,0:T(8,128)(2,1)} %copy-done, bf16[64,2048]{1,0:T(8,128)(2,1)} %copy-done.1, bf16[64,2048]{1,0:T(8,128)(2,1)} %copy-done.3, bf16[64,2048]{1,0:T(8,128)(2,1)} %copy-done.5, ...), custom_call_target="tpu_custom_call" | custom-call | flops 2415919104 | bytes 18874368 | tf_op jit(solution)/shard_map/pallas_call | solution.py:328
  69.1 0.0 copy-done.7
  69.1 0.0 copy-done.9
  69.1 0.0 collective-permute-done.10.refs_5_
  69.1 1.3 collective-permute-start.11
  70.4 0.0 collective-permute-done.5.refs_2_
  70.4 0.7 collective-permute-start.9
  71.1 5.4 %all-to-all-start.1 = ((bf16[32,8,2048]{2,1,0:T(8,128)(2,1)}), bf16[32,8,2048]{2,1,0:T(8,128)(2,1)S(1)}, u32[]{:S(2)}, u32[]{:S(2)}) async-start(bf16[32,8,2048]{2,1,0:T(8,128)(2,1)} %bitcast.20), calls=%async_computation.1 | async-start | bytes 2097152 | tf_op jit(solution)/shard_map/all_to_all | solution.py:594
  76.5 1.2 collective-permute-done.11.refs_6_
  77.8 0.0 collective-permute-done.9.refs_3_
  77.8 0.7 copy-done.12
  78.5 0.1 copy-done.13
  78.6 12.5 %shard_map.155 = (bf16[256,2048]{1,0:T(8,128)(2,1)}, bf16[4,64,2176]{2,1,0:T(8,128)(2,1)}, bf16[256,1664]{1,0:T(8,128)(2,1)}) custom-call(bf16[64,2048]{1,0:T(8,128)(2,1)} %copy-done.7, bf16[64,2048]{1,0:T(8,128)(2,1)} %copy-done.9, bf16[64,2048]{1,0:T(8,128)(2,1)} %collective-permute-done.5.refs_2_, bf16[64,2048]{1,0:T(8,128)(2,1)} %copy-done.13, ...), custom_call_target="tpu_custom_call" | custom-call | flops 40265318400 | bytes 157286400 | tf_op jit(solution)/shard_map/pallas_call | solution.py:466
  91.1 11.6 %all-to-all-done.1 = bf16[32,8,2048]{2,1,0:T(8,128)(2,1)S(1)} async-done(((bf16[32,8,2048]{2,1,0:T(8,128)(2,1)}), bf16[32,8,2048]{2,1,0:T(8,128)(2,1)S(1)}, u32[]{:S(2)}, u32[]{:S(2)}) %all-to-all-start.1) | async-done | bytes 1048608 | tf_op jit(solution)/shard_map/all_to_all | solution.py:594
  102.8 3.8 %all-to-all-start.2 = ((bf16[32,8,2176]{2,1,0:T(8,128)(2,1)}), bf16[32,8,2176]{2,1,0:T(8,128)(2,1)S(1)}, u32[]{:S(2)}, u32[]{:S(2)}) async-start(bf16[32,8,2176]{2,1,0:T(8,128)(2,1)} %bitcast.19), calls=%async_computation.2 | async-start | bytes 2228224 | tf_op jit(solution)/shard_map/all_to_all | solution.py:594
  106.6 5.5 %shard_map.159 = f32[1,384,4096]{2,1,0:T(8,128)} custom-call(bf16[256,2048]{1,0:T(8,128)(2,1)} %get-tuple-element.45.c_ref, bf16[256,768]{1,0:T(8,128)(2,1)} %get-tuple-element.46.hidden_ref), custom_call_target="tpu_custom_call" | custom-call | flops 805306368 | bytes 6291456 | tf_op jit(solution)/shard_map/pallas_call | solution.py:527
  112.0 6.9 %shard_map.158 = (f32[2,2048,384]{2,1,0:T(8,128)}, f32[2,2048,384]{2,1,0:T(8,128)}) custom-call(bf16[256,2048]{1,0:T(8,128)(2,1)} %get-tuple-element.34.refs_11_.x_ref, bf16[256,1664]{1,0:T(8,128)(2,1)} %get-tuple-element.42.delta_ref), custom_call_target="tpu_custom_call" | custom-call | flops 1610612736 | bytes 12582912 | tf_op jit(solution)/shard_map/pallas_call | solution.py:505
  118.9 2.9 %shard_map.156 = bf16[256,4096]{1,0:T(8,128)(2,1)} custom-call(bf16[2,64,256]{2,1,0:T(8,128)(2,1)} %get-tuple-element.27.hot_ref, bf16[256,2048]{1,0:T(8,128)(2,1)S(1)} %bitcast.17), custom_call_target="tpu_custom_call" | custom-call | flops 536870912 | bytes 2097152 | tf_op jit(solution)/shard_map/pallas_call | solution.py:174
  121.8 12.2 %all-to-all-done.2 = bf16[32,8,2176]{2,1,0:T(8,128)(2,1)S(1)} async-done(((bf16[32,8,2176]{2,1,0:T(8,128)(2,1)}), bf16[32,8,2176]{2,1,0:T(8,128)(2,1)S(1)}, u32[]{:S(2)}, u32[]{:S(2)}) %all-to-all-start.2) | async-done | bytes 1114144 | tf_op jit(solution)/shard_map/all_to_all | solution.py:594
  134.0 3.5 %shard_map.157 = (bf16[256,4096]{1,0:T(8,128)(2,1)}, f32[8,128]{1,0:T(8,128)}, f32[1,8]{1,0:T(1,128)}) custom-call(bf16[2,64,256]{2,1,0:T(8,128)(2,1)} %get-tuple-element.27.hot_ref, bf16[256,2176]{1,0:T(8,128)(2,1)S(1)} %bitcast.18), custom_call_target="tpu_custom_call" | custom-call | flops 536870912 | bytes 2097152 | tf_op jit(solution)/shard_map/pallas_call | solution.py:174
  (21 shorter events, 0.1 us)
Async XLA Ops:
  0.6 46.9 %copy-start.8 = (bf16[4096,8]{0,1:T(8,128)(2,1)S(1)}, bf16[4096,8]{0,1:T(8,128)(2,1)}, u32[]{:S(2)}) copy-start(bf16[4096,8]{0,1:T(8,128)(2,1)} %param.12) | copy-start | bytes 196612
  19.6 39.7 %copy-start = (bf16[64,2048]{1,0:T(8,128)(2,1)}, bf16[64,2048]{1,0:T(8,128)(2,1)S(1)}, u32[]{:S(2)}) copy-start(bf16[64,2048]{1,0:T(8,128)(2,1)S(1)} %get-tuple-element.30.refs_0_) | copy-start | bytes 786436
  19.6 49.4 %copy-start.7 = (bf16[64,2048]{1,0:T(8,128)(2,1)}, bf16[64,2048]{1,0:T(8,128)(2,1)S(1)}, u32[]{:S(2)}) copy-start(bf16[64,2048]{1,0:T(8,128)(2,1)S(1)} %get-tuple-element.29.refs_0_) | copy-start | bytes 786436
  19.6 8.4 %collective-permute-start = (bf16[64,2048]{1,0:T(8,128)(2,1)S(1)}, bf16[64,2048]{1,0:T(8,128)(2,1)S(1)}, u32[]{:S(2)}, u32[]{:S(2)}) collective-permute-start(bf16[64,2048]{1,0:T(8,128)(2,1)S(1)} %get-tuple-element.30.refs_0_), channel_id=1, source_target_pairs={{0,8},{8,16},{16,24},{1,9},{9,17},{17,25},{2,10},{10,18},{18,26},{... | collective-permute-start | bytes 786440 | tf_op jit(solution)/shard_map/ppermute | solution.py:543
  23.2 9.0 %collective-permute-start.2 = (bf16[64,2048]{1,0:T(8,128)(2,1)S(1)}, bf16[64,2048]{1,0:T(8,128)(2,1)S(1)}, u32[]{:S(2)}, u32[]{:S(2)}) collective-permute-start(bf16[64,2048]{1,0:T(8,128)(2,1)S(1)} %get-tuple-element.30.refs_0_), channel_id=1, source_target_pairs={{8,0},{16,8},{24,16},{9,1},{17,9},{25,17},{10,2},{18,10},{26,18},{... | collective-permute-start | bytes 786440 | tf_op jit(solution)/shard_map/ppermute | solution.py:548
  28.0 31.3 %copy-start.1 = (bf16[64,2048]{1,0:T(8,128)(2,1)}, bf16[64,2048]{1,0:T(8,128)(2,1)S(1)}, u32[]{:S(2)}) copy-start(bf16[64,2048]{1,0:T(8,128)(2,1)S(1)} %collective-permute-done.refs_1_) | copy-start | bytes 786436
  28.0 5.4 %collective-permute-start.1 = (bf16[64,2048]{1,0:T(8,128)(2,1)S(1)}, bf16[64,2048]{1,0:T(8,128)(2,1)S(1)}, u32[]{:S(2)}, u32[]{:S(2)}) collective-permute-start(bf16[64,2048]{1,0:T(8,128)(2,1)S(1)} %collective-permute-done.refs_1_), channel_id=1, source_target_pairs={{8,16},{16,24},{9,17},{17,25},{10,18},{18,26},{11,19},{19,27},{12,... | collective-permute-start | bytes 786440 | tf_op jit(solution)/shard_map/ppermute | solution.py:543
  32.2 27.1 %copy-start.2 = (bf16[64,2048]{1,0:T(8,128)(2,1)}, bf16[64,2048]{1,0:T(8,128)(2,1)S(1)}, u32[]{:S(2)}) copy-start(bf16[64,2048]{1,0:T(8,128)(2,1)S(1)} %collective-permute-done.2.refs_4_) | copy-start | bytes 786436
  32.2 8.3 %collective-permute-start.3 = (bf16[64,2048]{1,0:T(8,128)(2,1)S(1)}, bf16[64,2048]{1,0:T(8,128)(2,1)S(1)}, u32[]{:S(2)}, u32[]{:S(2)}) collective-permute-start(bf16[64,2048]{1,0:T(8,128)(2,1)S(1)} %collective-permute-done.2.refs_4_), channel_id=1, source_target_pairs={{8,0},{16,8},{9,1},{17,9},{10,2},{18,10},{11,3},{19,11},{12,4},{20... | collective-permute-start | bytes 786440 | tf_op jit(solution)/shard_map/ppermute | solution.py:548
  33.5 25.9 %copy-start.3 = (bf16[64,2048]{1,0:T(8,128)(2,1)}, bf16[64,2048]{1,0:T(8,128)(2,1)S(1)}, u32[]{:S(2)}) copy-start(bf16[64,2048]{1,0:T(8,128)(2,1)S(1)} %collective-permute-done.1.refs_2_) | copy-start | bytes 786436
  40.4 18.9 %copy-start.4 = (bf16[64,2048]{1,0:T(8,128)(2,1)}, bf16[64,2048]{1,0:T(8,128)(2,1)S(1)}, u32[]{:S(2)}) copy-start(bf16[64,2048]{1,0:T(8,128)(2,1)S(1)} %collective-permute-done.3.refs_5_) | copy-start | bytes 786436
  40.4 15.8 %collective-permute-start.4 = (bf16[64,2048]{1,0:T(8,128)(2,1)S(1)}, bf16[64,2048]{1,0:T(8,128)(2,1)S(1)}, u32[]{:S(2)}, u32[]{:S(2)}) collective-permute-start(bf16[64,2048]{1,0:T(8,128)(2,1)S(1)} %get-tuple-element.29.refs_0_), channel_id=1, source_target_pairs={{0,8},{8,16},{16,24},{1,9},{9,17},{17,25},{2,10},{10,18},{18,26},{... | collective-permute-start | bytes 786440 | tf_op jit(solution)/shard_map/ppermute | solution.py:543
  44.2 10.7 %collective-permute-start.6 = (bf16[64,2048]{1,0:T(8,128)(2,1)S(1)}, bf16[64,2048]{1,0:T(8,128)(2,1)S(1)}, u32[]{:S(2)}, u32[]{:S(2)}) collective-permute-start(bf16[64,2048]{1,0:T(8,128)(2,1)S(1)} %get-tuple-element.29.refs_0_), channel_id=1, source_target_pairs={{8,0},{16,8},{24,16},{9,1},{17,9},{25,17},{10,2},{18,10},{26,18},{... | collective-permute-start | bytes 786440 | tf_op jit(solution)/shard_map/ppermute | solution.py:548
  45.5 13.3 %collective-permute-start.7 = (bf16[64,2048]{1,0:T(8,128)(2,1)S(1)}, bf16[64,2048]{1,0:T(8,128)(2,1)S(1)}, u32[]{:S(2)}, u32[]{:S(2)}) collective-permute-start(bf16[64,2048]{1,0:T(8,128)(2,1)S(1)} %collective-permute-done.1.refs_2_), channel_id=1, source_target_pairs={{16,24},{17,25},{18,26},{19,27},{20,28},{21,29},{22,30},{23,31}} | collective-permute-start | bytes 786440 | tf_op jit(solution)/shard_map/ppermute | solution.py:543
  46.2 13.1 %collective-permute-start.8 = (bf16[64,2048]{1,0:T(8,128)(2,1)S(1)}, bf16[64,2048]{1,0:T(8,128)(2,1)S(1)}, u32[]{:S(2)}, u32[]{:S(2)}) collective-permute-start(bf16[64,2048]{1,0:T(8,128)(2,1)S(1)} %collective-permute-done.3.refs_5_), channel_id=1, source_target_pairs={{8,0},{9,1},{10,2},{11,3},{12,4},{13,5},{14,6},{15,7}} | collective-permute-start | bytes 786440 | tf_op jit(solution)/shard_map/ppermute | solution.py:548
  54.9 22.8 %copy-start.10 = (bf16[64,2048]{1,0:T(8,128)(2,1)}, bf16[64,2048]{1,0:T(8,128)(2,1)S(1)}, u32[]{:S(2)}) copy-start(bf16[64,2048]{1,0:T(8,128)(2,1)S(1)} %collective-permute-done.6.refs_4_) | copy-start | bytes 786436
  54.9 14.1 %collective-permute-start.10 = (bf16[64,2048]{1,0:T(8,128)(2,1)S(1)}, bf16[64,2048]{1,0:T(8,128)(2,1)S(1)}, u32[]{:S(2)}, u32[]{:S(2)}) collective-permute-start(bf16[64,2048]{1,0:T(8,128)(2,1)S(1)} %collective-permute-done.6.refs_4_), channel_id=1, source_target_pairs={{8,0},{16,8},{9,1},{17,9},{10,2},{18,10},{11,3},{19,11},{12,4},{20... | collective-permute-start | bytes 786440 | tf_op jit(solution)/shard_map/ppermute | solution.py:548
  56.2 12.8 %copy-start.9 = (bf16[64,2048]{1,0:T(8,128)(2,1)}, bf16[64,2048]{1,0:T(8,128)(2,1)S(1)}, u32[]{:S(2)}) copy-start(bf16[64,2048]{1,0:T(8,128)(2,1)S(1)} %collective-permute-done.4.refs_1_) | copy-start | bytes 786436
  56.2 14.2 %collective-permute-start.5 = (bf16[64,2048]{1,0:T(8,128)(2,1)S(1)}, bf16[64,2048]{1,0:T(8,128)(2,1)}, u32[]{:S(2)}, u32[]{:S(2)}) collective-permute-start(bf16[64,2048]{1,0:T(8,128)(2,1)S(1)} %collective-permute-done.4.refs_1_), channel_id=1, source_target_pairs={{8,16},{16,24},{9,17},{17,25},{10,18},{18,26},{11,19},{19,27},{12,... | collective-permute-start | bytes 786440 | tf_op jit(solution)/shard_map/ppermute | solution.py:543
  58.8 0.7 copy-start.5
  59.3 0.7 copy-start.6
  69.1 8.7 %copy-start.11 = (bf16[64,2048]{1,0:T(8,128)(2,1)}, bf16[64,2048]{1,0:T(8,128)(2,1)S(1)}, u32[]{:S(2)}) copy-start(bf16[64,2048]{1,0:T(8,128)(2,1)S(1)} %collective-permute-done.10.refs_5_) | copy-start | bytes 786436
  69.1 8.7 %collective-permute-start.11 = (bf16[64,2048]{1,0:T(8,128)(2,1)S(1)}, bf16[64,2048]{1,0:T(8,128)(2,1)S(1)}, u32[]{:S(2)}, u32[]{:S(2)}) collective-permute-start(bf16[64,2048]{1,0:T(8,128)(2,1)S(1)} %collective-permute-done.10.refs_5_), channel_id=1, source_target_pairs={{8,0},{9,1},{10,2},{11,3},{12,4},{13,5},{14,6},{15,7}} | collective-permute-start | bytes 786440 | tf_op jit(solution)/shard_map/ppermute | solution.py:548
  70.4 7.4 %collective-permute-start.9 = (bf16[64,2048]{1,0:T(8,128)(2,1)}, bf16[64,2048]{1,0:T(8,128)(2,1)S(1)}, u32[]{:S(2)}, u32[]{:S(2)}) collective-permute-start(bf16[64,2048]{1,0:T(8,128)(2,1)} %collective-permute-done.5.refs_2_), channel_id=1, source_target_pairs={{16,24},{17,25},{18,26},{19,27},{20,28},{21,29},{22,30},{23,31}} | collective-permute-start | bytes 786440 | tf_op jit(solution)/shard_map/ppermute | solution.py:543
  71.1 31.7 %all-to-all-start.1 = ((bf16[32,8,2048]{2,1,0:T(8,128)(2,1)}), bf16[32,8,2048]{2,1,0:T(8,128)(2,1)S(1)}, u32[]{:S(2)}, u32[]{:S(2)}) async-start(bf16[32,8,2048]{2,1,0:T(8,128)(2,1)} %bitcast.20), calls=%async_computation.1 | async-start | bytes 2097152 | tf_op jit(solution)/shard_map/all_to_all | solution.py:594
  77.8 0.7 copy-start.12
  77.8 0.8 copy-start.13
  102.8 31.3 %all-to-all-start.2 = ((bf16[32,8,2176]{2,1,0:T(8,128)(2,1)}), bf16[32,8,2176]{2,1,0:T(8,128)(2,1)S(1)}, u32[]{:S(2)}, u32[]{:S(2)}) async-start(bf16[32,8,2176]{2,1,0:T(8,128)(2,1)} %bitcast.19), calls=%async_computation.2 | async-start | bytes 2228224 | tf_op jit(solution)/shard_map/all_to_all | solution.py:594

commit v11 on v9

--- a/solution.py
+++ b/solution.py
@@ -48,16 +48,17 @@
 
     def body(picks_ref, counts_ref, c_ref, x_ref, out_ref, hot_ref, picks_s, counts_s, c_v, x_v, out_v, sems, out_sems):
         small = [
-            pltpu.make_async_copy(picks_ref, picks_s, sems.at[2 * STEPS]),
-            pltpu.make_async_copy(counts_ref, counts_s, sems.at[2 * STEPS + 1]),
+            pltpu.make_async_copy(picks_ref, picks_s, sems.at[STEPS, 0]),
+            pltpu.make_async_copy(counts_ref, counts_s, sems.at[STEPS, 1]),
         ]
         for copy in small:
             copy.start()
         large = []
         for j in range(STEPS):
-            now = pl.ds(j * pack * width, pack * width)
-            large.append(pltpu.make_async_copy(x_ref.at[:, now], x_v.at[:, now], sems.at[2 * j]))
-            large.append(pltpu.make_async_copy(c_ref.at[:, now], c_v.at[:, now], sems.at[2 * j + 1]))
+            for h in range(pack):
+                now = pl.ds(h * part + j * width, width)
+                for n, (ref, held) in enumerate(((x_ref, x_v), (c_ref, c_v))):
+                    large.append(pltpu.make_async_copy(ref.at[:, now], held.at[:, now], sems.at[j, 2 * h + n]))
         for copy in large:
             copy.start()
         for copy in small:
@@ -84,10 +85,10 @@
                 [live[h][(2 * e + 1) * group : (2 * e + 2) * group] for e in range(experts)]
             ).astype(BF16)
         live = [value.astype(BF16) for value in live]
-        for copy in large:
-            copy.wait()
         leaving = []
         for j in range(STEPS):
+            for copy in large[2 * pack * j : 2 * pack * (j + 1)]:
+                copy.wait()
             total = 0.0
             for h in range(pack):
                 now = slice(h * part + j * width, h * part + (j + 1) * width)
@@ -110,7 +111,7 @@
             pltpu.VMEM(tokens.shape, BF16),
             pltpu.VMEM(tokens.shape, BF16),
             pltpu.VMEM((count, part), BF16),
-            pltpu.SemaphoreType.DMA((2 * STEPS + 2,)),
+            pltpu.SemaphoreType.DMA((STEPS + 1, 2 * pack)),
             pltpu.SemaphoreType.DMA((STEPS,)),
         ],
         compiler_params=PARAMS,
@@ -544,6 +545,11 @@
     return lax.ppermute(block, "seq", [(s, s - 1) for s in range(first, last)])
 
 
+def cyclic_gather(block, n):
+    shifts = [lax.ppermute(block, "seq", [(s, (s + k) % n) for s in range(n)]) for k in range(1, n)]
+    return Arrivals([block] + shifts, [(k, k, 0) for k in range(n)])
+
+
 def line_gather(block, n):
     ups, downs = [], []
     up = down = block
@@ -579,7 +585,9 @@
     sent, hot = choose_rows(tokens, cotangent, chosen, counts, pack)
     sent = sent.reshape(experts, 2, -1, sent.shape[1])
     here = lax.all_to_all(sent, "exp", split_axis=0, concat_axis=0, tiled=True)
-    x_in, c_in = (line_gather(here[:, n].reshape(-1, here.shape[3]), seq_n) for n in range(2))
+    x_rows, c_rows = (here[:, n].reshape(-1, here.shape[3]) for n in range(2))
+    x_in = cyclic_gather(x_rows, seq_n)
+    c_in = line_gather(c_rows, seq_n)
     halves = list(router.reshape(pack, features // pack, experts))
     router_side = jnp.concatenate(halves + halves, axis=1)
     router_side = jnp.pad(router_side, ((0, 0), (0, LANES - router_side.shape[1])))

time: 132 us -> 137 us (1.038)
  waiting for transfers between devices: 42.8 us -> 46 us
  starting transfers between devices: 25.6 us -> 27.5 us
    ppermute x6 -> x3, waiting for transfers between devices: 13.5 us -> 20.9 us  [down_line(): return lax.ppermute(block, 'seq', [(s, s - 1) for s in range(first, last)])]
    ppermute x0 -> x3, starting transfers between devices: none -> 6.62 us  [cyclic_gather(): lax.ppermute(block, 'seq', [(s, (s + k) % n) for s in range(n)])]
    ppermute x6 -> x3, starting transfers between devices: 11.4 us -> 4.84 us  [up_line(): return lax.ppermute(block, 'seq', [(s, s + 1) for s in range(first, last)])]
    all_to_all x2, starting transfers between devices: 6.43 us -> 12.2 us  [to_owners(): lax.all_to_all(parts, BOTH, split_axis=0, concat_axis=0, tiled=True)]
    ppermute x6 -> x3, starting transfers between devices: 7.72 us -> 3.85 us  [down_line(): return lax.ppermute(block, 'seq', [(s, s - 1) for s in range(first, last)])]
    ppermute x6 -> x3, waiting for transfers between devices: 3.44 us -> 0.01 us  [up_line(): return lax.ppermute(block, 'seq', [(s, s + 1) for s in range(first, last)])]
  transfers between devices with their start and end apart: 14 -> 11, of which waited for: 8 -> 4; matrix products, arithmetic and copies ran while one was open for 1% -> 1% of each run, Pallas kernels for 28% -> 27%
where the time goes in v11:
time: 137 us
  waiting for transfers between devices  46 us (34%)
  Pallas kernels  44.3 us (32%)
  starting transfers between devices  27.5 us (20%)
  blocking collectives  14.9 us (11%)
  local copies, waits for them, and re-layouts  2.88 us (2%)
    all_to_all x2, waiting for transfers between devices, to_owners(): lax.all_to_all(parts, BOTH, split_axis=0, concat_axis=0, tiled=True)  25.1 us
    ppermute x3, waiting for transfers between devices, down_line(): return lax.ppermute(block, 'seq', [(s, s - 1) for s in range(first, last)])  20.9 us
    all_to_all x1, blocking collectives, on_device(): here = lax.all_to_all(sent, 'exp', split_axis=0, concat_axis=0, tiled=True)  14.9 us
    pallas_call x1, Pallas kernels, expert_backward(): pl.pallas_call(body, in_specs=[ANYWHERE] * (n_blocks + 6) + [IN_VMEM], ou...  12.5 us
    all_to_all x2, starting transfers between devices, to_owners(): lax.all_to_all(parts, BOTH, split_axis=0, concat_axis=0, tiled=True)  12.2 us
    pallas_call x1, Pallas kernels, expert_forward(): pl.pallas_call(body, in_specs=[ANYWHERE] * (n_blocks + 4) + [IN_VMEM] * 2...  9.01 us
    pallas_call x1, Pallas kernels, side_grads(): pl.pallas_call(body, grid=(STEPS,), in_specs=[pl.BlockSpec((rows, width),...  6.86 us
    ppermute x3, starting transfers between devices, cyclic_gather(): lax.ppermute(block, 'seq', [(s, (s + k) % n) for s in range(n)])  6.62 us
  transfers between devices with their start and end apart: 11, of which 4 were waited for; matrix products, arithmetic and copies ran while one was open for 1% of the time, Pallas kernels for 27%

profile of v11, /device:TPU:0, one launch (start us, length us, event | category | flops | bytes accessed | tf_op | source)
XLA Modules:
  0.0 136.6 jit_solution(5816765216233576527)
XLA Ops:
  0.6 0.0 copy-start.5
  0.6 4.0 %shard_map.153 = (bf16[128,2048]{1,0:T(8,128)(2,1)}, bf16[2,64,256]{2,1,0:T(8,128)(2,1)}) custom-call(s32[4,8]{1,0:T(4,128)} %bitcast.22, s32[1,8]{1,0:T(1,128)} %counts_ref.1, bf16[256,4096]{1,0:T(8,128)(2,1)} %c_ref.1, bf16[256,4096]{1,0:T(8,128)(2,1)} %x_ref.1), custom_call_target="tpu_custom_call" | custom-call | flops 536870912 | bytes 4194304 | tf_op jit(solution)/shard_map/pallas_call | solution.py:103
  4.6 14.9 %all_to_all.15 = bf16[8,2,8,2048]{3,2,1,0:T(8,128)(2,1)S(1)} all-to-all(bf16[8,2,8,2048]{3,2,1,0:T(8,128)(2,1)} %bitcast.21), channel_id=1, replica_groups=mesh['seq'=4,'exp'=8] {'exp'}, dimensions={0} | all-to-all | bytes 1048576 | tf_op jit(solution)/shard_map/all_to_all | solution.py:587
  19.6 0.0 copy-start
  19.6 0.0 copy-start.4
  19.6 3.5 %collective-permute-start = (bf16[64,2048]{1,0:T(8,128)(2,1)S(1)}, bf16[64,2048]{1,0:T(8,128)(2,1)S(1)}, u32[]{:S(2)}, u32[]{:S(2)}) collective-permute-start(bf16[64,2048]{1,0:T(8,128)(2,1)S(1)} %get-tuple-element.40.refs_0_), channel_id=1, source_target_pairs={{0,8},{8,16},{16,24},{1,9},{9,17},{17,25},{2,10},{10,18},{18,26},{... | collective-permute-start | bytes 786440 | tf_op jit(solution)/shard_map/ppermute | solution.py:540
  23.1 1.3 collective-permute-start.3
  24.4 2.7 %collective-permute-start.6 = (bf16[64,2048]{1,0:T(8,128)(2,1)S(1)}, bf16[64,2048]{1,0:T(8,128)(2,1)S(1)}, u32[]{:S(2)}, u32[]{:S(2)}) collective-permute-start(bf16[64,2048]{1,0:T(8,128)(2,1)S(1)} %get-tuple-element.39.refs_0_), channel_id=1, source_target_pairs={{0,8},{8,16},{16,24},{24,0},{1,9},{9,17},{17,25},{25,1},{2,10},{10... | collective-permute-start | bytes 786440 | tf_op jit(solution)/shard_map/ppermute | solution.py:549
  27.1 2.6 %collective-permute-start.7 = (bf16[64,2048]{1,0:T(8,128)(2,1)S(1)}, bf16[64,2048]{1,0:T(8,128)(2,1)S(1)}, u32[]{:S(2)}, u32[]{:S(2)}) collective-permute-start(bf16[64,2048]{1,0:T(8,128)(2,1)S(1)} %get-tuple-element.39.refs_0_), channel_id=1, source_target_pairs={{0,16},{8,24},{16,0},{24,8},{1,17},{9,25},{17,1},{25,9},{2,18},{10... | collective-permute-start | bytes 786440 | tf_op jit(solution)/shard_map/ppermute | solution.py:549
  29.7 1.3 collective-permute-start.8
  31.1 0.0 collective-permute-done.refs_1_
  31.1 0.7 collective-permute-start.1
  31.7 8.4 %collective-permute-done.3.refs_4_ = bf16[64,2048]{1,0:T(8,128)(2,1)S(1)} collective-permute-done((bf16[64,2048]{1,0:T(8,128)(2,1)S(1)}, bf16[64,2048]{1,0:T(8,128)(2,1)S(1)}, u32[]{:S(2)}, u32[]{:S(2)}) %collective-permute-start.3) | collective-permute-done | bytes 262176 | tf_op jit(solution)/shard_map/ppermute | solution.py:545
  40.1 1.3 collective-permute-start.4
  41.4 0.0 copy-done.5
  41.5 0.0 collective-permute-done.1.refs_2_
  41.5 0.0 copy-start.8
  41.5 0.7 collective-permute-start.2
  42.2 12.5 %collective-permute-done.4.refs_5_ = bf16[64,2048]{1,0:T(8,128)(2,1)S(1)} collective-permute-done((bf16[64,2048]{1,0:T(8,128)(2,1)S(1)}, bf16[64,2048]{1,0:T(8,128)(2,1)S(1)}, u32[]{:S(2)}, u32[]{:S(2)}) %collective-permute-start.4) | collective-permute-done | bytes 262176 | tf_op jit(solution)/shard_map/ppermute | solution.py:545
  54.6 1.3 collective-permute-start.5
  55.9 0.3 copy.22
  56.2 0.9 pad.4.refs_4_.refs_7_
  57.1 0.0 collective-permute-done.6.refs_1_
  57.1 0.0 collective-permute-done.7.refs_2_
  57.1 0.0 copy-start.2
  57.2 0.0 collective-permute-done.8.refs_3_
  57.2 0.0 copy-start.3
  57.2 0.0 copy-done
  57.2 0.7 copy-done.1
  57.8 0.1 copy-done.2
  57.9 0.1 copy-done.3
  58.0 9.0 %shard_map.154 = (bf16[256,2048]{1,0:T(8,128)(2,1)}, bf16[4,64,2048]{2,1,0:T(8,128)(2,1)}, f32[256,896]{1,0:T(8,128)}, bf16[256,768]{1,0:T(8,128)(2,1)}) custom-call(bf16[64,2048]{1,0:T(8,128)(2,1)} %copy-done, bf16[64,2048]{1,0:T(8,128)(2,1)} %copy-done.1, bf16[64,2048]{1,0:T(8,128)(2,1)} %copy-done.2, bf16[64,2048]{1,0:T(8,128)(2,1)} %copy-done.3, ...), custom_call_target="tpu_custom_call" | custom-call | flops 2415919104 | bytes 18874368 | tf_op jit(solution)/shard_map/pallas_call | solution.py:325
  67.0 0.0 copy-done.4
  67.0 0.0 copy-done.6
  67.1 8.4 %all-to-all-start.1 = ((bf16[32,8,2048]{2,1,0:T(8,128)(2,1)}), bf16[32,8,2048]{2,1,0:T(8,128)(2,1)S(1)}, u32[]{:S(2)}, u32[]{:S(2)}) async-start(bf16[32,8,2048]{2,1,0:T(8,128)(2,1)} %bitcast.20), calls=%async_computation.1 | async-start | bytes 2097152 | tf_op jit(solution)/shard_map/all_to_all | solution.py:583
  75.5 0.0 collective-permute-done.2.refs_3_
  75.5 0.0 copy-start.10
  75.5 0.0 collective-permute-done.5.refs_6_
  75.5 0.7 copy-done.10
  76.2 0.1 copy-done.11
  76.3 12.5 %shard_map.155 = (bf16[256,2048]{1,0:T(8,128)(2,1)}, bf16[4,64,2176]{2,1,0:T(8,128)(2,1)}, bf16[256,1664]{1,0:T(8,128)(2,1)}) custom-call(bf16[64,2048]{1,0:T(8,128)(2,1)} %copy-done.4, bf16[64,2048]{1,0:T(8,128)(2,1)} %copy-done.6, bf16[64,2048]{1,0:T(8,128)(2,1)} %copy-done.8, bf16[64,2048]{1,0:T(8,128)(2,1)} %copy-done.10, bf16[64,2048]{1,0:T(8,128)(2,1)} %copy-done.7, ...), custom_call_target="tpu_custom_call" | custom-call | flops 40265318400 | bytes 157286400 | tf_op jit(solution)/shard_map/pallas_call | solution.py:463
  88.8 12.9 %all-to-all-done.1 = bf16[32,8,2048]{2,1,0:T(8,128)(2,1)S(1)} async-done(((bf16[32,8,2048]{2,1,0:T(8,128)(2,1)}), bf16[32,8,2048]{2,1,0:T(8,128)(2,1)S(1)}, u32[]{:S(2)}, u32[]{:S(2)}) %all-to-all-start.1) | async-done | bytes 1048608 | tf_op jit(solution)/shard_map/all_to_all | solution.py:583
  101.7 3.8 %all-to-all-start.2 = ((bf16[32,8,2176]{2,1,0:T(8,128)(2,1)}), bf16[32,8,2176]{2,1,0:T(8,128)(2,1)S(1)}, u32[]{:S(2)}, u32[]{:S(2)}) async-start(bf16[32,8,2176]{2,1,0:T(8,128)(2,1)} %bitcast.19), calls=%async_computation.2 | async-start | bytes 2228224 | tf_op jit(solution)/shard_map/all_to_all | solution.py:583
  105.5 5.5 %shard_map.159 = f32[1,384,4096]{2,1,0:T(8,128)} custom-call(bf16[256,2048]{1,0:T(8,128)(2,1)} %get-tuple-element.37.c_ref, bf16[256,768]{1,0:T(8,128)(2,1)} %get-tuple-element.38.hidden_ref), custom_call_target="tpu_custom_call" | custom-call | flops 805306368 | bytes 6291456 | tf_op jit(solution)/shard_map/pallas_call | solution.py:524
  111.0 6.9 %shard_map.158 = (f32[2,2048,384]{2,1,0:T(8,128)}, f32[2,2048,384]{2,1,0:T(8,128)}) custom-call(bf16[256,2048]{1,0:T(8,128)(2,1)} %get-tuple-element.25.refs_11_.x_ref, bf16[256,1664]{1,0:T(8,128)(2,1)} %get-tuple-element.34.delta_ref), custom_call_target="tpu_custom_call" | custom-call | flops 1610612736 | bytes 12582912 | tf_op jit(solution)/shard_map/pallas_call | solution.py:502
  117.8 2.9 %shard_map.156 = bf16[256,4096]{1,0:T(8,128)(2,1)} custom-call(bf16[2,64,256]{2,1,0:T(8,128)(2,1)} %get-tuple-element.23.hot_ref, bf16[256,2048]{1,0:T(8,128)(2,1)S(1)} %bitcast.17), custom_call_target="tpu_custom_call" | custom-call | flops 536870912 | bytes 2097152 | tf_op jit(solution)/shard_map/pallas_call | solution.py:174
  120.7 12.2 %all-to-all-done.2 = bf16[32,8,2176]{2,1,0:T(8,128)(2,1)S(1)} async-done(((bf16[32,8,2176]{2,1,0:T(8,128)(2,1)}), bf16[32,8,2176]{2,1,0:T(8,128)(2,1)S(1)}, u32[]{:S(2)}, u32[]{:S(2)}) %all-to-all-start.2) | async-done | bytes 1114144 | tf_op jit(solution)/shard_map/all_to_all | solution.py:583
  133.0 3.5 %shard_map.157 = (bf16[256,4096]{1,0:T(8,128)(2,1)}, f32[8,128]{1,0:T(8,128)}, f32[1,8]{1,0:T(1,128)}) custom-call(bf16[2,64,256]{2,1,0:T(8,128)(2,1)} %get-tuple-element.23.hot_ref, bf16[256,2176]{1,0:T(8,128)(2,1)S(1)} %bitcast.18), custom_call_target="tpu_custom_call" | custom-call | flops 536870912 | bytes 2097152 | tf_op jit(solution)/shard_map/pallas_call | solution.py:174
  (11 shorter events, 0.1 us)
Async XLA Ops:
  0.6 40.8 %copy-start.5 = (bf16[4096,8]{0,1:T(8,128)(2,1)S(1)}, bf16[4096,8]{0,1:T(8,128)(2,1)}, u32[]{:S(2)}) copy-start(bf16[4096,8]{0,1:T(8,128)(2,1)} %param.12) | copy-start | bytes 196612
  19.6 37.6 %copy-start = (bf16[64,2048]{1,0:T(8,128)(2,1)}, bf16[64,2048]{1,0:T(8,128)(2,1)S(1)}, u32[]{:S(2)}) copy-start(bf16[64,2048]{1,0:T(8,128)(2,1)S(1)} %get-tuple-element.39.refs_0_) | copy-start | bytes 786436
  19.6 47.4 %copy-start.4 = (bf16[64,2048]{1,0:T(8,128)(2,1)}, bf16[64,2048]{1,0:T(8,128)(2,1)S(1)}, u32[]{:S(2)}) copy-start(bf16[64,2048]{1,0:T(8,128)(2,1)S(1)} %get-tuple-element.40.refs_0_) | copy-start | bytes 786436
  19.6 11.4 %collective-permute-start = (bf16[64,2048]{1,0:T(8,128)(2,1)S(1)}, bf16[64,2048]{1,0:T(8,128)(2,1)S(1)}, u32[]{:S(2)}, u32[]{:S(2)}) collective-permute-start(bf16[64,2048]{1,0:T(8,128)(2,1)S(1)} %get-tuple-element.40.refs_0_), channel_id=1, source_target_pairs={{0,8},{8,16},{16,24},{1,9},{9,17},{17,25},{2,10},{10,18},{18,26},{... | collective-permute-start | bytes 786440 | tf_op jit(solution)/shard_map/ppermute | solution.py:540
  23.1 17.0 %collective-permute-start.3 = (bf16[64,2048]{1,0:T(8,128)(2,1)S(1)}, bf16[64,2048]{1,0:T(8,128)(2,1)S(1)}, u32[]{:S(2)}, u32[]{:S(2)}) collective-permute-start(bf16[64,2048]{1,0:T(8,128)(2,1)S(1)} %get-tuple-element.40.refs_0_), channel_id=1, source_target_pairs={{8,0},{16,8},{24,16},{9,1},{17,9},{25,17},{10,2},{18,10},{26,18},{... | collective-permute-start | bytes 786440 | tf_op jit(solution)/shard_map/ppermute | solution.py:545
  24.4 32.7 %collective-permute-start.6 = (bf16[64,2048]{1,0:T(8,128)(2,1)S(1)}, bf16[64,2048]{1,0:T(8,128)(2,1)S(1)}, u32[]{:S(2)}, u32[]{:S(2)}) collective-permute-start(bf16[64,2048]{1,0:T(8,128)(2,1)S(1)} %get-tuple-element.39.refs_0_), channel_id=1, source_target_pairs={{0,8},{8,16},{16,24},{24,0},{1,9},{9,17},{17,25},{25,1},{2,10},{10... | collective-permute-start | bytes 786440 | tf_op jit(solution)/shard_map/ppermute | solution.py:549
  27.1 30.0 %collective-permute-start.7 = (bf16[64,2048]{1,0:T(8,128)(2,1)S(1)}, bf16[64,2048]{1,0:T(8,128)(2,1)S(1)}, u32[]{:S(2)}, u32[]{:S(2)}) collective-permute-start(bf16[64,2048]{1,0:T(8,128)(2,1)S(1)} %get-tuple-element.39.refs_0_), channel_id=1, source_target_pairs={{0,16},{8,24},{16,0},{24,8},{1,17},{9,25},{17,1},{25,9},{2,18},{10... | collective-permute-start | bytes 786440 | tf_op jit(solution)/shard_map/ppermute | solution.py:549
  29.7 27.4 %collective-permute-start.8 = (bf16[64,2048]{1,0:T(8,128)(2,1)S(1)}, bf16[64,2048]{1,0:T(8,128)(2,1)S(1)}, u32[]{:S(2)}, u32[]{:S(2)}) collective-permute-start(bf16[64,2048]{1,0:T(8,128)(2,1)S(1)} %get-tuple-element.39.refs_0_), channel_id=1, source_target_pairs={{0,24},{8,0},{16,8},{24,16},{1,25},{9,1},{17,9},{25,17},{2,26},{10... | collective-permute-start | bytes 786440 | tf_op jit(solution)/shard_map/ppermute | solution.py:549
  31.1 36.0 %copy-start.6 = (bf16[64,2048]{1,0:T(8,128)(2,1)}, bf16[64,2048]{1,0:T(8,128)(2,1)S(1)}, u32[]{:S(2)}) copy-start(bf16[64,2048]{1,0:T(8,128)(2,1)S(1)} %collective-permute-done.refs_1_) | copy-start | bytes 786436
  31.1 10.4 %collective-permute-start.1 = (bf16[64,2048]{1,0:T(8,128)(2,1)S(1)}, bf16[64,2048]{1,0:T(8,128)(2,1)S(1)}, u32[]{:S(2)}, u32[]{:S(2)}) collective-permute-start(bf16[64,2048]{1,0:T(8,128)(2,1)S(1)} %collective-permute-done.refs_1_), channel_id=1, source_target_pairs={{8,16},{16,24},{9,17},{17,25},{10,18},{18,26},{11,19},{19,27},{12,... | collective-permute-start | bytes 786440 | tf_op jit(solution)/shard_map/ppermute | solution.py:540
  40.1 26.9 %copy-start.7 = (bf16[64,2048]{1,0:T(8,128)(2,1)}, bf16[64,2048]{1,0:T(8,128)(2,1)S(1)}, u32[]{:S(2)}) copy-start(bf16[64,2048]{1,0:T(8,128)(2,1)S(1)} %collective-permute-done.3.refs_4_) | copy-start | bytes 786436
  40.1 14.5 %collective-permute-start.4 = (bf16[64,2048]{1,0:T(8,128)(2,1)S(1)}, bf16[64,2048]{1,0:T(8,128)(2,1)S(1)}, u32[]{:S(2)}, u32[]{:S(2)}) collective-permute-start(bf16[64,2048]{1,0:T(8,128)(2,1)S(1)} %collective-permute-done.3.refs_4_), channel_id=1, source_target_pairs={{8,0},{16,8},{9,1},{17,9},{10,2},{18,10},{11,3},{19,11},{12,4},{20... | collective-permute-start | bytes 786440 | tf_op jit(solution)/shard_map/ppermute | solution.py:545
  41.5 25.6 %copy-start.8 = (bf16[64,2048]{1,0:T(8,128)(2,1)}, bf16[64,2048]{1,0:T(8,128)(2,1)S(1)}, u32[]{:S(2)}) copy-start(bf16[64,2048]{1,0:T(8,128)(2,1)S(1)} %collective-permute-done.1.refs_2_) | copy-start | bytes 786436
  41.5 34.0 %collective-permute-start.2 = (bf16[64,2048]{1,0:T(8,128)(2,1)S(1)}, bf16[64,2048]{1,0:T(8,128)(2,1)S(1)}, u32[]{:S(2)}, u32[]{:S(2)}) collective-permute-start(bf16[64,2048]{1,0:T(8,128)(2,1)S(1)} %collective-permute-done.1.refs_2_), channel_id=1, source_target_pairs={{16,24},{17,25},{18,26},{19,27},{20,28},{21,29},{22,30},{23,31}} | collective-permute-start | bytes 786440 | tf_op jit(solution)/shard_map/ppermute | solution.py:540
  54.6 12.5 %copy-start.9 = (bf16[64,2048]{1,0:T(8,128)(2,1)}, bf16[64,2048]{1,0:T(8,128)(2,1)S(1)}, u32[]{:S(2)}) copy-start(bf16[64,2048]{1,0:T(8,128)(2,1)S(1)} %collective-permute-done.4.refs_5_) | copy-start | bytes 786436
  54.6 20.9 %collective-permute-start.5 = (bf16[64,2048]{1,0:T(8,128)(2,1)S(1)}, bf16[64,2048]{1,0:T(8,128)(2,1)S(1)}, u32[]{:S(2)}, u32[]{:S(2)}) collective-permute-start(bf16[64,2048]{1,0:T(8,128)(2,1)S(1)} %collective-permute-done.4.refs_5_), channel_id=1, source_target_pairs={{8,0},{9,1},{10,2},{11,3},{12,4},{13,5},{14,6},{15,7}} | collective-permute-start | bytes 786440 | tf_op jit(solution)/shard_map/ppermute | solution.py:545
  57.1 0.7 copy-start.1
  57.1 0.8 copy-start.2
  57.2 0.9 copy-start.3
  67.1 34.6 %all-to-all-start.1 = ((bf16[32,8,2048]{2,1,0:T(8,128)(2,1)}), bf16[32,8,2048]{2,1,0:T(8,128)(2,1)S(1)}, u32[]{:S(2)}, u32[]{:S(2)}) async-start(bf16[32,8,2048]{2,1,0:T(8,128)(2,1)} %bitcast.20), calls=%async_computation.1 | async-start | bytes 2097152 | tf_op jit(solution)/shard_map/all_to_all | solution.py:583
  75.5 0.7 copy-start.10
  75.5 0.8 copy-start.11
  101.7 31.3 %all-to-all-start.2 = ((bf16[32,8,2176]{2,1,0:T(8,128)(2,1)}), bf16[32,8,2176]{2,1,0:T(8,128)(2,1)S(1)}, u32[]{:S(2)}, u32[]{:S(2)}) async-start(bf16[32,8,2176]{2,1,0:T(8,128)(2,1)} %bitcast.19), calls=%async_computation.2 | async-start | bytes 2228224 | tf_op jit(solution)/shard_map/all_to_all | solution.py:583

commit v12 on v11

--- a/solution.py
+++ b/solution.py
@@ -18,7 +18,7 @@
     return lax.dot_general(a, b, (dims, ((), ())), preferred_element_type=F32)
 
 
-PARAMS = pltpu.CompilerParams(vmem_limit_bytes=56 * 2**20)
+PARAMS = pltpu.CompilerParams(vmem_limit_bytes=32 * 2**20)
 SMALL = pltpu.CompilerParams(vmem_limit_bytes=12 * 2**20)
 
 
@@ -31,7 +31,7 @@
 
 
 def shape(dims, dtype=BF16):
-    return jax.ShapeDtypeStruct(dims, dtype)
+    return pltpu.HBM(dims, dtype)
 
 
 ANYWHERE = pl.BlockSpec(memory_space=pl.ANY)
@@ -346,7 +346,7 @@
         ],
         compiler_params=PARAMS,
         cost_estimate=cost(6 * rows * part * pack * hidden_n, 12 * part * pack * hidden_n),
-    )(*to_hbm(*arrivals.blocks, router_side, w_gate, w_up, w_down), threshold.reshape(1, -1), hid_scale)
+    )(*to_hbm(*arrivals.blocks, router_side), w_gate, w_up, *to_hbm(w_down), threshold.reshape(1, -1), hid_scale)
 
 
 def split3(v):
@@ -545,11 +545,6 @@
     return lax.ppermute(block, "seq", [(s, s - 1) for s in range(first, last)])
 
 
-def cyclic_gather(block, n):
-    shifts = [lax.ppermute(block, "seq", [(s, (s + k) % n) for s in range(n)]) for k in range(1, n)]
-    return Arrivals([block] + shifts, [(k, k, 0) for k in range(n)])
-
-
 def line_gather(block, n):
     ups, downs = [], []
     up = down = block
@@ -585,9 +580,7 @@
     sent, hot = choose_rows(tokens, cotangent, chosen, counts, pack)
     sent = sent.reshape(experts, 2, -1, sent.shape[1])
     here = lax.all_to_all(sent, "exp", split_axis=0, concat_axis=0, tiled=True)
-    x_rows, c_rows = (here[:, n].reshape(-1, here.shape[3]) for n in range(2))
-    x_in = cyclic_gather(x_rows, seq_n)
-    c_in = line_gather(c_rows, seq_n)
+    x_in, c_in = (line_gather(here[:, n].reshape(-1, here.shape[3]), seq_n) for n in range(2))
     halves = list(router.reshape(pack, features // pack, experts))
     router_side = jnp.concatenate(halves + halves, axis=1)
     router_side = jnp.pad(router_side, ((0, 0), (0, LANES - router_side.shape[1])))

time: 137 us -> 132 us (0.964)
  waiting for transfers between devices: 46 us -> 39.8 us
  Pallas kernels: 44.3 us -> 40.7 us
  local copies, waits for them, and re-layouts: 2.88 us -> 4.94 us
  starting transfers between devices: 27.5 us -> 29.3 us
    ppermute x3 -> x6, waiting for transfers between devices: 20.9 us -> 10.5 us  [down_line(): return lax.ppermute(block, 'seq', [(s, s - 1) for s in range(first, last)])]
    ppermute x3 -> x6, starting transfers between devices: 4.84 us -> 13.5 us  [up_line(): return lax.ppermute(block, 'seq', [(s, s + 1) for s in range(first, last)])]
    ppermute x3 -> x0, starting transfers between devices: 6.62 us -> none  [cyclic_gather(): lax.ppermute(block, 'seq', [(s, (s + k) % n) for s in range(n)])]
    all_to_all x2, starting transfers between devices: 12.2 us -> 8.12 us  [to_owners(): lax.all_to_all(parts, BOTH, split_axis=0, concat_axis=0, tiled=True)]
    ppermute x3 -> x6, starting transfers between devices: 3.85 us -> 7.72 us  [down_line(): return lax.ppermute(block, 'seq', [(s, s - 1) for s in range(first, last)])]
    pallas_call x1, Pallas kernels: 9.01 us -> 5.95 us  [expert_forward(): pl.pallas_call(body, in_specs=[ANYWHERE] * (n_blocks + 4) + [IN_VMEM] * 2...]
    ppermute x3 -> x6, waiting for transfers between devices: 0.01 us -> 2.75 us  [up_line(): return lax.ppermute(block, 'seq', [(s, s + 1) for s in range(first, last)])]
    all_to_all x2, waiting for transfers between devices: 25.1 us -> 26.5 us  [to_owners(): lax.all_to_all(parts, BOTH, split_axis=0, concat_axis=0, tiled=True)]
  transfers between devices with their start and end apart: 11 -> 14, of which waited for: 4 -> 8; matrix products, arithmetic and copies ran while one was open for 1% -> 2% of each run, Pallas kernels for 27% -> 25%
where the time goes in v12:
time: 132 us; the launch traced here: 131 us
  Pallas kernels  40.7 us (31%)
  waiting for transfers between devices  39.8 us (30%)
  starting transfers between devices  29.3 us (22%)
  blocking collectives  14.9 us (11%)
  local copies, waits for them, and re-layouts  4.94 us (4%)
    all_to_all x2, waiting for transfers between devices, to_owners(): lax.all_to_all(parts, BOTH, split_axis=0, concat_axis=0, tiled=True)  26.5 us
    all_to_all x1, blocking collectives, on_device(): here = lax.all_to_all(sent, 'exp', split_axis=0, concat_axis=0, tiled=True)  14.9 us
    ppermute x6, starting transfers between devices, up_line(): return lax.ppermute(block, 'seq', [(s, s + 1) for s in range(first, last)])  13.5 us
    pallas_call x1, Pallas kernels, expert_backward(): pl.pallas_call(body, in_specs=[ANYWHERE] * (n_blocks + 6) + [IN_VMEM], ou...  11.9 us
    ppermute x6, waiting for transfers between devices, down_line(): return lax.ppermute(block, 'seq', [(s, s - 1) for s in range(first, last)])  10.5 us
    all_to_all x2, starting transfers between devices, to_owners(): lax.all_to_all(parts, BOTH, split_axis=0, concat_axis=0, tiled=True)  8.12 us
    ppermute x6, starting transfers between devices, down_line(): return lax.ppermute(block, 'seq', [(s, s - 1) for s in range(first, last)])  7.72 us
    pallas_call x1, Pallas kernels, side_grads(): pl.pallas_call(body, grid=(STEPS,), in_specs=[pl.BlockSpec((rows, width),...  6.86 us
  transfers between devices with their start and end apart: 14, of which 8 were waited for; matrix products, arithmetic and copies ran while one was open for 2% of the time, Pallas kernels for 25%

profile of v12, /device:TPU:0, one launch (start us, length us, event | category | flops | bytes accessed | tf_op | source)
XLA Modules:
  0.0 130.8 jit_solution(3024696546686572541)
XLA Ops:
  0.6 0.0 copy-start.8
  0.6 0.0 copy-start
  0.7 0.0 copy-start.2
  0.7 0.0 copy-start.3
  0.7 4.1 %shard_map.153 = (bf16[128,2048]{1,0:T(8,128)(2,1)}, bf16[2,64,256]{2,1,0:T(8,128)(2,1)}) custom-call(s32[4,8]{1,0:T(4,128)} %bitcast.23, s32[1,8]{1,0:T(1,128)} %counts_ref.1, bf16[256,4096]{1,0:T(8,128)(2,1)} %c_ref.1, bf16[256,4096]{1,0:T(8,128)(2,1)} %x_ref.1), custom_call_target="tpu_custom_call" | custom-call | flops 536870912 | bytes 4194304 | tf_op jit(solution)/shard_map/pallas_call | solution.py:103
  4.8 14.9 %all_to_all.15 = bf16[8,2,8,2048]{3,2,1,0:T(8,128)(2,1)S(1)} all-to-all(bf16[8,2,8,2048]{3,2,1,0:T(8,128)(2,1)} %bitcast.22), channel_id=1, replica_groups=mesh['seq'=4,'exp'=8] {'exp'}, dimensions={0} | all-to-all | bytes 1048576 | tf_op jit(solution)/shard_map/all_to_all | solution.py:582
  19.8 0.0 copy-start.7
  19.8 0.0 copy-start.4
  19.8 1.3 collective-permute-start.9
  21.1 4.6 %collective-permute-start.6 = (bf16[64,2048]{1,0:T(8,128)(2,1)S(1)}, bf16[64,2048]{1,0:T(8,128)(2,1)S(1)}, u32[]{:S(2)}, u32[]{:S(2)}) collective-permute-start(bf16[64,2048]{1,0:T(8,128)(2,1)S(1)} %get-tuple-element.39.refs_0_), channel_id=1, source_target_pairs={{0,8},{8,16},{16,24},{1,9},{9,17},{17,25},{2,10},{10,18},{18,26},{... | collective-permute-start | bytes 786440 | tf_op jit(solution)/shard_map/ppermute | solution.py:540
  25.7 3.5 %collective-permute-start = (bf16[64,2048]{1,0:T(8,128)(2,1)S(1)}, bf16[64,2048]{1,0:T(8,128)(2,1)S(1)}, u32[]{:S(2)}, u32[]{:S(2)}) collective-permute-start(bf16[64,2048]{1,0:T(8,128)(2,1)S(1)} %get-tuple-element.40.refs_0_), channel_id=1, source_target_pairs={{0,8},{8,16},{16,24},{1,9},{9,17},{17,25},{2,10},{10,18},{18,26},{... | collective-permute-start | bytes 786440 | tf_op jit(solution)/shard_map/ppermute | solution.py:540
  29.2 1.3 collective-permute-start.3
  30.5 0.0 collective-permute-done.9.refs_4_
  30.5 1.3 collective-permute-start.10
  31.8 0.6 collective-permute-done.6.refs_1_
  32.4 0.0 copy-done.5
  32.4 1.4 %collective-permute-start.7 = (bf16[64,2048]{1,0:T(8,128)(2,1)S(1)}, bf16[64,2048]{1,0:T(8,128)(2,1)}, u32[]{:S(2)}, u32[]{:S(2)}) collective-permute-start(bf16[64,2048]{1,0:T(8,128)(2,1)S(1)} %collective-permute-done.6.refs_1_), channel_id=1, source_target_pairs={{8,16},{16,24},{9,17},{17,25},{10,18},{18,26},{11,19},{19,27},{12,... | collective-permute-start | bytes 786440 | tf_op jit(solution)/shard_map/ppermute | solution.py:540
  33.8 2.1 %collective-permute-done.refs_1_ = bf16[64,2048]{1,0:T(8,128)(2,1)S(1)} collective-permute-done((bf16[64,2048]{1,0:T(8,128)(2,1)S(1)}, bf16[64,2048]{1,0:T(8,128)(2,1)S(1)}, u32[]{:S(2)}, u32[]{:S(2)}) %collective-permute-start) | collective-permute-done | bytes 262176 | tf_op jit(solution)/shard_map/ppermute | solution.py:540
  35.9 1.3 %collective-permute-start.1 = (bf16[64,2048]{1,0:T(8,128)(2,1)S(1)}, bf16[64,2048]{1,0:T(8,128)(2,1)}, u32[]{:S(2)}, u32[]{:S(2)}) collective-permute-start(bf16[64,2048]{1,0:T(8,128)(2,1)S(1)} %collective-permute-done.refs_1_), channel_id=1, source_target_pairs={{8,16},{16,24},{9,17},{17,25},{10,18},{18,26},{11,19},{19,27},{12,... | collective-permute-start | bytes 786440 | tf_op jit(solution)/shard_map/ppermute | solution.py:540
  37.2 3.1 %collective-permute-done.3.refs_4_ = bf16[64,2048]{1,0:T(8,128)(2,1)S(1)} collective-permute-done((bf16[64,2048]{1,0:T(8,128)(2,1)S(1)}, bf16[64,2048]{1,0:T(8,128)(2,1)S(1)}, u32[]{:S(2)}, u32[]{:S(2)}) %collective-permute-start.3) | collective-permute-done | bytes 262176 | tf_op jit(solution)/shard_map/ppermute | solution.py:545
  40.3 1.3 collective-permute-start.4
  41.6 1.9 %collective-permute-done.10.refs_5_ = bf16[64,2048]{1,0:T(8,128)(2,1)} collective-permute-done((bf16[64,2048]{1,0:T(8,128)(2,1)S(1)}, bf16[64,2048]{1,0:T(8,128)(2,1)}, u32[]{:S(2)}, u32[]{:S(2)}) %collective-permute-start.10) | collective-permute-done | bytes 262176 | tf_op jit(solution)/shard_map/ppermute | solution.py:545
  43.5 1.3 collective-permute-start.11
  44.8 0.0 collective-permute-done.7.refs_2_
  44.8 1.4 %collective-permute-start.8 = (bf16[64,2048]{1,0:T(8,128)(2,1)}, bf16[64,2048]{1,0:T(8,128)(2,1)}, u32[]{:S(2)}, u32[]{:S(2)}) collective-permute-start(bf16[64,2048]{1,0:T(8,128)(2,1)} %collective-permute-done.7.refs_2_), channel_id=1, source_target_pairs={{16,24},{17,25},{18,26},{19,27},{20,28},{21,29},{22,30},{23,31}} | collective-permute-start | bytes 786440 | tf_op jit(solution)/shard_map/ppermute | solution.py:540
  46.2 0.0 collective-permute-done.1.refs_2_
  46.2 1.4 %collective-permute-start.2 = (bf16[64,2048]{1,0:T(8,128)(2,1)}, bf16[64,2048]{1,0:T(8,128)(2,1)}, u32[]{:S(2)}, u32[]{:S(2)}) collective-permute-start(bf16[64,2048]{1,0:T(8,128)(2,1)} %collective-permute-done.1.refs_2_), channel_id=1, source_target_pairs={{16,24},{17,25},{18,26},{19,27},{20,28},{21,29},{22,30},{23,31}} | collective-permute-start | bytes 786440 | tf_op jit(solution)/shard_map/ppermute | solution.py:540
  47.6 4.5 %collective-permute-done.4.refs_5_ = bf16[64,2048]{1,0:T(8,128)(2,1)} collective-permute-done((bf16[64,2048]{1,0:T(8,128)(2,1)S(1)}, bf16[64,2048]{1,0:T(8,128)(2,1)}, u32[]{:S(2)}, u32[]{:S(2)}) %collective-permute-start.4) | collective-permute-done | bytes 262176 | tf_op jit(solution)/shard_map/ppermute | solution.py:545
  52.0 1.3 collective-permute-start.5
  53.4 1.0 copy.22
  54.4 2.0 %pad.4.refs_7_ = bf16[2048,128]{1,0:T(8,128)(2,1)} pad(bf16[2048,32]{1,0:T(8,128)(2,1)} %copy.22, bf16[]{:T(256)} %constant.2.clone.1), padding=0_0x0_96 | pad | bytes 655362 | tf_op jit(solution)/shard_map/jit(_pad)/pad | solution.py:586
  56.3 1.0 collective-permute-done.11.refs_6_
  57.4 0.0 collective-permute-done.8.refs_3_
  57.4 0.0 copy-done.4
  57.4 0.0 copy-start.1
  57.4 1.9 %copy-done.1 = bf16[1,4096,384]{2,1,0:T(8,128)(2,1)S(1)} copy-done((bf16[1,4096,384]{2,1,0:T(8,128)(2,1)S(1)}, bf16[1,4096,384]{2,1,0:T(8,128)(2,1)}, u32[]{:S(2)}) %copy-start.1) | copy-done | bytes 3145752
  59.3 5.9 %shard_map.154 = (bf16[256,2048]{1,0:T(8,128)(2,1)}, bf16[4,64,2048]{2,1,0:T(8,128)(2,1)}, f32[256,896]{1,0:T(8,128)}, bf16[256,768]{1,0:T(8,128)(2,1)}) custom-call(bf16[64,2048]{1,0:T(8,128)(2,1)} %copy-done.4, bf16[64,2048]{1,0:T(8,128)(2,1)} %copy-done.6, bf16[64,2048]{1,0:T(8,128)(2,1)} %collective-permute-done.7.refs_2_, ...), custom_call_target="tpu_custom_call" | custom-call | flops 2415919104 | bytes 18874368 | tf_op jit(solution)/shard_map/pallas_call | solution.py:325
  65.3 4.3 %all-to-all-start.1 = ((bf16[32,8,2048]{2,1,0:T(8,128)(2,1)}), bf16[32,8,2048]{2,1,0:T(8,128)(2,1)S(1)}, u32[]{:S(2)}, u32[]{:S(2)}) async-start(bf16[32,8,2048]{2,1,0:T(8,128)(2,1)} %bitcast.21), calls=%async_computation.1 | async-start | bytes 2097152 | tf_op jit(solution)/shard_map/all_to_all | solution.py:578
  69.6 0.0 collective-permute-done.2.refs_3_
  69.6 0.0 collective-permute-done.5.refs_6_
  69.6 11.9 %shard_map.155 = (bf16[256,2048]{1,0:T(8,128)(2,1)}, bf16[4,64,2176]{2,1,0:T(8,128)(2,1)}, bf16[256,1664]{1,0:T(8,128)(2,1)}) custom-call(bf16[64,2048]{1,0:T(8,128)(2,1)} %copy-done.7, bf16[64,2048]{1,0:T(8,128)(2,1)} %copy-done.9, bf16[64,2048]{1,0:T(8,128)(2,1)} %collective-permute-done.1.refs_2_, bf16[64,2048]{1,0:T(8,128)(2,1)} %collective-permute-done.2.refs_3_, ...), custom_call_target="tpu_custom_call" | custom-call | flops 40265318400 | bytes 157286400 | tf_op jit(solution)/shard_map/pallas_call | solution.py:463
  81.5 14.3 %all-to-all-done.1 = bf16[32,8,2048]{2,1,0:T(8,128)(2,1)S(1)} async-done(((bf16[32,8,2048]{2,1,0:T(8,128)(2,1)}), bf16[32,8,2048]{2,1,0:T(8,128)(2,1)S(1)}, u32[]{:S(2)}, u32[]{:S(2)}) %all-to-all-start.1) | async-done | bytes 1048608 | tf_op jit(solution)/shard_map/all_to_all | solution.py:578
  95.8 3.8 %all-to-all-start.2 = ((bf16[32,8,2176]{2,1,0:T(8,128)(2,1)}), bf16[32,8,2176]{2,1,0:T(8,128)(2,1)S(1)}, u32[]{:S(2)}, u32[]{:S(2)}) async-start(bf16[32,8,2176]{2,1,0:T(8,128)(2,1)} %bitcast.20), calls=%async_computation.2 | async-start | bytes 2228224 | tf_op jit(solution)/shard_map/all_to_all | solution.py:578
  99.6 5.5 %shard_map.159 = f32[1,384,4096]{2,1,0:T(8,128)} custom-call(bf16[256,2048]{1,0:T(8,128)(2,1)} %get-tuple-element.37.c_ref, bf16[256,768]{1,0:T(8,128)(2,1)} %get-tuple-element.38.hidden_ref), custom_call_target="tpu_custom_call" | custom-call | flops 805306368 | bytes 6291456 | tf_op jit(solution)/shard_map/pallas_call | solution.py:524
  105.1 6.9 %shard_map.158 = (f32[2,2048,384]{2,1,0:T(8,128)}, f32[2,2048,384]{2,1,0:T(8,128)}) custom-call(bf16[256,2048]{1,0:T(8,128)(2,1)} %get-tuple-element.25.refs_11_.x_ref, bf16[256,1664]{1,0:T(8,128)(2,1)} %get-tuple-element.34.delta_ref), custom_call_target="tpu_custom_call" | custom-call | flops 1610612736 | bytes 12582912 | tf_op jit(solution)/shard_map/pallas_call | solution.py:502
  111.9 2.9 %shard_map.156 = bf16[256,4096]{1,0:T(8,128)(2,1)} custom-call(bf16[2,64,256]{2,1,0:T(8,128)(2,1)} %get-tuple-element.23.hot_ref, bf16[256,2048]{1,0:T(8,128)(2,1)S(1)} %bitcast.17), custom_call_target="tpu_custom_call" | custom-call | flops 536870912 | bytes 2097152 | tf_op jit(solution)/shard_map/pallas_call | solution.py:174
  114.9 12.2 %all-to-all-done.2 = bf16[32,8,2176]{2,1,0:T(8,128)(2,1)S(1)} async-done(((bf16[32,8,2176]{2,1,0:T(8,128)(2,1)}), bf16[32,8,2176]{2,1,0:T(8,128)(2,1)S(1)}, u32[]{:S(2)}, u32[]{:S(2)}) %all-to-all-start.2) | async-done | bytes 1114144 | tf_op jit(solution)/shard_map/all_to_all | solution.py:578
  127.1 3.5 %shard_map.157 = (bf16[256,4096]{1,0:T(8,128)(2,1)}, f32[8,128]{1,0:T(8,128)}, f32[1,8]{1,0:T(1,128)}) custom-call(bf16[2,64,256]{2,1,0:T(8,128)(2,1)} %get-tuple-element.23.hot_ref, bf16[256,2176]{1,0:T(8,128)(2,1)S(1)} %bitcast.18), custom_call_target="tpu_custom_call" | custom-call | flops 536870912 | bytes 2097152 | tf_op jit(solution)/shard_map/pallas_call | solution.py:174
  (15 shorter events, 0.1 us)
Async XLA Ops:
  0.6 45.5 %copy-start.8 = (bf16[4096,8]{0,1:T(8,128)(2,1)S(1)}, bf16[4096,8]{0,1:T(8,128)(2,1)}, u32[]{:S(2)}) copy-start(bf16[4096,8]{0,1:T(8,128)(2,1)} %param.12) | copy-start | bytes 196612
  0.6 56.7 %copy-start = (bf16[1,4096,384]{2,1,0:T(8,128)(2,1)S(1)}, bf16[1,4096,384]{2,1,0:T(8,128)(2,1)}, u32[]{:S(2)}) copy-start(bf16[1,4096,384]{2,1,0:T(8,128)(2,1)} %refs_8_.3) | copy-start | bytes 9437188
  0.7 56.7 %copy-start.2 = (f32[1,384]{1,0:T(1,128)S(1)}, f32[1,384]{1,0:T(1,128)}, u32[]{:S(2)}) copy-start(f32[1,384]{1,0:T(1,128)} %refs_13_.1) | copy-start | bytes 4612
  0.7 56.7 %copy-start.3 = (f32[8]{0:T(128)S(1)}, f32[8]{0:T(128)}, u32[]{:S(2)}) copy-start(f32[8]{0:T(128)} %param.13) | copy-start | bytes 100
  19.8 33.5 %copy-start.7 = (bf16[64,2048]{1,0:T(8,128)(2,1)}, bf16[64,2048]{1,0:T(8,128)(2,1)S(1)}, u32[]{:S(2)}) copy-start(bf16[64,2048]{1,0:T(8,128)(2,1)S(1)} %get-tuple-element.40.refs_0_) | copy-start | bytes 786436
  19.8 37.6 %copy-start.4 = (bf16[64,2048]{1,0:T(8,128)(2,1)}, bf16[64,2048]{1,0:T(8,128)(2,1)S(1)}, u32[]{:S(2)}) copy-start(bf16[64,2048]{1,0:T(8,128)(2,1)S(1)} %get-tuple-element.39.refs_0_) | copy-start | bytes 786436
  19.8 10.7 %collective-permute-start.9 = (bf16[64,2048]{1,0:T(8,128)(2,1)S(1)}, bf16[64,2048]{1,0:T(8,128)(2,1)S(1)}, u32[]{:S(2)}, u32[]{:S(2)}) collective-permute-start(bf16[64,2048]{1,0:T(8,128)(2,1)S(1)} %get-tuple-element.39.refs_0_), channel_id=1, source_target_pairs={{8,0},{16,8},{24,16},{9,1},{17,9},{25,17},{10,2},{18,10},{26,18},{... | collective-permute-start | bytes 786440 | tf_op jit(solution)/shard_map/ppermute | solution.py:545
  21.1 11.3 %collective-permute-start.6 = (bf16[64,2048]{1,0:T(8,128)(2,1)S(1)}, bf16[64,2048]{1,0:T(8,128)(2,1)S(1)}, u32[]{:S(2)}, u32[]{:S(2)}) collective-permute-start(bf16[64,2048]{1,0:T(8,128)(2,1)S(1)} %get-tuple-element.39.refs_0_), channel_id=1, source_target_pairs={{0,8},{8,16},{16,24},{1,9},{9,17},{17,25},{2,10},{10,18},{18,26},{... | collective-permute-start | bytes 786440 | tf_op jit(solution)/shard_map/ppermute | solution.py:540
  25.7 10.2 %collective-permute-start = (bf16[64,2048]{1,0:T(8,128)(2,1)S(1)}, bf16[64,2048]{1,0:T(8,128)(2,1)S(1)}, u32[]{:S(2)}, u32[]{:S(2)}) collective-permute-start(bf16[64,2048]{1,0:T(8,128)(2,1)S(1)} %get-tuple-element.40.refs_0_), channel_id=1, source_target_pairs={{0,8},{8,16},{16,24},{1,9},{9,17},{17,25},{2,10},{10,18},{18,26},{... | collective-permute-start | bytes 786440 | tf_op jit(solution)/shard_map/ppermute | solution.py:540
  29.2 11.1 %collective-permute-start.3 = (bf16[64,2048]{1,0:T(8,128)(2,1)S(1)}, bf16[64,2048]{1,0:T(8,128)(2,1)S(1)}, u32[]{:S(2)}, u32[]{:S(2)}) collective-permute-start(bf16[64,2048]{1,0:T(8,128)(2,1)S(1)} %get-tuple-element.40.refs_0_), channel_id=1, source_target_pairs={{8,0},{16,8},{24,16},{9,1},{17,9},{25,17},{10,2},{18,10},{26,18},{... | collective-permute-start | bytes 786440 | tf_op jit(solution)/shard_map/ppermute | solution.py:545
  30.5 1.9 %copy-start.5 = (bf16[64,2048]{1,0:T(8,128)(2,1)}, bf16[64,2048]{1,0:T(8,128)(2,1)S(1)}, u32[]{:S(2)}) copy-start(bf16[64,2048]{1,0:T(8,128)(2,1)S(1)} %collective-permute-done.9.refs_4_) | copy-start | bytes 786436
  30.5 13.0 %collective-permute-start.10 = (bf16[64,2048]{1,0:T(8,128)(2,1)S(1)}, bf16[64,2048]{1,0:T(8,128)(2,1)}, u32[]{:S(2)}, u32[]{:S(2)}) collective-permute-start(bf16[64,2048]{1,0:T(8,128)(2,1)S(1)} %collective-permute-done.9.refs_4_), channel_id=1, source_target_pairs={{8,0},{16,8},{9,1},{17,9},{10,2},{18,10},{11,3},{19,11},{12,4},{20... | collective-permute-start | bytes 786440 | tf_op jit(solution)/shard_map/ppermute | solution.py:545
  32.4 11.1 %copy-start.6 = (bf16[64,2048]{1,0:T(8,128)(2,1)}, bf16[64,2048]{1,0:T(8,128)(2,1)S(1)}, u32[]{:S(2)}) copy-start(bf16[64,2048]{1,0:T(8,128)(2,1)S(1)} %collective-permute-done.6.refs_1_) | copy-start | bytes 786436
  32.4 12.4 %collective-permute-start.7 = (bf16[64,2048]{1,0:T(8,128)(2,1)S(1)}, bf16[64,2048]{1,0:T(8,128)(2,1)}, u32[]{:S(2)}, u32[]{:S(2)}) collective-permute-start(bf16[64,2048]{1,0:T(8,128)(2,1)S(1)} %collective-permute-done.6.refs_1_), channel_id=1, source_target_pairs={{8,16},{16,24},{9,17},{17,25},{10,18},{18,26},{11,19},{19,27},{12,... | collective-permute-start | bytes 786440 | tf_op jit(solution)/shard_map/ppermute | solution.py:540
  35.9 17.4 %copy-start.9 = (bf16[64,2048]{1,0:T(8,128)(2,1)}, bf16[64,2048]{1,0:T(8,128)(2,1)S(1)}, u32[]{:S(2)}) copy-start(bf16[64,2048]{1,0:T(8,128)(2,1)S(1)} %collective-permute-done.refs_1_) | copy-start | bytes 786436
  35.9 10.3 %collective-permute-start.1 = (bf16[64,2048]{1,0:T(8,128)(2,1)S(1)}, bf16[64,2048]{1,0:T(8,128)(2,1)}, u32[]{:S(2)}, u32[]{:S(2)}) collective-permute-start(bf16[64,2048]{1,0:T(8,128)(2,1)S(1)} %collective-permute-done.refs_1_), channel_id=1, source_target_pairs={{8,16},{16,24},{9,17},{17,25},{10,18},{18,26},{11,19},{19,27},{12,... | collective-permute-start | bytes 786440 | tf_op jit(solution)/shard_map/ppermute | solution.py:540
  40.3 13.0 %copy-start.10 = (bf16[64,2048]{1,0:T(8,128)(2,1)}, bf16[64,2048]{1,0:T(8,128)(2,1)S(1)}, u32[]{:S(2)}) copy-start(bf16[64,2048]{1,0:T(8,128)(2,1)S(1)} %collective-permute-done.3.refs_4_) | copy-start | bytes 786436
  40.3 11.7 %collective-permute-start.4 = (bf16[64,2048]{1,0:T(8,128)(2,1)S(1)}, bf16[64,2048]{1,0:T(8,128)(2,1)}, u32[]{:S(2)}, u32[]{:S(2)}) collective-permute-start(bf16[64,2048]{1,0:T(8,128)(2,1)S(1)} %collective-permute-done.3.refs_4_), channel_id=1, source_target_pairs={{8,0},{16,8},{9,1},{17,9},{10,2},{18,10},{11,3},{19,11},{12,4},{20... | collective-permute-start | bytes 786440 | tf_op jit(solution)/shard_map/ppermute | solution.py:545
  43.5 13.9 %collective-permute-start.11 = (bf16[64,2048]{1,0:T(8,128)(2,1)}, bf16[64,2048]{1,0:T(8,128)(2,1)}, u32[]{:S(2)}, u32[]{:S(2)}) collective-permute-start(bf16[64,2048]{1,0:T(8,128)(2,1)} %collective-permute-done.10.refs_5_), channel_id=1, source_target_pairs={{8,0},{9,1},{10,2},{11,3},{12,4},{13,5},{14,6},{15,7}} | collective-permute-start | bytes 786440 | tf_op jit(solution)/shard_map/ppermute | solution.py:545
  44.8 12.6 %collective-permute-start.8 = (bf16[64,2048]{1,0:T(8,128)(2,1)}, bf16[64,2048]{1,0:T(8,128)(2,1)}, u32[]{:S(2)}, u32[]{:S(2)}) collective-permute-start(bf16[64,2048]{1,0:T(8,128)(2,1)} %collective-permute-done.7.refs_2_), channel_id=1, source_target_pairs={{16,24},{17,25},{18,26},{19,27},{20,28},{21,29},{22,30},{23,31}} | collective-permute-start | bytes 786440 | tf_op jit(solution)/shard_map/ppermute | solution.py:540
  46.2 23.4 %collective-permute-start.2 = (bf16[64,2048]{1,0:T(8,128)(2,1)}, bf16[64,2048]{1,0:T(8,128)(2,1)}, u32[]{:S(2)}, u32[]{:S(2)}) collective-permute-start(bf16[64,2048]{1,0:T(8,128)(2,1)} %collective-permute-done.1.refs_2_), channel_id=1, source_target_pairs={{16,24},{17,25},{18,26},{19,27},{20,28},{21,29},{22,30},{23,31}} | collective-permute-start | bytes 786440 | tf_op jit(solution)/shard_map/ppermute | solution.py:540
  52.0 17.6 %collective-permute-start.5 = (bf16[64,2048]{1,0:T(8,128)(2,1)}, bf16[64,2048]{1,0:T(8,128)(2,1)}, u32[]{:S(2)}, u32[]{:S(2)}) collective-permute-start(bf16[64,2048]{1,0:T(8,128)(2,1)} %collective-permute-done.4.refs_5_), channel_id=1, source_target_pairs={{8,0},{9,1},{10,2},{11,3},{12,4},{13,5},{14,6},{15,7}} | collective-permute-start | bytes 786440 | tf_op jit(solution)/shard_map/ppermute | solution.py:545
  57.4 1.9 %copy-start.1 = (bf16[1,4096,384]{2,1,0:T(8,128)(2,1)S(1)}, bf16[1,4096,384]{2,1,0:T(8,128)(2,1)}, u32[]{:S(2)}) copy-start(bf16[1,4096,384]{2,1,0:T(8,128)(2,1)} %refs_9_.3) | copy-start | bytes 9437188
  65.3 30.6 %all-to-all-start.1 = ((bf16[32,8,2048]{2,1,0:T(8,128)(2,1)}), bf16[32,8,2048]{2,1,0:T(8,128)(2,1)S(1)}, u32[]{:S(2)}, u32[]{:S(2)}) async-start(bf16[32,8,2048]{2,1,0:T(8,128)(2,1)} %bitcast.21), calls=%async_computation.1 | async-start | bytes 2097152 | tf_op jit(solution)/shard_map/all_to_all | solution.py:578
  95.8 31.3 %all-to-all-start.2 = ((bf16[32,8,2176]{2,1,0:T(8,128)(2,1)}), bf16[32,8,2176]{2,1,0:T(8,128)(2,1)S(1)}, u32[]{:S(2)}, u32[]{:S(2)}) async-start(bf16[32,8,2176]{2,1,0:T(8,128)(2,1)} %bitcast.20), calls=%async_computation.2 | async-start | bytes 2228224 | tf_op jit(solution)/shard_map/all_to_all | solution.py:578

commit v13 on v12

--- a/solution.py
+++ b/solution.py
@@ -229,7 +229,17 @@
             pltpu.make_async_copy(refs[a], places[k], sems.at[k]).wait()
 
 
-def side_copies(gate_ref, up_ref, router_ref, side, sems, pack, j, width):
+def router_rows(ref, pack, copies, rows):
+    part = ref.shape[1] // pack
+    wide = ref[...].astype(F32)
+    pieces = [wide[:, h * part : (h + 1) * part] for h in range(pack)] * copies
+    left = rows - len(pieces) * ref.shape[0]
+    if left:
+        pieces.append(jnp.zeros((left, part), F32))
+    return jnp.concatenate(pieces).astype(BF16)
+
+
+def side_copies(gate_ref, up_ref, side, sems, pack, j, width):
     part = side.shape[0]
     hidden_n = gate_ref.shape[2]
     rows = pl.ds(j * width, width)
@@ -238,7 +248,6 @@
         for n, ref in enumerate((gate_ref, up_ref)):
             columns = pl.ds((2 * h + n) * hidden_n, hidden_n)
             copies.append((ref.at[0, pl.ds(h * part + j * width, width), :], side.at[rows, columns]))
-    copies.append((router_ref.at[rows, :], side.at[rows, pl.ds(2 * pack * hidden_n, LANES)]))
     return [pltpu.make_async_copy(a, b, sems.at[j, n]) for n, (a, b) in enumerate(copies)]
 
 
@@ -260,39 +269,39 @@
         target[lax.rem(here - k + seq_n, seq_n), :, columns] = out[k * rows : (k + 1) * rows]
 
 
-def expert_forward(arrivals, seq_n, slots, experts, pack, router_side, threshold, w_gate, w_up, w_down, hid_scale):
+def expert_forward(arrivals, seq_n, slots, experts, pack, router_t, threshold, w_gate, w_up, w_down, hid_scale):
     block_rows, part = arrivals.blocks[0].shape
     rows = block_rows * seq_n
     hidden_n = w_gate.shape[2]
     both = 2 * hidden_n
     width = part // STEPS
-    total = pack * both + LANES
+    total = pack * both
     n_blocks = len(arrivals.blocks)
 
     def body(*refs):
         blocks = refs[:n_blocks]
-        router_ref, gate_ref, up_ref, down_ref, threshold_ref, scale_ref = refs[n_blocks : n_blocks + 6]
+        gate_ref, up_ref, down_ref, router_ref, threshold_ref, scale_ref = refs[n_blocks : n_blocks + 6]
         x_ref, out_ref, pre_ref, hidden_ref = refs[n_blocks + 6 : n_blocks + 10]
         pre_v, hidden_v, x_v, out_v, side, stack, x_sems, side_sems, stack_sems, out_sems = refs[n_blocks + 10 :]
         places = [x_v.at[pl.ds(k * block_rows, block_rows), :] for k in range(seq_n)]
         arrivals.start(blocks, places, x_sems)
-        chunks = [side_copies(gate_ref, up_ref, router_ref, side, side_sems, pack, j, width) for j in range(STEPS)]
+        chunks = [side_copies(gate_ref, up_ref, side, side_sems, pack, j, width) for j in range(STEPS)]
         downs = down_copies(down_ref, stack, stack_sems, pack)
         for copy in sum(chunks, []) + downs:
             copy.start()
         arrivals.wait(blocks, places, x_sems)
         leaving = [pltpu.make_async_copy(x_v, x_ref, out_sems.at[STEPS])]
         leaving[0].start()
-        sums = [0.0] * (pack + 1)
+        sums = [0.0] * pack
+        scores = mm(x_v[...], router_rows(router_ref, pack, 1, pack * experts), LAST)
         for j, chunk in enumerate(chunks):
             for copy in chunk:
                 copy.wait()
             now = slice(j * width, (j + 1) * width)
-            for n in range(pack + 1):
-                sums[n] = sums[n] + mm(x_v[:, now], side[now, n * both : min((n + 1) * both, total)])
-        gate = fold([y[:, :hidden_n] for y in sums[:pack]], slots)
-        up = fold([y[:, hidden_n:] for y in sums[:pack]], slots)
-        scores = sums[pack]
+            for n in range(pack):
+                sums[n] = sums[n] + mm(x_v[:, now], side[now, n * both : (n + 1) * both])
+        gate = fold([y[:, :hidden_n] for y in sums], slots)
+        up = fold([y[:, hidden_n:] for y in sums], slots)
         lane = lax.broadcasted_iota(jnp.int32, scores.shape, 1)
         expert = lax.axis_index("exp")
         score = fold([jnp.where(lane == h * experts + expert, scores, 0.0) for h in range(pack)], slots)
@@ -324,7 +333,7 @@
 
     return pl.pallas_call(
         body,
-        in_specs=[ANYWHERE] * (n_blocks + 4) + [IN_VMEM] * 2,
+        in_specs=[ANYWHERE] * (n_blocks + 3) + [IN_VMEM] * 3,
         out_specs=[ANYWHERE] * 4,
         out_shape=[
             shape((rows, part)),
@@ -340,13 +349,20 @@
             pltpu.VMEM((part, total), BF16),
             pltpu.VMEM((pack * hidden_n, part), BF16),
             pltpu.SemaphoreType.DMA((seq_n,)),
-            pltpu.SemaphoreType.DMA((STEPS, 2 * pack + 1)),
+            pltpu.SemaphoreType.DMA((STEPS, 2 * pack)),
             pltpu.SemaphoreType.DMA((pack,)),
             pltpu.SemaphoreType.DMA((STEPS + 3,)),
         ],
         compiler_params=PARAMS,
         cost_estimate=cost(6 * rows * part * pack * hidden_n, 12 * part * pack * hidden_n),
-    )(*to_hbm(*arrivals.blocks, router_side), w_gate, w_up, *to_hbm(w_down), threshold.reshape(1, -1), hid_scale)
+    )(
+        *to_hbm(*arrivals.blocks),
+        w_gate,
+        *to_hbm(w_up, w_down),
+        router_t,
+        threshold.reshape(1, -1),
+        hid_scale,
+    )
 
 
 def split3(v):
@@ -360,12 +376,12 @@
     return LANES * -(-2 * seq_n // group)
 
 
-def expert_backward(arrivals, seq_n, exp_n, slots, pack, x, pre, router_side, w_gate, w_up, w_down, hid_scale):
+def expert_backward(arrivals, seq_n, exp_n, slots, pack, x, pre, router_t, w_gate, w_up, w_down, hid_scale):
     block_rows, part = arrivals.blocks[0].shape
     rows = block_rows * seq_n
     hidden_n = w_gate.shape[2]
     width = part // STEPS
-    total = 2 * pack * hidden_n + LANES
+    total = 2 * pack * hidden_n
     group = pack * slots
     extra = riding(seq_n, group)
     per = part * pack // (seq_n * exp_n)
@@ -373,14 +389,14 @@
 
     def body(*refs):
         blocks = refs[:n_blocks]
-        router_ref, gate_ref, up_ref, down_ref, x_ref, pre_ref, scale_ref = refs[n_blocks : n_blocks + 7]
+        gate_ref, up_ref, down_ref, x_ref, pre_ref, router_ref, scale_ref = refs[n_blocks : n_blocks + 7]
         c_ref, out_ref, delta_ref = refs[n_blocks + 7 : n_blocks + 10]
-        c_v, x_v, pre_v, out_v, side, stack, columns, c_sems, x_sems, side_sems, stack_sems, out_sems = refs[
+        c_v, x_v, pre_v, out_v, side, stack, columns, router_v, c_sems, x_sems, side_sems, stack_sems, out_sems = refs[
             n_blocks + 10 :
         ]
         places = [c_v.at[pl.ds(k * block_rows, block_rows), :] for k in range(seq_n)]
         arrivals.start(blocks, places, c_sems)
-        chunks = [side_copies(gate_ref, up_ref, router_ref, side, side_sems, pack, j, width) for j in range(STEPS)]
+        chunks = [side_copies(gate_ref, up_ref, side, side_sems, pack, j, width) for j in range(STEPS)]
         downs = down_copies(down_ref, stack, stack_sems, pack)
         x_copy = pltpu.make_async_copy(x_ref, x_v, x_sems.at[0])
         pre_copy = pltpu.make_async_copy(pre_ref, pre_v, x_sems.at[1])
@@ -417,12 +433,13 @@
                 if n < 2:
                     by_expert = jnp.where(lane == (n * pack + h) * exp_n + expert, piece, by_expert)
         columns[...] = by_split.astype(BF16)
-        delta_ref[:, 2 * pack * hidden_n :] = by_expert.astype(BF16)
+        by_expert = by_expert.astype(BF16)
+        router_v[...] = router_rows(router_ref, pack, 2, LANES)
         for j, chunk in enumerate(chunks):
             for copy in chunk:
                 copy.wait()
             now = slice(j * width, (j + 1) * width)
-            put_blocks(mm(delta_ref[...], side[now, :], LAST).astype(BF16), out_v, now)
+            put_blocks((mm(delta_ref[...], side[now, :], LAST) + mm(by_expert, router_v[:, now])).astype(BF16), out_v, now)
             if j + 1 < STEPS:
                 now = pl.ds(j * width, width)
                 leaving.append(pltpu.make_async_copy(out_v.at[:, :, now], out_ref.at[:, :, now], out_sems.at[j]))
@@ -462,7 +479,7 @@
 
     return pl.pallas_call(
         body,
-        in_specs=[ANYWHERE] * (n_blocks + 6) + [IN_VMEM],
+        in_specs=[ANYWHERE] * (n_blocks + 5) + [IN_VMEM] * 2,
         out_specs=[ANYWHERE] * 2 + [IN_VMEM],
         out_shape=[
             shape((rows, part)),
@@ -477,15 +494,16 @@
             pltpu.VMEM((part, total), BF16),
             pltpu.VMEM((pack * hidden_n, part), BF16),
             pltpu.VMEM((rows, LANES), BF16),
+            pltpu.VMEM((LANES, part), BF16),
             pltpu.SemaphoreType.DMA((seq_n,)),
             pltpu.SemaphoreType.DMA((2,)),
-            pltpu.SemaphoreType.DMA((STEPS, 2 * pack + 1)),
+            pltpu.SemaphoreType.DMA((STEPS, 2 * pack)),
             pltpu.SemaphoreType.DMA((pack,)),
             pltpu.SemaphoreType.DMA((STEPS + 1,)),
         ],
         compiler_params=PARAMS,
         cost_estimate=cost(100 * rows * part * pack * hidden_n, 100 * part * pack * hidden_n),
-    )(*to_hbm(*arrivals.blocks, router_side, w_gate, w_up, w_down, x, pre), hid_scale)
+    )(*to_hbm(*arrivals.blocks, w_gate, w_up, w_down, x, pre), router_t, hid_scale)
 
 
 def side_grads(x, delta, pack, hidden_n):
@@ -581,16 +599,14 @@
     sent = sent.reshape(experts, 2, -1, sent.shape[1])
     here = lax.all_to_all(sent, "exp", split_axis=0, concat_axis=0, tiled=True)
     x_in, c_in = (line_gather(here[:, n].reshape(-1, here.shape[3]), seq_n) for n in range(2))
-    halves = list(router.reshape(pack, features // pack, experts))
-    router_side = jnp.concatenate(halves + halves, axis=1)
-    router_side = jnp.pad(router_side, ((0, 0), (0, LANES - router_side.shape[1])))
+    router_t = router.T
 
     x, out, pre, hidden = expert_forward(
-        x_in, seq_n, slots, experts, pack, router_side, threshold, w_gate, w_up, w_down, hid_scale
+        x_in, seq_n, slots, experts, pack, router_t, threshold, w_gate, w_up, w_down, hid_scale
     )
     out = to_owners(out)
     c, back, delta = expert_backward(
-        c_in, seq_n, exp_n, slots, pack, x, pre, router_side, w_gate, w_up, w_down, hid_scale
+        c_in, seq_n, exp_n, slots, pack, x, pre, router_t, w_gate, w_up, w_down, hid_scale
     )
     back, out = lax.optimization_barrier((back, out))
     back = to_owners(back)

time: 132 us -> 129 us (0.977)
  starting transfers between devices: 29.3 us -> 24.8 us
  waiting for transfers between devices: 39.8 us -> 44 us
  local copies, waits for them, and re-layouts: 4.94 us -> 1.57 us
    ppermute x6, waiting for transfers between devices: 10.5 us -> 15.4 us  [down_line(): return lax.ppermute(block, 'seq', [(s, s - 1) for s in range(first, last)])]
    ppermute x6, starting transfers between devices: 13.5 us -> 10.7 us  [up_line(): return lax.ppermute(block, 'seq', [(s, s + 1) for s in range(first, last)])]
    pad x1 -> x0, local copies, waits for them, and re-layouts: 1.96 us -> none  [on_device(): jnp.pad(router_side, ((0, 0), (0, LANES - router_side.shape[1])))]
    all_to_all x2, starting transfers between devices: 8.12 us -> 6.39 us  [to_owners(): lax.all_to_all(parts, BOTH, split_axis=0, concat_axis=0, tiled=True)]
    all_to_all x2, waiting for transfers between devices: 26.5 us -> 25.1 us  [to_owners(): lax.all_to_all(parts, BOTH, split_axis=0, concat_axis=0, tiled=True)]
  transfers between devices with their start and end apart: 14 -> 14, of which waited for: 8 -> 8; matrix products, arithmetic and copies ran while one was open for 2% -> 0% of each run, Pallas kernels for 25% -> 26%
where the time goes in v13:
time: 129 us; the launch traced here: 128 us
  waiting for transfers between devices  44 us (34%)
  Pallas kernels  41.4 us (32%)
  starting transfers between devices  24.8 us (19%)
  blocking collectives  14.9 us (12%)
  local copies, waits for them, and re-layouts  1.57 us (1%)
    all_to_all x2, waiting for transfers between devices, to_owners(): lax.all_to_all(parts, BOTH, split_axis=0, concat_axis=0, tiled=True)  25.1 us
    ppermute x6, waiting for transfers between devices, down_line(): return lax.ppermute(block, 'seq', [(s, s - 1) for s in range(first, last)])  15.4 us
    all_to_all x1, blocking collectives, on_device(): here = lax.all_to_all(sent, 'exp', split_axis=0, concat_axis=0, tiled=True)  14.9 us
    pallas_call x1, Pallas kernels, expert_backward(): pl.pallas_call(body, in_specs=[ANYWHERE] * (n_blocks + 5) + [IN_VMEM] * 2...  12.5 us
    ppermute x6, starting transfers between devices, up_line(): return lax.ppermute(block, 'seq', [(s, s + 1) for s in range(first, last)])  10.7 us
    ppermute x6, starting transfers between devices, down_line(): return lax.ppermute(block, 'seq', [(s, s - 1) for s in range(first, last)])  7.72 us
    pallas_call x1, Pallas kernels, side_grads(): pl.pallas_call(body, grid=(STEPS,), in_specs=[pl.BlockSpec((rows, width),...  6.84 us
    pallas_call x2, Pallas kernels, scatter_rows(): pl.pallas_call(body, in_specs=[ANYWHERE] * 2, out_specs=out_specs, out_sh...  6.42 us
  transfers between devices with their start and end apart: 14, of which 8 were waited for; matrix products, arithmetic and copies ran while one was open for 0% of the time, Pallas kernels for 26%

profile of v13, /device:TPU:0, one launch (start us, length us, event | category | flops | bytes accessed | tf_op | source)
XLA Modules:
  0.0 127.9 jit_solution(8277620621865546720)
XLA Ops:
  0.6 0.0 copy-start
  0.7 4.1 %shard_map.153 = (bf16[128,2048]{1,0:T(8,128)(2,1)}, bf16[2,64,256]{2,1,0:T(8,128)(2,1)}) custom-call(s32[4,8]{1,0:T(4,128)} %bitcast.26, s32[1,8]{1,0:T(1,128)} %counts_ref.1, bf16[256,4096]{1,0:T(8,128)(2,1)} %c_ref.1, bf16[256,4096]{1,0:T(8,128)(2,1)} %x_ref.1), custom_call_target="tpu_custom_call" | custom-call | flops 536870912 | bytes 4194304 | tf_op jit(solution)/shard_map/pallas_call | solution.py:103
  4.8 14.9 %all_to_all.15 = bf16[8,2,8,2048]{3,2,1,0:T(8,128)(2,1)S(1)} all-to-all(bf16[8,2,8,2048]{3,2,1,0:T(8,128)(2,1)} %bitcast.25), channel_id=1, replica_groups=mesh['seq'=4,'exp'=8] {'exp'}, dimensions={0} | all-to-all | bytes 1048576 | tf_op jit(solution)/shard_map/all_to_all | solution.py:600
  19.8 0.0 copy-start.4
  19.8 0.0 copy-start.11
  19.8 1.3 %collective-permute-start.9 = (bf16[64,2048]{1,0:T(8,128)(2,1)S(1)}, bf16[64,2048]{1,0:T(8,128)(2,1)S(1)}, u32[]{:S(2)}, u32[]{:S(2)}) collective-permute-start(bf16[64,2048]{1,0:T(8,128)(2,1)S(1)} %get-tuple-element.39.refs_0_), channel_id=1, source_target_pairs={{8,0},{16,8},{24,16},{9,1},{17,9},{25,17},{10,2},{18,10},{26,18},{... | collective-permute-start | bytes 786440 | tf_op jit(solution)/shard_map/ppermute | solution.py:563
  21.1 4.6 %collective-permute-start.6 = (bf16[64,2048]{1,0:T(8,128)(2,1)S(1)}, bf16[64,2048]{1,0:T(8,128)(2,1)S(1)}, u32[]{:S(2)}, u32[]{:S(2)}) collective-permute-start(bf16[64,2048]{1,0:T(8,128)(2,1)S(1)} %get-tuple-element.39.refs_0_), channel_id=1, source_target_pairs={{0,8},{8,16},{16,24},{1,9},{9,17},{17,25},{2,10},{10,18},{18,26},{... | collective-permute-start | bytes 786440 | tf_op jit(solution)/shard_map/ppermute | solution.py:558
  25.7 3.5 %collective-permute-start = (bf16[64,2048]{1,0:T(8,128)(2,1)S(1)}, bf16[64,2048]{1,0:T(8,128)(2,1)S(1)}, u32[]{:S(2)}, u32[]{:S(2)}) collective-permute-start(bf16[64,2048]{1,0:T(8,128)(2,1)S(1)} %get-tuple-element.40.refs_0_), channel_id=1, source_target_pairs={{0,8},{8,16},{16,24},{1,9},{9,17},{17,25},{2,10},{10,18},{18,26},{... | collective-permute-start | bytes 786440 | tf_op jit(solution)/shard_map/ppermute | solution.py:558
  29.1 1.3 %collective-permute-start.3 = (bf16[64,2048]{1,0:T(8,128)(2,1)S(1)}, bf16[64,2048]{1,0:T(8,128)(2,1)S(1)}, u32[]{:S(2)}, u32[]{:S(2)}) collective-permute-start(bf16[64,2048]{1,0:T(8,128)(2,1)S(1)} %get-tuple-element.40.refs_0_), channel_id=1, source_target_pairs={{8,0},{16,8},{24,16},{9,1},{17,9},{25,17},{10,2},{18,10},{26,18},{... | collective-permute-start | bytes 786440 | tf_op jit(solution)/shard_map/ppermute | solution.py:563
  30.4 0.0 collective-permute-done.9.refs_4_
  30.5 1.3 %collective-permute-start.10 = (bf16[64,2048]{1,0:T(8,128)(2,1)S(1)}, bf16[64,2048]{1,0:T(8,128)(2,1)S(1)}, u32[]{:S(2)}, u32[]{:S(2)}) collective-permute-start(bf16[64,2048]{1,0:T(8,128)(2,1)S(1)} %collective-permute-done.9.refs_4_), channel_id=1, source_target_pairs={{8,0},{16,8},{9,1},{17,9},{10,2},{18,10},{11,3},{19,11},{12,4},{20... | collective-permute-start | bytes 786440 | tf_op jit(solution)/shard_map/ppermute | solution.py:563
  31.8 0.6 collective-permute-done.6.refs_1_
  32.4 0.7 collective-permute-start.7
  33.1 2.8 %collective-permute-done.refs_1_ = bf16[64,2048]{1,0:T(8,128)(2,1)S(1)} collective-permute-done((bf16[64,2048]{1,0:T(8,128)(2,1)S(1)}, bf16[64,2048]{1,0:T(8,128)(2,1)S(1)}, u32[]{:S(2)}, u32[]{:S(2)}) %collective-permute-start) | collective-permute-done | bytes 262176 | tf_op jit(solution)/shard_map/ppermute | solution.py:558
  35.9 0.7 collective-permute-start.1
  36.5 3.7 %collective-permute-done.3.refs_4_ = bf16[64,2048]{1,0:T(8,128)(2,1)S(1)} collective-permute-done((bf16[64,2048]{1,0:T(8,128)(2,1)S(1)}, bf16[64,2048]{1,0:T(8,128)(2,1)S(1)}, u32[]{:S(2)}, u32[]{:S(2)}) %collective-permute-start.3) | collective-permute-done | bytes 262176 | tf_op jit(solution)/shard_map/ppermute | solution.py:563
  40.3 1.3 %collective-permute-start.4 = (bf16[64,2048]{1,0:T(8,128)(2,1)S(1)}, bf16[64,2048]{1,0:T(8,128)(2,1)S(1)}, u32[]{:S(2)}, u32[]{:S(2)}) collective-permute-start(bf16[64,2048]{1,0:T(8,128)(2,1)S(1)} %collective-permute-done.3.refs_4_), channel_id=1, source_target_pairs={{8,0},{16,8},{9,1},{17,9},{10,2},{18,10},{11,3},{19,11},{12,4},{20... | collective-permute-start | bytes 786440 | tf_op jit(solution)/shard_map/ppermute | solution.py:563
  41.6 2.5 %collective-permute-done.10.refs_5_ = bf16[64,2048]{1,0:T(8,128)(2,1)S(1)} collective-permute-done((bf16[64,2048]{1,0:T(8,128)(2,1)S(1)}, bf16[64,2048]{1,0:T(8,128)(2,1)S(1)}, u32[]{:S(2)}, u32[]{:S(2)}) %collective-permute-start.10) | collective-permute-done | bytes 262176 | tf_op jit(solution)/shard_map/ppermute | solution.py:563
  44.0 1.3 %collective-permute-start.11 = (bf16[64,2048]{1,0:T(8,128)(2,1)S(1)}, bf16[64,2048]{1,0:T(8,128)(2,1)S(1)}, u32[]{:S(2)}, u32[]{:S(2)}) collective-permute-start(bf16[64,2048]{1,0:T(8,128)(2,1)S(1)} %collective-permute-done.10.refs_5_), channel_id=1, source_target_pairs={{8,0},{9,1},{10,2},{11,3},{12,4},{13,5},{14,6},{15,7}} | collective-permute-start | bytes 786440 | tf_op jit(solution)/shard_map/ppermute | solution.py:563
  45.3 0.0 collective-permute-done.7.refs_2_
  45.3 0.7 collective-permute-start.8
  46.0 0.0 collective-permute-done.1.refs_2_
  46.1 0.7 collective-permute-start.2
  46.7 5.2 %collective-permute-done.4.refs_5_ = bf16[64,2048]{1,0:T(8,128)(2,1)S(1)} collective-permute-done((bf16[64,2048]{1,0:T(8,128)(2,1)S(1)}, bf16[64,2048]{1,0:T(8,128)(2,1)S(1)}, u32[]{:S(2)}, u32[]{:S(2)}) %collective-permute-start.4) | collective-permute-done | bytes 262176 | tf_op jit(solution)/shard_map/ppermute | solution.py:563
  51.9 1.3 %collective-permute-start.5 = (bf16[64,2048]{1,0:T(8,128)(2,1)S(1)}, bf16[64,2048]{1,0:T(8,128)(2,1)S(1)}, u32[]{:S(2)}, u32[]{:S(2)}) collective-permute-start(bf16[64,2048]{1,0:T(8,128)(2,1)S(1)} %collective-permute-done.4.refs_5_), channel_id=1, source_target_pairs={{8,0},{9,1},{10,2},{11,3},{12,4},{13,5},{14,6},{15,7}} | collective-permute-start | bytes 786440 | tf_op jit(solution)/shard_map/ppermute | solution.py:563
  53.2 4.1 %collective-permute-done.11.refs_6_ = bf16[64,2048]{1,0:T(8,128)(2,1)S(1)} collective-permute-done((bf16[64,2048]{1,0:T(8,128)(2,1)S(1)}, bf16[64,2048]{1,0:T(8,128)(2,1)S(1)}, u32[]{:S(2)}, u32[]{:S(2)}) %collective-permute-start.11) | collective-permute-done | bytes 262176 | tf_op jit(solution)/shard_map/ppermute | solution.py:563
  57.3 0.0 collective-permute-done.8.refs_3_
  57.3 0.0 copy-done.5
  57.3 0.0 copy-done.6
  57.3 0.0 copy-done.7
  57.3 0.0 copy-done.8
  57.3 0.7 copy-done.9
  58.0 0.1 copy-done.10
  58.1 0.0 copy-done.1
  58.1 6.0 %shard_map.154 = (bf16[256,2048]{1,0:T(8,128)(2,1)}, bf16[4,64,2048]{2,1,0:T(8,128)(2,1)}, f32[256,896]{1,0:T(8,128)}, bf16[256,768]{1,0:T(8,128)(2,1)}) custom-call(bf16[64,2048]{1,0:T(8,128)(2,1)} %copy-done.4, bf16[64,2048]{1,0:T(8,128)(2,1)} %copy-done.6, bf16[64,2048]{1,0:T(8,128)(2,1)} %copy-done.8, bf16[64,2048]{1,0:T(8,128)(2,1)} %copy-done.10, ...), custom_call_target="tpu_custom_call" | custom-call | flops 2415919104 | bytes 18874368 | tf_op jit(solution)/shard_map/pallas_call | solution.py:334
  64.1 2.7 %all-to-all-start.1 = ((bf16[32,8,2048]{2,1,0:T(8,128)(2,1)}), bf16[32,8,2048]{2,1,0:T(8,128)(2,1)S(1)}, u32[]{:S(2)}, u32[]{:S(2)}) async-start(bf16[32,8,2048]{2,1,0:T(8,128)(2,1)} %bitcast.24), calls=%async_computation.1 | async-start | bytes 2097152 | tf_op jit(solution)/shard_map/all_to_all | solution.py:596
  66.8 0.0 collective-permute-done.2.refs_3_
  66.8 0.0 collective-permute-done.5.refs_6_
  66.9 0.6 copy-done.16
  67.5 0.1 copy-done.17
  67.6 12.5 %shard_map.155 = (bf16[256,2048]{1,0:T(8,128)(2,1)}, bf16[4,64,2176]{2,1,0:T(8,128)(2,1)}, bf16[256,1536]{1,0:T(8,128)(2,1)}) custom-call(bf16[64,2048]{1,0:T(8,128)(2,1)} %copy-done.11, bf16[64,2048]{1,0:T(8,128)(2,1)} %copy-done.12, bf16[64,2048]{1,0:T(8,128)(2,1)} %copy-done.14, bf16[64,2048]{1,0:T(8,128)(2,1)} %copy-done.16, ...), custom_call_target="tpu_custom_call" | custom-call | flops 40265318400 | bytes 157286400 | tf_op jit(solution)/shard_map/pallas_call | solution.py:480
  80.1 12.9 %all-to-all-done.1 = bf16[32,8,2048]{2,1,0:T(8,128)(2,1)S(1)} async-done(((bf16[32,8,2048]{2,1,0:T(8,128)(2,1)}), bf16[32,8,2048]{2,1,0:T(8,128)(2,1)S(1)}, u32[]{:S(2)}, u32[]{:S(2)}) %all-to-all-start.1) | async-done | bytes 1048608 | tf_op jit(solution)/shard_map/all_to_all | solution.py:596
  93.0 3.7 %all-to-all-start.2 = ((bf16[32,8,2176]{2,1,0:T(8,128)(2,1)}), bf16[32,8,2176]{2,1,0:T(8,128)(2,1)S(1)}, u32[]{:S(2)}, u32[]{:S(2)}) async-start(bf16[32,8,2176]{2,1,0:T(8,128)(2,1)} %bitcast.23), calls=%async_computation.2 | async-start | bytes 2228224 | tf_op jit(solution)/shard_map/all_to_all | solution.py:596
  96.8 5.5 %shard_map.159 = f32[1,384,4096]{2,1,0:T(8,128)} custom-call(bf16[256,2048]{1,0:T(8,128)(2,1)} %get-tuple-element.37.c_ref, bf16[256,768]{1,0:T(8,128)(2,1)} %get-tuple-element.38.hidden_ref), custom_call_target="tpu_custom_call" | custom-call | flops 805306368 | bytes 6291456 | tf_op jit(solution)/shard_map/pallas_call | solution.py:542
  102.2 6.8 %shard_map.158 = (f32[2,2048,384]{2,1,0:T(8,128)}, f32[2,2048,384]{2,1,0:T(8,128)}) custom-call(bf16[256,2048]{1,0:T(8,128)(2,1)} %get-tuple-element.25.refs_10_.x_ref, bf16[256,1536]{1,0:T(8,128)(2,1)} %get-tuple-element.34.delta_ref), custom_call_target="tpu_custom_call" | custom-call | flops 1610612736 | bytes 12582912 | tf_op jit(solution)/shard_map/pallas_call | solution.py:520
  109.1 2.9 %shard_map.156 = bf16[256,4096]{1,0:T(8,128)(2,1)} custom-call(bf16[2,64,256]{2,1,0:T(8,128)(2,1)} %get-tuple-element.23.hot_ref, bf16[256,2048]{1,0:T(8,128)(2,1)S(1)} %bitcast.18), custom_call_target="tpu_custom_call" | custom-call | flops 536870912 | bytes 2097152 | tf_op jit(solution)/shard_map/pallas_call | solution.py:174
  112.0 12.2 %all-to-all-done.2 = bf16[32,8,2176]{2,1,0:T(8,128)(2,1)S(1)} async-done(((bf16[32,8,2176]{2,1,0:T(8,128)(2,1)}), bf16[32,8,2176]{2,1,0:T(8,128)(2,1)S(1)}, u32[]{:S(2)}, u32[]{:S(2)}) %all-to-all-start.2) | async-done | bytes 1114144 | tf_op jit(solution)/shard_map/all_to_all | solution.py:596
  124.2 3.5 %shard_map.157 = (bf16[256,4096]{1,0:T(8,128)(2,1)}, f32[8,128]{1,0:T(8,128)}, f32[1,8]{1,0:T(1,128)}) custom-call(bf16[2,64,256]{2,1,0:T(8,128)(2,1)} %get-tuple-element.23.hot_ref, bf16[256,2176]{1,0:T(8,128)(2,1)S(1)} %bitcast.19), custom_call_target="tpu_custom_call" | custom-call | flops 536870912 | bytes 2097152 | tf_op jit(solution)/shard_map/pallas_call | solution.py:174
  (25 shorter events, 0.1 us)
Async XLA Ops:
  0.6 57.4 %copy-start = (bf16[1,4096,384]{2,1,0:T(8,128)(2,1)S(1)}, bf16[1,4096,384]{2,1,0:T(8,128)(2,1)}, u32[]{:S(2)}) copy-start(bf16[1,4096,384]{2,1,0:T(8,128)(2,1)} %refs_7_.3) | copy-start | bytes 9437188
  0.6 57.4 %copy-start.1 = (bf16[4096,8]{0,1:T(8,128)(2,1)S(1)}, bf16[4096,8]{0,1:T(8,128)(2,1)}, u32[]{:S(2)}) copy-start(bf16[4096,8]{0,1:T(8,128)(2,1)} %param.12) | copy-start | bytes 196612
  0.7 57.4 %copy-start.2 = (f32[1,384]{1,0:T(1,128)S(1)}, f32[1,384]{1,0:T(1,128)}, u32[]{:S(2)}) copy-start(f32[1,384]{1,0:T(1,128)} %refs_13_.1) | copy-start | bytes 4612
  0.7 57.4 %copy-start.3 = (f32[8]{0:T(128)S(1)}, f32[8]{0:T(128)}, u32[]{:S(2)}) copy-start(f32[8]{0:T(128)} %param.13) | copy-start | bytes 100
  19.8 37.5 %copy-start.4 = (bf16[64,2048]{1,0:T(8,128)(2,1)}, bf16[64,2048]{1,0:T(8,128)(2,1)S(1)}, u32[]{:S(2)}) copy-start(bf16[64,2048]{1,0:T(8,128)(2,1)S(1)} %get-tuple-element.39.refs_0_) | copy-start | bytes 786436
  19.8 47.1 %copy-start.11 = (bf16[64,2048]{1,0:T(8,128)(2,1)}, bf16[64,2048]{1,0:T(8,128)(2,1)S(1)}, u32[]{:S(2)}) copy-start(bf16[64,2048]{1,0:T(8,128)(2,1)S(1)} %get-tuple-element.40.refs_0_) | copy-start | bytes 786436
  19.8 10.7 %collective-permute-start.9 = (bf16[64,2048]{1,0:T(8,128)(2,1)S(1)}, bf16[64,2048]{1,0:T(8,128)(2,1)S(1)}, u32[]{:S(2)}, u32[]{:S(2)}) collective-permute-start(bf16[64,2048]{1,0:T(8,128)(2,1)S(1)} %get-tuple-element.39.refs_0_), channel_id=1, source_target_pairs={{8,0},{16,8},{24,16},{9,1},{17,9},{25,17},{10,2},{18,10},{26,18},{... | collective-permute-start | bytes 786440 | tf_op jit(solution)/shard_map/ppermute | solution.py:563
  21.1 11.3 %collective-permute-start.6 = (bf16[64,2048]{1,0:T(8,128)(2,1)S(1)}, bf16[64,2048]{1,0:T(8,128)(2,1)S(1)}, u32[]{:S(2)}, u32[]{:S(2)}) collective-permute-start(bf16[64,2048]{1,0:T(8,128)(2,1)S(1)} %get-tuple-element.39.refs_0_), channel_id=1, source_target_pairs={{0,8},{8,16},{16,24},{1,9},{9,17},{17,25},{2,10},{10,18},{18,26},{... | collective-permute-start | bytes 786440 | tf_op jit(solution)/shard_map/ppermute | solution.py:558
  25.7 10.2 %collective-permute-start = (bf16[64,2048]{1,0:T(8,128)(2,1)S(1)}, bf16[64,2048]{1,0:T(8,128)(2,1)S(1)}, u32[]{:S(2)}, u32[]{:S(2)}) collective-permute-start(bf16[64,2048]{1,0:T(8,128)(2,1)S(1)} %get-tuple-element.40.refs_0_), channel_id=1, source_target_pairs={{0,8},{8,16},{16,24},{1,9},{9,17},{17,25},{2,10},{10,18},{18,26},{... | collective-permute-start | bytes 786440 | tf_op jit(solution)/shard_map/ppermute | solution.py:558
  29.1 11.1 %collective-permute-start.3 = (bf16[64,2048]{1,0:T(8,128)(2,1)S(1)}, bf16[64,2048]{1,0:T(8,128)(2,1)S(1)}, u32[]{:S(2)}, u32[]{:S(2)}) collective-permute-start(bf16[64,2048]{1,0:T(8,128)(2,1)S(1)} %get-tuple-element.40.refs_0_), channel_id=1, source_target_pairs={{8,0},{16,8},{24,16},{9,1},{17,9},{25,17},{10,2},{18,10},{26,18},{... | collective-permute-start | bytes 786440 | tf_op jit(solution)/shard_map/ppermute | solution.py:563
  30.5 26.8 %copy-start.5 = (bf16[64,2048]{1,0:T(8,128)(2,1)}, bf16[64,2048]{1,0:T(8,128)(2,1)S(1)}, u32[]{:S(2)}) copy-start(bf16[64,2048]{1,0:T(8,128)(2,1)S(1)} %collective-permute-done.9.refs_4_) | copy-start | bytes 786436
  30.5 13.6 %collective-permute-start.10 = (bf16[64,2048]{1,0:T(8,128)(2,1)S(1)}, bf16[64,2048]{1,0:T(8,128)(2,1)S(1)}, u32[]{:S(2)}, u32[]{:S(2)}) collective-permute-start(bf16[64,2048]{1,0:T(8,128)(2,1)S(1)} %collective-permute-done.9.refs_4_), channel_id=1, source_target_pairs={{8,0},{16,8},{9,1},{17,9},{10,2},{18,10},{11,3},{19,11},{12,4},{20... | collective-permute-start | bytes 786440 | tf_op jit(solution)/shard_map/ppermute | solution.py:563
  32.4 24.9 %copy-start.6 = (bf16[64,2048]{1,0:T(8,128)(2,1)}, bf16[64,2048]{1,0:T(8,128)(2,1)S(1)}, u32[]{:S(2)}) copy-start(bf16[64,2048]{1,0:T(8,128)(2,1)S(1)} %collective-permute-done.6.refs_1_) | copy-start | bytes 786436
  32.4 12.9 %collective-permute-start.7 = (bf16[64,2048]{1,0:T(8,128)(2,1)S(1)}, bf16[64,2048]{1,0:T(8,128)(2,1)S(1)}, u32[]{:S(2)}, u32[]{:S(2)}) collective-permute-start(bf16[64,2048]{1,0:T(8,128)(2,1)S(1)} %collective-permute-done.6.refs_1_), channel_id=1, source_target_pairs={{8,16},{16,24},{9,17},{17,25},{10,18},{18,26},{11,19},{19,27},{12,... | collective-permute-start | bytes 786440 | tf_op jit(solution)/shard_map/ppermute | solution.py:558
  35.9 31.0 %copy-start.12 = (bf16[64,2048]{1,0:T(8,128)(2,1)}, bf16[64,2048]{1,0:T(8,128)(2,1)S(1)}, u32[]{:S(2)}) copy-start(bf16[64,2048]{1,0:T(8,128)(2,1)S(1)} %collective-permute-done.refs_1_) | copy-start | bytes 786436
  35.9 10.2 %collective-permute-start.1 = (bf16[64,2048]{1,0:T(8,128)(2,1)S(1)}, bf16[64,2048]{1,0:T(8,128)(2,1)S(1)}, u32[]{:S(2)}, u32[]{:S(2)}) collective-permute-start(bf16[64,2048]{1,0:T(8,128)(2,1)S(1)} %collective-permute-done.refs_1_), channel_id=1, source_target_pairs={{8,16},{16,24},{9,17},{17,25},{10,18},{18,26},{11,19},{19,27},{12,... | collective-permute-start | bytes 786440 | tf_op jit(solution)/shard_map/ppermute | solution.py:558
  40.3 26.6 %copy-start.13 = (bf16[64,2048]{1,0:T(8,128)(2,1)}, bf16[64,2048]{1,0:T(8,128)(2,1)S(1)}, u32[]{:S(2)}) copy-start(bf16[64,2048]{1,0:T(8,128)(2,1)S(1)} %collective-permute-done.3.refs_4_) | copy-start | bytes 786436
  40.3 11.6 %collective-permute-start.4 = (bf16[64,2048]{1,0:T(8,128)(2,1)S(1)}, bf16[64,2048]{1,0:T(8,128)(2,1)S(1)}, u32[]{:S(2)}, u32[]{:S(2)}) collective-permute-start(bf16[64,2048]{1,0:T(8,128)(2,1)S(1)} %collective-permute-done.3.refs_4_), channel_id=1, source_target_pairs={{8,0},{16,8},{9,1},{17,9},{10,2},{18,10},{11,3},{19,11},{12,4},{20... | collective-permute-start | bytes 786440 | tf_op jit(solution)/shard_map/ppermute | solution.py:563
  44.0 13.3 %copy-start.7 = (bf16[64,2048]{1,0:T(8,128)(2,1)}, bf16[64,2048]{1,0:T(8,128)(2,1)S(1)}, u32[]{:S(2)}) copy-start(bf16[64,2048]{1,0:T(8,128)(2,1)S(1)} %collective-permute-done.10.refs_5_) | copy-start | bytes 786436
  44.0 13.2 %collective-permute-start.11 = (bf16[64,2048]{1,0:T(8,128)(2,1)S(1)}, bf16[64,2048]{1,0:T(8,128)(2,1)S(1)}, u32[]{:S(2)}, u32[]{:S(2)}) collective-permute-start(bf16[64,2048]{1,0:T(8,128)(2,1)S(1)} %collective-permute-done.10.refs_5_), channel_id=1, source_target_pairs={{8,0},{9,1},{10,2},{11,3},{12,4},{13,5},{14,6},{15,7}} | collective-permute-start | bytes 786440 | tf_op jit(solution)/shard_map/ppermute | solution.py:563
  45.3 12.0 %copy-start.8 = (bf16[64,2048]{1,0:T(8,128)(2,1)}, bf16[64,2048]{1,0:T(8,128)(2,1)S(1)}, u32[]{:S(2)}) copy-start(bf16[64,2048]{1,0:T(8,128)(2,1)S(1)} %collective-permute-done.7.refs_2_) | copy-start | bytes 786436
  45.3 11.9 %collective-permute-start.8 = (bf16[64,2048]{1,0:T(8,128)(2,1)S(1)}, bf16[64,2048]{1,0:T(8,128)(2,1)S(1)}, u32[]{:S(2)}, u32[]{:S(2)}) collective-permute-start(bf16[64,2048]{1,0:T(8,128)(2,1)S(1)} %collective-permute-done.7.refs_2_), channel_id=1, source_target_pairs={{16,24},{17,25},{18,26},{19,27},{20,28},{21,29},{22,30},{23,31}} | collective-permute-start | bytes 786440 | tf_op jit(solution)/shard_map/ppermute | solution.py:558
  46.0 20.8 %copy-start.14 = (bf16[64,2048]{1,0:T(8,128)(2,1)}, bf16[64,2048]{1,0:T(8,128)(2,1)S(1)}, u32[]{:S(2)}) copy-start(bf16[64,2048]{1,0:T(8,128)(2,1)S(1)} %collective-permute-done.1.refs_2_) | copy-start | bytes 786436
  46.1 20.8 %collective-permute-start.2 = (bf16[64,2048]{1,0:T(8,128)(2,1)S(1)}, bf16[64,2048]{1,0:T(8,128)(2,1)S(1)}, u32[]{:S(2)}, u32[]{:S(2)}) collective-permute-start(bf16[64,2048]{1,0:T(8,128)(2,1)S(1)} %collective-permute-done.1.refs_2_), channel_id=1, source_target_pairs={{16,24},{17,25},{18,26},{19,27},{20,28},{21,29},{22,30},{23,31}} | collective-permute-start | bytes 786440 | tf_op jit(solution)/shard_map/ppermute | solution.py:558
  51.9 15.0 %copy-start.15 = (bf16[64,2048]{1,0:T(8,128)(2,1)}, bf16[64,2048]{1,0:T(8,128)(2,1)S(1)}, u32[]{:S(2)}) copy-start(bf16[64,2048]{1,0:T(8,128)(2,1)S(1)} %collective-permute-done.4.refs_5_) | copy-start | bytes 786436
  51.9 14.9 %collective-permute-start.5 = (bf16[64,2048]{1,0:T(8,128)(2,1)S(1)}, bf16[64,2048]{1,0:T(8,128)(2,1)S(1)}, u32[]{:S(2)}, u32[]{:S(2)}) collective-permute-start(bf16[64,2048]{1,0:T(8,128)(2,1)S(1)} %collective-permute-done.4.refs_5_), channel_id=1, source_target_pairs={{8,0},{9,1},{10,2},{11,3},{12,4},{13,5},{14,6},{15,7}} | collective-permute-start | bytes 786440 | tf_op jit(solution)/shard_map/ppermute | solution.py:563
  57.3 0.7 copy-start.9
  57.3 0.8 copy-start.10
  64.1 28.9 %all-to-all-start.1 = ((bf16[32,8,2048]{2,1,0:T(8,128)(2,1)}), bf16[32,8,2048]{2,1,0:T(8,128)(2,1)S(1)}, u32[]{:S(2)}, u32[]{:S(2)}) async-start(bf16[32,8,2048]{2,1,0:T(8,128)(2,1)} %bitcast.24), calls=%async_computation.1 | async-start | bytes 2097152 | tf_op jit(solution)/shard_map/all_to_all | solution.py:596
  66.8 0.7 copy-start.16
  66.8 0.8 copy-start.17
  93.0 31.2 %all-to-all-start.2 = ((bf16[32,8,2176]{2,1,0:T(8,128)(2,1)}), bf16[32,8,2176]{2,1,0:T(8,128)(2,1)S(1)}, u32[]{:S(2)}, u32[]{:S(2)}) async-start(bf16[32,8,2176]{2,1,0:T(8,128)(2,1)} %bitcast.23), calls=%async_computation.2 | async-start | bytes 2228224 | tf_op jit(solution)/shard_map/all_to_all | solution.py:596

commit v14 on v13

--- a/solution.py
+++ b/solution.py
@@ -563,10 +563,12 @@
     return lax.ppermute(block, "seq", [(s, s - 1) for s in range(first, last)])
 
 
-def line_gather(block, n):
+def line_gather(block, n, hold=()):
     ups, downs = [], []
     up = down = block
     for j in range(1, n):
+        if hold and j == n - 1:
+            up, down = lax.optimization_barrier((up, down, *hold))[:2]
         up = up_line(up, n, j - 1)
         down = down_line(down, n, 1, n - j + 1)
         ups.append(up)
@@ -598,7 +600,9 @@
     sent, hot = choose_rows(tokens, cotangent, chosen, counts, pack)
     sent = sent.reshape(experts, 2, -1, sent.shape[1])
     here = lax.all_to_all(sent, "exp", split_axis=0, concat_axis=0, tiled=True)
-    x_in, c_in = (line_gather(here[:, n].reshape(-1, here.shape[3]), seq_n) for n in range(2))
+    x_rows, c_rows = (here[:, n].reshape(-1, here.shape[3]) for n in range(2))
+    x_in = line_gather(x_rows, seq_n)
+    c_in = line_gather(c_rows, seq_n, (x_in.blocks[seq_n - 1], x_in.blocks[-1]))
     router_t = router.T
 
     x, out, pre, hidden = expert_forward(

time: 129 us -> 129 us (level)
    ppermute x6, waiting for transfers between devices: 3.44 us -> 0.02 us  [up_line(): return lax.ppermute(block, 'seq', [(s, s + 1) for s in range(first, last)])]
    ppermute x6, waiting for transfers between devices: 15.4 us -> 18.3 us  [down_line(): return lax.ppermute(block, 'seq', [(s, s - 1) for s in range(first, last)])]
  transfers between devices with their start and end apart: 14 -> 14, of which waited for: 8 -> 7; matrix products, arithmetic and copies ran while one was open for 0% -> 0% of each run, Pallas kernels for 26% -> 26%
where the time goes in v14:
time: 129 us; the launch traced here: 128 us
  waiting for transfers between devices  43.5 us (34%)
  Pallas kernels  41.4 us (32%)
  starting transfers between devices  26 us (20%)
  blocking collectives  14.9 us (12%)
    all_to_all x2, waiting for transfers between devices, to_owners(): lax.all_to_all(parts, BOTH, split_axis=0, concat_axis=0, tiled=True)  25.2 us
    ppermute x6, waiting for transfers between devices, down_line(): return lax.ppermute(block, 'seq', [(s, s - 1) for s in range(first, last)])  18.3 us
    all_to_all x1, blocking collectives, on_device(): here = lax.all_to_all(sent, 'exp', split_axis=0, concat_axis=0, tiled=True)  14.9 us
    pallas_call x1, Pallas kernels, expert_backward(): pl.pallas_call(body, in_specs=[ANYWHERE] * (n_blocks + 5) + [IN_VMEM] * 2...  12.5 us
    ppermute x6, starting transfers between devices, up_line(): return lax.ppermute(block, 'seq', [(s, s + 1) for s in range(first, last)])  10.8 us
    ppermute x6, starting transfers between devices, down_line(): return lax.ppermute(block, 'seq', [(s, s - 1) for s in range(first, last)])  7.72 us
    all_to_all x2, starting transfers between devices, to_owners(): lax.all_to_all(parts, BOTH, split_axis=0, concat_axis=0, tiled=True)  7.57 us
    pallas_call x1, Pallas kernels, side_grads(): pl.pallas_call(body, grid=(STEPS,), in_specs=[pl.BlockSpec((rows, width),...  6.84 us
  transfers between devices with their start and end apart: 14, of which 7 were waited for; matrix products, arithmetic and copies ran while one was open for 0% of the time, Pallas kernels for 26%

profile of v14, /device:TPU:0, one launch (start us, length us, event | category | flops | bytes accessed | tf_op | source)
XLA Modules:
  0.0 127.9 jit_solution(4935489581967589060)
XLA Ops:
  0.6 0.0 copy-start
  0.7 4.1 %shard_map.153 = (bf16[128,2048]{1,0:T(8,128)(2,1)}, bf16[2,64,256]{2,1,0:T(8,128)(2,1)}) custom-call(s32[4,8]{1,0:T(4,128)} %bitcast.26, s32[1,8]{1,0:T(1,128)} %counts_ref.1, bf16[256,4096]{1,0:T(8,128)(2,1)} %c_ref.1, bf16[256,4096]{1,0:T(8,128)(2,1)} %x_ref.1), custom_call_target="tpu_custom_call" | custom-call | flops 536870912 | bytes 4194304 | tf_op jit(solution)/shard_map/pallas_call | solution.py:103
  4.8 14.9 %all_to_all.15 = bf16[8,2,8,2048]{3,2,1,0:T(8,128)(2,1)S(1)} all-to-all(bf16[8,2,8,2048]{3,2,1,0:T(8,128)(2,1)} %bitcast.25), channel_id=1, replica_groups=mesh['seq'=4,'exp'=8] {'exp'}, dimensions={0} | all-to-all | bytes 1048576 | tf_op jit(solution)/shard_map/all_to_all | solution.py:602
  19.8 0.0 copy-start.4
  19.8 0.0 copy-start.11
  19.8 3.5 %collective-permute-start.4 = (bf16[64,2048]{1,0:T(8,128)(2,1)S(1)}, bf16[64,2048]{1,0:T(8,128)(2,1)S(1)}, u32[]{:S(2)}, u32[]{:S(2)}) collective-permute-start(bf16[64,2048]{1,0:T(8,128)(2,1)S(1)} %get-tuple-element.43.refs_0_), channel_id=1, source_target_pairs={{0,8},{8,16},{16,24},{1,9},{9,17},{17,25},{2,10},{10,18},{18,26},{... | collective-permute-start | bytes 786440 | tf_op jit(solution)/shard_map/ppermute | solution.py:558
  23.3 1.3 %collective-permute-start.7 = (bf16[64,2048]{1,0:T(8,128)(2,1)S(1)}, bf16[64,2048]{1,0:T(8,128)(2,1)S(1)}, u32[]{:S(2)}, u32[]{:S(2)}) collective-permute-start(bf16[64,2048]{1,0:T(8,128)(2,1)S(1)} %get-tuple-element.43.refs_0_), channel_id=1, source_target_pairs={{8,0},{16,8},{24,16},{9,1},{17,9},{25,17},{10,2},{18,10},{26,18},{... | collective-permute-start | bytes 786440 | tf_op jit(solution)/shard_map/ppermute | solution.py:563
  24.6 4.6 %collective-permute-start = (bf16[64,2048]{1,0:T(8,128)(2,1)S(1)}, bf16[64,2048]{1,0:T(8,128)(2,1)S(1)}, u32[]{:S(2)}, u32[]{:S(2)}) collective-permute-start(bf16[64,2048]{1,0:T(8,128)(2,1)S(1)} %get-tuple-element.44.refs_0_), channel_id=1, source_target_pairs={{0,8},{8,16},{16,24},{1,9},{9,17},{17,25},{2,10},{10,18},{18,26},{... | collective-permute-start | bytes 786440 | tf_op jit(solution)/shard_map/ppermute | solution.py:558
  29.2 1.3 %collective-permute-start.2 = (bf16[64,2048]{1,0:T(8,128)(2,1)S(1)}, bf16[64,2048]{1,0:T(8,128)(2,1)S(1)}, u32[]{:S(2)}, u32[]{:S(2)}) collective-permute-start(bf16[64,2048]{1,0:T(8,128)(2,1)S(1)} %get-tuple-element.44.refs_0_), channel_id=1, source_target_pairs={{8,0},{16,8},{24,16},{9,1},{17,9},{25,17},{10,2},{18,10},{26,18},{... | collective-permute-start | bytes 786440 | tf_op jit(solution)/shard_map/ppermute | solution.py:563
  30.5 0.0 collective-permute-done.4.refs_1_
  30.5 0.0 copy-start.5
  30.5 0.7 collective-permute-start.5
  31.2 1.4 %collective-permute-done.7.refs_4_ = bf16[64,2048]{1,0:T(8,128)(2,1)S(1)} collective-permute-done((bf16[64,2048]{1,0:T(8,128)(2,1)S(1)}, bf16[64,2048]{1,0:T(8,128)(2,1)S(1)}, u32[]{:S(2)}, u32[]{:S(2)}) %collective-permute-start.7) | collective-permute-done | bytes 262176 | tf_op jit(solution)/shard_map/ppermute | solution.py:563
  32.5 1.3 %collective-permute-start.8 = (bf16[64,2048]{1,0:T(8,128)(2,1)S(1)}, bf16[64,2048]{1,0:T(8,128)(2,1)S(1)}, u32[]{:S(2)}, u32[]{:S(2)}) collective-permute-start(bf16[64,2048]{1,0:T(8,128)(2,1)S(1)} %collective-permute-done.7.refs_4_), channel_id=1, source_target_pairs={{8,0},{16,8},{9,1},{17,9},{10,2},{18,10},{11,3},{19,11},{12,4},{20... | collective-permute-start | bytes 786440 | tf_op jit(solution)/shard_map/ppermute | solution.py:563
  33.8 0.0 collective-permute-done.refs_1_
  33.8 0.7 collective-permute-start.1
  34.5 4.1 %collective-permute-done.2.refs_4_ = bf16[64,2048]{1,0:T(8,128)(2,1)S(1)} collective-permute-done((bf16[64,2048]{1,0:T(8,128)(2,1)S(1)}, bf16[64,2048]{1,0:T(8,128)(2,1)S(1)}, u32[]{:S(2)}, u32[]{:S(2)}) %collective-permute-start.2) | collective-permute-done | bytes 262176 | tf_op jit(solution)/shard_map/ppermute | solution.py:563
  38.6 1.3 %collective-permute-start.3 = (bf16[64,2048]{1,0:T(8,128)(2,1)S(1)}, bf16[64,2048]{1,0:T(8,128)(2,1)S(1)}, u32[]{:S(2)}, u32[]{:S(2)}) collective-permute-start(bf16[64,2048]{1,0:T(8,128)(2,1)S(1)} %collective-permute-done.2.refs_4_), channel_id=1, source_target_pairs={{8,0},{16,8},{9,1},{17,9},{10,2},{18,10},{11,3},{19,11},{12,4},{20... | collective-permute-start | bytes 786440 | tf_op jit(solution)/shard_map/ppermute | solution.py:563
  39.9 0.0 collective-permute-done.5.refs_2_
  39.9 0.7 collective-permute-start.6
  40.6 3.9 %collective-permute-done.8.refs_5_ = bf16[64,2048]{1,0:T(8,128)(2,1)S(1)} collective-permute-done((bf16[64,2048]{1,0:T(8,128)(2,1)S(1)}, bf16[64,2048]{1,0:T(8,128)(2,1)S(1)}, u32[]{:S(2)}, u32[]{:S(2)}) %collective-permute-start.8) | collective-permute-done | bytes 262176 | tf_op jit(solution)/shard_map/ppermute | solution.py:563
  44.5 1.3 %collective-permute-start.9 = (bf16[64,2048]{1,0:T(8,128)(2,1)S(1)}, bf16[64,2048]{1,0:T(8,128)(2,1)S(1)}, u32[]{:S(2)}, u32[]{:S(2)}) collective-permute-start(bf16[64,2048]{1,0:T(8,128)(2,1)S(1)} %collective-permute-done.8.refs_5_), channel_id=1, source_target_pairs={{8,0},{9,1},{10,2},{11,3},{12,4},{13,5},{14,6},{15,7}} | collective-permute-start | bytes 786440 | tf_op jit(solution)/shard_map/ppermute | solution.py:563
  45.8 0.0 collective-permute-done.1.refs_2_
  45.8 5.9 %collective-permute-done.3.refs_5_ = bf16[64,2048]{1,0:T(8,128)(2,1)S(1)} collective-permute-done((bf16[64,2048]{1,0:T(8,128)(2,1)S(1)}, bf16[64,2048]{1,0:T(8,128)(2,1)S(1)}, u32[]{:S(2)}, u32[]{:S(2)}) %collective-permute-start.3) | collective-permute-done | bytes 262176 | tf_op jit(solution)/shard_map/ppermute | solution.py:563
  51.7 0.0 collective-permute-done.6.refs_3_
  51.7 3.1 %collective-permute-done.9.refs_6_ = bf16[64,2048]{1,0:T(8,128)(2,1)S(1)} collective-permute-done((bf16[64,2048]{1,0:T(8,128)(2,1)S(1)}, bf16[64,2048]{1,0:T(8,128)(2,1)S(1)}, u32[]{:S(2)}, u32[]{:S(2)}) %collective-permute-start.9) | collective-permute-done | bytes 262176 | tf_op jit(solution)/shard_map/ppermute | solution.py:563
  54.8 0.7 collective-permute-start.10
  55.4 1.3 %collective-permute-start.11 = (bf16[64,2048]{1,0:T(8,128)(2,1)S(1)}, bf16[64,2048]{1,0:T(8,128)(2,1)S(1)}, u32[]{:S(2)}, u32[]{:S(2)}) collective-permute-start(bf16[64,2048]{1,0:T(8,128)(2,1)S(1)} %collective-permute-done.3.refs_5_), channel_id=1, source_target_pairs={{8,0},{9,1},{10,2},{11,3},{12,4},{13,5},{14,6},{15,7}} | collective-permute-start | bytes 786440 | tf_op jit(solution)/shard_map/ppermute | solution.py:563
  56.7 0.0 copy-done.4
  56.8 0.0 copy-done.5
  56.8 0.0 copy-done.6
  56.8 0.0 copy-done.7
  56.8 0.0 copy-done.8
  56.8 0.0 copy-done.9
  56.9 6.0 %shard_map.154 = (bf16[256,2048]{1,0:T(8,128)(2,1)}, bf16[4,64,2048]{2,1,0:T(8,128)(2,1)}, f32[256,896]{1,0:T(8,128)}, bf16[256,768]{1,0:T(8,128)(2,1)}) custom-call(bf16[64,2048]{1,0:T(8,128)(2,1)} %copy-done.4, bf16[64,2048]{1,0:T(8,128)(2,1)} %copy-done.5, bf16[64,2048]{1,0:T(8,128)(2,1)} %copy-done.7, bf16[64,2048]{1,0:T(8,128)(2,1)} %copy-done.9, ...), custom_call_target="tpu_custom_call" | custom-call | flops 2415919104 | bytes 18874368 | tf_op jit(solution)/shard_map/pallas_call | solution.py:334
  62.9 3.8 %all-to-all-start.1 = ((bf16[32,8,2048]{2,1,0:T(8,128)(2,1)}), bf16[32,8,2048]{2,1,0:T(8,128)(2,1)S(1)}, u32[]{:S(2)}, u32[]{:S(2)}) async-start(bf16[32,8,2048]{2,1,0:T(8,128)(2,1)} %bitcast.24), calls=%async_computation.1 | async-start | bytes 2097152 | tf_op jit(solution)/shard_map/all_to_all | solution.py:598
  66.7 0.0 collective-permute-done.10.refs_3_
  66.7 0.0 collective-permute-done.11.refs_6_
  66.8 0.6 copy-done.16
  67.4 0.1 copy-done.17
  67.5 12.5 %shard_map.155 = (bf16[256,2048]{1,0:T(8,128)(2,1)}, bf16[4,64,2176]{2,1,0:T(8,128)(2,1)}, bf16[256,1536]{1,0:T(8,128)(2,1)}) custom-call(bf16[64,2048]{1,0:T(8,128)(2,1)} %copy-done.11, bf16[64,2048]{1,0:T(8,128)(2,1)} %copy-done.12, bf16[64,2048]{1,0:T(8,128)(2,1)} %copy-done.14, bf16[64,2048]{1,0:T(8,128)(2,1)} %copy-done.16, ...), custom_call_target="tpu_custom_call" | custom-call | flops 40265318400 | bytes 157286400 | tf_op jit(solution)/shard_map/pallas_call | solution.py:480
  80.0 12.9 %all-to-all-done.1 = bf16[32,8,2048]{2,1,0:T(8,128)(2,1)S(1)} async-done(((bf16[32,8,2048]{2,1,0:T(8,128)(2,1)}), bf16[32,8,2048]{2,1,0:T(8,128)(2,1)S(1)}, u32[]{:S(2)}, u32[]{:S(2)}) %all-to-all-start.1) | async-done | bytes 1048608 | tf_op jit(solution)/shard_map/all_to_all | solution.py:598
  92.9 3.8 %all-to-all-start.2 = ((bf16[32,8,2176]{2,1,0:T(8,128)(2,1)}), bf16[32,8,2176]{2,1,0:T(8,128)(2,1)S(1)}, u32[]{:S(2)}, u32[]{:S(2)}) async-start(bf16[32,8,2176]{2,1,0:T(8,128)(2,1)} %bitcast.23), calls=%async_computation.2 | async-start | bytes 2228224 | tf_op jit(solution)/shard_map/all_to_all | solution.py:598
  96.7 5.5 %shard_map.159 = f32[1,384,4096]{2,1,0:T(8,128)} custom-call(bf16[256,2048]{1,0:T(8,128)(2,1)} %get-tuple-element.41.c_ref, bf16[256,768]{1,0:T(8,128)(2,1)} %get-tuple-element.42.hidden_ref), custom_call_target="tpu_custom_call" | custom-call | flops 805306368 | bytes 6291456 | tf_op jit(solution)/shard_map/pallas_call | solution.py:542
  102.2 6.8 %shard_map.158 = (f32[2,2048,384]{2,1,0:T(8,128)}, f32[2,2048,384]{2,1,0:T(8,128)}) custom-call(bf16[256,2048]{1,0:T(8,128)(2,1)} %get-tuple-element.29.refs_10_.x_ref, bf16[256,1536]{1,0:T(8,128)(2,1)} %get-tuple-element.38.delta_ref), custom_call_target="tpu_custom_call" | custom-call | flops 1610612736 | bytes 12582912 | tf_op jit(solution)/shard_map/pallas_call | solution.py:520
  109.0 2.9 %shard_map.156 = bf16[256,4096]{1,0:T(8,128)(2,1)} custom-call(bf16[2,64,256]{2,1,0:T(8,128)(2,1)} %get-tuple-element.25.hot_ref, bf16[256,2048]{1,0:T(8,128)(2,1)S(1)} %bitcast.18), custom_call_target="tpu_custom_call" | custom-call | flops 536870912 | bytes 2097152 | tf_op jit(solution)/shard_map/pallas_call | solution.py:174
  111.9 12.2 %all-to-all-done.2 = bf16[32,8,2176]{2,1,0:T(8,128)(2,1)S(1)} async-done(((bf16[32,8,2176]{2,1,0:T(8,128)(2,1)}), bf16[32,8,2176]{2,1,0:T(8,128)(2,1)S(1)}, u32[]{:S(2)}, u32[]{:S(2)}) %all-to-all-start.2) | async-done | bytes 1114144 | tf_op jit(solution)/shard_map/all_to_all | solution.py:598
  124.2 3.5 %shard_map.157 = (bf16[256,4096]{1,0:T(8,128)(2,1)}, f32[8,128]{1,0:T(8,128)}, f32[1,8]{1,0:T(1,128)}) custom-call(bf16[2,64,256]{2,1,0:T(8,128)(2,1)} %get-tuple-element.25.hot_ref, bf16[256,2176]{1,0:T(8,128)(2,1)S(1)} %bitcast.19), custom_call_target="tpu_custom_call" | custom-call | flops 536870912 | bytes 2097152 | tf_op jit(solution)/shard_map/pallas_call | solution.py:174
  (25 shorter events, 0.1 us)
Async XLA Ops:
  0.6 56.2 %copy-start = (bf16[1,4096,384]{2,1,0:T(8,128)(2,1)S(1)}, bf16[1,4096,384]{2,1,0:T(8,128)(2,1)}, u32[]{:S(2)}) copy-start(bf16[1,4096,384]{2,1,0:T(8,128)(2,1)} %refs_7_.3) | copy-start | bytes 9437188
  0.6 56.2 %copy-start.1 = (bf16[4096,8]{0,1:T(8,128)(2,1)S(1)}, bf16[4096,8]{0,1:T(8,128)(2,1)}, u32[]{:S(2)}) copy-start(bf16[4096,8]{0,1:T(8,128)(2,1)} %param.12) | copy-start | bytes 196612
  0.7 56.2 %copy-start.2 = (f32[1,384]{1,0:T(1,128)S(1)}, f32[1,384]{1,0:T(1,128)}, u32[]{:S(2)}) copy-start(f32[1,384]{1,0:T(1,128)} %refs_13_.1) | copy-start | bytes 4612
  0.7 56.2 %copy-start.3 = (f32[8]{0:T(128)S(1)}, f32[8]{0:T(128)}, u32[]{:S(2)}) copy-start(f32[8]{0:T(128)} %param.13) | copy-start | bytes 100
  19.8 37.0 %copy-start.4 = (bf16[64,2048]{1,0:T(8,128)(2,1)}, bf16[64,2048]{1,0:T(8,128)(2,1)S(1)}, u32[]{:S(2)}) copy-start(bf16[64,2048]{1,0:T(8,128)(2,1)S(1)} %get-tuple-element.43.refs_0_) | copy-start | bytes 786436
  19.8 46.9 %copy-start.11 = (bf16[64,2048]{1,0:T(8,128)(2,1)}, bf16[64,2048]{1,0:T(8,128)(2,1)S(1)}, u32[]{:S(2)}) copy-start(bf16[64,2048]{1,0:T(8,128)(2,1)S(1)} %get-tuple-element.44.refs_0_) | copy-start | bytes 786436
  19.8 10.7 %collective-permute-start.4 = (bf16[64,2048]{1,0:T(8,128)(2,1)S(1)}, bf16[64,2048]{1,0:T(8,128)(2,1)S(1)}, u32[]{:S(2)}, u32[]{:S(2)}) collective-permute-start(bf16[64,2048]{1,0:T(8,128)(2,1)S(1)} %get-tuple-element.43.refs_0_), channel_id=1, source_target_pairs={{0,8},{8,16},{16,24},{1,9},{9,17},{17,25},{2,10},{10,18},{18,26},{... | collective-permute-start | bytes 786440 | tf_op jit(solution)/shard_map/ppermute | solution.py:558
  23.3 9.2 %collective-permute-start.7 = (bf16[64,2048]{1,0:T(8,128)(2,1)S(1)}, bf16[64,2048]{1,0:T(8,128)(2,1)S(1)}, u32[]{:S(2)}, u32[]{:S(2)}) collective-permute-start(bf16[64,2048]{1,0:T(8,128)(2,1)S(1)} %get-tuple-element.43.refs_0_), channel_id=1, source_target_pairs={{8,0},{16,8},{24,16},{9,1},{17,9},{25,17},{10,2},{18,10},{26,18},{... | collective-permute-start | bytes 786440 | tf_op jit(solution)/shard_map/ppermute | solution.py:563
  24.6 9.2 %collective-permute-start = (bf16[64,2048]{1,0:T(8,128)(2,1)S(1)}, bf16[64,2048]{1,0:T(8,128)(2,1)S(1)}, u32[]{:S(2)}, u32[]{:S(2)}) collective-permute-start(bf16[64,2048]{1,0:T(8,128)(2,1)S(1)} %get-tuple-element.44.refs_0_), channel_id=1, source_target_pairs={{0,8},{8,16},{16,24},{1,9},{9,17},{17,25},{2,10},{10,18},{18,26},{... | collective-permute-start | bytes 786440 | tf_op jit(solution)/shard_map/ppermute | solution.py:558
  29.2 9.4 %collective-permute-start.2 = (bf16[64,2048]{1,0:T(8,128)(2,1)S(1)}, bf16[64,2048]{1,0:T(8,128)(2,1)S(1)}, u32[]{:S(2)}, u32[]{:S(2)}) collective-permute-start(bf16[64,2048]{1,0:T(8,128)(2,1)S(1)} %get-tuple-element.44.refs_0_), channel_id=1, source_target_pairs={{8,0},{16,8},{24,16},{9,1},{17,9},{25,17},{10,2},{18,10},{26,18},{... | collective-permute-start | bytes 786440 | tf_op jit(solution)/shard_map/ppermute | solution.py:563
  30.5 26.3 %copy-start.5 = (bf16[64,2048]{1,0:T(8,128)(2,1)}, bf16[64,2048]{1,0:T(8,128)(2,1)S(1)}, u32[]{:S(2)}) copy-start(bf16[64,2048]{1,0:T(8,128)(2,1)S(1)} %collective-permute-done.4.refs_1_) | copy-start | bytes 786436
  30.5 9.4 %collective-permute-start.5 = (bf16[64,2048]{1,0:T(8,128)(2,1)S(1)}, bf16[64,2048]{1,0:T(8,128)(2,1)S(1)}, u32[]{:S(2)}, u32[]{:S(2)}) collective-permute-start(bf16[64,2048]{1,0:T(8,128)(2,1)S(1)} %collective-permute-done.4.refs_1_), channel_id=1, source_target_pairs={{8,16},{16,24},{9,17},{17,25},{10,18},{18,26},{11,19},{19,27},{12,... | collective-permute-start | bytes 786440 | tf_op jit(solution)/shard_map/ppermute | solution.py:558
  32.5 24.2 %copy-start.6 = (bf16[64,2048]{1,0:T(8,128)(2,1)}, bf16[64,2048]{1,0:T(8,128)(2,1)S(1)}, u32[]{:S(2)}) copy-start(bf16[64,2048]{1,0:T(8,128)(2,1)S(1)} %collective-permute-done.7.refs_4_) | copy-start | bytes 786436
  32.5 11.9 %collective-permute-start.8 = (bf16[64,2048]{1,0:T(8,128)(2,1)S(1)}, bf16[64,2048]{1,0:T(8,128)(2,1)S(1)}, u32[]{:S(2)}, u32[]{:S(2)}) collective-permute-start(bf16[64,2048]{1,0:T(8,128)(2,1)S(1)} %collective-permute-done.7.refs_4_), channel_id=1, source_target_pairs={{8,0},{16,8},{9,1},{17,9},{10,2},{18,10},{11,3},{19,11},{12,4},{20... | collective-permute-start | bytes 786440 | tf_op jit(solution)/shard_map/ppermute | solution.py:563
  33.8 32.9 %copy-start.12 = (bf16[64,2048]{1,0:T(8,128)(2,1)}, bf16[64,2048]{1,0:T(8,128)(2,1)S(1)}, u32[]{:S(2)}) copy-start(bf16[64,2048]{1,0:T(8,128)(2,1)S(1)} %collective-permute-done.refs_1_) | copy-start | bytes 786436
  33.8 11.9 %collective-permute-start.1 = (bf16[64,2048]{1,0:T(8,128)(2,1)S(1)}, bf16[64,2048]{1,0:T(8,128)(2,1)S(1)}, u32[]{:S(2)}, u32[]{:S(2)}) collective-permute-start(bf16[64,2048]{1,0:T(8,128)(2,1)S(1)} %collective-permute-done.refs_1_), channel_id=1, source_target_pairs={{8,16},{16,24},{9,17},{17,25},{10,18},{18,26},{11,19},{19,27},{12,... | collective-permute-start | bytes 786440 | tf_op jit(solution)/shard_map/ppermute | solution.py:558
  38.6 28.1 %copy-start.13 = (bf16[64,2048]{1,0:T(8,128)(2,1)}, bf16[64,2048]{1,0:T(8,128)(2,1)S(1)}, u32[]{:S(2)}) copy-start(bf16[64,2048]{1,0:T(8,128)(2,1)S(1)} %collective-permute-done.2.refs_4_) | copy-start | bytes 786436
  38.6 13.1 %collective-permute-start.3 = (bf16[64,2048]{1,0:T(8,128)(2,1)S(1)}, bf16[64,2048]{1,0:T(8,128)(2,1)S(1)}, u32[]{:S(2)}, u32[]{:S(2)}) collective-permute-start(bf16[64,2048]{1,0:T(8,128)(2,1)S(1)} %collective-permute-done.2.refs_4_), channel_id=1, source_target_pairs={{8,0},{16,8},{9,1},{17,9},{10,2},{18,10},{11,3},{19,11},{12,4},{20... | collective-permute-start | bytes 786440 | tf_op jit(solution)/shard_map/ppermute | solution.py:563
  39.9 16.9 %copy-start.7 = (bf16[64,2048]{1,0:T(8,128)(2,1)}, bf16[64,2048]{1,0:T(8,128)(2,1)S(1)}, u32[]{:S(2)}) copy-start(bf16[64,2048]{1,0:T(8,128)(2,1)S(1)} %collective-permute-done.5.refs_2_) | copy-start | bytes 786436
  39.9 11.8 %collective-permute-start.6 = (bf16[64,2048]{1,0:T(8,128)(2,1)S(1)}, bf16[64,2048]{1,0:T(8,128)(2,1)S(1)}, u32[]{:S(2)}, u32[]{:S(2)}) collective-permute-start(bf16[64,2048]{1,0:T(8,128)(2,1)S(1)} %collective-permute-done.5.refs_2_), channel_id=1, source_target_pairs={{16,24},{17,25},{18,26},{19,27},{20,28},{21,29},{22,30},{23,31}} | collective-permute-start | bytes 786440 | tf_op jit(solution)/shard_map/ppermute | solution.py:558
  44.5 12.3 %copy-start.8 = (bf16[64,2048]{1,0:T(8,128)(2,1)}, bf16[64,2048]{1,0:T(8,128)(2,1)S(1)}, u32[]{:S(2)}) copy-start(bf16[64,2048]{1,0:T(8,128)(2,1)S(1)} %collective-permute-done.8.refs_5_) | copy-start | bytes 786436
  44.5 10.3 %collective-permute-start.9 = (bf16[64,2048]{1,0:T(8,128)(2,1)S(1)}, bf16[64,2048]{1,0:T(8,128)(2,1)S(1)}, u32[]{:S(2)}, u32[]{:S(2)}) collective-permute-start(bf16[64,2048]{1,0:T(8,128)(2,1)S(1)} %collective-permute-done.8.refs_5_), channel_id=1, source_target_pairs={{8,0},{9,1},{10,2},{11,3},{12,4},{13,5},{14,6},{15,7}} | collective-permute-start | bytes 786440 | tf_op jit(solution)/shard_map/ppermute | solution.py:563
  45.8 21.0 %copy-start.14 = (bf16[64,2048]{1,0:T(8,128)(2,1)}, bf16[64,2048]{1,0:T(8,128)(2,1)S(1)}, u32[]{:S(2)}) copy-start(bf16[64,2048]{1,0:T(8,128)(2,1)S(1)} %collective-permute-done.1.refs_2_) | copy-start | bytes 786436
  51.7 15.1 %copy-start.15 = (bf16[64,2048]{1,0:T(8,128)(2,1)}, bf16[64,2048]{1,0:T(8,128)(2,1)S(1)}, u32[]{:S(2)}) copy-start(bf16[64,2048]{1,0:T(8,128)(2,1)S(1)} %collective-permute-done.3.refs_5_) | copy-start | bytes 786436
  51.7 5.1 %copy-start.9 = (bf16[64,2048]{1,0:T(8,128)(2,1)}, bf16[64,2048]{1,0:T(8,128)(2,1)S(1)}, u32[]{:S(2)}) copy-start(bf16[64,2048]{1,0:T(8,128)(2,1)S(1)} %collective-permute-done.6.refs_3_) | copy-start | bytes 786436
  54.8 2.0 %copy-start.10 = (bf16[64,2048]{1,0:T(8,128)(2,1)}, bf16[64,2048]{1,0:T(8,128)(2,1)S(1)}, u32[]{:S(2)}) copy-start(bf16[64,2048]{1,0:T(8,128)(2,1)S(1)} %collective-permute-done.9.refs_6_) | copy-start | bytes 786436
  54.8 11.9 %collective-permute-start.10 = (bf16[64,2048]{1,0:T(8,128)(2,1)S(1)}, bf16[64,2048]{1,0:T(8,128)(2,1)S(1)}, u32[]{:S(2)}, u32[]{:S(2)}) collective-permute-start(bf16[64,2048]{1,0:T(8,128)(2,1)S(1)} %collective-permute-done.1.refs_2_), channel_id=1, source_target_pairs={{16,24},{17,25},{18,26},{19,27},{20,28},{21,29},{22,30},{23,31}} | collective-permute-start | bytes 786440 | tf_op jit(solution)/shard_map/ppermute | solution.py:558
  55.4 11.3 %collective-permute-start.11 = (bf16[64,2048]{1,0:T(8,128)(2,1)S(1)}, bf16[64,2048]{1,0:T(8,128)(2,1)S(1)}, u32[]{:S(2)}, u32[]{:S(2)}) collective-permute-start(bf16[64,2048]{1,0:T(8,128)(2,1)S(1)} %collective-permute-done.3.refs_5_), channel_id=1, source_target_pairs={{8,0},{9,1},{10,2},{11,3},{12,4},{13,5},{14,6},{15,7}} | collective-permute-start | bytes 786440 | tf_op jit(solution)/shard_map/ppermute | solution.py:563
  62.9 30.0 %all-to-all-start.1 = ((bf16[32,8,2048]{2,1,0:T(8,128)(2,1)}), bf16[32,8,2048]{2,1,0:T(8,128)(2,1)S(1)}, u32[]{:S(2)}, u32[]{:S(2)}) async-start(bf16[32,8,2048]{2,1,0:T(8,128)(2,1)} %bitcast.24), calls=%async_computation.1 | async-start | bytes 2097152 | tf_op jit(solution)/shard_map/all_to_all | solution.py:598
  66.7 0.7 copy-start.16
  66.7 0.8 copy-start.17
  92.9 31.3 %all-to-all-start.2 = ((bf16[32,8,2176]{2,1,0:T(8,128)(2,1)}), bf16[32,8,2176]{2,1,0:T(8,128)(2,1)S(1)}, u32[]{:S(2)}, u32[]{:S(2)}) async-start(bf16[32,8,2176]{2,1,0:T(8,128)(2,1)} %bitcast.23), calls=%async_computation.2 | async-start | bytes 2228224 | tf_op jit(solution)/shard_map/all_to_all | solution.py:598

commit v15 on v13

--- a/solution.py
+++ b/solution.py
@@ -455,6 +455,7 @@
         threshold_row = jnp.zeros((group, LANES), F32)
         for n, piece in enumerate(pieces):
             threshold_row = jnp.where(lane == n, piece, threshold_row)
+        rides = {}
         for owner in range(seq_n * exp_n):
             h, first = divmod(owner * per, part)
             shift = first % LANES
@@ -467,10 +468,11 @@
             d, place = divmod(owner, exp_n)
             for t in range(extra // LANES):
                 row = sub + t * group
-                now = slice(part + t * LANES, part + (t + 1) * LANES)
-                out_v[d, place * group : (place + 1) * group, now] = jnp.where(
-                    row == 2 * here, value, jnp.where(row == 2 * here + 1, threshold_row, 0.0)
-                ).astype(BF16)
+                pieces = rides.setdefault((d, t), [])
+                pieces.append(jnp.where(row == 2 * here, value, jnp.where(row == 2 * here + 1, threshold_row, 0.0)))
+                if place == exp_n - 1:
+                    now = slice(part + t * LANES, part + (t + 1) * LANES)
+                    out_v[d, :, now] = jnp.concatenate(pieces).astype(BF16)
         now = pl.ds((STEPS - 1) * width, width + extra)
         leaving.append(pltpu.make_async_copy(out_v.at[:, :, now], out_ref.at[:, :, now], out_sems.at[STEPS - 1]))
         leaving[-1].start()

time: 129 us -> 129 us (level)
  no operation moved by 1% of the time
where the time goes in v15:
time: 129 us; the launch traced here: 128 us
  waiting for transfers between devices  44 us (34%)
  Pallas kernels  41.4 us (32%)
  starting transfers between devices  24.8 us (19%)
  blocking collectives  14.9 us (12%)
  local copies, waits for them, and re-layouts  1.57 us (1%)
    all_to_all x2, waiting for transfers between devices, to_owners(): lax.all_to_all(parts, BOTH, split_axis=0, concat_axis=0, tiled=True)  25.1 us
    ppermute x6, waiting for transfers between devices, down_line(): return lax.ppermute(block, 'seq', [(s, s - 1) for s in range(first, last)])  15.4 us
    all_to_all x1, blocking collectives, on_device(): here = lax.all_to_all(sent, 'exp', split_axis=0, concat_axis=0, tiled=True)  14.9 us
    pallas_call x1, Pallas kernels, expert_backward(): pl.pallas_call(body, in_specs=[ANYWHERE] * (n_blocks + 5) + [IN_VMEM] * 2...  12.5 us
    ppermute x6, starting transfers between devices, up_line(): return lax.ppermute(block, 'seq', [(s, s + 1) for s in range(first, last)])  10.7 us
    ppermute x6, starting transfers between devices, down_line(): return lax.ppermute(block, 'seq', [(s, s - 1) for s in range(first, last)])  7.72 us
    pallas_call x1, Pallas kernels, side_grads(): pl.pallas_call(body, grid=(STEPS,), in_specs=[pl.BlockSpec((rows, width),...  6.84 us
    pallas_call x2, Pallas kernels, scatter_rows(): pl.pallas_call(body, in_specs=[ANYWHERE] * 2, out_specs=out_specs, out_sh...  6.42 us
  transfers between devices with their start and end apart: 14, of which 8 were waited for; matrix products, arithmetic and copies ran while one was open for 0% of the time, Pallas kernels for 26%

profile of v15, /device:TPU:0, one launch (start us, length us, event | category | flops | bytes accessed | tf_op | source)
XLA Modules:
  0.0 127.9 jit_solution(8277620621865546720)
XLA Ops:
  0.6 0.0 copy-start
  0.7 4.1 %shard_map.153 = (bf16[128,2048]{1,0:T(8,128)(2,1)}, bf16[2,64,256]{2,1,0:T(8,128)(2,1)}) custom-call(s32[4,8]{1,0:T(4,128)} %bitcast.26, s32[1,8]{1,0:T(1,128)} %counts_ref.1, bf16[256,4096]{1,0:T(8,128)(2,1)} %c_ref.1, bf16[256,4096]{1,0:T(8,128)(2,1)} %x_ref.1), custom_call_target="tpu_custom_call" | custom-call | flops 536870912 | bytes 4194304 | tf_op jit(solution)/shard_map/pallas_call | solution.py:103
  4.8 14.9 %all_to_all.15 = bf16[8,2,8,2048]{3,2,1,0:T(8,128)(2,1)S(1)} all-to-all(bf16[8,2,8,2048]{3,2,1,0:T(8,128)(2,1)} %bitcast.25), channel_id=1, replica_groups=mesh['seq'=4,'exp'=8] {'exp'}, dimensions={0} | all-to-all | bytes 1048576 | tf_op jit(solution)/shard_map/all_to_all | solution.py:602
  19.8 0.0 copy-start.4
  19.8 0.0 copy-start.11
  19.8 1.3 %collective-permute-start.9 = (bf16[64,2048]{1,0:T(8,128)(2,1)S(1)}, bf16[64,2048]{1,0:T(8,128)(2,1)S(1)}, u32[]{:S(2)}, u32[]{:S(2)}) collective-permute-start(bf16[64,2048]{1,0:T(8,128)(2,1)S(1)} %get-tuple-element.39.refs_0_), channel_id=1, source_target_pairs={{8,0},{16,8},{24,16},{9,1},{17,9},{25,17},{10,2},{18,10},{26,18},{... | collective-permute-start | bytes 786440 | tf_op jit(solution)/shard_map/ppermute | solution.py:565
  21.1 4.6 %collective-permute-start.6 = (bf16[64,2048]{1,0:T(8,128)(2,1)S(1)}, bf16[64,2048]{1,0:T(8,128)(2,1)S(1)}, u32[]{:S(2)}, u32[]{:S(2)}) collective-permute-start(bf16[64,2048]{1,0:T(8,128)(2,1)S(1)} %get-tuple-element.39.refs_0_), channel_id=1, source_target_pairs={{0,8},{8,16},{16,24},{1,9},{9,17},{17,25},{2,10},{10,18},{18,26},{... | collective-permute-start | bytes 786440 | tf_op jit(solution)/shard_map/ppermute | solution.py:560
  25.7 3.5 %collective-permute-start = (bf16[64,2048]{1,0:T(8,128)(2,1)S(1)}, bf16[64,2048]{1,0:T(8,128)(2,1)S(1)}, u32[]{:S(2)}, u32[]{:S(2)}) collective-permute-start(bf16[64,2048]{1,0:T(8,128)(2,1)S(1)} %get-tuple-element.40.refs_0_), channel_id=1, source_target_pairs={{0,8},{8,16},{16,24},{1,9},{9,17},{17,25},{2,10},{10,18},{18,26},{... | collective-permute-start | bytes 786440 | tf_op jit(solution)/shard_map/ppermute | solution.py:560
  29.1 1.3 %collective-permute-start.3 = (bf16[64,2048]{1,0:T(8,128)(2,1)S(1)}, bf16[64,2048]{1,0:T(8,128)(2,1)S(1)}, u32[]{:S(2)}, u32[]{:S(2)}) collective-permute-start(bf16[64,2048]{1,0:T(8,128)(2,1)S(1)} %get-tuple-element.40.refs_0_), channel_id=1, source_target_pairs={{8,0},{16,8},{24,16},{9,1},{17,9},{25,17},{10,2},{18,10},{26,18},{... | collective-permute-start | bytes 786440 | tf_op jit(solution)/shard_map/ppermute | solution.py:565
  30.4 0.0 collective-permute-done.9.refs_4_
  30.5 1.3 %collective-permute-start.10 = (bf16[64,2048]{1,0:T(8,128)(2,1)S(1)}, bf16[64,2048]{1,0:T(8,128)(2,1)S(1)}, u32[]{:S(2)}, u32[]{:S(2)}) collective-permute-start(bf16[64,2048]{1,0:T(8,128)(2,1)S(1)} %collective-permute-done.9.refs_4_), channel_id=1, source_target_pairs={{8,0},{16,8},{9,1},{17,9},{10,2},{18,10},{11,3},{19,11},{12,4},{20... | collective-permute-start | bytes 786440 | tf_op jit(solution)/shard_map/ppermute | solution.py:565
  31.8 0.6 collective-permute-done.6.refs_1_
  32.4 0.7 collective-permute-start.7
  33.1 2.8 %collective-permute-done.refs_1_ = bf16[64,2048]{1,0:T(8,128)(2,1)S(1)} collective-permute-done((bf16[64,2048]{1,0:T(8,128)(2,1)S(1)}, bf16[64,2048]{1,0:T(8,128)(2,1)S(1)}, u32[]{:S(2)}, u32[]{:S(2)}) %collective-permute-start) | collective-permute-done | bytes 262176 | tf_op jit(solution)/shard_map/ppermute | solution.py:560
  35.9 0.7 collective-permute-start.1
  36.5 3.7 %collective-permute-done.3.refs_4_ = bf16[64,2048]{1,0:T(8,128)(2,1)S(1)} collective-permute-done((bf16[64,2048]{1,0:T(8,128)(2,1)S(1)}, bf16[64,2048]{1,0:T(8,128)(2,1)S(1)}, u32[]{:S(2)}, u32[]{:S(2)}) %collective-permute-start.3) | collective-permute-done | bytes 262176 | tf_op jit(solution)/shard_map/ppermute | solution.py:565
  40.3 1.3 %collective-permute-start.4 = (bf16[64,2048]{1,0:T(8,128)(2,1)S(1)}, bf16[64,2048]{1,0:T(8,128)(2,1)S(1)}, u32[]{:S(2)}, u32[]{:S(2)}) collective-permute-start(bf16[64,2048]{1,0:T(8,128)(2,1)S(1)} %collective-permute-done.3.refs_4_), channel_id=1, source_target_pairs={{8,0},{16,8},{9,1},{17,9},{10,2},{18,10},{11,3},{19,11},{12,4},{20... | collective-permute-start | bytes 786440 | tf_op jit(solution)/shard_map/ppermute | solution.py:565
  41.6 2.5 %collective-permute-done.10.refs_5_ = bf16[64,2048]{1,0:T(8,128)(2,1)S(1)} collective-permute-done((bf16[64,2048]{1,0:T(8,128)(2,1)S(1)}, bf16[64,2048]{1,0:T(8,128)(2,1)S(1)}, u32[]{:S(2)}, u32[]{:S(2)}) %collective-permute-start.10) | collective-permute-done | bytes 262176 | tf_op jit(solution)/shard_map/ppermute | solution.py:565
  44.0 1.3 %collective-permute-start.11 = (bf16[64,2048]{1,0:T(8,128)(2,1)S(1)}, bf16[64,2048]{1,0:T(8,128)(2,1)S(1)}, u32[]{:S(2)}, u32[]{:S(2)}) collective-permute-start(bf16[64,2048]{1,0:T(8,128)(2,1)S(1)} %collective-permute-done.10.refs_5_), channel_id=1, source_target_pairs={{8,0},{9,1},{10,2},{11,3},{12,4},{13,5},{14,6},{15,7}} | collective-permute-start | bytes 786440 | tf_op jit(solution)/shard_map/ppermute | solution.py:565
  45.3 0.0 collective-permute-done.7.refs_2_
  45.3 0.7 collective-permute-start.8
  46.0 0.0 collective-permute-done.1.refs_2_
  46.1 0.7 collective-permute-start.2
  46.7 5.2 %collective-permute-done.4.refs_5_ = bf16[64,2048]{1,0:T(8,128)(2,1)S(1)} collective-permute-done((bf16[64,2048]{1,0:T(8,128)(2,1)S(1)}, bf16[64,2048]{1,0:T(8,128)(2,1)S(1)}, u32[]{:S(2)}, u32[]{:S(2)}) %collective-permute-start.4) | collective-permute-done | bytes 262176 | tf_op jit(solution)/shard_map/ppermute | solution.py:565
  51.9 1.3 %collective-permute-start.5 = (bf16[64,2048]{1,0:T(8,128)(2,1)S(1)}, bf16[64,2048]{1,0:T(8,128)(2,1)S(1)}, u32[]{:S(2)}, u32[]{:S(2)}) collective-permute-start(bf16[64,2048]{1,0:T(8,128)(2,1)S(1)} %collective-permute-done.4.refs_5_), channel_id=1, source_target_pairs={{8,0},{9,1},{10,2},{11,3},{12,4},{13,5},{14,6},{15,7}} | collective-permute-start | bytes 786440 | tf_op jit(solution)/shard_map/ppermute | solution.py:565
  53.2 4.1 %collective-permute-done.11.refs_6_ = bf16[64,2048]{1,0:T(8,128)(2,1)S(1)} collective-permute-done((bf16[64,2048]{1,0:T(8,128)(2,1)S(1)}, bf16[64,2048]{1,0:T(8,128)(2,1)S(1)}, u32[]{:S(2)}, u32[]{:S(2)}) %collective-permute-start.11) | collective-permute-done | bytes 262176 | tf_op jit(solution)/shard_map/ppermute | solution.py:565
  57.3 0.0 collective-permute-done.8.refs_3_
  57.3 0.0 copy-done.5
  57.3 0.0 copy-done.6
  57.3 0.0 copy-done.7
  57.3 0.0 copy-done.8
  57.3 0.7 copy-done.9
  58.0 0.1 copy-done.10
  58.1 0.0 copy-done.1
  58.1 6.0 %shard_map.154 = (bf16[256,2048]{1,0:T(8,128)(2,1)}, bf16[4,64,2048]{2,1,0:T(8,128)(2,1)}, f32[256,896]{1,0:T(8,128)}, bf16[256,768]{1,0:T(8,128)(2,1)}) custom-call(bf16[64,2048]{1,0:T(8,128)(2,1)} %copy-done.4, bf16[64,2048]{1,0:T(8,128)(2,1)} %copy-done.6, bf16[64,2048]{1,0:T(8,128)(2,1)} %copy-done.8, bf16[64,2048]{1,0:T(8,128)(2,1)} %copy-done.10, ...), custom_call_target="tpu_custom_call" | custom-call | flops 2415919104 | bytes 18874368 | tf_op jit(solution)/shard_map/pallas_call | solution.py:334
  64.1 2.7 %all-to-all-start.1 = ((bf16[32,8,2048]{2,1,0:T(8,128)(2,1)}), bf16[32,8,2048]{2,1,0:T(8,128)(2,1)S(1)}, u32[]{:S(2)}, u32[]{:S(2)}) async-start(bf16[32,8,2048]{2,1,0:T(8,128)(2,1)} %bitcast.24), calls=%async_computation.1 | async-start | bytes 2097152 | tf_op jit(solution)/shard_map/all_to_all | solution.py:598
  66.8 0.0 collective-permute-done.2.refs_3_
  66.8 0.0 collective-permute-done.5.refs_6_
  66.9 0.6 copy-done.16
  67.5 0.1 copy-done.17
  67.6 12.5 %shard_map.155 = (bf16[256,2048]{1,0:T(8,128)(2,1)}, bf16[4,64,2176]{2,1,0:T(8,128)(2,1)}, bf16[256,1536]{1,0:T(8,128)(2,1)}) custom-call(bf16[64,2048]{1,0:T(8,128)(2,1)} %copy-done.11, bf16[64,2048]{1,0:T(8,128)(2,1)} %copy-done.12, bf16[64,2048]{1,0:T(8,128)(2,1)} %copy-done.14, bf16[64,2048]{1,0:T(8,128)(2,1)} %copy-done.16, ...), custom_call_target="tpu_custom_call" | custom-call | flops 40265318400 | bytes 157286400 | tf_op jit(solution)/shard_map/pallas_call | solution.py:482
  80.1 12.9 %all-to-all-done.1 = bf16[32,8,2048]{2,1,0:T(8,128)(2,1)S(1)} async-done(((bf16[32,8,2048]{2,1,0:T(8,128)(2,1)}), bf16[32,8,2048]{2,1,0:T(8,128)(2,1)S(1)}, u32[]{:S(2)}, u32[]{:S(2)}) %all-to-all-start.1) | async-done | bytes 1048608 | tf_op jit(solution)/shard_map/all_to_all | solution.py:598
  93.0 3.7 %all-to-all-start.2 = ((bf16[32,8,2176]{2,1,0:T(8,128)(2,1)}), bf16[32,8,2176]{2,1,0:T(8,128)(2,1)S(1)}, u32[]{:S(2)}, u32[]{:S(2)}) async-start(bf16[32,8,2176]{2,1,0:T(8,128)(2,1)} %bitcast.23), calls=%async_computation.2 | async-start | bytes 2228224 | tf_op jit(solution)/shard_map/all_to_all | solution.py:598
  96.8 5.5 %shard_map.159 = f32[1,384,4096]{2,1,0:T(8,128)} custom-call(bf16[256,2048]{1,0:T(8,128)(2,1)} %get-tuple-element.37.c_ref, bf16[256,768]{1,0:T(8,128)(2,1)} %get-tuple-element.38.hidden_ref), custom_call_target="tpu_custom_call" | custom-call | flops 805306368 | bytes 6291456 | tf_op jit(solution)/shard_map/pallas_call | solution.py:544
  102.2 6.8 %shard_map.158 = (f32[2,2048,384]{2,1,0:T(8,128)}, f32[2,2048,384]{2,1,0:T(8,128)}) custom-call(bf16[256,2048]{1,0:T(8,128)(2,1)} %get-tuple-element.25.refs_10_.x_ref, bf16[256,1536]{1,0:T(8,128)(2,1)} %get-tuple-element.34.delta_ref), custom_call_target="tpu_custom_call" | custom-call | flops 1610612736 | bytes 12582912 | tf_op jit(solution)/shard_map/pallas_call | solution.py:522
  109.1 2.9 %shard_map.156 = bf16[256,4096]{1,0:T(8,128)(2,1)} custom-call(bf16[2,64,256]{2,1,0:T(8,128)(2,1)} %get-tuple-element.23.hot_ref, bf16[256,2048]{1,0:T(8,128)(2,1)S(1)} %bitcast.18), custom_call_target="tpu_custom_call" | custom-call | flops 536870912 | bytes 2097152 | tf_op jit(solution)/shard_map/pallas_call | solution.py:174
  112.0 12.2 %all-to-all-done.2 = bf16[32,8,2176]{2,1,0:T(8,128)(2,1)S(1)} async-done(((bf16[32,8,2176]{2,1,0:T(8,128)(2,1)}), bf16[32,8,2176]{2,1,0:T(8,128)(2,1)S(1)}, u32[]{:S(2)}, u32[]{:S(2)}) %all-to-all-start.2) | async-done | bytes 1114144 | tf_op jit(solution)/shard_map/all_to_all | solution.py:598
  124.2 3.5 %shard_map.157 = (bf16[256,4096]{1,0:T(8,128)(2,1)}, f32[8,128]{1,0:T(8,128)}, f32[1,8]{1,0:T(1,128)}) custom-call(bf16[2,64,256]{2,1,0:T(8,128)(2,1)} %get-tuple-element.23.hot_ref, bf16[256,2176]{1,0:T(8,128)(2,1)S(1)} %bitcast.19), custom_call_target="tpu_custom_call" | custom-call | flops 536870912 | bytes 2097152 | tf_op jit(solution)/shard_map/pallas_call | solution.py:174
  (25 shorter events, 0.1 us)
Async XLA Ops:
  0.6 57.4 %copy-start = (bf16[1,4096,384]{2,1,0:T(8,128)(2,1)S(1)}, bf16[1,4096,384]{2,1,0:T(8,128)(2,1)}, u32[]{:S(2)}) copy-start(bf16[1,4096,384]{2,1,0:T(8,128)(2,1)} %refs_7_.3) | copy-start | bytes 9437188
  0.6 57.4 %copy-start.1 = (bf16[4096,8]{0,1:T(8,128)(2,1)S(1)}, bf16[4096,8]{0,1:T(8,128)(2,1)}, u32[]{:S(2)}) copy-start(bf16[4096,8]{0,1:T(8,128)(2,1)} %param.12) | copy-start | bytes 196612
  0.7 57.4 %copy-start.2 = (f32[1,384]{1,0:T(1,128)S(1)}, f32[1,384]{1,0:T(1,128)}, u32[]{:S(2)}) copy-start(f32[1,384]{1,0:T(1,128)} %refs_13_.1) | copy-start | bytes 4612
  0.7 57.4 %copy-start.3 = (f32[8]{0:T(128)S(1)}, f32[8]{0:T(128)}, u32[]{:S(2)}) copy-start(f32[8]{0:T(128)} %param.13) | copy-start | bytes 100
  19.8 37.5 %copy-start.4 = (bf16[64,2048]{1,0:T(8,128)(2,1)}, bf16[64,2048]{1,0:T(8,128)(2,1)S(1)}, u32[]{:S(2)}) copy-start(bf16[64,2048]{1,0:T(8,128)(2,1)S(1)} %get-tuple-element.39.refs_0_) | copy-start | bytes 786436
  19.8 47.1 %copy-start.11 = (bf16[64,2048]{1,0:T(8,128)(2,1)}, bf16[64,2048]{1,0:T(8,128)(2,1)S(1)}, u32[]{:S(2)}) copy-start(bf16[64,2048]{1,0:T(8,128)(2,1)S(1)} %get-tuple-element.40.refs_0_) | copy-start | bytes 786436
  19.8 10.7 %collective-permute-start.9 = (bf16[64,2048]{1,0:T(8,128)(2,1)S(1)}, bf16[64,2048]{1,0:T(8,128)(2,1)S(1)}, u32[]{:S(2)}, u32[]{:S(2)}) collective-permute-start(bf16[64,2048]{1,0:T(8,128)(2,1)S(1)} %get-tuple-element.39.refs_0_), channel_id=1, source_target_pairs={{8,0},{16,8},{24,16},{9,1},{17,9},{25,17},{10,2},{18,10},{26,18},{... | collective-permute-start | bytes 786440 | tf_op jit(solution)/shard_map/ppermute | solution.py:565
  21.1 11.3 %collective-permute-start.6 = (bf16[64,2048]{1,0:T(8,128)(2,1)S(1)}, bf16[64,2048]{1,0:T(8,128)(2,1)S(1)}, u32[]{:S(2)}, u32[]{:S(2)}) collective-permute-start(bf16[64,2048]{1,0:T(8,128)(2,1)S(1)} %get-tuple-element.39.refs_0_), channel_id=1, source_target_pairs={{0,8},{8,16},{16,24},{1,9},{9,17},{17,25},{2,10},{10,18},{18,26},{... | collective-permute-start | bytes 786440 | tf_op jit(solution)/shard_map/ppermute | solution.py:560
  25.7 10.2 %collective-permute-start = (bf16[64,2048]{1,0:T(8,128)(2,1)S(1)}, bf16[64,2048]{1,0:T(8,128)(2,1)S(1)}, u32[]{:S(2)}, u32[]{:S(2)}) collective-permute-start(bf16[64,2048]{1,0:T(8,128)(2,1)S(1)} %get-tuple-element.40.refs_0_), channel_id=1, source_target_pairs={{0,8},{8,16},{16,24},{1,9},{9,17},{17,25},{2,10},{10,18},{18,26},{... | collective-permute-start | bytes 786440 | tf_op jit(solution)/shard_map/ppermute | solution.py:560
  29.1 11.1 %collective-permute-start.3 = (bf16[64,2048]{1,0:T(8,128)(2,1)S(1)}, bf16[64,2048]{1,0:T(8,128)(2,1)S(1)}, u32[]{:S(2)}, u32[]{:S(2)}) collective-permute-start(bf16[64,2048]{1,0:T(8,128)(2,1)S(1)} %get-tuple-element.40.refs_0_), channel_id=1, source_target_pairs={{8,0},{16,8},{24,16},{9,1},{17,9},{25,17},{10,2},{18,10},{26,18},{... | collective-permute-start | bytes 786440 | tf_op jit(solution)/shard_map/ppermute | solution.py:565
  30.5 26.8 %copy-start.5 = (bf16[64,2048]{1,0:T(8,128)(2,1)}, bf16[64,2048]{1,0:T(8,128)(2,1)S(1)}, u32[]{:S(2)}) copy-start(bf16[64,2048]{1,0:T(8,128)(2,1)S(1)} %collective-permute-done.9.refs_4_) | copy-start | bytes 786436
  30.5 13.6 %collective-permute-start.10 = (bf16[64,2048]{1,0:T(8,128)(2,1)S(1)}, bf16[64,2048]{1,0:T(8,128)(2,1)S(1)}, u32[]{:S(2)}, u32[]{:S(2)}) collective-permute-start(bf16[64,2048]{1,0:T(8,128)(2,1)S(1)} %collective-permute-done.9.refs_4_), channel_id=1, source_target_pairs={{8,0},{16,8},{9,1},{17,9},{10,2},{18,10},{11,3},{19,11},{12,4},{20... | collective-permute-start | bytes 786440 | tf_op jit(solution)/shard_map/ppermute | solution.py:565
  32.4 24.9 %copy-start.6 = (bf16[64,2048]{1,0:T(8,128)(2,1)}, bf16[64,2048]{1,0:T(8,128)(2,1)S(1)}, u32[]{:S(2)}) copy-start(bf16[64,2048]{1,0:T(8,128)(2,1)S(1)} %collective-permute-done.6.refs_1_) | copy-start | bytes 786436
  32.4 12.9 %collective-permute-start.7 = (bf16[64,2048]{1,0:T(8,128)(2,1)S(1)}, bf16[64,2048]{1,0:T(8,128)(2,1)S(1)}, u32[]{:S(2)}, u32[]{:S(2)}) collective-permute-start(bf16[64,2048]{1,0:T(8,128)(2,1)S(1)} %collective-permute-done.6.refs_1_), channel_id=1, source_target_pairs={{8,16},{16,24},{9,17},{17,25},{10,18},{18,26},{11,19},{19,27},{12,... | collective-permute-start | bytes 786440 | tf_op jit(solution)/shard_map/ppermute | solution.py:560
  35.9 31.0 %copy-start.12 = (bf16[64,2048]{1,0:T(8,128)(2,1)}, bf16[64,2048]{1,0:T(8,128)(2,1)S(1)}, u32[]{:S(2)}) copy-start(bf16[64,2048]{1,0:T(8,128)(2,1)S(1)} %collective-permute-done.refs_1_) | copy-start | bytes 786436
  35.9 10.2 %collective-permute-start.1 = (bf16[64,2048]{1,0:T(8,128)(2,1)S(1)}, bf16[64,2048]{1,0:T(8,128)(2,1)S(1)}, u32[]{:S(2)}, u32[]{:S(2)}) collective-permute-start(bf16[64,2048]{1,0:T(8,128)(2,1)S(1)} %collective-permute-done.refs_1_), channel_id=1, source_target_pairs={{8,16},{16,24},{9,17},{17,25},{10,18},{18,26},{11,19},{19,27},{12,... | collective-permute-start | bytes 786440 | tf_op jit(solution)/shard_map/ppermute | solution.py:560
  40.3 26.6 %copy-start.13 = (bf16[64,2048]{1,0:T(8,128)(2,1)}, bf16[64,2048]{1,0:T(8,128)(2,1)S(1)}, u32[]{:S(2)}) copy-start(bf16[64,2048]{1,0:T(8,128)(2,1)S(1)} %collective-permute-done.3.refs_4_) | copy-start | bytes 786436
  40.3 11.6 %collective-permute-start.4 = (bf16[64,2048]{1,0:T(8,128)(2,1)S(1)}, bf16[64,2048]{1,0:T(8,128)(2,1)S(1)}, u32[]{:S(2)}, u32[]{:S(2)}) collective-permute-start(bf16[64,2048]{1,0:T(8,128)(2,1)S(1)} %collective-permute-done.3.refs_4_), channel_id=1, source_target_pairs={{8,0},{16,8},{9,1},{17,9},{10,2},{18,10},{11,3},{19,11},{12,4},{20... | collective-permute-start | bytes 786440 | tf_op jit(solution)/shard_map/ppermute | solution.py:565
  44.0 13.3 %copy-start.7 = (bf16[64,2048]{1,0:T(8,128)(2,1)}, bf16[64,2048]{1,0:T(8,128)(2,1)S(1)}, u32[]{:S(2)}) copy-start(bf16[64,2048]{1,0:T(8,128)(2,1)S(1)} %collective-permute-done.10.refs_5_) | copy-start | bytes 786436
  44.0 13.2 %collective-permute-start.11 = (bf16[64,2048]{1,0:T(8,128)(2,1)S(1)}, bf16[64,2048]{1,0:T(8,128)(2,1)S(1)}, u32[]{:S(2)}, u32[]{:S(2)}) collective-permute-start(bf16[64,2048]{1,0:T(8,128)(2,1)S(1)} %collective-permute-done.10.refs_5_), channel_id=1, source_target_pairs={{8,0},{9,1},{10,2},{11,3},{12,4},{13,5},{14,6},{15,7}} | collective-permute-start | bytes 786440 | tf_op jit(solution)/shard_map/ppermute | solution.py:565
  45.3 12.0 %copy-start.8 = (bf16[64,2048]{1,0:T(8,128)(2,1)}, bf16[64,2048]{1,0:T(8,128)(2,1)S(1)}, u32[]{:S(2)}) copy-start(bf16[64,2048]{1,0:T(8,128)(2,1)S(1)} %collective-permute-done.7.refs_2_) | copy-start | bytes 786436
  45.3 11.9 %collective-permute-start.8 = (bf16[64,2048]{1,0:T(8,128)(2,1)S(1)}, bf16[64,2048]{1,0:T(8,128)(2,1)S(1)}, u32[]{:S(2)}, u32[]{:S(2)}) collective-permute-start(bf16[64,2048]{1,0:T(8,128)(2,1)S(1)} %collective-permute-done.7.refs_2_), channel_id=1, source_target_pairs={{16,24},{17,25},{18,26},{19,27},{20,28},{21,29},{22,30},{23,31}} | collective-permute-start | bytes 786440 | tf_op jit(solution)/shard_map/ppermute | solution.py:560
  46.0 20.8 %copy-start.14 = (bf16[64,2048]{1,0:T(8,128)(2,1)}, bf16[64,2048]{1,0:T(8,128)(2,1)S(1)}, u32[]{:S(2)}) copy-start(bf16[64,2048]{1,0:T(8,128)(2,1)S(1)} %collective-permute-done.1.refs_2_) | copy-start | bytes 786436
  46.1 20.8 %collective-permute-start.2 = (bf16[64,2048]{1,0:T(8,128)(2,1)S(1)}, bf16[64,2048]{1,0:T(8,128)(2,1)S(1)}, u32[]{:S(2)}, u32[]{:S(2)}) collective-permute-start(bf16[64,2048]{1,0:T(8,128)(2,1)S(1)} %collective-permute-done.1.refs_2_), channel_id=1, source_target_pairs={{16,24},{17,25},{18,26},{19,27},{20,28},{21,29},{22,30},{23,31}} | collective-permute-start | bytes 786440 | tf_op jit(solution)/shard_map/ppermute | solution.py:560
  51.9 15.0 %copy-start.15 = (bf16[64,2048]{1,0:T(8,128)(2,1)}, bf16[64,2048]{1,0:T(8,128)(2,1)S(1)}, u32[]{:S(2)}) copy-start(bf16[64,2048]{1,0:T(8,128)(2,1)S(1)} %collective-permute-done.4.refs_5_) | copy-start | bytes 786436
  51.9 14.9 %collective-permute-start.5 = (bf16[64,2048]{1,0:T(8,128)(2,1)S(1)}, bf16[64,2048]{1,0:T(8,128)(2,1)S(1)}, u32[]{:S(2)}, u32[]{:S(2)}) collective-permute-start(bf16[64,2048]{1,0:T(8,128)(2,1)S(1)} %collective-permute-done.4.refs_5_), channel_id=1, source_target_pairs={{8,0},{9,1},{10,2},{11,3},{12,4},{13,5},{14,6},{15,7}} | collective-permute-start | bytes 786440 | tf_op jit(solution)/shard_map/ppermute | solution.py:565
  57.3 0.7 copy-start.9
  57.3 0.8 copy-start.10
  64.1 28.9 %all-to-all-start.1 = ((bf16[32,8,2048]{2,1,0:T(8,128)(2,1)}), bf16[32,8,2048]{2,1,0:T(8,128)(2,1)S(1)}, u32[]{:S(2)}, u32[]{:S(2)}) async-start(bf16[32,8,2048]{2,1,0:T(8,128)(2,1)} %bitcast.24), calls=%async_computation.1 | async-start | bytes 2097152 | tf_op jit(solution)/shard_map/all_to_all | solution.py:598
  66.8 0.7 copy-start.16
  66.8 0.8 copy-start.17
  93.0 31.2 %all-to-all-start.2 = ((bf16[32,8,2176]{2,1,0:T(8,128)(2,1)}), bf16[32,8,2176]{2,1,0:T(8,128)(2,1)S(1)}, u32[]{:S(2)}, u32[]{:S(2)}) async-start(bf16[32,8,2176]{2,1,0:T(8,128)(2,1)} %bitcast.23), calls=%async_computation.2 | async-start | bytes 2228224 | tf_op jit(solution)/shard_map/all_to_all | solution.py:598
